TPU v7x, 32 devices: a whole 2x2x4 slice. The times are simulated.
32 devices in a mesh: scene: 2 (over x), blk: 4 (over y, core), grp: 4 (over z).
Axes of the slice: x: 2, y: 2, z: 4, core: 2. Of those that a mesh axis runs over, the one named last changes fastest.
Arguments:
- unary: float32 [32, 8192], P(None, ('scene', 'blk', 'grp')), parts along dimension 1, may hold values from -6 to 6
- member: int32 [8192], P(('scene', 'blk', 'grp')), parts along dimension 0, may hold values from 0 to 4095, each once
- features: bfloat16 [6, 8192], P(None, 'scene'), parts along dimension 1, may hold values from 0 to 3, as said below
- compat: float32 [32, 32], replicated, may hold values from -0.3125 to 0.3125
Outputs:
- marginals: float32 [32, 8192], P(None, ('scene', 'blk', 'grp')), parts along dimension 1
- pairwise: float32 [32, 8192], P(None, ('scene', 'blk', 'grp')), parts along dimension 1
There are 2 independent parts, one for each index of `scene`. A program takes and returns all parts, laid end to end along the dimension named above; an argument that names none is the same for every part. Nothing has to cross between parts.
Inputs may be any that keep to these rules, and one draw needn't show every extreme that they name: `member`: each superpoint appears in exactly one slot. features are non-negative.
All inputs are finite; a program needn't handle non-finite values.
Results may differ from a plain program's by a relative error of at most 0.0004.
Values may be sent and summed in bfloat16 or wider, within the bound.
No kernel may reach another device: no remote copies, remote signals or barrier semaphores. Data moves between devices by JAX's collectives and lax.ppermute only.
A program may use at most 64 MiB of HBM per device.

v0:
```python
import jax
import jax.numpy as jnp
from jax import lax
from jax.sharding import PartitionSpec as P

ITERS = 2


def from_behind(value, axis, steps):
    count = lax.axis_size(axis)
    pairs = [(source, (source + steps) % count) for source in range(count)]
    return lax.ppermute(value, axis, pairs)


def normalize(logits):
    raised = jnp.exp(logits)
    return raised / jnp.sum(raised, axis=0, keepdims=True)


def kernel_tile(rows_f, cols_f):
    left = rows_f.astype(jnp.float32)
    right = cols_f.astype(jnp.float32)
    cross = jnp.dot(
        left.T, right, precision=lax.Precision.HIGHEST, preferred_element_type=jnp.float32
    )
    dist = (
        jnp.sum(left * left, axis=0)[:, None]
        + jnp.sum(right * right, axis=0)[None, :]
        - 2.0 * cross
    )
    return jnp.exp(-0.5 * dist).astype(jnp.bfloat16)


def own_term(full_q, tile):
    return lax.dot_general(
        full_q, tile, (((1,), (1,)), ((), ())), preferred_element_type=jnp.float32
    )


def spread(labels_part, feats_part):
    return (
        lax.all_gather(labels_part, "grp", axis=1, tiled=True),
        lax.all_gather(feats_part, "grp", axis=1, tiled=True),
    )


def travel(visitor):
    return from_behind((visitor[0], visitor[1]), "blk", 1)


def fetch(visitor):
    return spread(visitor[0], visitor[1])


def collect(qb, own_feat, count):
    whole_q, whole_f = spread(qb, own_feat)
    total = own_term(whole_q, kernel_tile(own_feat, whole_f))
    start = (qb, own_feat)

    def advance(step, carry):
        visitor, total = carry
        visitor = travel(visitor)
        full_q, full_f = fetch(visitor)
        return (visitor, total + own_term(full_q, kernel_tile(own_feat, full_f)))

    visitor, total = lax.fori_loop(0, count - 1, advance, (start, total))
    return total


def shards(unary, member, features, compat):
    count = lax.axis_size("blk")
    own_feat = jnp.take(features, member, axis=1)
    probs = normalize(-unary)
    pairwise = jnp.zeros_like(unary)
    for sweep_index in range(ITERS):
        qb = probs.astype(jnp.bfloat16)
        message = collect(qb, own_feat, count) - qb.astype(jnp.float32)
        pairwise = jnp.dot(
            compat, message, precision=lax.Precision.HIGHEST, preferred_element_type=jnp.float32
        )
        probs = normalize(-unary - pairwise)
    return (probs, pairwise)


def solution(mesh):
    in_specs = (P(None, ("scene", "blk", "grp")), P(("scene", "blk", "grp")), P(None, "scene"), P())
    out_specs = (P(None, ("scene", "blk", "grp")), P(None, ("scene", "blk", "grp")))
    return jax.shard_map(shards, mesh=mesh, in_specs=in_specs, out_specs=out_specs, check_vma=False)
```

profile of v0, /device:TPU:0, one launch (start us, length us, event | category | flops | bytes accessed | tf_op | source)
XLA Modules:
  0.0 228.9 jit_solution(11178927463384446548)
XLA Ops:
  3.1 15.6 %all_gather.23 = bf16[6,1024]{0,1:T(8,128)(2,1)S(1)} all-gather(bf16[6,256]{0,1:T(8,128)(2,1)S(1)} %get-tuple-element.89), channel_id=1, replica_groups=mesh['scene'=2,'blk'=4,'grp'=4] {'grp'}, dimensions={1}, use_global_device_ids=true | all-gather | bytes 15360 | tf_op jit(solution)/shard_map/all_gather | solution.py:43
  19.8 13.3 %all_gather.22 = bf16[32,1024]{1,0:T(8,128)(2,1)S(1)} all-gather(bf16[32,256]{1,0:T(8,128)(2,1)S(1)} %divide_convert_fusion.1), channel_id=1, replica_groups=mesh['scene'=2,'blk'=4,'grp'=4] {'grp'}, dimensions={1}, use_global_device_ids=true | all-gather | bytes 81920 | tf_op jit(solution)/shard_map/all_gather | solution.py:42
  33.4 90.5 %while.28 = (s32[]{:T(128)}, bf16[32,256]{1,0:T(8,128)(2,1)S(1)}, bf16[6,256]{1,0:T(8,128)(2,1)S(1)}, f32[32,256]{1,0:T(8,128)S(1)}, bf16[6,256]{1,0:T(8,128)(2,1)S(1)}, /*index=5*/s32[]{:T(128)}) while((s32[]{:T(128)}, bf16[32,256]{1,0:T(8,128)(2,1)S(1)}, bf16[6,256]{1,0:T(8,128)(2,1)S(1)}, f32[32,256]{1,0:T(8,128)S(1)}, ...), condition=%wide.region_6.7_spmd, body=%wide.region_3.0_spmd.sunk | while | flops 21263616 | bytes 1434773 | solution.py:66
  33.5 1.6 collective-permute-start
  36.5 13.1 %all_gather.29 = bf16[6,1024]{1,0:T(8,128)(2,1)S(1)} all-gather(bf16[6,256]{1,0:T(8,128)(2,1)S(1)} %collective-permute-done.1), channel_id=1, replica_groups=mesh['scene'=2,'blk'=4,'grp'=4] {'grp'}, dimensions={1}, use_global_device_ids=true | all-gather | bytes 15360 | tf_op jit(solution)/shard_map/while/body/eval_jaxpr/all_gather | solution.py:43
  50.1 13.3 %all_gather.30 = bf16[32,1024]{1,0:T(8,128)(2,1)S(1)} all-gather(bf16[32,256]{1,0:T(8,128)(2,1)S(1)} %collective-permute-done), channel_id=1, replica_groups=mesh['scene'=2,'blk'=4,'grp'=4] {'grp'}, dimensions={1}, use_global_device_ids=true | all-gather | bytes 81920 | tf_op jit(solution)/shard_map/while/body/eval_jaxpr/all_gather | solution.py:42
  63.7 1.6 collective-permute-start
  66.7 13.1 %all_gather.29 = bf16[6,1024]{1,0:T(8,128)(2,1)S(1)} all-gather(bf16[6,256]{1,0:T(8,128)(2,1)S(1)} %collective-permute-done.1), channel_id=1, replica_groups=mesh['scene'=2,'blk'=4,'grp'=4] {'grp'}, dimensions={1}, use_global_device_ids=true | all-gather | bytes 15360 | tf_op jit(solution)/shard_map/while/body/eval_jaxpr/all_gather | solution.py:43
  80.3 13.2 %all_gather.30 = bf16[32,1024]{1,0:T(8,128)(2,1)S(1)} all-gather(bf16[32,256]{1,0:T(8,128)(2,1)S(1)} %collective-permute-done), channel_id=1, replica_groups=mesh['scene'=2,'blk'=4,'grp'=4] {'grp'}, dimensions={1}, use_global_device_ids=true | all-gather | bytes 81920 | tf_op jit(solution)/shard_map/while/body/eval_jaxpr/all_gather | solution.py:42
  93.8 1.6 collective-permute-start
  96.9 13.1 %all_gather.29 = bf16[6,1024]{1,0:T(8,128)(2,1)S(1)} all-gather(bf16[6,256]{1,0:T(8,128)(2,1)S(1)} %collective-permute-done.1), channel_id=1, replica_groups=mesh['scene'=2,'blk'=4,'grp'=4] {'grp'}, dimensions={1}, use_global_device_ids=true | all-gather | bytes 15360 | tf_op jit(solution)/shard_map/while/body/eval_jaxpr/all_gather | solution.py:43
  110.5 13.2 %all_gather.30 = bf16[32,1024]{1,0:T(8,128)(2,1)S(1)} all-gather(bf16[32,256]{1,0:T(8,128)(2,1)S(1)} %collective-permute-done), channel_id=1, replica_groups=mesh['scene'=2,'blk'=4,'grp'=4] {'grp'}, dimensions={1}, use_global_device_ids=true | all-gather | bytes 81920 | tf_op jit(solution)/shard_map/while/body/eval_jaxpr/all_gather | solution.py:42
  124.1 13.1 %all_gather.24 = bf16[32,1024]{1,0:T(8,128)(2,1)S(1)} all-gather(bf16[32,256]{1,0:T(8,128)(2,1)S(1)} %divide_convert_fusion), channel_id=1, replica_groups=mesh['scene'=2,'blk'=4,'grp'=4] {'grp'}, dimensions={1}, use_global_device_ids=true | all-gather | bytes 81920 | tf_op jit(solution)/shard_map/all_gather | solution.py:42
  137.5 90.5 %while.29 = (s32[]{:T(128)}, bf16[32,256]{1,0:T(8,128)(2,1)S(1)}, bf16[6,256]{1,0:T(8,128)(2,1)S(1)}, f32[32,256]{1,0:T(8,128)S(1)}, bf16[6,256]{1,0:T(8,128)(2,1)S(1)}, /*index=5*/s32[]{:T(128)}) while((s32[]{:T(128)}, bf16[32,256]{1,0:T(8,128)(2,1)S(1)}, bf16[6,256]{1,0:T(8,128)(2,1)S(1)}, f32[32,256]{1,0:T(8,128)S(1)}, ...), condition=%wide.region_11.12_spmd, body=%wide.region_8.0_spmd.sunk | while | flops 21263616 | bytes 1434773 | solution.py:66
  137.6 1.6 collective-permute-start.2
  140.6 13.1 %all_gather.31 = bf16[6,1024]{1,0:T(8,128)(2,1)S(1)} all-gather(bf16[6,256]{1,0:T(8,128)(2,1)S(1)} %collective-permute-done.3), channel_id=1, replica_groups=mesh['scene'=2,'blk'=4,'grp'=4] {'grp'}, dimensions={1}, use_global_device_ids=true | all-gather | bytes 15360 | tf_op jit(solution)/shard_map/while/body/eval_jaxpr/all_gather | solution.py:43
  154.3 13.2 %all_gather.32 = bf16[32,1024]{1,0:T(8,128)(2,1)S(1)} all-gather(bf16[32,256]{1,0:T(8,128)(2,1)S(1)} %collective-permute-done.2), channel_id=1, replica_groups=mesh['scene'=2,'blk'=4,'grp'=4] {'grp'}, dimensions={1}, use_global_device_ids=true | all-gather | bytes 81920 | tf_op jit(solution)/shard_map/while/body/eval_jaxpr/all_gather | solution.py:42
  167.8 1.6 collective-permute-start.2
  169.4 1.4 collective-permute-done.3
  170.8 13.1 %all_gather.31 = bf16[6,1024]{1,0:T(8,128)(2,1)S(1)} all-gather(bf16[6,256]{1,0:T(8,128)(2,1)S(1)} %collective-permute-done.3), channel_id=1, replica_groups=mesh['scene'=2,'blk'=4,'grp'=4] {'grp'}, dimensions={1}, use_global_device_ids=true | all-gather | bytes 15360 | tf_op jit(solution)/shard_map/while/body/eval_jaxpr/all_gather | solution.py:43
  184.4 13.2 %all_gather.32 = bf16[32,1024]{1,0:T(8,128)(2,1)S(1)} all-gather(bf16[32,256]{1,0:T(8,128)(2,1)S(1)} %collective-permute-done.2), channel_id=1, replica_groups=mesh['scene'=2,'blk'=4,'grp'=4] {'grp'}, dimensions={1}, use_global_device_ids=true | all-gather | bytes 81920 | tf_op jit(solution)/shard_map/while/body/eval_jaxpr/all_gather | solution.py:42
  198.0 1.6 collective-permute-start.2
  201.0 13.1 %all_gather.31 = bf16[6,1024]{1,0:T(8,128)(2,1)S(1)} all-gather(bf16[6,256]{1,0:T(8,128)(2,1)S(1)} %collective-permute-done.3), channel_id=1, replica_groups=mesh['scene'=2,'blk'=4,'grp'=4] {'grp'}, dimensions={1}, use_global_device_ids=true | all-gather | bytes 15360 | tf_op jit(solution)/shard_map/while/body/eval_jaxpr/all_gather | solution.py:43
  214.6 13.2 %all_gather.32 = bf16[32,1024]{1,0:T(8,128)(2,1)S(1)} all-gather(bf16[32,256]{1,0:T(8,128)(2,1)S(1)} %collective-permute-done.2), channel_id=1, replica_groups=mesh['scene'=2,'blk'=4,'grp'=4] {'grp'}, dimensions={1}, use_global_device_ids=true | all-gather | bytes 81920 | tf_op jit(solution)/shard_map/while/body/eval_jaxpr/all_gather | solution.py:42
  (81 shorter events, 16.8 us)
Async XLA Ops:
  0.6 123.3 %copy-start = (f32[32,32]{1,0:T(8,128)S(1)}, f32[32,32]{1,0:T(8,128)}, u32[]{:S(2)}) copy-start(f32[32,32]{1,0:T(8,128)} %param.11) | copy-start | bytes 12292
  0.6 1.4 copy-start.3
  18.9 0.8 copy-start.1
  33.4 3.1 %collective-permute-start.1 = (bf16[6,256]{1,0:T(8,128)(2,1)S(1)}, bf16[6,256]{1,0:T(8,128)(2,1)S(1)}, u32[]{:S(2)}, u32[]{:S(2)}) collective-permute-start(bf16[6,256]{1,0:T(8,128)(2,1)S(1)} %get-tuple-element.164), channel_id=1, source_target_pairs={{0,4},{4,8},{8,12},{12,0},{1,5},{5,9},{9,13},{13,1},{2,6},{6,10},{... | collective-permute-start | bytes 9224 | tf_op jit(solution)/shard_map/while/body/eval_jaxpr/ppermute | solution.py:12
  33.5 16.6 %collective-permute-start = (bf16[32,256]{1,0:T(8,128)(2,1)S(1)}, bf16[32,256]{1,0:T(8,128)(2,1)S(1)}, u32[]{:S(2)}, u32[]{:S(2)}) collective-permute-start(bf16[32,256]{1,0:T(8,128)(2,1)S(1)} %get-tuple-element.163), channel_id=1, source_target_pairs={{0,4},{4,8},{8,12},{12,0},{1,5},{5,9},{9,13},{13,1},{2,6},{6,10},{... | collective-permute-start | bytes 49160 | tf_op jit(solution)/shard_map/while/body/eval_jaxpr/ppermute | solution.py:12
  63.6 3.1 %collective-permute-start.1 = (bf16[6,256]{1,0:T(8,128)(2,1)S(1)}, bf16[6,256]{1,0:T(8,128)(2,1)S(1)}, u32[]{:S(2)}, u32[]{:S(2)}) collective-permute-start(bf16[6,256]{1,0:T(8,128)(2,1)S(1)} %get-tuple-element.164), channel_id=1, source_target_pairs={{0,4},{4,8},{8,12},{12,0},{1,5},{5,9},{9,13},{13,1},{2,6},{6,10},{... | collective-permute-start | bytes 9224 | tf_op jit(solution)/shard_map/while/body/eval_jaxpr/ppermute | solution.py:12
  63.7 16.6 %collective-permute-start = (bf16[32,256]{1,0:T(8,128)(2,1)S(1)}, bf16[32,256]{1,0:T(8,128)(2,1)S(1)}, u32[]{:S(2)}, u32[]{:S(2)}) collective-permute-start(bf16[32,256]{1,0:T(8,128)(2,1)S(1)} %get-tuple-element.163), channel_id=1, source_target_pairs={{0,4},{4,8},{8,12},{12,0},{1,5},{5,9},{9,13},{13,1},{2,6},{6,10},{... | collective-permute-start | bytes 49160 | tf_op jit(solution)/shard_map/while/body/eval_jaxpr/ppermute | solution.py:12
  93.8 3.1 %collective-permute-start.1 = (bf16[6,256]{1,0:T(8,128)(2,1)S(1)}, bf16[6,256]{1,0:T(8,128)(2,1)S(1)}, u32[]{:S(2)}, u32[]{:S(2)}) collective-permute-start(bf16[6,256]{1,0:T(8,128)(2,1)S(1)} %get-tuple-element.164), channel_id=1, source_target_pairs={{0,4},{4,8},{8,12},{12,0},{1,5},{5,9},{9,13},{13,1},{2,6},{6,10},{... | collective-permute-start | bytes 9224 | tf_op jit(solution)/shard_map/while/body/eval_jaxpr/ppermute | solution.py:12
  93.8 16.6 %collective-permute-start = (bf16[32,256]{1,0:T(8,128)(2,1)S(1)}, bf16[32,256]{1,0:T(8,128)(2,1)S(1)}, u32[]{:S(2)}, u32[]{:S(2)}) collective-permute-start(bf16[32,256]{1,0:T(8,128)(2,1)S(1)} %get-tuple-element.163), channel_id=1, source_target_pairs={{0,4},{4,8},{8,12},{12,0},{1,5},{5,9},{9,13},{13,1},{2,6},{6,10},{... | collective-permute-start | bytes 49160 | tf_op jit(solution)/shard_map/while/body/eval_jaxpr/ppermute | solution.py:12
  137.6 3.1 %collective-permute-start.3 = (bf16[6,256]{1,0:T(8,128)(2,1)S(1)}, bf16[6,256]{1,0:T(8,128)(2,1)S(1)}, u32[]{:S(2)}, u32[]{:S(2)}) collective-permute-start(bf16[6,256]{1,0:T(8,128)(2,1)S(1)} %get-tuple-element.182), channel_id=1, source_target_pairs={{0,4},{4,8},{8,12},{12,0},{1,5},{5,9},{9,13},{13,1},{2,6},{6,10},{... | collective-permute-start | bytes 9224 | tf_op jit(solution)/shard_map/while/body/eval_jaxpr/ppermute | solution.py:12
  137.6 16.6 %collective-permute-start.2 = (bf16[32,256]{1,0:T(8,128)(2,1)S(1)}, bf16[32,256]{1,0:T(8,128)(2,1)S(1)}, u32[]{:S(2)}, u32[]{:S(2)}) collective-permute-start(bf16[32,256]{1,0:T(8,128)(2,1)S(1)} %get-tuple-element.181), channel_id=1, source_target_pairs={{0,4},{4,8},{8,12},{12,0},{1,5},{5,9},{9,13},{13,1},{2,6},{6,10},{... | collective-permute-start | bytes 49160 | tf_op jit(solution)/shard_map/while/body/eval_jaxpr/ppermute | solution.py:12
  167.8 3.1 %collective-permute-start.3 = (bf16[6,256]{1,0:T(8,128)(2,1)S(1)}, bf16[6,256]{1,0:T(8,128)(2,1)S(1)}, u32[]{:S(2)}, u32[]{:S(2)}) collective-permute-start(bf16[6,256]{1,0:T(8,128)(2,1)S(1)} %get-tuple-element.182), channel_id=1, source_target_pairs={{0,4},{4,8},{8,12},{12,0},{1,5},{5,9},{9,13},{13,1},{2,6},{6,10},{... | collective-permute-start | bytes 9224 | tf_op jit(solution)/shard_map/while/body/eval_jaxpr/ppermute | solution.py:12
  167.8 16.6 %collective-permute-start.2 = (bf16[32,256]{1,0:T(8,128)(2,1)S(1)}, bf16[32,256]{1,0:T(8,128)(2,1)S(1)}, u32[]{:S(2)}, u32[]{:S(2)}) collective-permute-start(bf16[32,256]{1,0:T(8,128)(2,1)S(1)} %get-tuple-element.181), channel_id=1, source_target_pairs={{0,4},{4,8},{8,12},{12,0},{1,5},{5,9},{9,13},{13,1},{2,6},{6,10},{... | collective-permute-start | bytes 49160 | tf_op jit(solution)/shard_map/while/body/eval_jaxpr/ppermute | solution.py:12
  197.9 3.1 %collective-permute-start.3 = (bf16[6,256]{1,0:T(8,128)(2,1)S(1)}, bf16[6,256]{1,0:T(8,128)(2,1)S(1)}, u32[]{:S(2)}, u32[]{:S(2)}) collective-permute-start(bf16[6,256]{1,0:T(8,128)(2,1)S(1)} %get-tuple-element.182), channel_id=1, source_target_pairs={{0,4},{4,8},{8,12},{12,0},{1,5},{5,9},{9,13},{13,1},{2,6},{6,10},{... | collective-permute-start | bytes 9224 | tf_op jit(solution)/shard_map/while/body/eval_jaxpr/ppermute | solution.py:12
  198.0 16.6 %collective-permute-start.2 = (bf16[32,256]{1,0:T(8,128)(2,1)S(1)}, bf16[32,256]{1,0:T(8,128)(2,1)S(1)}, u32[]{:S(2)}, u32[]{:S(2)}) collective-permute-start(bf16[32,256]{1,0:T(8,128)(2,1)S(1)} %get-tuple-element.181), channel_id=1, source_target_pairs={{0,4},{4,8},{8,12},{12,0},{1,5},{5,9},{9,13},{13,1},{2,6},{6,10},{... | collective-permute-start | bytes 49160 | tf_op jit(solution)/shard_map/while/body/eval_jaxpr/ppermute | solution.py:12
  228.2 0.6 copy-start.2
where the time goes:
time: 229 us
  blocking collectives  200 us (87%)
  starting transfers between devices  9.93 us (4%)
  waiting for transfers between devices  8.41 us (4%)
  matrix products  5.49 us (2%)
  local copies, waits for them, and re-layouts  2.72 us (1%)
    all_gather x8, blocking collectives, spread(): lax.all_gather(labels_part, 'grp', axis=1, tiled=True)  106 us
    all_gather x7, blocking collectives, spread(): lax.all_gather(feats_part, 'grp', axis=1, tiled=True)  94.3 us
    ppermute x12, starting transfers between devices, from_behind(): return lax.ppermute(value, axis, pairs)  9.93 us
    ppermute x12, waiting for transfers between devices, from_behind(): return lax.ppermute(value, axis, pairs)  8.41 us
  transfers between devices with their start and end apart: 12, of which 6 were waited for; matrix products, arithmetic and copies ran while one was open for 1% of the time, Pallas kernels for 0%

commit v1 on v0

v1 whole, which is shorter than its diff:
```python
import jax
import jax.numpy as jnp
from jax import lax
from jax.experimental import pallas as pl
from jax.experimental.pallas import tpu as pltpu
from jax.sharding import PartitionSpec as P

AUX = 16
VMEM_LIMIT = 56 * 1024 * 1024


def normalize(logits):
    raised = jnp.exp(logits)
    return raised / jnp.sum(raised, axis=0, keepdims=True)


def three_parts(value):
    high = value.astype(jnp.bfloat16).astype(jnp.float32)
    middle = (value - high).astype(jnp.bfloat16).astype(jnp.float32)
    return [high, middle, value - high - middle]


def prepare_kernel(feats_ref, unary_ref, packed_ref, rows_ref):
    labels, own = unary_ref.shape
    feats = feats_ref[...].astype(jnp.float32)
    norms = three_parts(-0.5 * jnp.sum(feats * feats, axis=0, keepdims=True))
    ones = jnp.ones((3, own), jnp.float32)
    spare = jnp.zeros((AUX - feats.shape[0] - 6, own), jnp.float32)
    columns = jnp.concatenate([feats] + norms + [ones, spare], axis=0)
    rows = jnp.concatenate([feats, ones] + norms + [spare], axis=0)
    packed_ref[pl.ds(0, labels), :] = normalize(-unary_ref[...]).astype(jnp.bfloat16)
    packed_ref[pl.ds(labels, AUX), :] = columns.astype(jnp.bfloat16)
    rows_ref[...] = rows.astype(jnp.bfloat16)


def over_blocks(count, body, start):
    if count <= 16:
        for index in range(count):
            start = body(index, start)
        return start
    return lax.fori_loop(0, count, body, start)


def finish(message, qb, unary_ref, compat_ref):
    message = message - qb.astype(jnp.float32)
    pairwise = jnp.dot(
        compat_ref[...], message, precision=lax.Precision.HIGHEST,
        preferred_element_type=jnp.float32,
    )
    return normalize(-unary_ref[...] - pairwise), pairwise


def first_kernel(labels, count, rows_ref, own_ref, unary_ref, compat_ref, packed_ref, tile_ref, q_ref):
    rows = rows_ref[...]

    def body(index, total):
        columns = packed_ref[index, pl.ds(labels, AUX), :]
        exponent = lax.dot_general(
            columns, rows, (((0,), (0,)), ((), ())), preferred_element_type=jnp.float32
        )
        tile = jnp.exp(exponent).astype(jnp.bfloat16)
        tile_ref[index] = tile
        return total + jnp.dot(
            packed_ref[index, pl.ds(0, labels), :], tile, preferred_element_type=jnp.float32
        )

    total = over_blocks(count, body, jnp.zeros(unary_ref.shape, jnp.float32))
    probs, _ = finish(total, own_ref[pl.ds(0, labels), :], unary_ref, compat_ref)
    q_ref[...] = probs.astype(jnp.bfloat16)


def second_kernel(count, own_ref, unary_ref, compat_ref, q_ref, tile_ref, probs_ref, pairwise_ref):
    def body(index, total):
        return total + jnp.dot(q_ref[index], tile_ref[index], preferred_element_type=jnp.float32)

    total = over_blocks(count, body, jnp.zeros(unary_ref.shape, jnp.float32))
    probs, pairwise = finish(total, own_ref[...], unary_ref, compat_ref)
    probs_ref[...] = probs
    pairwise_ref[...] = pairwise


def exchange(value):
    for axis in ("grp", "blk"):
        count = lax.axis_size(axis)
        copies = jnp.broadcast_to(value[None], (count,) + value.shape)
        value = lax.all_to_all(copies, axis, 0, 0)
    return value.reshape((-1,) + value.shape[2:])


def shards(unary, member, features, compat):
    labels, own = unary.shape
    count = lax.axis_size("blk") * lax.axis_size("grp")
    own_feat = jnp.take(features, member, axis=1)
    params = pltpu.CompilerParams(vmem_limit_bytes=VMEM_LIMIT)
    packed, rows = pl.pallas_call(
        prepare_kernel,
        out_shape=(
            jax.ShapeDtypeStruct((labels + AUX, own), jnp.bfloat16),
            jax.ShapeDtypeStruct((AUX, own), jnp.bfloat16),
        ),
        compiler_params=params,
    )(own_feat, unary)
    everything = exchange(packed)
    tile, qb = pl.pallas_call(
        lambda *refs: first_kernel(labels, count, *refs),
        out_shape=(
            jax.ShapeDtypeStruct((count, own, own), jnp.bfloat16),
            jax.ShapeDtypeStruct((labels, own), jnp.bfloat16),
        ),
        compiler_params=params,
    )(rows, packed, unary, compat, everything)
    return pl.pallas_call(
        lambda *refs: second_kernel(count, *refs),
        out_shape=(
            jax.ShapeDtypeStruct((labels, own), jnp.float32),
            jax.ShapeDtypeStruct((labels, own), jnp.float32),
        ),
        compiler_params=params,
    )(qb, unary, compat, exchange(qb), tile)


def solution(mesh):
    in_specs = (P(None, ("scene", "blk", "grp")), P(("scene", "blk", "grp")), P(None, "scene"), P())
    out_specs = (P(None, ("scene", "blk", "grp")), P(None, ("scene", "blk", "grp")))
    return jax.shard_map(shards, mesh=mesh, in_specs=in_specs, out_specs=out_specs, check_vma=False)
```

time: 229 us -> 55.1 us (0.24)
  blocking collectives: 200 us -> 39.7 us
  starting transfers between devices: 9.93 us -> 0 us
  waiting for transfers between devices: 8.41 us -> 0 us
  Pallas kernels: 0 us -> 8.4 us
  matrix products: 5.49 us -> 0 us
    all_gather x15 -> x0, blocking collectives: 200 us -> none  [the longest x8 106 us: spread(): lax.all_gather(labels_part, 'grp', axis=1, tiled=True)]
    all_to_all x0 -> x4, blocking collectives: none -> 39.7 us  [exchange(): value = lax.all_to_all(copies, axis, 0, 0)]
    ppermute x12 -> x0, starting transfers between devices: 9.93 us -> none  [from_behind(): return lax.ppermute(value, axis, pairs)]
    ppermute x12 -> x0, waiting for transfers between devices: 8.41 us -> none  [from_behind(): return lax.ppermute(value, axis, pairs)]
    pallas_call x0 -> x3, Pallas kernels: none -> 8.4 us  [the longest x1 3.96 us: shards(): pl.pallas_call(lambda *refs: first_kernel(labels, count, *refs), out_shap...]
    dot_general x17 -> x0, matrix products: 5.49 us -> none  [the longest x7 3.03 us: kernel_tile(): jnp.dot(left.T, right, precision=lax.Precision.HIGHEST, preferred_element...]
  transfers between devices with their start and end apart: 12 -> 0, of which waited for: 6 -> 0; matrix products, arithmetic and copies ran while one was open for 1% -> 0% of each run, Pallas kernels for 0% -> 0%
where the time goes in v1:
time: 55.1 us; the launch traced here: 54.5 us
  blocking collectives  39.7 us (72%)
  Pallas kernels  8.4 us (15%)
  local copies, waits for them, and re-layouts  3.8 us (7%)
  other arithmetic  1.99 us (4%)
  between operations  0.65 us (1%)
    all_to_all x4, blocking collectives, exchange(): value = lax.all_to_all(copies, axis, 0, 0)  39.7 us
    pallas_call x1, Pallas kernels, shards(): pl.pallas_call(lambda *refs: first_kernel(labels, count, *refs), out_shap...  3.96 us
    pallas_call x1, Pallas kernels, shards(): pl.pallas_call(lambda *refs: second_kernel(count, *refs), out_shape=(jax....  3.05 us
    broadcast_in_dim x4, local copies, waits for them, and re-layouts, exchange(): copies = jnp.broadcast_to(value[None], (count,) + value.shape)  1.51 us
    pallas_call x1, Pallas kernels, shards(): pl.pallas_call(prepare_kernel, out_shape=(jax.ShapeDtypeStruct((labels +...  1.4 us
    unnamed x1, local copies, waits for them, and re-layouts  1.35 us
    select_n x2, other arithmetic, shards(): own_feat = jnp.take(features, member, axis=1)  1.3 us

profile of v1, /device:TPU:0, one launch (start us, length us, event | category | flops | bytes accessed | tf_op | source)
XLA Modules:
  0.0 54.5 jit_solution(14818747984820601196)
XLA Ops:
  0.6 0.7 %compare_and_fusion = pred[256]{0:T(512)(128)(4,1)S(1)} fusion(s32[256]{0:T(256)} %param.5), kind=kLoop, calls=%fused_computation.4 | loop fusion | flops 1536 | bytes 1280 | tf_op jit(solution)/shard_map/jit(_take)/and | solution.py:93
  1.3 0.7 %compare_select_fusion = s32[256]{0:T(256)S(1)} fusion(s32[256]{0:T(256)} %param.5), kind=kLoop, calls=%fused_computation.3 | loop fusion | flops 768 | bytes 2048 | tf_op jit(solution)/shard_map/jit(_take)/jit(_where)/select_n | solution.py:93
  2.0 1.4 %copy.6 = bf16[6,4096]{0,1:T(8,128)(2,1)S(1)} copy(bf16[6,4096]{1,0:T(8,128)(2,1)} %param.6) | data formatting | bytes 98304 | tf_op args[2]
  3.4 0.9 %gather_fusion = bf16[256,6]{1,0:T(8,128)(2,1)S(1)} fusion(bf16[6,4096]{0,1:T(8,128)(2,1)S(1)} %copy.6, s32[1024]{0:T(1024)S(1)} %pad_clamp_fusion), kind=kCustom, calls=%fused_computation | custom fusion | bytes 7168 | tf_op jit(solution)/shard_map/jit(_take)/gather | solution.py:93
  4.2 0.1 copy.7
  4.3 0.6 %select_bitcast_fusion.feats_ref = bf16[6,256]{1,0:T(8,128)(2,1)} fusion(bf16[256,6]{0,1:T(8,128)(2,1)S(1)} %copy.7, pred[256]{0:T(512)(128)(4,1)S(1)} %compare_and_fusion), kind=kLoop, calls=%fused_computation.2 | loop fusion | flops 1536 | bytes 6400 | tf_op jit(solution)/shard_map/jit(_take)/select_n | solution.py:93
  4.9 1.4 %shard_map.59 = (bf16[48,256]{1,0:T(8,128)(2,1)}, bf16[16,256]{1,0:T(8,128)(2,1)}) custom-call(bf16[6,256]{1,0:T(8,128)(2,1)} %select_bitcast_fusion.feats_ref, f32[32,256]{1,0:T(8,128)} %refs_1_.1), custom_call_target="tpu_custom_call" | custom-call | tf_op jit(solution)/shard_map/pallas_call | solution.py:95
  6.3 0.7 %broadcast_in_dim.39 = bf16[4,48,256]{2,1,0:T(8,128)(2,1)S(1)} broadcast(bf16[48,256]{1,0:T(8,128)(2,1)} %get-tuple-element.7.refs_1_), dimensions={1,2} | broadcast | bytes 122880 | tf_op jit(solution)/shard_map/broadcast_in_dim | solution.py:85
  7.1 11.9 %all_to_all.20 = bf16[4,48,256]{2,1,0:T(8,128)(2,1)S(1)} all-to-all(bf16[4,48,256]{2,1,0:T(8,128)(2,1)S(1)} %broadcast_in_dim.39), channel_id=1, replica_groups=mesh['scene'=2,'blk'=4,'grp'=4] {'grp'}, dimensions={0} | all-to-all | bytes 196608 | tf_op jit(solution)/shard_map/all_to_all | solution.py:86
  19.0 10.5 %all_to_all.21 = bf16[4,4,48,256]{3,2,1,0:T(8,128)(2,1)} all-to-all(bf16[4,4,48,256]{3,2,1,0:T(8,128)(2,1)S(1)} %broadcast_in_dim.40), channel_id=1, replica_groups=mesh['scene'=2,'blk'=4,'grp'=4] {'blk'}, dimensions={0} | all-to-all | bytes 786432 | tf_op jit(solution)/shard_map/all_to_all | solution.py:86
  29.6 4.0 %shard_map.60 = (bf16[16,256,256]{2,1,0:T(8,128)(2,1)}, bf16[32,256]{1,0:T(8,128)(2,1)}) custom-call(bf16[16,256]{1,0:T(8,128)(2,1)} %get-tuple-element.6.refs_0_, bf16[48,256]{1,0:T(8,128)(2,1)} %get-tuple-element.7.refs_1_, f32[32,256]{1,0:T(8,128)} %refs_1_.1, f32[32,32]{1,0:T(8,128)} %refs_2_.3, bf16[16,48,256]{2,1,0:T(8,128)(2,1)} %bitcast.4), custom_call_target="tpu_custom_call" | custom-call | tf_op jit(solution)/shard_map/pallas_call | solution.py:104
  33.5 0.7 %broadcast_in_dim.41 = bf16[4,32,256]{2,1,0:T(8,128)(2,1)S(1)} broadcast(bf16[32,256]{1,0:T(8,128)(2,1)} %get-tuple-element.8.refs_0_), dimensions={1,2} | broadcast | bytes 81920 | tf_op jit(solution)/shard_map/broadcast_in_dim | solution.py:85
  34.2 8.1 %all_to_all.22 = bf16[4,32,256]{2,1,0:T(8,128)(2,1)S(1)} all-to-all(bf16[4,32,256]{2,1,0:T(8,128)(2,1)S(1)} %broadcast_in_dim.41), channel_id=1, replica_groups=mesh['scene'=2,'blk'=4,'grp'=4] {'grp'}, dimensions={0} | all-to-all | bytes 131072 | tf_op jit(solution)/shard_map/all_to_all | solution.py:86
  42.4 9.1 %all_to_all.23 = bf16[4,4,32,256]{3,2,1,0:T(8,128)(2,1)} all-to-all(bf16[4,4,32,256]{3,2,1,0:T(8,128)(2,1)S(1)} %broadcast_in_dim.42), channel_id=1, replica_groups=mesh['scene'=2,'blk'=4,'grp'=4] {'blk'}, dimensions={0} | all-to-all | bytes 524288 | tf_op jit(solution)/shard_map/all_to_all | solution.py:86
  51.5 3.0 %shard_map.61 = (f32[32,256]{1,0:T(8,128)}, f32[32,256]{1,0:T(8,128)}) custom-call(bf16[32,256]{1,0:T(8,128)(2,1)} %get-tuple-element.8.refs_0_, f32[32,256]{1,0:T(8,128)} %refs_1_.1, f32[32,32]{1,0:T(8,128)} %refs_2_.3, bf16[16,32,256]{2,1,0:T(8,128)(2,1)} %bitcast.5, bf16[16,256,256]{2,1,0:T(8,128)(2,1)} %get-tuple-element.9.refs_4_), custom_call_target="tpu_custom_call" | custom-call | tf_op jit(solution)/shard_map/pallas_call | solution.py:112
  (3 shorter events, 0.1 us)

commit v2 on v1

--- a/solution.py
+++ b/solution.py
@@ -1,3 +1,4 @@
+import functools
 import jax
 import jax.numpy as jnp
 from jax import lax
@@ -33,12 +34,18 @@
     rows_ref[...] = rows.astype(jnp.bfloat16)
 
 
-def over_blocks(count, body, start):
-    if count <= 16:
-        for index in range(count):
-            start = body(index, start)
-        return start
-    return lax.fori_loop(0, count, body, start)
+def over_blocks(refs, body, start):
+    base = 0
+    for ref in refs:
+        size = ref.shape[0]
+        if size <= 16:
+            for index in range(size):
+                start = body(ref, index, base + index, start)
+        else:
+            step = lambda index, total, ref=ref, base=base: body(ref, index, base + index, total)
+            start = lax.fori_loop(0, size, step, start)
+        base += size
+    return start
 
 
 def finish(message, qb, unary_ref, compat_ref):
@@ -50,41 +57,65 @@
     return normalize(-unary_ref[...] - pairwise), pairwise
 
 
-def first_kernel(labels, count, rows_ref, own_ref, unary_ref, compat_ref, packed_ref, tile_ref, q_ref):
+def first_kernel(labels, *refs):
+    rows_ref, own_ref, unary_ref, compat_ref, *packed_refs = refs[:-2]
+    tile_ref, q_ref = refs[-2:]
     rows = rows_ref[...]
 
-    def body(index, total):
+    def body(packed_ref, index, place, total):
         columns = packed_ref[index, pl.ds(labels, AUX), :]
         exponent = lax.dot_general(
             columns, rows, (((0,), (0,)), ((), ())), preferred_element_type=jnp.float32
         )
         tile = jnp.exp(exponent).astype(jnp.bfloat16)
-        tile_ref[index] = tile
+        tile_ref[place] = tile
         return total + jnp.dot(
             packed_ref[index, pl.ds(0, labels), :], tile, preferred_element_type=jnp.float32
         )
 
-    total = over_blocks(count, body, jnp.zeros(unary_ref.shape, jnp.float32))
+    total = over_blocks(packed_refs, body, jnp.zeros(unary_ref.shape, jnp.float32))
     probs, _ = finish(total, own_ref[pl.ds(0, labels), :], unary_ref, compat_ref)
     q_ref[...] = probs.astype(jnp.bfloat16)
 
 
-def second_kernel(count, own_ref, unary_ref, compat_ref, q_ref, tile_ref, probs_ref, pairwise_ref):
-    def body(index, total):
-        return total + jnp.dot(q_ref[index], tile_ref[index], preferred_element_type=jnp.float32)
+def second_kernel(*refs):
+    own_ref, unary_ref, compat_ref, tile_ref, *q_refs = refs[:-2]
+    probs_ref, pairwise_ref = refs[-2:]
 
-    total = over_blocks(count, body, jnp.zeros(unary_ref.shape, jnp.float32))
+    def body(q_ref, index, place, total):
+        return total + jnp.dot(
+            q_ref[index], tile_ref[place], preferred_element_type=jnp.float32
+        )
+
+    total = over_blocks(q_refs, body, jnp.zeros(unary_ref.shape, jnp.float32))
     probs, pairwise = finish(total, own_ref[...], unary_ref, compat_ref)
     probs_ref[...] = probs
     pairwise_ref[...] = pairwise
 
 
-def exchange(value):
-    for axis in ("grp", "blk"):
-        count = lax.axis_size(axis)
-        copies = jnp.broadcast_to(value[None], (count,) + value.shape)
-        value = lax.all_to_all(copies, axis, 0, 0)
-    return value.reshape((-1,) + value.shape[2:])
+def shifted(value, blk_steps, grp_steps):
+    blks, grps = lax.axis_size("blk"), lax.axis_size("grp")
+    pairs = [
+        (blk * grps + grp, (blk + blk_steps) % blks * grps + (grp + grp_steps) % grps)
+        for blk in range(blks)
+        for grp in range(grps)
+    ]
+    return lax.ppermute(value, ("blk", "grp"), pairs)
+
+
+def direct(value):
+    value = value[None]
+    return [
+        shifted(value, blk_steps, grp_steps) if blk_steps or grp_steps else value
+        for blk_steps in range(lax.axis_size("blk"))
+        for grp_steps in range(lax.axis_size("grp"))
+    ]
+
+
+def two_phase(value):
+    near = [value] + [shifted(value, 0, steps) for steps in range(1, lax.axis_size("grp"))]
+    near = jnp.stack(near)
+    return [near] + [shifted(near, steps, 0) for steps in range(1, lax.axis_size("blk"))]
 
 
 def shards(unary, member, features, compat):
@@ -100,23 +131,23 @@
         ),
         compiler_params=params,
     )(own_feat, unary)
-    everything = exchange(packed)
+    spread = direct if count <= 16 else two_phase
     tile, qb = pl.pallas_call(
-        lambda *refs: first_kernel(labels, count, *refs),
+        functools.partial(first_kernel, labels),
         out_shape=(
             jax.ShapeDtypeStruct((count, own, own), jnp.bfloat16),
             jax.ShapeDtypeStruct((labels, own), jnp.bfloat16),
         ),
         compiler_params=params,
-    )(rows, packed, unary, compat, everything)
+    )(rows, packed, unary, compat, *spread(packed))
     return pl.pallas_call(
-        lambda *refs: second_kernel(count, *refs),
+        second_kernel,
         out_shape=(
             jax.ShapeDtypeStruct((labels, own), jnp.float32),
             jax.ShapeDtypeStruct((labels, own), jnp.float32),
         ),
         compiler_params=params,
-    )(qb, unary, compat, exchange(qb), tile)
+    )(qb, unary, compat, tile, *two_phase(qb))
 
 
 def solution(mesh):

time: 55.1 us -> 56.8 us (1.031)
  blocking collectives: 39.7 us -> 0 us
  starting transfers between devices: 0 us -> 27.7 us
  waiting for transfers between devices: 0 us -> 13.4 us
  other arithmetic: 1.99 us -> 2.73 us
    all_to_all x4 -> x0, blocking collectives: 39.7 us -> none  [exchange(): value = lax.all_to_all(copies, axis, 0, 0)]
    ppermute x0 -> x21, starting transfers between devices: none -> 27.7 us  [shifted(): return lax.ppermute(value, ('blk', 'grp'), pairs)]
    ppermute x0 -> x21, waiting for transfers between devices: none -> 13.4 us  [shifted(): return lax.ppermute(value, ('blk', 'grp'), pairs)]
    broadcast_in_dim x4 -> x0, local copies, waits for them, and re-layouts: 1.51 us -> none  [exchange(): copies = jnp.broadcast_to(value[None], (count,) + value.shape)]
    unnamed x1 -> x39, local copies, waits for them, and re-layouts: 1.35 us -> 2.51 us
    another operation x0 -> x1, other arithmetic: none -> 0.73 us  [two_phase(): near = jnp.stack(near)]
  transfers between devices with their start and end apart: 0 -> 21, of which waited for: 0 -> 9; matrix products, arithmetic and copies ran while one was open for 0% -> 0% of each run, Pallas kernels for 0% -> 0%
where the time goes in v2:
time: 56.8 us; the launch traced here: 56.4 us
  starting transfers between devices  27.7 us (49%)
  waiting for transfers between devices  13.4 us (24%)
  Pallas kernels  8.22 us (14%)
  local copies, waits for them, and re-layouts  3.45 us (6%)
  other arithmetic  2.73 us (5%)
  between operations  0.82 us (1%)
    ppermute x21, starting transfers between devices, shifted(): return lax.ppermute(value, ('blk', 'grp'), pairs)  27.7 us
    ppermute x21, waiting for transfers between devices, shifted(): return lax.ppermute(value, ('blk', 'grp'), pairs)  13.4 us
    pallas_call x1, Pallas kernels, shards(): pl.pallas_call(functools.partial(first_kernel, labels), out_shape=(jax.Sh...  3.88 us
    pallas_call x1, Pallas kernels, shards(): pl.pallas_call(second_kernel, out_shape=(jax.ShapeDtypeStruct((labels, ow...  2.92 us
    unnamed x39, local copies, waits for them, and re-layouts  2.51 us
    pallas_call x1, Pallas kernels, shards(): pl.pallas_call(prepare_kernel, out_shape=(jax.ShapeDtypeStruct((labels +...  1.41 us
    select_n x2, other arithmetic, shards(): own_feat = jnp.take(features, member, axis=1)  1.3 us
  transfers between devices with their start and end apart: 21, of which 9 were waited for; matrix products, arithmetic and copies ran while one was open for 0% of the time, Pallas kernels for 0%

profile of v2, /device:TPU:0, one launch (start us, length us, event | category | flops | bytes accessed | tf_op | source)
XLA Modules:
  0.0 56.4 jit_solution(11663420529530372318)
XLA Ops:
  2.0 1.4 %copy.6 = bf16[6,4096]{0,1:T(8,128)(2,1)S(1)} copy(bf16[6,4096]{1,0:T(8,128)(2,1)} %param.6) | data formatting | bytes 98304 | tf_op args[2]
  3.4 0.9 %gather_fusion = bf16[256,6]{1,0:T(8,128)(2,1)S(1)} fusion(bf16[6,4096]{0,1:T(8,128)(2,1)S(1)} %copy.6, s32[1024]{0:T(1024)S(1)} %pad_clamp_fusion), kind=kCustom, calls=%fused_computation | custom fusion | bytes 7168 | tf_op jit(solution)/shard_map/jit(_take)/gather | solution.py:124
  4.9 1.4 %shard_map.59 = (bf16[48,256]{1,0:T(8,128)(2,1)}, bf16[16,256]{1,0:T(8,128)(2,1)}) custom-call(bf16[6,256]{1,0:T(8,128)(2,1)} %select_bitcast_fusion.feats_ref, f32[32,256]{1,0:T(8,128)} %refs_1_.1), custom_call_target="tpu_custom_call" | custom-call | tf_op jit(solution)/shard_map/pallas_call | solution.py:126
  6.3 5.4 %collective-permute-start.14 = (bf16[1,48,256]{2,1,0:T(8,128)(2,1)}, bf16[1,48,256]{2,1,0:T(8,128)(2,1)S(1)}, u32[]{:S(2)}, u32[]{:S(2)}) collective-permute-start(bf16[1,48,256]{2,1,0:T(8,128)(2,1)} %bitcast.7), channel_id=1, source_target_pairs={{0,15},{1,12},{2,13},{3,14},{4,3},{5,0},{6,1},{7,2},{8,7},{9,4},{1... | collective-permute-start | bytes 73736 | tf_op jit(solution)/shard_map/ppermute | solution.py:103
  13.3 3.5 %collective-permute-start.10 = (bf16[1,48,256]{2,1,0:T(8,128)(2,1)}, bf16[1,48,256]{2,1,0:T(8,128)(2,1)S(1)}, u32[]{:S(2)}, u32[]{:S(2)}) collective-permute-start(bf16[1,48,256]{2,1,0:T(8,128)(2,1)} %bitcast.11), channel_id=1, source_target_pairs={{0,11},{1,8},{2,9},{3,10},{4,15},{5,12},{6,13},{7,14},{8,3},{9,0},... | collective-permute-start | bytes 73736 | tf_op jit(solution)/shard_map/ppermute | solution.py:103
  16.8 1.4 %collective-permute-start.9 = (bf16[1,48,256]{2,1,0:T(8,128)(2,1)}, bf16[1,48,256]{2,1,0:T(8,128)(2,1)S(1)}, u32[]{:S(2)}, u32[]{:S(2)}) collective-permute-start(bf16[1,48,256]{2,1,0:T(8,128)(2,1)} %bitcast.12), channel_id=1, source_target_pairs={{0,10},{1,11},{2,8},{3,9},{4,14},{5,15},{6,12},{7,13},{8,2},{9,3},... | collective-permute-start | bytes 73736 | tf_op jit(solution)/shard_map/ppermute | solution.py:103
  18.9 1.2 %collective-permute-start.7 = (bf16[1,48,256]{2,1,0:T(8,128)(2,1)}, bf16[1,48,256]{2,1,0:T(8,128)(2,1)S(1)}, u32[]{:S(2)}, u32[]{:S(2)}) collective-permute-start(bf16[1,48,256]{2,1,0:T(8,128)(2,1)} %bitcast.14), channel_id=1, source_target_pairs={{0,8},{1,9},{2,10},{3,11},{4,12},{5,13},{6,14},{7,15},{8,0},{9,1},... | collective-permute-start | bytes 73736 | tf_op jit(solution)/shard_map/ppermute | solution.py:103
  20.0 1.8 %collective-permute-start.6 = (bf16[1,48,256]{2,1,0:T(8,128)(2,1)}, bf16[1,48,256]{2,1,0:T(8,128)(2,1)S(1)}, u32[]{:S(2)}, u32[]{:S(2)}) collective-permute-start(bf16[1,48,256]{2,1,0:T(8,128)(2,1)} %bitcast.15), channel_id=1, source_target_pairs={{0,7},{1,4},{2,5},{3,6},{4,11},{5,8},{6,9},{7,10},{8,15},{9,12},{1... | collective-permute-start | bytes 73736 | tf_op jit(solution)/shard_map/ppermute | solution.py:103
  21.8 2.0 %collective-permute-start.5 = (bf16[1,48,256]{2,1,0:T(8,128)(2,1)}, bf16[1,48,256]{2,1,0:T(8,128)(2,1)S(1)}, u32[]{:S(2)}, u32[]{:S(2)}) collective-permute-start(bf16[1,48,256]{2,1,0:T(8,128)(2,1)} %bitcast.16), channel_id=1, source_target_pairs={{0,6},{1,7},{2,4},{3,5},{4,10},{5,11},{6,8},{7,9},{8,14},{9,15},{1... | collective-permute-start | bytes 73736 | tf_op jit(solution)/shard_map/ppermute | solution.py:103
  23.9 0.9 %collective-permute-start.4 = (bf16[1,48,256]{2,1,0:T(8,128)(2,1)}, bf16[1,48,256]{2,1,0:T(8,128)(2,1)S(1)}, u32[]{:S(2)}, u32[]{:S(2)}) collective-permute-start(bf16[1,48,256]{2,1,0:T(8,128)(2,1)} %bitcast.17), channel_id=1, source_target_pairs={{0,5},{1,6},{2,7},{3,4},{4,9},{5,10},{6,11},{7,8},{8,13},{9,14},{1... | collective-permute-start | bytes 73736 | tf_op jit(solution)/shard_map/ppermute | solution.py:103
  25.0 3.1 %collective-permute-start.2 = (bf16[1,48,256]{2,1,0:T(8,128)(2,1)}, bf16[1,48,256]{2,1,0:T(8,128)(2,1)S(1)}, u32[]{:S(2)}, u32[]{:S(2)}) collective-permute-start(bf16[1,48,256]{2,1,0:T(8,128)(2,1)} %bitcast.19), channel_id=1, source_target_pairs={{0,3},{1,0},{2,1},{3,2},{4,7},{5,4},{6,5},{7,6},{8,11},{9,8},{10,9... | collective-permute-start | bytes 73736 | tf_op jit(solution)/shard_map/ppermute | solution.py:103
  28.1 1.0 %collective-permute-start.1 = (bf16[1,48,256]{2,1,0:T(8,128)(2,1)}, bf16[1,48,256]{2,1,0:T(8,128)(2,1)S(1)}, u32[]{:S(2)}, u32[]{:S(2)}) collective-permute-start(bf16[1,48,256]{2,1,0:T(8,128)(2,1)} %bitcast.20), channel_id=1, source_target_pairs={{0,2},{1,3},{2,0},{3,1},{4,6},{5,7},{6,4},{7,5},{8,10},{9,11},{10,... | collective-permute-start | bytes 73736 | tf_op jit(solution)/shard_map/ppermute | solution.py:103
  29.2 1.2 %collective-permute-start = (bf16[1,48,256]{2,1,0:T(8,128)(2,1)}, bf16[1,48,256]{2,1,0:T(8,128)(2,1)S(1)}, u32[]{:S(2)}, u32[]{:S(2)}) collective-permute-start(bf16[1,48,256]{2,1,0:T(8,128)(2,1)} %bitcast.21), channel_id=1, source_target_pairs={{0,1},{1,2},{2,3},{3,0},{4,5},{5,6},{6,7},{7,4},{8,9},{9,10},{10,1... | collective-permute-start | bytes 73736 | tf_op jit(solution)/shard_map/ppermute | solution.py:103
  30.4 2.7 %collective-permute-done.1.refs_6_ = bf16[1,48,256]{2,1,0:T(8,128)(2,1)S(1)} collective-permute-done((bf16[1,48,256]{2,1,0:T(8,128)(2,1)}, bf16[1,48,256]{2,1,0:T(8,128)(2,1)S(1)}, u32[]{:S(2)}, u32[]{:S(2)}) %collective-permute-start.1) | collective-permute-done | bytes 24608 | tf_op jit(solution)/shard_map/ppermute | solution.py:103
  33.1 1.9 %collective-permute-done.refs_5_ = bf16[1,48,256]{2,1,0:T(8,128)(2,1)S(1)} collective-permute-done((bf16[1,48,256]{2,1,0:T(8,128)(2,1)}, bf16[1,48,256]{2,1,0:T(8,128)(2,1)S(1)}, u32[]{:S(2)}, u32[]{:S(2)}) %collective-permute-start) | collective-permute-done | bytes 24608 | tf_op jit(solution)/shard_map/ppermute | solution.py:103
  35.6 3.9 %shard_map.60 = (bf16[16,256,256]{2,1,0:T(8,128)(2,1)}, bf16[32,256]{1,0:T(8,128)(2,1)}) custom-call(bf16[16,256]{1,0:T(8,128)(2,1)} %get-tuple-element.6.refs_0_, bf16[48,256]{1,0:T(8,128)(2,1)} %get-tuple-element.7.refs_1_, f32[32,256]{1,0:T(8,128)} %refs_1_.1, f32[32,32]{1,0:T(8,128)} %refs_2_.3, bf16[1,48,256]{2,1,0:T(8,128)(2,1)} %bitcast.22, ...), custom_call_target="tpu_custom_call" | custom-call | tf_op jit(solution)/shard_map/pallas_call | solution.py:135
  39.5 0.8 %collective-permute-start.16 = (bf16[32,256]{1,0:T(8,128)(2,1)}, bf16[32,256]{1,0:T(8,128)(2,1)S(1)}, u32[]{:S(2)}, u32[]{:S(2)}) collective-permute-start(bf16[32,256]{1,0:T(8,128)(2,1)} %get-tuple-element.8.refs_0_), channel_id=1, source_target_pairs={{0,2},{1,3},{2,0},{3,1},{4,6},{5,7},{6,4},{7,5},{8,10},{9,11},{10,... | collective-permute-start | bytes 49160 | tf_op jit(solution)/shard_map/ppermute | solution.py:103
  40.4 1.3 %collective-permute-start.15 = (bf16[32,256]{1,0:T(8,128)(2,1)}, bf16[32,256]{1,0:T(8,128)(2,1)S(1)}, u32[]{:S(2)}, u32[]{:S(2)}) collective-permute-start(bf16[32,256]{1,0:T(8,128)(2,1)} %get-tuple-element.8.refs_0_), channel_id=1, source_target_pairs={{0,1},{1,2},{2,3},{3,0},{4,5},{5,6},{6,7},{7,4},{8,9},{9,10},{10,1... | collective-permute-start | bytes 49160 | tf_op jit(solution)/shard_map/ppermute | solution.py:103
  41.6 1.9 %collective-permute-done.17 = bf16[32,256]{1,0:T(8,128)(2,1)S(1)} collective-permute-done((bf16[32,256]{1,0:T(8,128)(2,1)}, bf16[32,256]{1,0:T(8,128)(2,1)S(1)}, u32[]{:S(2)}, u32[]{:S(2)}) %collective-permute-start.17) | collective-permute-done | bytes 16416 | tf_op jit(solution)/shard_map/ppermute | solution.py:103
  43.5 1.0 %collective-permute-done.16 = bf16[32,256]{1,0:T(8,128)(2,1)S(1)} collective-permute-done((bf16[32,256]{1,0:T(8,128)(2,1)}, bf16[32,256]{1,0:T(8,128)(2,1)S(1)}, u32[]{:S(2)}, u32[]{:S(2)}) %collective-permute-start.16) | collective-permute-done | bytes 16416 | tf_op jit(solution)/shard_map/ppermute | solution.py:103
  44.4 1.7 %collective-permute-done.15 = bf16[32,256]{1,0:T(8,128)(2,1)S(1)} collective-permute-done((bf16[32,256]{1,0:T(8,128)(2,1)}, bf16[32,256]{1,0:T(8,128)(2,1)S(1)}, u32[]{:S(2)}, u32[]{:S(2)}) %collective-permute-start.15) | collective-permute-done | bytes 16416 | tf_op jit(solution)/shard_map/ppermute | solution.py:103
  46.9 1.6 %collective-permute-start.19 = (bf16[4,32,256]{2,1,0:T(8,128)(2,1)S(1)}, bf16[4,32,256]{2,1,0:T(8,128)(2,1)S(1)}, u32[]{:S(2)}, u32[]{:S(2)}) collective-permute-start(bf16[4,32,256]{2,1,0:T(8,128)(2,1)S(1)} %pad_maximum_fusion.refs_4_), channel_id=1, source_target_pairs={{0,8},{1,9},{2,10},{3,11},{4,12},{5,13},{6,14},{7,15},{8,0},{9,1},... | collective-permute-start | bytes 196616 | tf_op jit(solution)/shard_map/ppermute | solution.py:103
  48.8 3.8 %collective-permute-done.19.refs_6_ = bf16[4,32,256]{2,1,0:T(8,128)(2,1)S(1)} collective-permute-done((bf16[4,32,256]{2,1,0:T(8,128)(2,1)S(1)}, bf16[4,32,256]{2,1,0:T(8,128)(2,1)S(1)}, u32[]{:S(2)}, u32[]{:S(2)}) %collective-permute-start.19) | collective-permute-done | bytes 65568 | tf_op jit(solution)/shard_map/ppermute | solution.py:103
  53.4 2.9 %shard_map.61 = (f32[32,256]{1,0:T(8,128)}, f32[32,256]{1,0:T(8,128)}) custom-call(bf16[32,256]{1,0:T(8,128)(2,1)} %get-tuple-element.8.refs_0_, f32[32,256]{1,0:T(8,128)} %refs_1_.1, f32[32,32]{1,0:T(8,128)} %refs_2_.3, bf16[16,256,256]{2,1,0:T(8,128)(2,1)} %get-tuple-element.9.refs_3_, bf16[4,32,256]{2,1,0:T(8,128)(2,1)} %copy-done, ...), custom_call_target="tpu_custom_call" | custom-call | tf_op jit(solution)/shard_map/pallas_call | solution.py:143
  (67 shorter events, 6.9 us)
Async XLA Ops:
  6.3 10.5 %collective-permute-start.14 = (bf16[1,48,256]{2,1,0:T(8,128)(2,1)}, bf16[1,48,256]{2,1,0:T(8,128)(2,1)S(1)}, u32[]{:S(2)}, u32[]{:S(2)}) collective-permute-start(bf16[1,48,256]{2,1,0:T(8,128)(2,1)} %bitcast.7), channel_id=1, source_target_pairs={{0,15},{1,12},{2,13},{3,14},{4,3},{5,0},{6,1},{7,2},{8,7},{9,4},{1... | collective-permute-start | bytes 73736 | tf_op jit(solution)/shard_map/ppermute | solution.py:103
  11.8 6.4 %collective-permute-start.13 = (bf16[1,48,256]{2,1,0:T(8,128)(2,1)}, bf16[1,48,256]{2,1,0:T(8,128)(2,1)S(1)}, u32[]{:S(2)}, u32[]{:S(2)}) collective-permute-start(bf16[1,48,256]{2,1,0:T(8,128)(2,1)} %bitcast.8), channel_id=1, source_target_pairs={{0,14},{1,15},{2,12},{3,13},{4,2},{5,3},{6,0},{7,1},{8,6},{9,7},{1... | collective-permute-start | bytes 73736 | tf_op jit(solution)/shard_map/ppermute | solution.py:103
  11.8 7.1 %collective-permute-start.12 = (bf16[1,48,256]{2,1,0:T(8,128)(2,1)}, bf16[1,48,256]{2,1,0:T(8,128)(2,1)S(1)}, u32[]{:S(2)}, u32[]{:S(2)}) collective-permute-start(bf16[1,48,256]{2,1,0:T(8,128)(2,1)} %bitcast.9), channel_id=1, source_target_pairs={{0,13},{1,14},{2,15},{3,12},{4,1},{5,2},{6,3},{7,0},{8,5},{9,6},{1... | collective-permute-start | bytes 73736 | tf_op jit(solution)/shard_map/ppermute | solution.py:103
  12.6 7.4 %collective-permute-start.11 = (bf16[1,48,256]{2,1,0:T(8,128)(2,1)}, bf16[1,48,256]{2,1,0:T(8,128)(2,1)S(1)}, u32[]{:S(2)}, u32[]{:S(2)}) collective-permute-start(bf16[1,48,256]{2,1,0:T(8,128)(2,1)} %bitcast.10), channel_id=1, source_target_pairs={{0,12},{1,13},{2,14},{3,15},{4,0},{5,1},{6,2},{7,3},{8,4},{9,5},{1... | collective-permute-start | bytes 73736 | tf_op jit(solution)/shard_map/ppermute | solution.py:103
  13.3 8.5 %collective-permute-start.10 = (bf16[1,48,256]{2,1,0:T(8,128)(2,1)}, bf16[1,48,256]{2,1,0:T(8,128)(2,1)S(1)}, u32[]{:S(2)}, u32[]{:S(2)}) collective-permute-start(bf16[1,48,256]{2,1,0:T(8,128)(2,1)} %bitcast.11), channel_id=1, source_target_pairs={{0,11},{1,8},{2,9},{3,10},{4,15},{5,12},{6,13},{7,14},{8,3},{9,0},... | collective-permute-start | bytes 73736 | tf_op jit(solution)/shard_map/ppermute | solution.py:103
  16.8 18.2 %copy-start.4 = (bf16[1,48,256]{2,1,0:T(8,128)(2,1)}, bf16[1,48,256]{2,1,0:T(8,128)(2,1)S(1)}, u32[]{:S(2)}) copy-start(bf16[1,48,256]{2,1,0:T(8,128)(2,1)S(1)} %collective-permute-done.14.refs_19_) | copy-start | bytes 73732
  16.8 7.1 %collective-permute-start.9 = (bf16[1,48,256]{2,1,0:T(8,128)(2,1)}, bf16[1,48,256]{2,1,0:T(8,128)(2,1)S(1)}, u32[]{:S(2)}, u32[]{:S(2)}) collective-permute-start(bf16[1,48,256]{2,1,0:T(8,128)(2,1)} %bitcast.12), channel_id=1, source_target_pairs={{0,10},{1,11},{2,8},{3,9},{4,14},{5,15},{6,12},{7,13},{8,2},{9,3},... | collective-permute-start | bytes 73736 | tf_op jit(solution)/shard_map/ppermute | solution.py:103
  18.1 16.9 %copy-start.5 = (bf16[1,48,256]{2,1,0:T(8,128)(2,1)}, bf16[1,48,256]{2,1,0:T(8,128)(2,1)S(1)}, u32[]{:S(2)}) copy-start(bf16[1,48,256]{2,1,0:T(8,128)(2,1)S(1)} %collective-permute-done.13.refs_18_) | copy-start | bytes 73732
  18.1 6.8 %collective-permute-start.8 = (bf16[1,48,256]{2,1,0:T(8,128)(2,1)}, bf16[1,48,256]{2,1,0:T(8,128)(2,1)S(1)}, u32[]{:S(2)}, u32[]{:S(2)}) collective-permute-start(bf16[1,48,256]{2,1,0:T(8,128)(2,1)} %bitcast.13), channel_id=1, source_target_pairs={{0,9},{1,10},{2,11},{3,8},{4,13},{5,14},{6,15},{7,12},{8,1},{9,2},... | collective-permute-start | bytes 73736 | tf_op jit(solution)/shard_map/ppermute | solution.py:103
  18.9 16.2 %copy-start.6 = (bf16[1,48,256]{2,1,0:T(8,128)(2,1)}, bf16[1,48,256]{2,1,0:T(8,128)(2,1)S(1)}, u32[]{:S(2)}) copy-start(bf16[1,48,256]{2,1,0:T(8,128)(2,1)S(1)} %collective-permute-done.12.refs_17_) | copy-start | bytes 73732
  18.9 6.1 %collective-permute-start.7 = (bf16[1,48,256]{2,1,0:T(8,128)(2,1)}, bf16[1,48,256]{2,1,0:T(8,128)(2,1)S(1)}, u32[]{:S(2)}, u32[]{:S(2)}) collective-permute-start(bf16[1,48,256]{2,1,0:T(8,128)(2,1)} %bitcast.14), channel_id=1, source_target_pairs={{0,8},{1,9},{2,10},{3,11},{4,12},{5,13},{6,14},{7,15},{8,0},{9,1},... | collective-permute-start | bytes 73736 | tf_op jit(solution)/shard_map/ppermute | solution.py:103
  20.0 8.1 %collective-permute-start.6 = (bf16[1,48,256]{2,1,0:T(8,128)(2,1)}, bf16[1,48,256]{2,1,0:T(8,128)(2,1)S(1)}, u32[]{:S(2)}, u32[]{:S(2)}) collective-permute-start(bf16[1,48,256]{2,1,0:T(8,128)(2,1)} %bitcast.15), channel_id=1, source_target_pairs={{0,7},{1,4},{2,5},{3,6},{4,11},{5,8},{6,9},{7,10},{8,15},{9,12},{1... | collective-permute-start | bytes 73736 | tf_op jit(solution)/shard_map/ppermute | solution.py:103
  21.8 7.3 %collective-permute-start.5 = (bf16[1,48,256]{2,1,0:T(8,128)(2,1)}, bf16[1,48,256]{2,1,0:T(8,128)(2,1)S(1)}, u32[]{:S(2)}, u32[]{:S(2)}) collective-permute-start(bf16[1,48,256]{2,1,0:T(8,128)(2,1)} %bitcast.16), channel_id=1, source_target_pairs={{0,6},{1,7},{2,4},{3,5},{4,10},{5,11},{6,8},{7,9},{8,14},{9,15},{1... | collective-permute-start | bytes 73736 | tf_op jit(solution)/shard_map/ppermute | solution.py:103
  23.9 6.5 %collective-permute-start.4 = (bf16[1,48,256]{2,1,0:T(8,128)(2,1)}, bf16[1,48,256]{2,1,0:T(8,128)(2,1)S(1)}, u32[]{:S(2)}, u32[]{:S(2)}) collective-permute-start(bf16[1,48,256]{2,1,0:T(8,128)(2,1)} %bitcast.17), channel_id=1, source_target_pairs={{0,5},{1,6},{2,7},{3,4},{4,9},{5,10},{6,11},{7,8},{8,13},{9,14},{1... | collective-permute-start | bytes 73736 | tf_op jit(solution)/shard_map/ppermute | solution.py:103
  25.0 5.4 %collective-permute-start.3 = (bf16[1,48,256]{2,1,0:T(8,128)(2,1)}, bf16[1,48,256]{2,1,0:T(8,128)(2,1)S(1)}, u32[]{:S(2)}, u32[]{:S(2)}) collective-permute-start(bf16[1,48,256]{2,1,0:T(8,128)(2,1)} %bitcast.18), channel_id=1, source_target_pairs={{0,4},{1,5},{2,6},{3,7},{4,8},{5,9},{6,10},{7,11},{8,12},{9,13},{1... | collective-permute-start | bytes 73736 | tf_op jit(solution)/shard_map/ppermute | solution.py:103
  25.0 5.4 %collective-permute-start.2 = (bf16[1,48,256]{2,1,0:T(8,128)(2,1)}, bf16[1,48,256]{2,1,0:T(8,128)(2,1)S(1)}, u32[]{:S(2)}, u32[]{:S(2)}) collective-permute-start(bf16[1,48,256]{2,1,0:T(8,128)(2,1)} %bitcast.19), channel_id=1, source_target_pairs={{0,3},{1,0},{2,1},{3,2},{4,7},{5,4},{6,5},{7,6},{8,11},{9,8},{10,9... | collective-permute-start | bytes 73736 | tf_op jit(solution)/shard_map/ppermute | solution.py:103
  28.1 4.9 %collective-permute-start.1 = (bf16[1,48,256]{2,1,0:T(8,128)(2,1)}, bf16[1,48,256]{2,1,0:T(8,128)(2,1)S(1)}, u32[]{:S(2)}, u32[]{:S(2)}) collective-permute-start(bf16[1,48,256]{2,1,0:T(8,128)(2,1)} %bitcast.20), channel_id=1, source_target_pairs={{0,2},{1,3},{2,0},{3,1},{4,6},{5,7},{6,4},{7,5},{8,10},{9,11},{10,... | collective-permute-start | bytes 73736 | tf_op jit(solution)/shard_map/ppermute | solution.py:103
  29.2 5.8 %collective-permute-start = (bf16[1,48,256]{2,1,0:T(8,128)(2,1)}, bf16[1,48,256]{2,1,0:T(8,128)(2,1)S(1)}, u32[]{:S(2)}, u32[]{:S(2)}) collective-permute-start(bf16[1,48,256]{2,1,0:T(8,128)(2,1)} %bitcast.21), channel_id=1, source_target_pairs={{0,1},{1,2},{2,3},{3,0},{4,5},{5,6},{6,7},{7,4},{8,9},{9,10},{10,1... | collective-permute-start | bytes 73736 | tf_op jit(solution)/shard_map/ppermute | solution.py:103
  39.5 4.0 %collective-permute-start.17 = (bf16[32,256]{1,0:T(8,128)(2,1)}, bf16[32,256]{1,0:T(8,128)(2,1)S(1)}, u32[]{:S(2)}, u32[]{:S(2)}) collective-permute-start(bf16[32,256]{1,0:T(8,128)(2,1)} %get-tuple-element.8.refs_0_), channel_id=1, source_target_pairs={{0,3},{1,0},{2,1},{3,2},{4,7},{5,4},{6,5},{7,6},{8,11},{9,8},{10,9... | collective-permute-start | bytes 49160 | tf_op jit(solution)/shard_map/ppermute | solution.py:103
  39.5 4.9 %collective-permute-start.16 = (bf16[32,256]{1,0:T(8,128)(2,1)}, bf16[32,256]{1,0:T(8,128)(2,1)S(1)}, u32[]{:S(2)}, u32[]{:S(2)}) collective-permute-start(bf16[32,256]{1,0:T(8,128)(2,1)} %get-tuple-element.8.refs_0_), channel_id=1, source_target_pairs={{0,2},{1,3},{2,0},{3,1},{4,6},{5,7},{6,4},{7,5},{8,10},{9,11},{10,... | collective-permute-start | bytes 49160 | tf_op jit(solution)/shard_map/ppermute | solution.py:103
  40.4 5.7 %collective-permute-start.15 = (bf16[32,256]{1,0:T(8,128)(2,1)}, bf16[32,256]{1,0:T(8,128)(2,1)S(1)}, u32[]{:S(2)}, u32[]{:S(2)}) collective-permute-start(bf16[32,256]{1,0:T(8,128)(2,1)} %get-tuple-element.8.refs_0_), channel_id=1, source_target_pairs={{0,1},{1,2},{2,3},{3,0},{4,5},{5,6},{6,7},{7,4},{8,9},{9,10},{10,1... | collective-permute-start | bytes 49160 | tf_op jit(solution)/shard_map/ppermute | solution.py:103
  46.8 2.0 %collective-permute-start.20 = (bf16[4,32,256]{2,1,0:T(8,128)(2,1)S(1)}, bf16[4,32,256]{2,1,0:T(8,128)(2,1)S(1)}, u32[]{:S(2)}, u32[]{:S(2)}) collective-permute-start(bf16[4,32,256]{2,1,0:T(8,128)(2,1)S(1)} %pad_maximum_fusion.refs_4_), channel_id=1, source_target_pairs={{0,12},{1,13},{2,14},{3,15},{4,0},{5,1},{6,2},{7,3},{8,4},{9,5},{1... | collective-permute-start | bytes 196616 | tf_op jit(solution)/shard_map/ppermute | solution.py:103
  46.9 5.7 %collective-permute-start.19 = (bf16[4,32,256]{2,1,0:T(8,128)(2,1)S(1)}, bf16[4,32,256]{2,1,0:T(8,128)(2,1)S(1)}, u32[]{:S(2)}, u32[]{:S(2)}) collective-permute-start(bf16[4,32,256]{2,1,0:T(8,128)(2,1)S(1)} %pad_maximum_fusion.refs_4_), channel_id=1, source_target_pairs={{0,8},{1,9},{2,10},{3,11},{4,12},{5,13},{6,14},{7,15},{8,0},{9,1},... | collective-permute-start | bytes 196616 | tf_op jit(solution)/shard_map/ppermute | solution.py:103
  48.5 4.3 %collective-permute-start.18 = (bf16[4,32,256]{2,1,0:T(8,128)(2,1)S(1)}, bf16[4,32,256]{2,1,0:T(8,128)(2,1)S(1)}, u32[]{:S(2)}, u32[]{:S(2)}) collective-permute-start(bf16[4,32,256]{2,1,0:T(8,128)(2,1)S(1)} %pad_maximum_fusion.refs_4_), channel_id=1, source_target_pairs={{0,4},{1,5},{2,6},{3,7},{4,8},{5,9},{6,10},{7,11},{8,12},{9,13},{1... | collective-permute-start | bytes 196616 | tf_op jit(solution)/shard_map/ppermute | solution.py:103
  (16 other events, 100.5 us)

commit v3 on v2

--- a/solution.py
+++ b/solution.py
@@ -93,29 +93,8 @@
     pairwise_ref[...] = pairwise
 
 
-def shifted(value, blk_steps, grp_steps):
-    blks, grps = lax.axis_size("blk"), lax.axis_size("grp")
-    pairs = [
-        (blk * grps + grp, (blk + blk_steps) % blks * grps + (grp + grp_steps) % grps)
-        for blk in range(blks)
-        for grp in range(grps)
-    ]
-    return lax.ppermute(value, ("blk", "grp"), pairs)
-
-
-def direct(value):
-    value = value[None]
-    return [
-        shifted(value, blk_steps, grp_steps) if blk_steps or grp_steps else value
-        for blk_steps in range(lax.axis_size("blk"))
-        for grp_steps in range(lax.axis_size("grp"))
-    ]
-
-
-def two_phase(value):
-    near = [value] + [shifted(value, 0, steps) for steps in range(1, lax.axis_size("grp"))]
-    near = jnp.stack(near)
-    return [near] + [shifted(near, steps, 0) for steps in range(1, lax.axis_size("blk"))]
+def gathered(value):
+    return lax.all_gather(value, ("blk", "grp"), axis=0, tiled=False)
 
 
 def shards(unary, member, features, compat):
@@ -131,7 +110,6 @@
         ),
         compiler_params=params,
     )(own_feat, unary)
-    spread = direct if count <= 16 else two_phase
     tile, qb = pl.pallas_call(
         functools.partial(first_kernel, labels),
         out_shape=(
@@ -139,7 +117,7 @@
             jax.ShapeDtypeStruct((labels, own), jnp.bfloat16),
         ),
         compiler_params=params,
-    )(rows, packed, unary, compat, *spread(packed))
+    )(rows, packed, unary, compat, gathered(packed))
     return pl.pallas_call(
         second_kernel,
         out_shape=(
@@ -147,7 +125,7 @@
             jax.ShapeDtypeStruct((labels, own), jnp.float32),
         ),
         compiler_params=params,
-    )(qb, unary, compat, tile, *two_phase(qb))
+    )(qb, unary, compat, tile, gathered(qb))
 
 
 def solution(mesh):

time: 56.8 us -> 86.9 us (1.53)
  blocking collectives: 0 us -> 73.3 us
  starting transfers between devices: 27.7 us -> 0 us
  waiting for transfers between devices: 13.4 us -> 0 us
  local copies, waits for them, and re-layouts: 3.45 us -> 2.29 us
    all_gather x0 -> x2, blocking collectives: none -> 73.3 us  [gathered(): return lax.all_gather(value, ('blk', 'grp'), axis=0, tiled=False)]
    ppermute x21 -> x0, starting transfers between devices: 27.7 us -> none  [shifted(): return lax.ppermute(value, ('blk', 'grp'), pairs)]
    ppermute x21 -> x0, waiting for transfers between devices: 13.4 us -> none  [shifted(): return lax.ppermute(value, ('blk', 'grp'), pairs)]
    unnamed x39 -> x1, local copies, waits for them, and re-layouts: 2.51 us -> 1.35 us
  transfers between devices with their start and end apart: 21 -> 0, of which waited for: 9 -> 0; matrix products, arithmetic and copies ran while one was open for 0% -> 0% of each run, Pallas kernels for 0% -> 0%
where the time goes in v3:
time: 86.9 us; the launch traced here: 86.5 us
  blocking collectives  73.3 us (84%)
  Pallas kernels  8.29 us (10%)
  local copies, waits for them, and re-layouts  2.29 us (3%)
  other arithmetic  1.99 us (2%)
    all_gather x2, blocking collectives, gathered(): return lax.all_gather(value, ('blk', 'grp'), axis=0, tiled=False)  73.3 us
    pallas_call x1, Pallas kernels, shards(): pl.pallas_call(functools.partial(first_kernel, labels), out_shape=(jax.Sh...  3.95 us
    pallas_call x1, Pallas kernels, shards(): pl.pallas_call(second_kernel, out_shape=(jax.ShapeDtypeStruct((labels, ow...  2.94 us

profile of v3, /device:TPU:0, one launch (start us, length us, event | category | flops | bytes accessed | tf_op | source)
XLA Modules:
  0.0 86.5 jit_solution(15861762946189126643)
XLA Ops:
  0.6 0.7 compare_and_fusion
  1.3 0.7 compare_select_fusion
  2.0 1.4 %copy.6 = bf16[6,4096]{0,1:T(8,128)(2,1)S(1)} copy(bf16[6,4096]{1,0:T(8,128)(2,1)} %param.6) | data formatting | bytes 98304 | tf_op args[2]
  3.4 0.9 gather_fusion
  4.2 0.1 copy.7
  4.3 0.6 select_bitcast_fusion.feats_ref
  4.9 1.4 %shard_map.59 = (bf16[48,256]{1,0:T(8,128)(2,1)}, bf16[16,256]{1,0:T(8,128)(2,1)}) custom-call(bf16[6,256]{1,0:T(8,128)(2,1)} %select_bitcast_fusion.feats_ref, f32[32,256]{1,0:T(8,128)} %refs_1_.1), custom_call_target="tpu_custom_call" | custom-call | tf_op jit(solution)/shard_map/pallas_call | solution.py:105
  6.3 39.9 %all-gather = bf16[768,256]{1,0:T(8,128)(2,1)} all-gather(bf16[48,256]{1,0:T(8,128)(2,1)} %get-tuple-element.7.refs_1_), channel_id=2, replica_groups=mesh['scene'=2,'blk'=4,'grp'=4] {'blk','grp'}, dimensions={0}, use_global_device_ids=true | all-gather | bytes 417792 | tf_op jit(solution)/shard_map/all_gather | solution.py:97
  46.2 4.0 %shard_map.60 = (bf16[16,256,256]{2,1,0:T(8,128)(2,1)}, bf16[32,256]{1,0:T(8,128)(2,1)}) custom-call(bf16[16,256]{1,0:T(8,128)(2,1)} %get-tuple-element.6.refs_0_, bf16[48,256]{1,0:T(8,128)(2,1)} %get-tuple-element.7.refs_1_, f32[32,256]{1,0:T(8,128)} %refs_1_.1, f32[32,32]{1,0:T(8,128)} %refs_2_.3, bf16[16,48,256]{2,1,0:T(8,128)(2,1)} %bitcast.4), custom_call_target="tpu_custom_call" | custom-call | tf_op jit(solution)/shard_map/pallas_call | solution.py:113
  50.1 33.4 %all-gather.1 = bf16[512,256]{1,0:T(8,128)(2,1)} all-gather(bf16[32,256]{1,0:T(8,128)(2,1)} %get-tuple-element.8.refs_0_), channel_id=3, replica_groups=mesh['scene'=2,'blk'=4,'grp'=4] {'blk','grp'}, dimensions={0}, use_global_device_ids=true | all-gather | bytes 278528 | tf_op jit(solution)/shard_map/all_gather | solution.py:97
  83.6 2.9 %shard_map.61 = (f32[32,256]{1,0:T(8,128)}, f32[32,256]{1,0:T(8,128)}) custom-call(bf16[32,256]{1,0:T(8,128)(2,1)} %get-tuple-element.8.refs_0_, f32[32,256]{1,0:T(8,128)} %refs_1_.1, f32[32,32]{1,0:T(8,128)} %refs_2_.3, bf16[16,256,256]{2,1,0:T(8,128)(2,1)} %get-tuple-element.9.refs_3_, bf16[16,32,256]{2,1,0:T(8,128)(2,1)} %bitcast.5), custom_call_target="tpu_custom_call" | custom-call | tf_op jit(solution)/shard_map/pallas_call | solution.py:121
  (1 shorter events, 0.0 us)

commit v4 on v3

v4 whole, which is shorter than its diff:
```python
import functools
import math

import jax
import jax.numpy as jnp
from jax import lax
from jax.experimental import pallas as pl
from jax.experimental.pallas import tpu as pltpu
from jax.sharding import PartitionSpec as P

AUX = 16
LANES = 128
VMEM_LIMIT = 56 * 1024 * 1024
KEPT_BYTES = 4 * 1024 * 1024


def normalize(logits):
    raised = jnp.exp(logits)
    return raised / jnp.sum(raised, axis=0, keepdims=True)


def three_parts(value):
    high = value.astype(jnp.bfloat16).astype(jnp.float32)
    middle = (value - high).astype(jnp.bfloat16).astype(jnp.float32)
    return [high, middle, value - high - middle]


def pick_features(features_ref, member):
    feats, points = features_ref.shape
    own = member.shape[1]
    groups = points // LANES
    wide = features_ref[...].astype(jnp.float32)
    wide = jnp.concatenate([wide, jnp.zeros((8 - feats, points), jnp.float32)], axis=0)
    table = jnp.concatenate(
        [wide[:, group * LANES:(group + 1) * LANES] for group in range(groups)], axis=0
    ).astype(jnp.bfloat16)
    lane = lax.broadcasted_iota(jnp.int32, (LANES, own), 0)
    chosen = jnp.where(lane == member % LANES, 1.0, 0.0).astype(jnp.bfloat16)
    found = jnp.dot(table, chosen, preferred_element_type=jnp.float32)
    found = found.reshape(groups, 8, own)
    group = lax.broadcasted_iota(jnp.int32, (groups, 8, own), 0)
    return jnp.sum(jnp.where(group == (member // LANES)[None], found, 0.0), axis=0)


def prepare_kernel(features_ref, member_ref, unary_ref, sent_ref):
    labels = unary_ref.shape[0]
    sent_ref[pl.ds(0, labels), :] = unary_ref[...]
    sent_ref[pl.ds(labels, 8), :] = pick_features(features_ref, member_ref[...])


def pack_kernel(labels, feats, *refs):
    near_refs, packed_ref, rows_ref = refs[:-2], refs[-2], refs[-1]
    for place, near_ref in enumerate(near_refs):
        own = near_ref.shape[1]
        chosen = near_ref[pl.ds(labels, 8), :][:feats]
        norms = three_parts(-0.5 * jnp.sum(chosen * chosen, axis=0, keepdims=True))
        ones = jnp.ones((3, own), jnp.float32)
        spare = jnp.zeros((AUX - feats - 6, own), jnp.float32)
        columns = jnp.concatenate([chosen] + norms + [ones, spare], axis=0)
        rows = jnp.concatenate([chosen, ones] + norms + [spare], axis=0)
        labels_now = normalize(-near_ref[pl.ds(0, labels), :])
        packed_ref[place, pl.ds(0, labels), :] = labels_now.astype(jnp.bfloat16)
        packed_ref[place, pl.ds(labels, AUX), :] = columns.astype(jnp.bfloat16)
        rows_ref[:, pl.ds(place * own, own)] = rows.astype(jnp.bfloat16)


def over_blocks(refs, body, start):
    base = 0
    unrolled = sum(ref.shape[0] for ref in refs) <= 16
    for ref in refs:
        size = ref.shape[0]
        if unrolled:
            for index in range(size):
                start = body(ref, index, base + index, start)
        else:
            step = lambda index, total, ref=ref, base=base: body(ref, index, base + index, total)
            start = lax.fori_loop(0, size, step, start)
        base += size
    return start


def finish(message, qb, unary, compat_ref):
    message = message - qb.astype(jnp.float32)
    pairwise = jnp.dot(
        compat_ref[...], message, precision=lax.Precision.HIGHEST,
        preferred_element_type=jnp.float32,
    )
    return normalize(-unary - pairwise), pairwise


def first_kernel(labels, nears, *refs):
    rows_ref, compat_ref = refs[:2]
    near_refs = refs[2:2 + nears]
    packed_refs = refs[2 + nears:-2]
    tile_ref, q_ref = refs[-2:]
    own = near_refs[0].shape[1]
    rows = rows_ref[...]

    def body(packed_ref, index, place, total):
        columns = packed_ref[index, pl.ds(labels, AUX), :]
        exponent = lax.dot_general(
            columns, rows, (((0,), (0,)), ((), ())), preferred_element_type=jnp.float32
        )
        tile = jnp.exp(exponent).astype(jnp.bfloat16)
        tile_ref[place] = tile[:, :own]
        return total + jnp.dot(
            packed_ref[index, pl.ds(0, labels), :], tile, preferred_element_type=jnp.float32
        )

    total = over_blocks(packed_refs, body, jnp.zeros((labels, nears * own), jnp.float32))
    labels_now = [packed_refs[0][near, pl.ds(0, labels), :] for near in range(nears)]
    unary = [near_ref[pl.ds(0, labels), :] for near_ref in near_refs]
    probs, _ = finish(
        total, jnp.concatenate(labels_now, axis=1), jnp.concatenate(unary, axis=1), compat_ref
    )
    for near in range(nears):
        q_ref[near] = probs[:, near * own:(near + 1) * own].astype(jnp.bfloat16)


def second_kernel(*refs):
    unary_ref, compat_ref, tile_ref, *q_refs = refs[:-2]
    probs_ref, pairwise_ref = refs[-2:]

    def body(q_ref, index, place, total):
        return total + jnp.dot(
            q_ref[index], tile_ref[place], preferred_element_type=jnp.float32
        )

    total = over_blocks(q_refs, body, jnp.zeros(unary_ref.shape, jnp.float32))
    probs, pairwise = finish(total, q_refs[0][0], unary_ref[...], compat_ref)
    probs_ref[...] = probs
    pairwise_ref[...] = pairwise


def all_shifts(value, axis):
    count = lax.axis_size(axis)
    found = [value]
    for steps in range(1, count):
        pairs = [(source, (source + steps) % count) for source in range(count)]
        found.append(lax.ppermute(value, axis, pairs))
    return found


def small(dims, kind):
    return math.prod(dims) * jnp.dtype(kind).itemsize <= KEPT_BYTES


def call(kernel, out_shapes, *operands):
    held = [
        pltpu.with_memory_space_constraint(operand, pltpu.VMEM)
        if small(operand.shape, operand.dtype) else operand
        for operand in operands
    ]
    return pl.pallas_call(
        kernel,
        out_shape=tuple(out_shapes),
        compiler_params=pltpu.CompilerParams(vmem_limit_bytes=VMEM_LIMIT),
    )(*held)


def kept(dims, kind):
    return pltpu.VMEM(dims, kind) if small(dims, kind) else jax.ShapeDtypeStruct(dims, kind)


def shards(unary, member, features, compat):
    labels, own = unary.shape
    nears = lax.axis_size("grp")
    count = lax.axis_size("blk") * nears
    (sent,) = call(
        prepare_kernel, [kept((labels + 8, own), jnp.float32)], features, member[None], unary
    )
    near = all_shifts(sent, "grp")
    packed, rows = call(
        functools.partial(pack_kernel, labels, features.shape[0]),
        [kept((nears, labels + AUX, own), jnp.bfloat16), kept((AUX, nears * own), jnp.bfloat16)],
        *near,
    )
    tile, q_near = call(
        functools.partial(first_kernel, labels, nears),
        [kept((count, own, own), jnp.bfloat16), kept((nears, labels, own), jnp.bfloat16)],
        rows, compat, *near, *all_shifts(packed, "blk"),
    )
    return call(
        second_kernel,
        [jax.ShapeDtypeStruct((labels, own), jnp.float32)] * 2,
        unary, compat, tile, *all_shifts(q_near, "blk"),
    )


def solution(mesh):
    in_specs = (P(None, ("scene", "blk", "grp")), P(("scene", "blk", "grp")), P(None, "scene"), P())
    out_specs = (P(None, ("scene", "blk", "grp")), P(None, ("scene", "blk", "grp")))
    return jax.shard_map(shards, mesh=mesh, in_specs=in_specs, out_specs=out_specs, check_vma=False)
```

time: 86.9 us -> 34.8 us (0.40)
  blocking collectives: 73.3 us -> 0 us
  waiting for transfers between devices: 0 us -> 14.8 us
  starting transfers between devices: 0 us -> 8.73 us
  other arithmetic: 1.99 us -> 0 us
  Pallas kernels: 8.29 us -> 6.54 us
  local copies, waits for them, and re-layouts: 2.29 us -> 3.75 us
    all_gather x2 -> x0, blocking collectives: 73.3 us -> none  [gathered(): return lax.all_gather(value, ('blk', 'grp'), axis=0, tiled=False)]
    ppermute x0 -> x9, waiting for transfers between devices: none -> 14.8 us  [all_shifts(): found.append(lax.ppermute(value, axis, pairs))]
    ppermute x0 -> x9, starting transfers between devices: none -> 8.73 us  [all_shifts(): found.append(lax.ppermute(value, axis, pairs))]
    unnamed x1 -> x10, local copies, waits for them, and re-layouts: 1.35 us -> 3.75 us
    pallas_call x3 -> x4, Pallas kernels: 8.29 us -> 6.54 us  [call(): pl.pallas_call(kernel, out_shape=tuple(out_shapes), compiler_params=pltpu...]
    select_n x2 -> x0, other arithmetic: 1.3 us -> none  [shards(): own_feat = jnp.take(features, member, axis=1)]
    gather x2 -> x0, local copies, waits for them, and re-layouts: 0.93 us -> none  [shards(): own_feat = jnp.take(features, member, axis=1)]
  transfers between devices with their start and end apart: 0 -> 9, of which waited for: 0 -> 9; matrix products, arithmetic and copies ran while one was open for 0% -> 0% of each run, Pallas kernels for 0% -> 0%
where the time goes in v4:
time: 34.8 us; the launch traced here: 34.5 us
  waiting for transfers between devices  14.8 us (43%)
  starting transfers between devices  8.73 us (25%)
  Pallas kernels  6.54 us (19%)
  local copies, waits for them, and re-layouts  3.75 us (11%)
  between operations  0.68 us (2%)
    ppermute x9, waiting for transfers between devices, all_shifts(): found.append(lax.ppermute(value, axis, pairs))  14.8 us
    ppermute x9, starting transfers between devices, all_shifts(): found.append(lax.ppermute(value, axis, pairs))  8.73 us
    pallas_call x4, Pallas kernels, call(): pl.pallas_call(kernel, out_shape=tuple(out_shapes), compiler_params=pltpu...  6.54 us
    unnamed x10, local copies, waits for them, and re-layouts  3.75 us
  transfers between devices with their start and end apart: 9, of which 9 were waited for; matrix products, arithmetic and copies ran while one was open for 0% of the time, Pallas kernels for 0%

profile of v4, /device:TPU:0, one launch (start us, length us, event | category | flops | bytes accessed | tf_op | source)
XLA Modules:
  0.0 34.5 jit_solution(8410895209303758310)
XLA Ops:
  0.6 0.7 %copy-done = f32[32,256]{1,0:T(8,128)S(1)} copy-done((f32[32,256]{1,0:T(8,128)S(1)}, f32[32,256]{1,0:T(8,128)}, u32[]{:S(2)}) %copy-start) | copy-done | bytes 32792
  1.4 0.8 %copy-done.3 = bf16[6,4096]{1,0:T(8,128)(2,1)S(1)} copy-done((bf16[6,4096]{1,0:T(8,128)(2,1)S(1)}, bf16[6,4096]{1,0:T(8,128)(2,1)}, u32[]{:S(2)}) %copy-start.3) | copy-done | bytes 49176
  2.2 0.7 %copy-done.4 = s32[256]{0:T(256)S(1)} copy-done((s32[256]{0:T(256)S(1)}, s32[256]{0:T(256)}, u32[]{:S(2)}) %copy-start.4) | copy-done | bytes 1048
  2.9 0.2 shard_map.59.refs_0_.refs_2_
  3.1 5.1 %collective-permute-start.2 = (f32[40,256]{1,0:T(8,128)S(1)}, f32[40,256]{1,0:T(8,128)S(1)}, u32[]{:S(2)}, u32[]{:S(2)}) collective-permute-start(f32[40,256]{1,0:T(8,128)S(1)} %shard_map.59.refs_0_.refs_2_), channel_id=1, source_target_pairs={{0,3},{1,0},{2,1},{3,2},{4,7},{5,4},{6,5},{7,6},{8,11},{9,8},{10,9... | collective-permute-start | bytes 122888 | tf_op jit(solution)/shard_map/ppermute | solution.py:140
  8.2 1.0 %collective-permute-start = (f32[40,256]{1,0:T(8,128)S(1)}, f32[40,256]{1,0:T(8,128)S(1)}, u32[]{:S(2)}, u32[]{:S(2)}) collective-permute-start(f32[40,256]{1,0:T(8,128)S(1)} %shard_map.59.refs_0_.refs_2_), channel_id=1, source_target_pairs={{0,1},{1,2},{2,3},{3,0},{4,5},{5,6},{6,7},{7,4},{8,9},{9,10},{10,1... | collective-permute-start | bytes 122888 | tf_op jit(solution)/shard_map/ppermute | solution.py:140
  9.2 0.7 %collective-permute-done.2.refs_3_.refs_5_ = f32[40,256]{1,0:T(8,128)S(1)} collective-permute-done((f32[40,256]{1,0:T(8,128)S(1)}, f32[40,256]{1,0:T(8,128)S(1)}, u32[]{:S(2)}, u32[]{:S(2)}) %collective-permute-start.2) | collective-permute-done | bytes 40992 | tf_op jit(solution)/shard_map/ppermute | solution.py:140
  9.9 3.2 %collective-permute-done.1.refs_2_.refs_4_ = f32[40,256]{1,0:T(8,128)S(1)} collective-permute-done((f32[40,256]{1,0:T(8,128)S(1)}, f32[40,256]{1,0:T(8,128)S(1)}, u32[]{:S(2)}, u32[]{:S(2)}) %collective-permute-start.1) | collective-permute-done | bytes 40992 | tf_op jit(solution)/shard_map/ppermute | solution.py:140
  13.1 0.9 %collective-permute-done.refs_1_.refs_3_ = f32[40,256]{1,0:T(8,128)S(1)} collective-permute-done((f32[40,256]{1,0:T(8,128)S(1)}, f32[40,256]{1,0:T(8,128)S(1)}, u32[]{:S(2)}, u32[]{:S(2)}) %collective-permute-start) | collective-permute-done | bytes 40992 | tf_op jit(solution)/shard_map/ppermute | solution.py:140
  14.0 0.1 shard_map.60
  14.2 1.6 %collective-permute-start.4 = (bf16[4,48,256]{2,1,0:T(8,128)(2,1)S(1)}, bf16[4,48,256]{2,1,0:T(8,128)(2,1)S(1)}, u32[]{:S(2)}, u32[]{:S(2)}) collective-permute-start(bf16[4,48,256]{2,1,0:T(8,128)(2,1)S(1)} %get-tuple-element.7.refs_6_), channel_id=1, source_target_pairs={{0,8},{4,12},{8,0},{12,4},{1,9},{5,13},{9,1},{13,5},{2,10},{6,14},... | collective-permute-start | bytes 294920 | tf_op jit(solution)/shard_map/ppermute | solution.py:140
  15.7 0.2 collective-permute-start.3
  15.9 0.5 %collective-permute-done.5.refs_9_ = bf16[4,48,256]{2,1,0:T(8,128)(2,1)S(1)} collective-permute-done((bf16[4,48,256]{2,1,0:T(8,128)(2,1)S(1)}, bf16[4,48,256]{2,1,0:T(8,128)(2,1)S(1)}, u32[]{:S(2)}, u32[]{:S(2)}) %collective-permute-start.5) | collective-permute-done | bytes 98336 | tf_op jit(solution)/shard_map/ppermute | solution.py:140
  16.4 5.0 %collective-permute-done.4.refs_8_ = bf16[4,48,256]{2,1,0:T(8,128)(2,1)S(1)} collective-permute-done((bf16[4,48,256]{2,1,0:T(8,128)(2,1)S(1)}, bf16[4,48,256]{2,1,0:T(8,128)(2,1)S(1)}, u32[]{:S(2)}, u32[]{:S(2)}) %collective-permute-start.4) | collective-permute-done | bytes 98336 | tf_op jit(solution)/shard_map/ppermute | solution.py:140
  21.4 0.1 collective-permute-done.3.refs_7_
  21.4 0.7 %copy-done.2 = f32[32,32]{1,0:T(8,128)S(1)} copy-done((f32[32,32]{1,0:T(8,128)S(1)}, f32[32,32]{1,0:T(8,128)}, u32[]{:S(2)}) %copy-start.2) | copy-done | bytes 4120
  22.1 5.0 %shard_map.61 = (bf16[16,256,256]{2,1,0:T(8,128)(2,1)S(1)}, bf16[4,32,256]{2,1,0:T(8,128)(2,1)S(1)}) custom-call(bf16[16,1024]{1,0:T(8,128)(2,1)S(1)} %get-tuple-element.6.refs_0_, f32[32,32]{1,0:T(8,128)S(1)} %copy-done.2, f32[40,256]{1,0:T(8,128)S(1)} %shard_map.59.refs_0_.refs_2_, f32[40,256]{1,0:T(8,128)S(1)} %collective-permute-done.refs_1_.refs_3_, ...), custom_call_target="tpu_custom_call" | custom-call | tf_op jit(solution)/shard_map/pallas_call | solution.py:154
  27.2 0.6 %collective-permute-start.7 = (bf16[4,32,256]{2,1,0:T(8,128)(2,1)S(1)}, bf16[4,32,256]{2,1,0:T(8,128)(2,1)S(1)}, u32[]{:S(2)}, u32[]{:S(2)}) collective-permute-start(bf16[4,32,256]{2,1,0:T(8,128)(2,1)S(1)} %get-tuple-element.9.refs_3_), channel_id=1, source_target_pairs={{0,8},{4,12},{8,0},{12,4},{1,9},{5,13},{9,1},{13,5},{2,10},{6,14},... | collective-permute-start | bytes 196616 | tf_op jit(solution)/shard_map/ppermute | solution.py:140
  27.8 0.2 collective-permute-start.6
  27.9 1.6 %collective-permute-done.8.refs_6_ = bf16[4,32,256]{2,1,0:T(8,128)(2,1)S(1)} collective-permute-done((bf16[4,32,256]{2,1,0:T(8,128)(2,1)S(1)}, bf16[4,32,256]{2,1,0:T(8,128)(2,1)S(1)}, u32[]{:S(2)}, u32[]{:S(2)}) %collective-permute-start.8) | collective-permute-done | bytes 65568 | tf_op jit(solution)/shard_map/ppermute | solution.py:140
  29.6 2.6 %collective-permute-done.7.refs_5_ = bf16[4,32,256]{2,1,0:T(8,128)(2,1)S(1)} collective-permute-done((bf16[4,32,256]{2,1,0:T(8,128)(2,1)S(1)}, bf16[4,32,256]{2,1,0:T(8,128)(2,1)S(1)}, u32[]{:S(2)}, u32[]{:S(2)}) %collective-permute-start.7) | collective-permute-done | bytes 65568 | tf_op jit(solution)/shard_map/ppermute | solution.py:140
  32.1 0.3 collective-permute-done.6.refs_4_
  32.4 0.8 %copy-done.1 = f32[32,256]{1,0:T(8,128)S(1)} copy-done((f32[32,256]{1,0:T(8,128)S(1)}, f32[32,256]{1,0:T(8,128)}, u32[]{:S(2)}) %copy-start.1) | copy-done | bytes 32792
  33.1 1.3 %shard_map.62 = (f32[32,256]{1,0:T(8,128)}, f32[32,256]{1,0:T(8,128)}) custom-call(f32[32,256]{1,0:T(8,128)S(1)} %copy-done.1, f32[32,32]{1,0:T(8,128)S(1)} %copy-done.2, bf16[16,256,256]{2,1,0:T(8,128)(2,1)S(1)} %get-tuple-element.8.refs_2_, bf16[4,32,256]{2,1,0:T(8,128)(2,1)S(1)} %get-tuple-element.9.refs_3_, ...), custom_call_target="tpu_custom_call" | custom-call | tf_op jit(solution)/shard_map/pallas_call | solution.py:154
  (8 shorter events, 0.1 us)
Async XLA Ops:
  0.6 0.8 %copy-start = (f32[32,256]{1,0:T(8,128)S(1)}, f32[32,256]{1,0:T(8,128)}, u32[]{:S(2)}) copy-start(f32[32,256]{1,0:T(8,128)} %refs_0_.1) | copy-start | bytes 98308
  1.4 0.8 %copy-start.3 = (bf16[6,4096]{1,0:T(8,128)(2,1)S(1)}, bf16[6,4096]{1,0:T(8,128)(2,1)}, u32[]{:S(2)}) copy-start(bf16[6,4096]{1,0:T(8,128)(2,1)} %features_ref.1) | copy-start | bytes 147460
  2.2 0.7 %copy-start.4 = (s32[256]{0:T(256)S(1)}, s32[256]{0:T(256)}, u32[]{:S(2)}) copy-start(s32[256]{0:T(256)} %param.5) | copy-start | bytes 3076
  3.1 6.8 %collective-permute-start.2 = (f32[40,256]{1,0:T(8,128)S(1)}, f32[40,256]{1,0:T(8,128)S(1)}, u32[]{:S(2)}, u32[]{:S(2)}) collective-permute-start(f32[40,256]{1,0:T(8,128)S(1)} %shard_map.59.refs_0_.refs_2_), channel_id=1, source_target_pairs={{0,3},{1,0},{2,1},{3,2},{4,7},{5,4},{6,5},{7,6},{8,11},{9,8},{10,9... | collective-permute-start | bytes 122888 | tf_op jit(solution)/shard_map/ppermute | solution.py:140
  8.2 4.9 %collective-permute-start.1 = (f32[40,256]{1,0:T(8,128)S(1)}, f32[40,256]{1,0:T(8,128)S(1)}, u32[]{:S(2)}, u32[]{:S(2)}) collective-permute-start(f32[40,256]{1,0:T(8,128)S(1)} %shard_map.59.refs_0_.refs_2_), channel_id=1, source_target_pairs={{0,2},{1,3},{2,0},{3,1},{4,6},{5,7},{6,4},{7,5},{8,10},{9,11},{10,... | collective-permute-start | bytes 122888 | tf_op jit(solution)/shard_map/ppermute | solution.py:140
  8.2 5.8 %collective-permute-start = (f32[40,256]{1,0:T(8,128)S(1)}, f32[40,256]{1,0:T(8,128)S(1)}, u32[]{:S(2)}, u32[]{:S(2)}) collective-permute-start(f32[40,256]{1,0:T(8,128)S(1)} %shard_map.59.refs_0_.refs_2_), channel_id=1, source_target_pairs={{0,1},{1,2},{2,3},{3,0},{4,5},{5,6},{6,7},{7,4},{8,9},{9,10},{10,1... | collective-permute-start | bytes 122888 | tf_op jit(solution)/shard_map/ppermute | solution.py:140
  14.1 2.3 %collective-permute-start.5 = (bf16[4,48,256]{2,1,0:T(8,128)(2,1)S(1)}, bf16[4,48,256]{2,1,0:T(8,128)(2,1)S(1)}, u32[]{:S(2)}, u32[]{:S(2)}) collective-permute-start(bf16[4,48,256]{2,1,0:T(8,128)(2,1)S(1)} %get-tuple-element.7.refs_6_), channel_id=1, source_target_pairs={{0,12},{4,0},{8,4},{12,8},{1,13},{5,1},{9,5},{13,9},{2,14},{6,2},{... | collective-permute-start | bytes 294920 | tf_op jit(solution)/shard_map/ppermute | solution.py:140
  14.2 7.2 %collective-permute-start.4 = (bf16[4,48,256]{2,1,0:T(8,128)(2,1)S(1)}, bf16[4,48,256]{2,1,0:T(8,128)(2,1)S(1)}, u32[]{:S(2)}, u32[]{:S(2)}) collective-permute-start(bf16[4,48,256]{2,1,0:T(8,128)(2,1)S(1)} %get-tuple-element.7.refs_6_), channel_id=1, source_target_pairs={{0,8},{4,12},{8,0},{12,4},{1,9},{5,13},{9,1},{13,5},{2,10},{6,14},... | collective-permute-start | bytes 294920 | tf_op jit(solution)/shard_map/ppermute | solution.py:140
  15.7 5.7 %collective-permute-start.3 = (bf16[4,48,256]{2,1,0:T(8,128)(2,1)S(1)}, bf16[4,48,256]{2,1,0:T(8,128)(2,1)S(1)}, u32[]{:S(2)}, u32[]{:S(2)}) collective-permute-start(bf16[4,48,256]{2,1,0:T(8,128)(2,1)S(1)} %get-tuple-element.7.refs_6_), channel_id=1, source_target_pairs={{0,4},{4,8},{8,12},{12,0},{1,5},{5,9},{9,13},{13,1},{2,6},{6,10},{... | collective-permute-start | bytes 294920 | tf_op jit(solution)/shard_map/ppermute | solution.py:140
  21.4 0.7 %copy-start.2 = (f32[32,32]{1,0:T(8,128)S(1)}, f32[32,32]{1,0:T(8,128)}, u32[]{:S(2)}) copy-start(f32[32,32]{1,0:T(8,128)} %refs_1_.3) | copy-start | bytes 12292
  27.1 2.5 %collective-permute-start.8 = (bf16[4,32,256]{2,1,0:T(8,128)(2,1)S(1)}, bf16[4,32,256]{2,1,0:T(8,128)(2,1)S(1)}, u32[]{:S(2)}, u32[]{:S(2)}) collective-permute-start(bf16[4,32,256]{2,1,0:T(8,128)(2,1)S(1)} %get-tuple-element.9.refs_3_), channel_id=1, source_target_pairs={{0,12},{4,0},{8,4},{12,8},{1,13},{5,1},{9,5},{13,9},{2,14},{6,2},{... | collective-permute-start | bytes 196616 | tf_op jit(solution)/shard_map/ppermute | solution.py:140
  27.2 5.0 %collective-permute-start.7 = (bf16[4,32,256]{2,1,0:T(8,128)(2,1)S(1)}, bf16[4,32,256]{2,1,0:T(8,128)(2,1)S(1)}, u32[]{:S(2)}, u32[]{:S(2)}) collective-permute-start(bf16[4,32,256]{2,1,0:T(8,128)(2,1)S(1)} %get-tuple-element.9.refs_3_), channel_id=1, source_target_pairs={{0,8},{4,12},{8,0},{12,4},{1,9},{5,13},{9,1},{13,5},{2,10},{6,14},... | collective-permute-start | bytes 196616 | tf_op jit(solution)/shard_map/ppermute | solution.py:140
  27.8 4.6 %collective-permute-start.6 = (bf16[4,32,256]{2,1,0:T(8,128)(2,1)S(1)}, bf16[4,32,256]{2,1,0:T(8,128)(2,1)S(1)}, u32[]{:S(2)}, u32[]{:S(2)}) collective-permute-start(bf16[4,32,256]{2,1,0:T(8,128)(2,1)S(1)} %get-tuple-element.9.refs_3_), channel_id=1, source_target_pairs={{0,4},{4,8},{8,12},{12,0},{1,5},{5,9},{9,13},{13,1},{2,6},{6,10},{... | collective-permute-start | bytes 196616 | tf_op jit(solution)/shard_map/ppermute | solution.py:140
  32.4 0.8 %copy-start.1 = (f32[32,256]{1,0:T(8,128)S(1)}, f32[32,256]{1,0:T(8,128)}, u32[]{:S(2)}) copy-start(f32[32,256]{1,0:T(8,128)} %refs_0_.1) | copy-start | bytes 98308

commit v5 on v4

v5 whole, which is shorter than its diff:
```python
import functools
import math

import jax
import jax.numpy as jnp
from jax import lax
from jax.experimental import pallas as pl
from jax.experimental.pallas import tpu as pltpu
from jax.sharding import PartitionSpec as P

AUX = 16
LANES = 128
VMEM_LIMIT = 56 * 1024 * 1024
KEPT_BYTES = 4 * 1024 * 1024


def normalize(logits):
    raised = jnp.exp(logits)
    return raised / jnp.sum(raised, axis=0, keepdims=True)


def three_parts(value):
    high = value.astype(jnp.bfloat16).astype(jnp.float32)
    middle = (value - high).astype(jnp.bfloat16).astype(jnp.float32)
    return [high, middle, value - high - middle]


def pick_features(features_ref, member):
    feats, points = features_ref.shape
    own = member.shape[1]
    groups = points // LANES
    wide = features_ref[...].astype(jnp.float32)
    wide = jnp.concatenate([wide, jnp.zeros((8 - feats, points), jnp.float32)], axis=0)
    table = jnp.concatenate(
        [wide[:, group * LANES:(group + 1) * LANES] for group in range(groups)], axis=0
    ).astype(jnp.bfloat16)
    lane = lax.broadcasted_iota(jnp.int32, (LANES, own), 0)
    chosen = jnp.where(lane == member % LANES, 1.0, 0.0).astype(jnp.bfloat16)
    found = jnp.dot(table, chosen, preferred_element_type=jnp.float32)
    found = found.reshape(groups, 8, own)
    group = lax.broadcasted_iota(jnp.int32, (groups, 8, own), 0)
    return jnp.sum(jnp.where(group == (member // LANES)[None], found, 0.0), axis=0)


def prepare_kernel(features_ref, member_ref, unary_ref, compat_ref, sent_ref, held_ref):
    labels = unary_ref.shape[0]
    sent_ref[pl.ds(0, labels), :] = unary_ref[...]
    sent_ref[pl.ds(labels, 8), :] = pick_features(features_ref, member_ref[...])
    held_ref[...] = compat_ref[...]


def half_norms(feats):
    return three_parts(-0.5 * jnp.sum(feats * feats, axis=0, keepdims=True))


def product_sides(feats):
    own = feats.shape[1]
    norms = half_norms(feats)
    ones = jnp.ones((3, own), jnp.float32)
    spare = jnp.zeros((AUX - 8 - 6, own), jnp.float32)
    columns = jnp.concatenate([feats] + norms + [ones, spare], axis=0)
    rows = jnp.concatenate([feats, ones] + norms + [spare], axis=0)
    return columns.astype(jnp.bfloat16), rows.astype(jnp.bfloat16)


def pack_kernel(labels, *refs):
    near_refs, packed_ref, rows_ref = refs[:-2], refs[-2], refs[-1]
    for place, near_ref in enumerate(near_refs):
        own = near_ref.shape[1]
        feats = near_ref[pl.ds(labels, 8), :]
        probs = normalize(-near_ref[pl.ds(0, labels), :])
        packed_ref[place] = jnp.concatenate([probs, feats], axis=0).astype(jnp.bfloat16)
        rows_ref[:, pl.ds(place * own, own)] = product_sides(feats)[1]


def over_blocks(refs, body, start):
    base = 0
    unrolled = sum(ref.shape[0] for ref in refs) <= 16
    for ref in refs:
        size = ref.shape[0]
        if unrolled:
            for index in range(size):
                start = body(ref, index, base + index, start)
        else:
            step = lambda index, total, ref=ref, base=base: body(ref, index, base + index, total)
            start = lax.fori_loop(0, size, step, start)
        base += size
    return start


def finish(message, qb, unary, compat_ref):
    message = message - qb.astype(jnp.float32)
    pairwise = jnp.dot(
        compat_ref[...], message, precision=lax.Precision.HIGHEST,
        preferred_element_type=jnp.float32,
    )
    return normalize(-unary - pairwise), pairwise


def first_kernel(labels, nears, *refs):
    rows_ref, compat_ref = refs[:2]
    near_refs = refs[2:2 + nears]
    packed_refs = refs[2 + nears:-3]
    tile_ref, q_ref, columns_ref = refs[-3:]
    own = near_refs[0].shape[1]

    def transpose(packed_ref, index, place, done):
        feats = packed_ref[index][labels:].astype(jnp.float32)
        columns_ref[place] = product_sides(feats)[0].T
        return done

    over_blocks(packed_refs, transpose, 0)
    for near in range(nears):
        rows = rows_ref[:, pl.ds(near * own, own)]

        def body(packed_ref, index, place, total, near=near, rows=rows):
            pieces = []
            for piece in range(own // LANES):
                exponent = jnp.dot(
                    columns_ref[place, pl.ds(piece * LANES, LANES), :], rows,
                    preferred_element_type=jnp.float32,
                )
                pieces.append(jnp.exp(exponent).astype(jnp.bfloat16))
            tile = jnp.concatenate(pieces, axis=0)
            if near == 0:
                tile_ref[place] = tile
            return total + jnp.dot(
                packed_ref[index][:labels], tile, preferred_element_type=jnp.float32
            )

        total = over_blocks(packed_refs, body, jnp.zeros((labels, own), jnp.float32))
        probs, _ = finish(
            total, packed_refs[0][near][:labels], near_refs[near][pl.ds(0, labels), :], compat_ref
        )
        q_ref[near] = probs.astype(jnp.bfloat16)


def second_kernel(near_ref, compat_ref, tile_ref, *refs):
    q_refs = refs[:-2]
    probs_ref, pairwise_ref = refs[-2:]
    unary = near_ref[pl.ds(0, probs_ref.shape[0]), :]

    def body(q_ref, index, place, total):
        return total + jnp.dot(
            q_ref[index], tile_ref[place], preferred_element_type=jnp.float32
        )

    total = over_blocks(q_refs, body, jnp.zeros(unary.shape, jnp.float32))
    probs, pairwise = finish(total, q_refs[0][0], unary, compat_ref)
    probs_ref[...] = probs
    pairwise_ref[...] = pairwise


def swap(value, axis, steps):
    count = lax.axis_size(axis)
    paired = count & (count - 1) == 0
    pairs = [
        (source, source ^ steps if paired else (source + steps) % count)
        for source in range(count)
    ]
    return lax.ppermute(value, axis, pairs)


def group_partners(value):
    return [value] + [swap(value, "grp", steps) for steps in range(1, lax.axis_size("grp"))]


def block_partners(value):
    count = lax.axis_size("blk")
    if count & (count - 1):
        return [value] + [swap(value, "blk", steps) for steps in range(1, count)]
    far = [swap(value, "blk", steps) for steps in range(2, count, 2)]
    held = [value] + far
    return held + [swap(stack, "blk", 1) for stack in held]


def small(dims, kind):
    return math.prod(dims) * jnp.dtype(kind).itemsize <= KEPT_BYTES


def call(kernel, out_shapes, *operands, scratch=()):
    return pl.pallas_call(
        kernel,
        out_shape=tuple(out_shapes),
        scratch_shapes=scratch,
        compiler_params=pltpu.CompilerParams(vmem_limit_bytes=VMEM_LIMIT),
    )(*operands)


def hold(*operands):
    return [
        pltpu.with_memory_space_constraint(operand, pltpu.VMEM)
        if small(operand.shape, operand.dtype) else operand
        for operand in operands
    ]


def kept(dims, kind):
    return pltpu.VMEM(dims, kind) if small(dims, kind) else jax.ShapeDtypeStruct(dims, kind)


def shards(unary, member, features, compat):
    labels, own = unary.shape
    nears = lax.axis_size("grp")
    count = lax.axis_size("blk") * nears
    sent, held = call(
        prepare_kernel,
        [kept((labels + 8, own), jnp.float32), kept(compat.shape, jnp.float32)],
        features, member[None], unary, compat,
    )
    near = group_partners(sent)
    packed, rows = call(
        functools.partial(pack_kernel, labels),
        [kept((nears, labels + 8, own), jnp.bfloat16), kept((AUX, nears * own), jnp.bfloat16)],
        *hold(*near),
    )
    tile, q_near = call(
        functools.partial(first_kernel, labels, nears),
        [kept((count, own, own), jnp.bfloat16), kept((nears, labels, own), jnp.bfloat16)],
        *hold(rows, held, *near, *block_partners(packed)),
        scratch=[pltpu.VMEM((count, own, AUX), jnp.bfloat16)],
    )
    return call(
        second_kernel,
        [jax.ShapeDtypeStruct((labels, own), jnp.float32)] * 2,
        *hold(sent, held, tile, *block_partners(q_near)),
    )


def solution(mesh):
    in_specs = (P(None, ("scene", "blk", "grp")), P(("scene", "blk", "grp")), P(None, "scene"), P())
    out_specs = (P(None, ("scene", "blk", "grp")), P(None, ("scene", "blk", "grp")))
    return jax.shard_map(shards, mesh=mesh, in_specs=in_specs, out_specs=out_specs, check_vma=False)
```

time: 34.8 us -> 34.4 us (0.989)
  Pallas kernels: 6.54 us -> 12.2 us
  local copies, waits for them, and re-layouts: 3.75 us -> 0 us
  waiting for transfers between devices: 14.8 us -> 12.4 us
    pallas_call x4, Pallas kernels: 6.54 us -> 12.2 us  [call(): pl.pallas_call(kernel, out_shape=tuple(out_shapes), scratch_shapes=scratc...]
    unnamed x10 -> x0, local copies, waits for them, and re-layouts: 3.75 us -> none
    ppermute x9, waiting for transfers between devices: 14.8 us -> 12.4 us  [swap(): return lax.ppermute(value, axis, pairs)]
  transfers between devices with their start and end apart: 9 -> 9, of which waited for: 9 -> 6; matrix products, arithmetic and copies ran while one was open for 0% -> 0% of each run, Pallas kernels for 0% -> 0%
where the time goes in v5:
time: 34.4 us; the launch traced here: 34.2 us
  waiting for transfers between devices  12.4 us (36%)
  Pallas kernels  12.2 us (35%)
  starting transfers between devices  8.94 us (26%)
  between operations  0.66 us (2%)
    ppermute x9, waiting for transfers between devices, swap(): return lax.ppermute(value, axis, pairs)  12.4 us
    pallas_call x4, Pallas kernels, call(): pl.pallas_call(kernel, out_shape=tuple(out_shapes), scratch_shapes=scratc...  12.2 us
    ppermute x9, starting transfers between devices, swap(): return lax.ppermute(value, axis, pairs)  8.94 us
  transfers between devices with their start and end apart: 9, of which 6 were waited for; matrix products, arithmetic and copies ran while one was open for 0% of the time, Pallas kernels for 0%

profile of v5, /device:TPU:0, one launch (start us, length us, event | category | flops | bytes accessed | tf_op | source)
XLA Modules:
  0.0 34.2 jit_solution(13479937184085575059)
XLA Ops:
  0.6 1.1 %shard_map.59 = (f32[40,256]{1,0:T(8,128)S(1)}, f32[32,32]{1,0:T(8,128)S(1)}) custom-call(bf16[6,4096]{1,0:T(8,128)(2,1)} %features_ref.1, s32[1,256]{1,0:T(1,128)} %bitcast.1, f32[32,256]{1,0:T(8,128)} %unary_ref.1, f32[32,32]{1,0:T(8,128)} %compat_ref.1), custom_call_target="tpu_custom_call" | custom-call | tf_op jit(solution)/shard_map/pallas_call | solution.py:182
  1.7 5.1 %collective-permute-start.2 = (f32[40,256]{1,0:T(8,128)S(1)}, f32[40,256]{1,0:T(8,128)S(1)}, u32[]{:S(2)}, u32[]{:S(2)}) collective-permute-start(f32[40,256]{1,0:T(8,128)S(1)} %get-tuple-element.8.refs_0_.refs_2_.near_ref), channel_id=1, source_target_pairs={{0,3},{1,2},{2,1},{3,0},{4,7},{5,6},{6,5},{7,4},{8,11},{9,10},{10,... | collective-permute-start | bytes 122888 | tf_op jit(solution)/shard_map/ppermute | solution.py:161
  6.8 0.0 collective-permute-start.1
  6.8 0.6 %collective-permute-start = (f32[40,256]{1,0:T(8,128)S(1)}, f32[40,256]{1,0:T(8,128)S(1)}, u32[]{:S(2)}, u32[]{:S(2)}) collective-permute-start(f32[40,256]{1,0:T(8,128)S(1)} %get-tuple-element.8.refs_0_.refs_2_.near_ref), channel_id=1, source_target_pairs={{0,1},{1,0},{2,3},{3,2},{4,5},{5,4},{6,7},{7,6},{8,9},{9,8},{10,11... | collective-permute-start | bytes 122888 | tf_op jit(solution)/shard_map/ppermute | solution.py:161
  7.5 1.4 %collective-permute-done.2.refs_3_.refs_5_ = f32[40,256]{1,0:T(8,128)S(1)} collective-permute-done((f32[40,256]{1,0:T(8,128)S(1)}, f32[40,256]{1,0:T(8,128)S(1)}, u32[]{:S(2)}, u32[]{:S(2)}) %collective-permute-start.2) | collective-permute-done | bytes 40992 | tf_op jit(solution)/shard_map/ppermute | solution.py:161
  8.8 2.9 %collective-permute-done.1.refs_2_.refs_4_ = f32[40,256]{1,0:T(8,128)S(1)} collective-permute-done((f32[40,256]{1,0:T(8,128)S(1)}, f32[40,256]{1,0:T(8,128)S(1)}, u32[]{:S(2)}, u32[]{:S(2)}) %collective-permute-start.1) | collective-permute-done | bytes 40992 | tf_op jit(solution)/shard_map/ppermute | solution.py:161
  11.7 0.0 collective-permute-done.refs_1_.refs_3_
  11.7 0.1 shard_map.60
  11.8 1.6 %collective-permute-start.3 = (bf16[4,40,256]{2,1,0:T(8,128)(2,1)S(1)}, bf16[4,40,256]{2,1,0:T(8,128)(2,1)S(1)}, u32[]{:S(2)}, u32[]{:S(2)}) collective-permute-start(bf16[4,40,256]{2,1,0:T(8,128)(2,1)S(1)} %get-tuple-element.11.refs_6_), channel_id=1, source_target_pairs={{0,8},{4,12},{8,0},{12,4},{1,9},{5,13},{9,1},{13,5},{2,10},{6,14},... | collective-permute-start | bytes 245768 | tf_op jit(solution)/shard_map/ppermute | solution.py:161
  13.4 0.0 collective-permute-start.4
  13.4 2.9 %collective-permute-done.3.refs_7_ = bf16[4,40,256]{2,1,0:T(8,128)(2,1)S(1)} collective-permute-done((bf16[4,40,256]{2,1,0:T(8,128)(2,1)S(1)}, bf16[4,40,256]{2,1,0:T(8,128)(2,1)S(1)}, u32[]{:S(2)}, u32[]{:S(2)}) %collective-permute-start.3) | collective-permute-done | bytes 81952 | tf_op jit(solution)/shard_map/ppermute | solution.py:161
  16.3 0.0 collective-permute-start.5
  16.3 0.0 collective-permute-done.4.refs_8_
  16.3 1.3 %collective-permute-done.5.refs_9_ = bf16[4,40,256]{2,1,0:T(8,128)(2,1)S(1)} collective-permute-done((bf16[4,40,256]{2,1,0:T(8,128)(2,1)S(1)}, bf16[4,40,256]{2,1,0:T(8,128)(2,1)S(1)}, u32[]{:S(2)}, u32[]{:S(2)}) %collective-permute-start.5) | collective-permute-done | bytes 81952 | tf_op jit(solution)/shard_map/ppermute | solution.py:161
  17.6 9.7 %shard_map.61 = (bf16[16,256,256]{2,1,0:T(8,128)(2,1)S(1)}, bf16[4,32,256]{2,1,0:T(8,128)(2,1)S(1)}) custom-call(bf16[16,1024]{1,0:T(8,128)(2,1)S(1)} %get-tuple-element.10.refs_0_, f32[32,32]{1,0:T(8,128)S(1)} %get-tuple-element.9.refs_1_.compat_ref, f32[40,256]{1,0:T(8,128)S(1)} %get-tuple-element.8.refs_0_.refs_2_.near_ref, ...), custom_call_target="tpu_custom_call" | custom-call | tf_op jit(solution)/shard_map/pallas_call | solution.py:182
  27.3 1.6 %collective-permute-start.6 = (bf16[4,32,256]{2,1,0:T(8,128)(2,1)S(1)}, bf16[4,32,256]{2,1,0:T(8,128)(2,1)S(1)}, u32[]{:S(2)}, u32[]{:S(2)}) collective-permute-start(bf16[4,32,256]{2,1,0:T(8,128)(2,1)S(1)} %get-tuple-element.13.refs_0_), channel_id=1, source_target_pairs={{0,8},{4,12},{8,0},{12,4},{1,9},{5,13},{9,1},{13,5},{2,10},{6,14},... | collective-permute-start | bytes 196616 | tf_op jit(solution)/shard_map/ppermute | solution.py:161
  28.9 0.0 collective-permute-start.7
  28.9 2.7 %collective-permute-done.6.refs_1_ = bf16[4,32,256]{2,1,0:T(8,128)(2,1)S(1)} collective-permute-done((bf16[4,32,256]{2,1,0:T(8,128)(2,1)S(1)}, bf16[4,32,256]{2,1,0:T(8,128)(2,1)S(1)}, u32[]{:S(2)}, u32[]{:S(2)}) %collective-permute-start.6) | collective-permute-done | bytes 65568 | tf_op jit(solution)/shard_map/ppermute | solution.py:161
  31.6 0.0 collective-permute-start.8
  31.6 0.0 collective-permute-done.7.refs_2_
  31.6 1.2 %collective-permute-done.8.refs_3_ = bf16[4,32,256]{2,1,0:T(8,128)(2,1)S(1)} collective-permute-done((bf16[4,32,256]{2,1,0:T(8,128)(2,1)S(1)}, bf16[4,32,256]{2,1,0:T(8,128)(2,1)S(1)}, u32[]{:S(2)}, u32[]{:S(2)}) %collective-permute-start.8) | collective-permute-done | bytes 65568 | tf_op jit(solution)/shard_map/ppermute | solution.py:161
  32.9 1.3 %shard_map.62 = (f32[32,256]{1,0:T(8,128)}, f32[32,256]{1,0:T(8,128)}) custom-call(f32[40,256]{1,0:T(8,128)S(1)} %get-tuple-element.8.refs_0_.refs_2_.near_ref, f32[32,32]{1,0:T(8,128)S(1)} %get-tuple-element.9.refs_1_.compat_ref, bf16[16,256,256]{2,1,0:T(8,128)(2,1)S(1)} %get-tuple-element.12.tile_ref, bf16[4,32,256]{2,1,0:T(8,128)(2,1)S(1)} %get-tuple-element.13.refs_0_, ...), custom_call_target="tpu_custom_call" | custom-call | tf_op jit(solution)/shard_map/pallas_call | solution.py:182
Async XLA Ops:
  1.7 7.1 %collective-permute-start.2 = (f32[40,256]{1,0:T(8,128)S(1)}, f32[40,256]{1,0:T(8,128)S(1)}, u32[]{:S(2)}, u32[]{:S(2)}) collective-permute-start(f32[40,256]{1,0:T(8,128)S(1)} %get-tuple-element.8.refs_0_.refs_2_.near_ref), channel_id=1, source_target_pairs={{0,3},{1,2},{2,1},{3,0},{4,7},{5,6},{6,5},{7,4},{8,11},{9,10},{10,... | collective-permute-start | bytes 122888 | tf_op jit(solution)/shard_map/ppermute | solution.py:161
  6.8 4.9 %collective-permute-start.1 = (f32[40,256]{1,0:T(8,128)S(1)}, f32[40,256]{1,0:T(8,128)S(1)}, u32[]{:S(2)}, u32[]{:S(2)}) collective-permute-start(f32[40,256]{1,0:T(8,128)S(1)} %get-tuple-element.8.refs_0_.refs_2_.near_ref), channel_id=1, source_target_pairs={{0,2},{1,3},{2,0},{3,1},{4,6},{5,7},{6,4},{7,5},{8,10},{9,11},{10,... | collective-permute-start | bytes 122888 | tf_op jit(solution)/shard_map/ppermute | solution.py:161
  6.8 4.9 %collective-permute-start = (f32[40,256]{1,0:T(8,128)S(1)}, f32[40,256]{1,0:T(8,128)S(1)}, u32[]{:S(2)}, u32[]{:S(2)}) collective-permute-start(f32[40,256]{1,0:T(8,128)S(1)} %get-tuple-element.8.refs_0_.refs_2_.near_ref), channel_id=1, source_target_pairs={{0,1},{1,0},{2,3},{3,2},{4,5},{5,4},{6,7},{7,6},{8,9},{9,8},{10,11... | collective-permute-start | bytes 122888 | tf_op jit(solution)/shard_map/ppermute | solution.py:161
  11.8 4.5 %collective-permute-start.3 = (bf16[4,40,256]{2,1,0:T(8,128)(2,1)S(1)}, bf16[4,40,256]{2,1,0:T(8,128)(2,1)S(1)}, u32[]{:S(2)}, u32[]{:S(2)}) collective-permute-start(bf16[4,40,256]{2,1,0:T(8,128)(2,1)S(1)} %get-tuple-element.11.refs_6_), channel_id=1, source_target_pairs={{0,8},{4,12},{8,0},{12,4},{1,9},{5,13},{9,1},{13,5},{2,10},{6,14},... | collective-permute-start | bytes 245768 | tf_op jit(solution)/shard_map/ppermute | solution.py:161
  13.4 2.9 %collective-permute-start.4 = (bf16[4,40,256]{2,1,0:T(8,128)(2,1)S(1)}, bf16[4,40,256]{2,1,0:T(8,128)(2,1)S(1)}, u32[]{:S(2)}, u32[]{:S(2)}) collective-permute-start(bf16[4,40,256]{2,1,0:T(8,128)(2,1)S(1)} %get-tuple-element.11.refs_6_), channel_id=1, source_target_pairs={{0,4},{4,0},{8,12},{12,8},{1,5},{5,1},{9,13},{13,9},{2,6},{6,2},{1... | collective-permute-start | bytes 245768 | tf_op jit(solution)/shard_map/ppermute | solution.py:161
  16.3 1.3 %collective-permute-start.5 = (bf16[4,40,256]{2,1,0:T(8,128)(2,1)S(1)}, bf16[4,40,256]{2,1,0:T(8,128)(2,1)S(1)}, u32[]{:S(2)}, u32[]{:S(2)}) collective-permute-start(bf16[4,40,256]{2,1,0:T(8,128)(2,1)S(1)} %collective-permute-done.3.refs_7_), channel_id=1, source_target_pairs={{0,4},{4,0},{8,12},{12,8},{1,5},{5,1},{9,13},{13,9},{2,6},{6,2},{1... | collective-permute-start | bytes 245768 | tf_op jit(solution)/shard_map/ppermute | solution.py:161
  27.3 4.3 %collective-permute-start.6 = (bf16[4,32,256]{2,1,0:T(8,128)(2,1)S(1)}, bf16[4,32,256]{2,1,0:T(8,128)(2,1)S(1)}, u32[]{:S(2)}, u32[]{:S(2)}) collective-permute-start(bf16[4,32,256]{2,1,0:T(8,128)(2,1)S(1)} %get-tuple-element.13.refs_0_), channel_id=1, source_target_pairs={{0,8},{4,12},{8,0},{12,4},{1,9},{5,13},{9,1},{13,5},{2,10},{6,14},... | collective-permute-start | bytes 196616 | tf_op jit(solution)/shard_map/ppermute | solution.py:161
  28.9 2.7 %collective-permute-start.7 = (bf16[4,32,256]{2,1,0:T(8,128)(2,1)S(1)}, bf16[4,32,256]{2,1,0:T(8,128)(2,1)S(1)}, u32[]{:S(2)}, u32[]{:S(2)}) collective-permute-start(bf16[4,32,256]{2,1,0:T(8,128)(2,1)S(1)} %get-tuple-element.13.refs_0_), channel_id=1, source_target_pairs={{0,4},{4,0},{8,12},{12,8},{1,5},{5,1},{9,13},{13,9},{2,6},{6,2},{1... | collective-permute-start | bytes 196616 | tf_op jit(solution)/shard_map/ppermute | solution.py:161
  31.6 1.3 %collective-permute-start.8 = (bf16[4,32,256]{2,1,0:T(8,128)(2,1)S(1)}, bf16[4,32,256]{2,1,0:T(8,128)(2,1)S(1)}, u32[]{:S(2)}, u32[]{:S(2)}) collective-permute-start(bf16[4,32,256]{2,1,0:T(8,128)(2,1)S(1)} %collective-permute-done.6.refs_1_), channel_id=1, source_target_pairs={{0,4},{4,0},{8,12},{12,8},{1,5},{5,1},{9,13},{13,9},{2,6},{6,2},{1... | collective-permute-start | bytes 196616 | tf_op jit(solution)/shard_map/ppermute | solution.py:161

commit v6 on v5

--- a/solution.py
+++ b/solution.py
@@ -73,19 +73,12 @@
         rows_ref[:, pl.ds(place * own, own)] = product_sides(feats)[1]
 
 
-def over_blocks(refs, body, start):
-    base = 0
-    unrolled = sum(ref.shape[0] for ref in refs) <= 16
-    for ref in refs:
-        size = ref.shape[0]
-        if unrolled:
-            for index in range(size):
-                start = body(ref, index, base + index, start)
-        else:
-            step = lambda index, total, ref=ref, base=base: body(ref, index, base + index, total)
-            start = lax.fori_loop(0, size, step, start)
-        base += size
-    return start
+def over_blocks(count, body, start):
+    if count <= 4:
+        for index in range(count):
+            start = body(index, start)
+        return start
+    return lax.fori_loop(0, count, body, start)
 
 
 def finish(message, qb, unary, compat_ref):
@@ -97,56 +90,64 @@
     return normalize(-unary - pairwise), pairwise
 
 
-def first_kernel(labels, nears, *refs):
-    rows_ref, compat_ref = refs[:2]
-    near_refs = refs[2:2 + nears]
-    packed_refs = refs[2 + nears:-3]
-    tile_ref, q_ref, columns_ref = refs[-3:]
-    own = near_refs[0].shape[1]
-
-    def transpose(packed_ref, index, place, done):
-        feats = packed_ref[index][labels:].astype(jnp.float32)
-        columns_ref[place] = product_sides(feats)[0].T
-        return done
-
-    over_blocks(packed_refs, transpose, 0)
+def first_part(labels, rows_ref, packed_ref, total, tile_ref):
+    blocks, _, own = packed_ref.shape
+    packed = jnp.concatenate([packed_ref[index] for index in range(blocks)], axis=1)
+    columns = product_sides(packed[labels:].astype(jnp.float32))[0]
+    exponent = lax.dot_general(
+        columns, rows_ref[...], (((0,), (0,)), ((), ())), preferred_element_type=jnp.float32
+    )
+    tile = jnp.exp(exponent).astype(jnp.bfloat16)
+    for index in range(blocks):
+        tile_ref[index] = tile[index * own:(index + 1) * own, :own]
+    return total + jnp.dot(packed[:labels], tile, preferred_element_type=jnp.float32)
+
+
+def first_opening(labels, rows_ref, packed_ref, total_ref, tile_ref):
+    start = jnp.zeros(total_ref.shape, jnp.float32)
+    total_ref[...] = first_part(labels, rows_ref, packed_ref, start, tile_ref)
+
+
+def first_middle(labels, rows_ref, packed_ref, sum_ref, total_ref, tile_ref):
+    total_ref[...] = first_part(labels, rows_ref, packed_ref, sum_ref[...], tile_ref)
+
+
+def first_closing(labels, nears, *refs):
+    rows_ref, packed_ref, sum_ref, own_ref, compat_ref = refs[:5]
+    near_refs, q_ref, tile_ref = refs[5:-2], refs[-2], refs[-1]
+    own = own_ref.shape[2]
+    total = first_part(labels, rows_ref, packed_ref, sum_ref[...], tile_ref)
+    labels_now = [own_ref[near][:labels] for near in range(nears)]
+    unary = [near_ref[pl.ds(0, labels), :] for near_ref in near_refs]
+    probs, _ = finish(
+        total, jnp.concatenate(labels_now, axis=1), jnp.concatenate(unary, axis=1), compat_ref
+    )
     for near in range(nears):
-        rows = rows_ref[:, pl.ds(near * own, own)]
-
-        def body(packed_ref, index, place, total, near=near, rows=rows):
-            pieces = []
-            for piece in range(own // LANES):
-                exponent = jnp.dot(
-                    columns_ref[place, pl.ds(piece * LANES, LANES), :], rows,
-                    preferred_element_type=jnp.float32,
-                )
-                pieces.append(jnp.exp(exponent).astype(jnp.bfloat16))
-            tile = jnp.concatenate(pieces, axis=0)
-            if near == 0:
-                tile_ref[place] = tile
-            return total + jnp.dot(
-                packed_ref[index][:labels], tile, preferred_element_type=jnp.float32
-            )
-
-        total = over_blocks(packed_refs, body, jnp.zeros((labels, own), jnp.float32))
-        probs, _ = finish(
-            total, packed_refs[0][near][:labels], near_refs[near][pl.ds(0, labels), :], compat_ref
+        q_ref[near] = probs[:, near * own:(near + 1) * own].astype(jnp.bfloat16)
+
+
+def second_part(pairs, total):
+    for q_ref, tile_ref in pairs:
+        body = lambda index, total, q_ref=q_ref, tile_ref=tile_ref: total + jnp.dot(
+            q_ref[index], tile_ref[index], preferred_element_type=jnp.float32
         )
-        q_ref[near] = probs.astype(jnp.bfloat16)
-
-
-def second_kernel(near_ref, compat_ref, tile_ref, *refs):
-    q_refs = refs[:-2]
-    probs_ref, pairwise_ref = refs[-2:]
-    unary = near_ref[pl.ds(0, probs_ref.shape[0]), :]
-
-    def body(q_ref, index, place, total):
-        return total + jnp.dot(
-            q_ref[index], tile_ref[place], preferred_element_type=jnp.float32
-        )
-
-    total = over_blocks(q_refs, body, jnp.zeros(unary.shape, jnp.float32))
-    probs, pairwise = finish(total, q_refs[0][0], unary, compat_ref)
+        total = over_blocks(q_ref.shape[0], body, total)
+    return total
+
+
+def second_opening(*refs):
+    total_ref = refs[-1]
+    stacks = len(refs) // 2
+    pairs = zip(refs[:stacks], refs[stacks:-1])
+    total_ref[...] = second_part(pairs, jnp.zeros(total_ref.shape, jnp.float32))
+
+
+def second_closing(
+    q_ref, tile_ref, sum_ref, own_ref, near_ref, compat_ref, probs_ref, pairwise_ref
+):
+    total = second_part([(q_ref, tile_ref)], sum_ref[...])
+    unary = near_ref[pl.ds(0, total.shape[0]), :]
+    probs, pairwise = finish(total, own_ref[0], unary, compat_ref)
     probs_ref[...] = probs
     pairwise_ref[...] = pairwise
 
@@ -162,27 +163,33 @@
 
 
 def group_partners(value):
-    return [value] + [swap(value, "grp", steps) for steps in range(1, lax.axis_size("grp"))]
-
-
-def block_partners(value):
+    count = lax.axis_size("grp")
+    order = sorted(range(1, count), key=lambda steps: (steps != count // 2, -steps))
+    return [value] + [swap(value, "grp", steps) for steps in reversed(order)]
+
+
+def block_partners(value, use_early=None):
     count = lax.axis_size("blk")
     if count & (count - 1):
-        return [value] + [swap(value, "blk", steps) for steps in range(1, count)]
+        stacks = [value] + [swap(value, "blk", steps) for steps in range(1, count)]
+        if use_early:
+            use_early(stacks[:2])
+        return stacks
     far = [swap(value, "blk", steps) for steps in range(2, count, 2)]
-    held = [value] + far
-    return held + [swap(stack, "blk", 1) for stack in held]
+    beside = swap(value, "blk", 1)
+    if use_early:
+        *far, _ = lax.optimization_barrier((*far, use_early([value, beside])))
+    return [value, beside] + far + [swap(stack, "blk", 1) for stack in far]
 
 
 def small(dims, kind):
     return math.prod(dims) * jnp.dtype(kind).itemsize <= KEPT_BYTES
 
 
-def call(kernel, out_shapes, *operands, scratch=()):
+def call(kernel, out_shapes, *operands):
     return pl.pallas_call(
         kernel,
         out_shape=tuple(out_shapes),
-        scratch_shapes=scratch,
         compiler_params=pltpu.CompilerParams(vmem_limit_bytes=VMEM_LIMIT),
     )(*operands)
 
@@ -195,8 +202,10 @@
     ]
 
 
-def kept(dims, kind):
-    return pltpu.VMEM(dims, kind) if small(dims, kind) else jax.ShapeDtypeStruct(dims, kind)
+def kept(dims, kind, copies=1):
+    if small((copies,) + dims, kind):
+        return pltpu.VMEM(dims, kind)
+    return jax.ShapeDtypeStruct(dims, kind)
 
 
 def shards(unary, member, features, compat):
@@ -214,16 +223,45 @@
         [kept((nears, labels + 8, own), jnp.bfloat16), kept((AUX, nears * own), jnp.bfloat16)],
         *hold(*near),
     )
-    tile, q_near = call(
-        functools.partial(first_kernel, labels, nears),
-        [kept((count, own, own), jnp.bfloat16), kept((nears, labels, own), jnp.bfloat16)],
-        *hold(rows, held, *near, *block_partners(packed)),
-        scratch=[pltpu.VMEM((count, own, AUX), jnp.bfloat16)],
-    )
+    parts = lax.axis_size("blk")
+    tile_kind = kept((nears, own, own), jnp.bfloat16, parts)
+    tiles, totals = [], []
+
+    def first(place, last, stack):
+        if last:
+            q_near, tile = call(
+                functools.partial(first_closing, labels, nears),
+                [kept((nears, labels, own), jnp.bfloat16), tile_kind],
+                *hold(rows, stack, *totals[-1:], packed, held, *near),
+            )
+            tiles.append(tile)
+            return q_near
+        total, tile = call(
+            functools.partial(first_middle if totals else first_opening, labels),
+            [kept((labels, nears * own), jnp.float32), tile_kind],
+            *hold(rows, stack, *totals[-1:]),
+        )
+        tiles.append(tile)
+        totals.append(total)
+        return total
+
+    def first_early(stacks):
+        for place, stack in enumerate(stacks):
+            result = first(place, place + 1 == parts, stack)
+        return result
+
+    stacks = block_partners(packed, first_early)
+    for place in range(2, parts):
+        q_near = first(place, place + 1 == parts, stacks[place])
+
+    if parts * math.prod(tile_kind.shape) * 2 <= KEPT_BYTES:
+        tiles = hold(*tiles)
+    *stacks, last = block_partners(q_near)
+    (total,) = call(second_opening, [kept((labels, own), jnp.float32)], *hold(*stacks), *tiles[:-1])
     return call(
-        second_kernel,
+        second_closing,
         [jax.ShapeDtypeStruct((labels, own), jnp.float32)] * 2,
-        *hold(sent, held, tile, *block_partners(q_near)),
+        *hold(last), tiles[-1], *hold(total, q_near, sent, held),
     )
 
 

time: 34.4 us -> 26 us (0.76)
  Pallas kernels: 12.2 us -> 7.05 us
  waiting for transfers between devices: 12.4 us -> 9.2 us
    pallas_call x4 -> x8, Pallas kernels: 12.2 us -> 7.05 us  [call(): pl.pallas_call(kernel, out_shape=tuple(out_shapes), compiler_params=pltpu...]
    ppermute x9, waiting for transfers between devices: 12.4 us -> 9.2 us  [swap(): return lax.ppermute(value, axis, pairs)]
  transfers between devices with their start and end apart: 9 -> 9, of which waited for: 6 -> 6; matrix products, arithmetic and copies ran while one was open for 0% -> 0% of each run, Pallas kernels for 0% -> 14%
where the time goes in v6:
time: 26 us; the launch traced here: 25.9 us
  waiting for transfers between devices  9.2 us (35%)
  starting transfers between devices  8.96 us (34%)
  Pallas kernels  7.05 us (27%)
  between operations  0.67 us (3%)
    ppermute x9, waiting for transfers between devices, swap(): return lax.ppermute(value, axis, pairs)  9.2 us
    ppermute x9, starting transfers between devices, swap(): return lax.ppermute(value, axis, pairs)  8.96 us
    pallas_call x8, Pallas kernels, call(): pl.pallas_call(kernel, out_shape=tuple(out_shapes), compiler_params=pltpu...  7.05 us
  transfers between devices with their start and end apart: 9, of which 6 were waited for; matrix products, arithmetic and copies ran while one was open for 0% of the time, Pallas kernels for 14%

profile of v6, /device:TPU:0, one launch (start us, length us, event | category | flops | bytes accessed | tf_op | source)
XLA Modules:
  0.0 25.9 jit_solution(7774521000436875598)
XLA Ops:
  0.6 1.1 %shard_map.59 = (f32[40,256]{1,0:T(8,128)S(1)}, f32[32,32]{1,0:T(8,128)S(1)}) custom-call(bf16[6,4096]{1,0:T(8,128)(2,1)} %features_ref.1, s32[1,256]{1,0:T(1,128)} %bitcast.1, f32[32,256]{1,0:T(8,128)} %unary_ref.1, f32[32,32]{1,0:T(8,128)} %compat_ref.1), custom_call_target="tpu_custom_call" | custom-call | tf_op jit(solution)/shard_map/pallas_call | solution.py:190
  1.7 4.1 %collective-permute-start.2 = (f32[40,256]{1,0:T(8,128)S(1)}, f32[40,256]{1,0:T(8,128)S(1)}, u32[]{:S(2)}, u32[]{:S(2)}) collective-permute-start(f32[40,256]{1,0:T(8,128)S(1)} %get-tuple-element.15.refs_0_.refs_5_.near_ref), channel_id=1, source_target_pairs={{0,2},{1,3},{2,0},{3,1},{4,6},{5,7},{6,4},{7,5},{8,10},{9,11},{10,... | collective-permute-start | bytes 122888 | tf_op jit(solution)/shard_map/ppermute | solution.py:162
  5.8 1.3 %collective-permute-start.1 = (f32[40,256]{1,0:T(8,128)S(1)}, f32[40,256]{1,0:T(8,128)S(1)}, u32[]{:S(2)}, u32[]{:S(2)}) collective-permute-start(f32[40,256]{1,0:T(8,128)S(1)} %get-tuple-element.15.refs_0_.refs_5_.near_ref), channel_id=1, source_target_pairs={{0,3},{1,2},{2,1},{3,0},{4,7},{5,6},{6,5},{7,4},{8,11},{9,10},{10,... | collective-permute-start | bytes 122888 | tf_op jit(solution)/shard_map/ppermute | solution.py:162
  7.1 0.2 collective-permute-start
  7.4 0.8 %collective-permute-done.2.refs_3_.refs_8_ = f32[40,256]{1,0:T(8,128)S(1)} collective-permute-done((f32[40,256]{1,0:T(8,128)S(1)}, f32[40,256]{1,0:T(8,128)S(1)}, u32[]{:S(2)}, u32[]{:S(2)}) %collective-permute-start.2) | collective-permute-done | bytes 40992 | tf_op jit(solution)/shard_map/ppermute | solution.py:162
  8.2 3.4 %collective-permute-done.1.refs_2_.refs_7_ = f32[40,256]{1,0:T(8,128)S(1)} collective-permute-done((f32[40,256]{1,0:T(8,128)S(1)}, f32[40,256]{1,0:T(8,128)S(1)}, u32[]{:S(2)}, u32[]{:S(2)}) %collective-permute-start.1) | collective-permute-done | bytes 40992 | tf_op jit(solution)/shard_map/ppermute | solution.py:162
  11.6 0.0 collective-permute-done.refs_1_.refs_6_
  11.6 0.1 shard_map.60
  11.7 0.1 collective-permute-start.4
  11.7 1.6 %collective-permute-start.3 = (bf16[4,40,256]{2,1,0:T(8,128)(2,1)S(1)}, bf16[4,40,256]{2,1,0:T(8,128)(2,1)S(1)}, u32[]{:S(2)}, u32[]{:S(2)}) collective-permute-start(bf16[4,40,256]{2,1,0:T(8,128)(2,1)S(1)} %get-tuple-element.17.packed_ref.refs_3_), channel_id=1, source_target_pairs={{0,8},{4,12},{8,0},{12,4},{1,9},{5,13},{9,1},{13,5},{2,10},{6,14},... | collective-permute-start | bytes 245768 | tf_op jit(solution)/shard_map/ppermute | solution.py:162
  13.3 1.1 %shard_map.61 = (f32[32,1024]{1,0:T(8,128)S(1)}, bf16[4,256,256]{2,1,0:T(8,128)(2,1)S(1)}) custom-call(bf16[16,1024]{1,0:T(8,128)(2,1)S(1)} %get-tuple-element.16.rows_ref.refs_0_, bf16[4,40,256]{2,1,0:T(8,128)(2,1)S(1)} %get-tuple-element.17.packed_ref.refs_3_), custom_call_target="tpu_custom_call" | custom-call | tf_op jit(solution)/shard_map/pallas_call | solution.py:190
  14.4 0.0 collective-permute-done.4.packed_ref
  14.4 1.1 %shard_map.62 = (f32[32,1024]{1,0:T(8,128)S(1)}, bf16[4,256,256]{2,1,0:T(8,128)(2,1)S(1)}) custom-call(bf16[16,1024]{1,0:T(8,128)(2,1)S(1)} %get-tuple-element.16.rows_ref.refs_0_, bf16[4,40,256]{2,1,0:T(8,128)(2,1)S(1)} %collective-permute-done.4.packed_ref, f32[32,1024]{1,0:T(8,128)S(1)} %get-tuple-element.18.sum_ref), custom_call_target="tpu_custom_call" | custom-call | tf_op jit(solution)/shard_map/pallas_call | solution.py:190
  15.5 1.1 %collective-permute-done.3.packed_ref = bf16[4,40,256]{2,1,0:T(8,128)(2,1)S(1)} collective-permute-done((bf16[4,40,256]{2,1,0:T(8,128)(2,1)S(1)}, bf16[4,40,256]{2,1,0:T(8,128)(2,1)S(1)}, u32[]{:S(2)}, u32[]{:S(2)}) %collective-permute-start.3) | collective-permute-done | bytes 81952 | tf_op jit(solution)/shard_map/ppermute | solution.py:162
  16.6 0.0 collective-permute-start.5
  16.6 1.1 %shard_map.63 = (f32[32,1024]{1,0:T(8,128)S(1)}, bf16[4,256,256]{2,1,0:T(8,128)(2,1)S(1)}) custom-call(bf16[16,1024]{1,0:T(8,128)(2,1)S(1)} %get-tuple-element.16.rows_ref.refs_0_, bf16[4,40,256]{2,1,0:T(8,128)(2,1)S(1)} %collective-permute-done.3.packed_ref, f32[32,1024]{1,0:T(8,128)S(1)} %get-tuple-element.19.sum_ref), custom_call_target="tpu_custom_call" | custom-call | tf_op jit(solution)/shard_map/pallas_call | solution.py:190
  17.7 0.2 collective-permute-done.5.refs_1_
  17.9 1.3 %shard_map.64 = (bf16[4,32,256]{2,1,0:T(8,128)(2,1)S(1)}, bf16[4,256,256]{2,1,0:T(8,128)(2,1)S(1)}) custom-call(bf16[16,1024]{1,0:T(8,128)(2,1)S(1)} %get-tuple-element.16.rows_ref.refs_0_, bf16[4,40,256]{2,1,0:T(8,128)(2,1)S(1)} %collective-permute-done.5.refs_1_, f32[32,1024]{1,0:T(8,128)S(1)} %get-tuple-element.21.refs_2_, ...), custom_call_target="tpu_custom_call" | custom-call | tf_op jit(solution)/shard_map/pallas_call | solution.py:190
  19.2 1.6 %collective-permute-start.6 = (bf16[4,32,256]{2,1,0:T(8,128)(2,1)S(1)}, bf16[4,32,256]{2,1,0:T(8,128)(2,1)S(1)}, u32[]{:S(2)}, u32[]{:S(2)}) collective-permute-start(bf16[4,32,256]{2,1,0:T(8,128)(2,1)S(1)} %get-tuple-element.23.refs_0_.own_ref), channel_id=1, source_target_pairs={{0,8},{4,12},{8,0},{12,4},{1,9},{5,13},{9,1},{13,5},{2,10},{6,14},... | collective-permute-start | bytes 196616 | tf_op jit(solution)/shard_map/ppermute | solution.py:162
  20.8 0.0 collective-permute-start.8
  20.8 2.8 %collective-permute-done.6.refs_2_ = bf16[4,32,256]{2,1,0:T(8,128)(2,1)S(1)} collective-permute-done((bf16[4,32,256]{2,1,0:T(8,128)(2,1)S(1)}, bf16[4,32,256]{2,1,0:T(8,128)(2,1)S(1)}, u32[]{:S(2)}, u32[]{:S(2)}) %collective-permute-start.6) | collective-permute-done | bytes 65568 | tf_op jit(solution)/shard_map/ppermute | solution.py:162
  23.6 0.4 %shard_map.65.sum_ref = f32[32,256]{1,0:T(8,128)S(1)} custom-call(bf16[4,32,256]{2,1,0:T(8,128)(2,1)S(1)} %get-tuple-element.23.refs_0_.own_ref, bf16[4,32,256]{2,1,0:T(8,128)(2,1)S(1)} %collective-permute-done.8.refs_1_, bf16[4,32,256]{2,1,0:T(8,128)(2,1)S(1)} %collective-permute-done.6.refs_2_, bf16[4,256,256]{2,1,0:T(8,128)(2,1)S(1)} %get-tuple-element.25.refs_3_, ...), custom_call_target="tpu_custom_call" | custom-call | tf_op jit(solution)/shard_map/pallas_call | solution.py:190
  24.0 0.9 %collective-permute-done.7.q_ref = bf16[4,32,256]{2,1,0:T(8,128)(2,1)S(1)} collective-permute-done((bf16[4,32,256]{2,1,0:T(8,128)(2,1)S(1)}, bf16[4,32,256]{2,1,0:T(8,128)(2,1)S(1)}, u32[]{:S(2)}, u32[]{:S(2)}) %collective-permute-start.7) | collective-permute-done | bytes 65568 | tf_op jit(solution)/shard_map/ppermute | solution.py:162
  24.8 1.0 %shard_map.66 = (f32[32,256]{1,0:T(8,128)}, f32[32,256]{1,0:T(8,128)}) custom-call(bf16[4,32,256]{2,1,0:T(8,128)(2,1)S(1)} %collective-permute-done.7.q_ref, bf16[4,256,256]{2,1,0:T(8,128)(2,1)S(1)} %get-tuple-element.24.tile_ref, f32[32,256]{1,0:T(8,128)S(1)} %shard_map.65.sum_ref, bf16[4,32,256]{2,1,0:T(8,128)(2,1)S(1)} %get-tuple-element.23.refs_0_.own_ref, ...), custom_call_target="tpu_custom_call" | custom-call | tf_op jit(solution)/shard_map/pallas_call | solution.py:190
  (2 shorter events, 0.0 us)
Async XLA Ops:
  1.7 6.5 %collective-permute-start.2 = (f32[40,256]{1,0:T(8,128)S(1)}, f32[40,256]{1,0:T(8,128)S(1)}, u32[]{:S(2)}, u32[]{:S(2)}) collective-permute-start(f32[40,256]{1,0:T(8,128)S(1)} %get-tuple-element.15.refs_0_.refs_5_.near_ref), channel_id=1, source_target_pairs={{0,2},{1,3},{2,0},{3,1},{4,6},{5,7},{6,4},{7,5},{8,10},{9,11},{10,... | collective-permute-start | bytes 122888 | tf_op jit(solution)/shard_map/ppermute | solution.py:162
  5.8 5.8 %collective-permute-start.1 = (f32[40,256]{1,0:T(8,128)S(1)}, f32[40,256]{1,0:T(8,128)S(1)}, u32[]{:S(2)}, u32[]{:S(2)}) collective-permute-start(f32[40,256]{1,0:T(8,128)S(1)} %get-tuple-element.15.refs_0_.refs_5_.near_ref), channel_id=1, source_target_pairs={{0,3},{1,2},{2,1},{3,0},{4,7},{5,6},{6,5},{7,4},{8,11},{9,10},{10,... | collective-permute-start | bytes 122888 | tf_op jit(solution)/shard_map/ppermute | solution.py:162
  7.1 4.5 %collective-permute-start = (f32[40,256]{1,0:T(8,128)S(1)}, f32[40,256]{1,0:T(8,128)S(1)}, u32[]{:S(2)}, u32[]{:S(2)}) collective-permute-start(f32[40,256]{1,0:T(8,128)S(1)} %get-tuple-element.15.refs_0_.refs_5_.near_ref), channel_id=1, source_target_pairs={{0,1},{1,0},{2,3},{3,2},{4,5},{5,4},{6,7},{7,6},{8,9},{9,8},{10,11... | collective-permute-start | bytes 122888 | tf_op jit(solution)/shard_map/ppermute | solution.py:162
  11.7 2.7 %collective-permute-start.4 = (bf16[4,40,256]{2,1,0:T(8,128)(2,1)S(1)}, bf16[4,40,256]{2,1,0:T(8,128)(2,1)S(1)}, u32[]{:S(2)}, u32[]{:S(2)}) collective-permute-start(bf16[4,40,256]{2,1,0:T(8,128)(2,1)S(1)} %get-tuple-element.17.packed_ref.refs_3_), channel_id=1, source_target_pairs={{0,4},{4,0},{8,12},{12,8},{1,5},{5,1},{9,13},{13,9},{2,6},{6,2},{1... | collective-permute-start | bytes 245768 | tf_op jit(solution)/shard_map/ppermute | solution.py:162
  11.7 4.9 %collective-permute-start.3 = (bf16[4,40,256]{2,1,0:T(8,128)(2,1)S(1)}, bf16[4,40,256]{2,1,0:T(8,128)(2,1)S(1)}, u32[]{:S(2)}, u32[]{:S(2)}) collective-permute-start(bf16[4,40,256]{2,1,0:T(8,128)(2,1)S(1)} %get-tuple-element.17.packed_ref.refs_3_), channel_id=1, source_target_pairs={{0,8},{4,12},{8,0},{12,4},{1,9},{5,13},{9,1},{13,5},{2,10},{6,14},... | collective-permute-start | bytes 245768 | tf_op jit(solution)/shard_map/ppermute | solution.py:162
  16.6 1.3 %collective-permute-start.5 = (bf16[4,40,256]{2,1,0:T(8,128)(2,1)S(1)}, bf16[4,40,256]{2,1,0:T(8,128)(2,1)S(1)}, u32[]{:S(2)}, u32[]{:S(2)}) collective-permute-start(bf16[4,40,256]{2,1,0:T(8,128)(2,1)S(1)} %collective-permute-done.3.packed_ref), channel_id=1, source_target_pairs={{0,4},{4,0},{8,12},{12,8},{1,5},{5,1},{9,13},{13,9},{2,6},{6,2},{1... | collective-permute-start | bytes 245768 | tf_op jit(solution)/shard_map/ppermute | solution.py:162
  19.2 4.4 %collective-permute-start.6 = (bf16[4,32,256]{2,1,0:T(8,128)(2,1)S(1)}, bf16[4,32,256]{2,1,0:T(8,128)(2,1)S(1)}, u32[]{:S(2)}, u32[]{:S(2)}) collective-permute-start(bf16[4,32,256]{2,1,0:T(8,128)(2,1)S(1)} %get-tuple-element.23.refs_0_.own_ref), channel_id=1, source_target_pairs={{0,8},{4,12},{8,0},{12,4},{1,9},{5,13},{9,1},{13,5},{2,10},{6,14},... | collective-permute-start | bytes 196616 | tf_op jit(solution)/shard_map/ppermute | solution.py:162
  20.8 2.8 %collective-permute-start.8 = (bf16[4,32,256]{2,1,0:T(8,128)(2,1)S(1)}, bf16[4,32,256]{2,1,0:T(8,128)(2,1)S(1)}, u32[]{:S(2)}, u32[]{:S(2)}) collective-permute-start(bf16[4,32,256]{2,1,0:T(8,128)(2,1)S(1)} %get-tuple-element.23.refs_0_.own_ref), channel_id=1, source_target_pairs={{0,4},{4,0},{8,12},{12,8},{1,5},{5,1},{9,13},{13,9},{2,6},{6,2},{1... | collective-permute-start | bytes 196616 | tf_op jit(solution)/shard_map/ppermute | solution.py:162
  23.6 1.3 %collective-permute-start.7 = (bf16[4,32,256]{2,1,0:T(8,128)(2,1)S(1)}, bf16[4,32,256]{2,1,0:T(8,128)(2,1)S(1)}, u32[]{:S(2)}, u32[]{:S(2)}) collective-permute-start(bf16[4,32,256]{2,1,0:T(8,128)(2,1)S(1)} %collective-permute-done.6.refs_2_), channel_id=1, source_target_pairs={{0,4},{4,0},{8,12},{12,8},{1,5},{5,1},{9,13},{13,9},{2,6},{6,2},{1... | collective-permute-start | bytes 196616 | tf_op jit(solution)/shard_map/ppermute | solution.py:162

commit v7 on v6

--- a/solution.py
+++ b/solution.py
@@ -98,8 +98,7 @@
         columns, rows_ref[...], (((0,), (0,)), ((), ())), preferred_element_type=jnp.float32
     )
     tile = jnp.exp(exponent).astype(jnp.bfloat16)
-    for index in range(blocks):
-        tile_ref[index] = tile[index * own:(index + 1) * own, :own]
+    tile_ref[...] = tile[:own]
     return total + jnp.dot(packed[:labels], tile, preferred_element_type=jnp.float32)
 
 
@@ -122,41 +121,34 @@
     probs, _ = finish(
         total, jnp.concatenate(labels_now, axis=1), jnp.concatenate(unary, axis=1), compat_ref
     )
-    for near in range(nears):
-        q_ref[near] = probs[:, near * own:(near + 1) * own].astype(jnp.bfloat16)
-
-
-def second_part(pairs, total):
-    for q_ref, tile_ref in pairs:
-        body = lambda index, total, q_ref=q_ref, tile_ref=tile_ref: total + jnp.dot(
-            q_ref[index], tile_ref[index], preferred_element_type=jnp.float32
+    q_ref[...] = probs.astype(jnp.bfloat16)
+
+
+def second_parts(q_ref, *refs):
+    count = len(refs) // 2
+    for tile_ref, part_ref in zip(refs[:count], refs[count:]):
+        part_ref[...] = lax.dot_general(
+            q_ref[...], tile_ref[...], (((1,), (1,)), ((), ())),
+            preferred_element_type=jnp.float32,
         )
-        total = over_blocks(q_ref.shape[0], body, total)
-    return total
-
-
-def second_opening(*refs):
-    total_ref = refs[-1]
-    stacks = len(refs) // 2
-    pairs = zip(refs[:stacks], refs[stacks:-1])
-    total_ref[...] = second_part(pairs, jnp.zeros(total_ref.shape, jnp.float32))
-
-
-def second_closing(
-    q_ref, tile_ref, sum_ref, own_ref, near_ref, compat_ref, probs_ref, pairwise_ref
-):
-    total = second_part([(q_ref, tile_ref)], sum_ref[...])
-    unary = near_ref[pl.ds(0, total.shape[0]), :]
-    probs, pairwise = finish(total, own_ref[0], unary, compat_ref)
+
+
+def second_closing(q_ref, near_ref, compat_ref, *refs):
+    probs_ref, pairwise_ref = refs[-2:]
+    labels, own = probs_ref.shape
+    total = refs[0][...]
+    for part_ref in refs[1:-2]:
+        total = total + part_ref[...]
+    unary = near_ref[pl.ds(0, labels), :]
+    probs, pairwise = finish(total, q_ref[:, pl.ds(0, own)], unary, compat_ref)
     probs_ref[...] = probs
     pairwise_ref[...] = pairwise
 
 
 def swap(value, axis, steps):
     count = lax.axis_size(axis)
-    paired = count & (count - 1) == 0
     pairs = [
-        (source, source ^ steps if paired else (source + steps) % count)
+        (source, source ^ steps if paired(axis) else (source + steps) % count)
         for source in range(count)
     ]
     return lax.ppermute(value, axis, pairs)
@@ -168,18 +160,27 @@
     return [value] + [swap(value, "grp", steps) for steps in reversed(order)]
 
 
-def block_partners(value, use_early=None):
+def paired(axis):
+    count = lax.axis_size(axis)
+    return count & (count - 1) == 0
+
+
+def block_partners(value, use_early):
     count = lax.axis_size("blk")
-    if count & (count - 1):
+    if not paired("blk"):
         stacks = [value] + [swap(value, "blk", steps) for steps in range(1, count)]
-        if use_early:
-            use_early(stacks[:2])
-        return stacks
-    far = [swap(value, "blk", steps) for steps in range(2, count, 2)]
+        use_early(stacks[:2])
+        return stacks, list(range(count))
+    steps = list(range(2, count, 2))
+    far = [swap(value, "blk", step) for step in steps]
     beside = swap(value, "blk", 1)
-    if use_early:
-        *far, _ = lax.optimization_barrier((*far, use_early([value, beside])))
-    return [value, beside] + far + [swap(stack, "blk", 1) for stack in far]
+    *far, _ = lax.optimization_barrier((*far, use_early([value, beside])))
+    stacks = [value, beside] + far + [swap(stack, "blk", 1) for stack in far]
+    return stacks, [0, 1] + steps + [step + 1 for step in steps]
+
+
+def send_back(value, steps):
+    return swap(value, "blk", steps if paired("blk") else lax.axis_size("blk") - steps)
 
 
 def small(dims, kind):
@@ -224,14 +225,14 @@
         *hold(*near),
     )
     parts = lax.axis_size("blk")
-    tile_kind = kept((nears, own, own), jnp.bfloat16, parts)
+    tile_kind = kept((own, nears * own), jnp.bfloat16, parts)
     tiles, totals = [], []
 
     def first(place, last, stack):
         if last:
             q_near, tile = call(
                 functools.partial(first_closing, labels, nears),
-                [kept((nears, labels, own), jnp.bfloat16), tile_kind],
+                [kept((labels, nears * own), jnp.bfloat16), tile_kind],
                 *hold(rows, stack, *totals[-1:], packed, held, *near),
             )
             tiles.append(tile)
@@ -250,18 +251,22 @@
             result = first(place, place + 1 == parts, stack)
         return result
 
-    stacks = block_partners(packed, first_early)
+    stacks, steps = block_partners(packed, first_early)
     for place in range(2, parts):
         q_near = first(place, place + 1 == parts, stacks[place])
 
     if parts * math.prod(tile_kind.shape) * 2 <= KEPT_BYTES:
         tiles = hold(*tiles)
-    *stacks, last = block_partners(q_near)
-    (total,) = call(second_opening, [kept((labels, own), jnp.float32)], *hold(*stacks), *tiles[:-1])
+    part_kind = kept((labels, own), jnp.float32)
+    far = call(second_parts, [part_kind] * (parts - 2), *hold(q_near), *tiles[2:])
+    if far:
+        q_near, *far = lax.optimization_barrier((q_near, *far))
+    here, beside = call(second_parts, [part_kind] * 2, *hold(q_near), *tiles[:2])
+    arrived = [send_back(part, step) for part, step in zip([beside, *far], steps[1:])]
     return call(
         second_closing,
         [jax.ShapeDtypeStruct((labels, own), jnp.float32)] * 2,
-        *hold(last), tiles[-1], *hold(total, q_near, sent, held),
+        *hold(q_near, sent, held, here, *arrived),
     )
 
 

time: 26 us -> 25.6 us (0.985)
  waiting for transfers between devices: 9.2 us -> 7.98 us
  starting transfers between devices: 8.96 us -> 9.52 us
    ppermute x9, waiting for transfers between devices: 9.2 us -> 7.98 us  [swap(): return lax.ppermute(value, axis, pairs)]
    ppermute x9, starting transfers between devices: 8.96 us -> 9.52 us  [swap(): return lax.ppermute(value, axis, pairs)]
    pallas_call x8 -> x9, Pallas kernels: 7.05 us -> 7.26 us  [call(): pl.pallas_call(kernel, out_shape=tuple(out_shapes), compiler_params=pltpu...]
where the time goes in v7:
time: 25.6 us; the launch traced here: 25.4 us
  starting transfers between devices  9.52 us (37%)
  waiting for transfers between devices  7.98 us (31%)
  Pallas kernels  7.26 us (28%)
  between operations  0.67 us (3%)
    ppermute x9, starting transfers between devices, swap(): return lax.ppermute(value, axis, pairs)  9.52 us
    ppermute x9, waiting for transfers between devices, swap(): return lax.ppermute(value, axis, pairs)  7.98 us
    pallas_call x9, Pallas kernels, call(): pl.pallas_call(kernel, out_shape=tuple(out_shapes), compiler_params=pltpu...  7.26 us
  transfers between devices with their start and end apart: 9, of which 6 were waited for; matrix products, arithmetic and copies ran while one was open for 0% of the time, Pallas kernels for 14%

profile of v7, /device:TPU:0, one launch (start us, length us, event | category | flops | bytes accessed | tf_op | source)
XLA Modules:
  0.0 25.4 jit_solution(2285571388106553523)
XLA Ops:
  0.6 1.1 %shard_map.59 = (f32[40,256]{1,0:T(8,128)S(1)}, f32[32,32]{1,0:T(8,128)S(1)}) custom-call(bf16[6,4096]{1,0:T(8,128)(2,1)} %features_ref.1, s32[1,256]{1,0:T(1,128)} %bitcast.1, f32[32,256]{1,0:T(8,128)} %unary_ref.1, f32[32,32]{1,0:T(8,128)} %compat_ref.1), custom_call_target="tpu_custom_call" | custom-call | tf_op jit(solution)/shard_map/pallas_call | solution.py:191
  1.7 4.1 %collective-permute-start.2 = (f32[40,256]{1,0:T(8,128)S(1)}, f32[40,256]{1,0:T(8,128)S(1)}, u32[]{:S(2)}, u32[]{:S(2)}) collective-permute-start(f32[40,256]{1,0:T(8,128)S(1)} %get-tuple-element.22.refs_0_.refs_5_.near_ref), channel_id=1, source_target_pairs={{0,2},{1,3},{2,0},{3,1},{4,6},{5,7},{6,4},{7,5},{8,10},{9,11},{10,... | collective-permute-start | bytes 122888 | tf_op jit(solution)/shard_map/ppermute | solution.py:154
  5.8 1.3 %collective-permute-start.1 = (f32[40,256]{1,0:T(8,128)S(1)}, f32[40,256]{1,0:T(8,128)S(1)}, u32[]{:S(2)}, u32[]{:S(2)}) collective-permute-start(f32[40,256]{1,0:T(8,128)S(1)} %get-tuple-element.22.refs_0_.refs_5_.near_ref), channel_id=1, source_target_pairs={{0,3},{1,2},{2,1},{3,0},{4,7},{5,6},{6,5},{7,4},{8,11},{9,10},{10,... | collective-permute-start | bytes 122888 | tf_op jit(solution)/shard_map/ppermute | solution.py:154
  7.1 0.2 collective-permute-start
  7.4 0.8 %collective-permute-done.2.refs_3_.refs_8_ = f32[40,256]{1,0:T(8,128)S(1)} collective-permute-done((f32[40,256]{1,0:T(8,128)S(1)}, f32[40,256]{1,0:T(8,128)S(1)}, u32[]{:S(2)}, u32[]{:S(2)}) %collective-permute-start.2) | collective-permute-done | bytes 40992 | tf_op jit(solution)/shard_map/ppermute | solution.py:154
  8.2 3.4 %collective-permute-done.1.refs_2_.refs_7_ = f32[40,256]{1,0:T(8,128)S(1)} collective-permute-done((f32[40,256]{1,0:T(8,128)S(1)}, f32[40,256]{1,0:T(8,128)S(1)}, u32[]{:S(2)}, u32[]{:S(2)}) %collective-permute-start.1) | collective-permute-done | bytes 40992 | tf_op jit(solution)/shard_map/ppermute | solution.py:154
  11.6 0.0 collective-permute-done.refs_1_.refs_6_
  11.6 0.1 shard_map.60
  11.7 0.1 collective-permute-start.4
  11.7 1.6 %collective-permute-start.3 = (bf16[4,40,256]{2,1,0:T(8,128)(2,1)S(1)}, bf16[4,40,256]{2,1,0:T(8,128)(2,1)S(1)}, u32[]{:S(2)}, u32[]{:S(2)}) collective-permute-start(bf16[4,40,256]{2,1,0:T(8,128)(2,1)S(1)} %get-tuple-element.24.packed_ref.refs_3_), channel_id=1, source_target_pairs={{0,8},{4,12},{8,0},{12,4},{1,9},{5,13},{9,1},{13,5},{2,10},{6,14},... | collective-permute-start | bytes 245768 | tf_op jit(solution)/shard_map/ppermute | solution.py:154
  13.3 1.1 %shard_map.61 = (f32[32,1024]{1,0:T(8,128)S(1)}, bf16[256,1024]{1,0:T(8,128)(2,1)S(1)}) custom-call(bf16[16,1024]{1,0:T(8,128)(2,1)S(1)} %get-tuple-element.23.rows_ref.refs_0_, bf16[4,40,256]{2,1,0:T(8,128)(2,1)S(1)} %get-tuple-element.24.packed_ref.refs_3_), custom_call_target="tpu_custom_call" | custom-call | tf_op jit(solution)/shard_map/pallas_call | solution.py:191
  14.4 1.1 %shard_map.62 = (f32[32,1024]{1,0:T(8,128)S(1)}, bf16[256,1024]{1,0:T(8,128)(2,1)S(1)}) custom-call(bf16[16,1024]{1,0:T(8,128)(2,1)S(1)} %get-tuple-element.23.rows_ref.refs_0_, bf16[4,40,256]{2,1,0:T(8,128)(2,1)S(1)} %collective-permute-done.4.packed_ref, f32[32,1024]{1,0:T(8,128)S(1)} %get-tuple-element.25.sum_ref), custom_call_target="tpu_custom_call" | custom-call | tf_op jit(solution)/shard_map/pallas_call | solution.py:191
  15.5 1.1 %collective-permute-done.3.packed_ref = bf16[4,40,256]{2,1,0:T(8,128)(2,1)S(1)} collective-permute-done((bf16[4,40,256]{2,1,0:T(8,128)(2,1)S(1)}, bf16[4,40,256]{2,1,0:T(8,128)(2,1)S(1)}, u32[]{:S(2)}, u32[]{:S(2)}) %collective-permute-start.3) | collective-permute-done | bytes 81952 | tf_op jit(solution)/shard_map/ppermute | solution.py:154
  16.6 1.1 %shard_map.63 = (f32[32,1024]{1,0:T(8,128)S(1)}, bf16[256,1024]{1,0:T(8,128)(2,1)S(1)}) custom-call(bf16[16,1024]{1,0:T(8,128)(2,1)S(1)} %get-tuple-element.23.rows_ref.refs_0_, bf16[4,40,256]{2,1,0:T(8,128)(2,1)S(1)} %collective-permute-done.3.packed_ref, f32[32,1024]{1,0:T(8,128)S(1)} %get-tuple-element.26.sum_ref), custom_call_target="tpu_custom_call" | custom-call | tf_op jit(solution)/shard_map/pallas_call | solution.py:191
  17.7 0.2 collective-permute-done.5.refs_1_
  17.9 1.3 %shard_map.64 = (bf16[32,1024]{1,0:T(8,128)(2,1)S(1)}, bf16[256,1024]{1,0:T(8,128)(2,1)S(1)}) custom-call(bf16[16,1024]{1,0:T(8,128)(2,1)S(1)} %get-tuple-element.23.rows_ref.refs_0_, bf16[4,40,256]{2,1,0:T(8,128)(2,1)S(1)} %collective-permute-done.5.refs_1_, f32[32,1024]{1,0:T(8,128)S(1)} %get-tuple-element.28.refs_2_, ...), custom_call_target="tpu_custom_call" | custom-call | tf_op jit(solution)/shard_map/pallas_call | solution.py:191
  19.2 0.4 %shard_map.65 = (f32[32,256]{1,0:T(8,128)S(1)}, f32[32,256]{1,0:T(8,128)S(1)}) custom-call(bf16[32,1024]{1,0:T(8,128)(2,1)S(1)} %get-tuple-element.35.q_ref, bf16[256,1024]{1,0:T(8,128)(2,1)S(1)} %get-tuple-element.31.refs_0_, bf16[256,1024]{1,0:T(8,128)(2,1)S(1)} %get-tuple-element.32.refs_1_), custom_call_target="tpu_custom_call" | custom-call | tf_op jit(solution)/shard_map/pallas_call | solution.py:191
  19.6 1.5 %collective-permute-start.7 = (f32[32,256]{1,0:T(8,128)S(1)}, f32[32,256]{1,0:T(8,128)S(1)}, u32[]{:S(2)}, u32[]{:S(2)}) collective-permute-start(f32[32,256]{1,0:T(8,128)S(1)} %get-tuple-element.40), channel_id=1, source_target_pairs={{0,8},{4,12},{8,0},{12,4},{1,9},{5,13},{9,1},{13,5},{2,10},{6,14},... | collective-permute-start | bytes 98312 | tf_op jit(solution)/shard_map/ppermute | solution.py:154
  21.1 0.1 collective-permute-start.8
  21.3 0.4 %shard_map.66 = (f32[32,256]{1,0:T(8,128)S(1)}, f32[32,256]{1,0:T(8,128)S(1)}) custom-call(bf16[32,1024]{1,0:T(8,128)(2,1)S(1)} %get-tuple-element.35.q_ref, bf16[256,1024]{1,0:T(8,128)(2,1)S(1)} %get-tuple-element.36.refs_0_, bf16[256,1024]{1,0:T(8,128)(2,1)S(1)} %get-tuple-element.37.refs_1_), custom_call_target="tpu_custom_call" | custom-call | tf_op jit(solution)/shard_map/pallas_call | solution.py:191
  21.7 0.5 %collective-permute-start.6 = (f32[32,256]{1,0:T(8,128)S(1)}, f32[32,256]{1,0:T(8,128)S(1)}, u32[]{:S(2)}, u32[]{:S(2)}) collective-permute-start(f32[32,256]{1,0:T(8,128)S(1)} %get-tuple-element.39), channel_id=1, source_target_pairs={{0,4},{4,0},{8,12},{12,8},{1,5},{5,1},{9,13},{13,9},{2,6},{6,2},{1... | collective-permute-start | bytes 98312 | tf_op jit(solution)/shard_map/ppermute | solution.py:154
  22.2 1.3 %collective-permute-done.7.refs_2_ = f32[32,256]{1,0:T(8,128)S(1)} collective-permute-done((f32[32,256]{1,0:T(8,128)S(1)}, f32[32,256]{1,0:T(8,128)S(1)}, u32[]{:S(2)}, u32[]{:S(2)}) %collective-permute-start.7) | collective-permute-done | bytes 32800 | tf_op jit(solution)/shard_map/ppermute | solution.py:154
  23.5 1.1 %collective-permute-done.8.refs_3_ = f32[32,256]{1,0:T(8,128)S(1)} collective-permute-done((f32[32,256]{1,0:T(8,128)S(1)}, f32[32,256]{1,0:T(8,128)S(1)}, u32[]{:S(2)}, u32[]{:S(2)}) %collective-permute-start.8) | collective-permute-done | bytes 32800 | tf_op jit(solution)/shard_map/ppermute | solution.py:154
  24.6 0.8 %shard_map.67 = (f32[32,256]{1,0:T(8,128)}, f32[32,256]{1,0:T(8,128)}) custom-call(bf16[32,1024]{1,0:T(8,128)(2,1)S(1)} %get-tuple-element.35.q_ref, f32[40,256]{1,0:T(8,128)S(1)} %get-tuple-element.22.refs_0_.refs_5_.near_ref, f32[32,32]{1,0:T(8,128)S(1)} %get-tuple-element.29.refs_4_.compat_ref, f32[32,256]{1,0:T(8,128)S(1)} %get-tuple-element.38.refs_0_, ...), custom_call_target="tpu_custom_call" | custom-call | tf_op jit(solution)/shard_map/pallas_call | solution.py:191
  (3 shorter events, 0.0 us)
Async XLA Ops:
  1.7 6.5 %collective-permute-start.2 = (f32[40,256]{1,0:T(8,128)S(1)}, f32[40,256]{1,0:T(8,128)S(1)}, u32[]{:S(2)}, u32[]{:S(2)}) collective-permute-start(f32[40,256]{1,0:T(8,128)S(1)} %get-tuple-element.22.refs_0_.refs_5_.near_ref), channel_id=1, source_target_pairs={{0,2},{1,3},{2,0},{3,1},{4,6},{5,7},{6,4},{7,5},{8,10},{9,11},{10,... | collective-permute-start | bytes 122888 | tf_op jit(solution)/shard_map/ppermute | solution.py:154
  5.8 5.8 %collective-permute-start.1 = (f32[40,256]{1,0:T(8,128)S(1)}, f32[40,256]{1,0:T(8,128)S(1)}, u32[]{:S(2)}, u32[]{:S(2)}) collective-permute-start(f32[40,256]{1,0:T(8,128)S(1)} %get-tuple-element.22.refs_0_.refs_5_.near_ref), channel_id=1, source_target_pairs={{0,3},{1,2},{2,1},{3,0},{4,7},{5,6},{6,5},{7,4},{8,11},{9,10},{10,... | collective-permute-start | bytes 122888 | tf_op jit(solution)/shard_map/ppermute | solution.py:154
  7.1 4.5 %collective-permute-start = (f32[40,256]{1,0:T(8,128)S(1)}, f32[40,256]{1,0:T(8,128)S(1)}, u32[]{:S(2)}, u32[]{:S(2)}) collective-permute-start(f32[40,256]{1,0:T(8,128)S(1)} %get-tuple-element.22.refs_0_.refs_5_.near_ref), channel_id=1, source_target_pairs={{0,1},{1,0},{2,3},{3,2},{4,5},{5,4},{6,7},{7,6},{8,9},{9,8},{10,11... | collective-permute-start | bytes 122888 | tf_op jit(solution)/shard_map/ppermute | solution.py:154
  11.7 2.7 %collective-permute-start.4 = (bf16[4,40,256]{2,1,0:T(8,128)(2,1)S(1)}, bf16[4,40,256]{2,1,0:T(8,128)(2,1)S(1)}, u32[]{:S(2)}, u32[]{:S(2)}) collective-permute-start(bf16[4,40,256]{2,1,0:T(8,128)(2,1)S(1)} %get-tuple-element.24.packed_ref.refs_3_), channel_id=1, source_target_pairs={{0,4},{4,0},{8,12},{12,8},{1,5},{5,1},{9,13},{13,9},{2,6},{6,2},{1... | collective-permute-start | bytes 245768 | tf_op jit(solution)/shard_map/ppermute | solution.py:154
  11.7 4.9 %collective-permute-start.3 = (bf16[4,40,256]{2,1,0:T(8,128)(2,1)S(1)}, bf16[4,40,256]{2,1,0:T(8,128)(2,1)S(1)}, u32[]{:S(2)}, u32[]{:S(2)}) collective-permute-start(bf16[4,40,256]{2,1,0:T(8,128)(2,1)S(1)} %get-tuple-element.24.packed_ref.refs_3_), channel_id=1, source_target_pairs={{0,8},{4,12},{8,0},{12,4},{1,9},{5,13},{9,1},{13,5},{2,10},{6,14},... | collective-permute-start | bytes 245768 | tf_op jit(solution)/shard_map/ppermute | solution.py:154
  16.6 1.3 %collective-permute-start.5 = (bf16[4,40,256]{2,1,0:T(8,128)(2,1)S(1)}, bf16[4,40,256]{2,1,0:T(8,128)(2,1)S(1)}, u32[]{:S(2)}, u32[]{:S(2)}) collective-permute-start(bf16[4,40,256]{2,1,0:T(8,128)(2,1)S(1)} %collective-permute-done.3.packed_ref), channel_id=1, source_target_pairs={{0,4},{4,0},{8,12},{12,8},{1,5},{5,1},{9,13},{13,9},{2,6},{6,2},{1... | collective-permute-start | bytes 245768 | tf_op jit(solution)/shard_map/ppermute | solution.py:154
  19.6 3.9 %collective-permute-start.7 = (f32[32,256]{1,0:T(8,128)S(1)}, f32[32,256]{1,0:T(8,128)S(1)}, u32[]{:S(2)}, u32[]{:S(2)}) collective-permute-start(f32[32,256]{1,0:T(8,128)S(1)} %get-tuple-element.40), channel_id=1, source_target_pairs={{0,8},{4,12},{8,0},{12,4},{1,9},{5,13},{9,1},{13,5},{2,10},{6,14},... | collective-permute-start | bytes 98312 | tf_op jit(solution)/shard_map/ppermute | solution.py:154
  21.1 3.5 %collective-permute-start.8 = (f32[32,256]{1,0:T(8,128)S(1)}, f32[32,256]{1,0:T(8,128)S(1)}, u32[]{:S(2)}, u32[]{:S(2)}) collective-permute-start(f32[32,256]{1,0:T(8,128)S(1)} %get-tuple-element.41), channel_id=1, source_target_pairs={{0,12},{4,8},{8,4},{12,0},{1,13},{5,9},{9,5},{13,1},{2,14},{6,10},... | collective-permute-start | bytes 98312 | tf_op jit(solution)/shard_map/ppermute | solution.py:154
  21.7 2.9 %collective-permute-start.6 = (f32[32,256]{1,0:T(8,128)S(1)}, f32[32,256]{1,0:T(8,128)S(1)}, u32[]{:S(2)}, u32[]{:S(2)}) collective-permute-start(f32[32,256]{1,0:T(8,128)S(1)} %get-tuple-element.39), channel_id=1, source_target_pairs={{0,4},{4,0},{8,12},{12,8},{1,5},{5,1},{9,13},{13,9},{2,6},{6,2},{1... | collective-permute-start | bytes 98312 | tf_op jit(solution)/shard_map/ppermute | solution.py:154

commit v8 on v7

--- a/solution.py
+++ b/solution.py
@@ -92,14 +92,26 @@
 
 def first_part(labels, rows_ref, packed_ref, total, tile_ref):
     blocks, _, own = packed_ref.shape
-    packed = jnp.concatenate([packed_ref[index] for index in range(blocks)], axis=1)
-    columns = product_sides(packed[labels:].astype(jnp.float32))[0]
-    exponent = lax.dot_general(
-        columns, rows_ref[...], (((0,), (0,)), ((), ())), preferred_element_type=jnp.float32
-    )
-    tile = jnp.exp(exponent).astype(jnp.bfloat16)
-    tile_ref[...] = tile[:own]
-    return total + jnp.dot(packed[:labels], tile, preferred_element_type=jnp.float32)
+    rows = rows_ref[...]
+
+    def exponents(index):
+        columns = product_sides(packed_ref[index][labels:].astype(jnp.float32))[0]
+        return lax.dot_general(
+            columns, rows, (((0,), (0,)), ((), ())), preferred_element_type=jnp.float32
+        )
+
+    ahead = exponents(0)
+    for index in range(blocks):
+        exponent = ahead
+        if index + 1 < blocks:
+            ahead = exponents(index + 1)
+        tile = jnp.exp(exponent).astype(jnp.bfloat16)
+        if index == 0:
+            tile_ref[...] = tile
+        total = total + jnp.dot(
+            packed_ref[index][:labels], tile, preferred_element_type=jnp.float32
+        )
+    return total
 
 
 def first_opening(labels, rows_ref, packed_ref, total_ref, tile_ref):

time: 25.6 us -> 25.5 us (level)
  no operation moved by 1% of the time
where the time goes in v8:
time: 25.5 us; the launch traced here: 25.4 us
  starting transfers between devices  9.52 us (37%)
  waiting for transfers between devices  8.04 us (32%)
  Pallas kernels  7.16 us (28%)
  between operations  0.67 us (3%)
    ppermute x9, starting transfers between devices, swap(): return lax.ppermute(value, axis, pairs)  9.52 us
    ppermute x9, waiting for transfers between devices, swap(): return lax.ppermute(value, axis, pairs)  8.04 us
    pallas_call x9, Pallas kernels, call(): pl.pallas_call(kernel, out_shape=tuple(out_shapes), compiler_params=pltpu...  7.16 us
  transfers between devices with their start and end apart: 9, of which 6 were waited for; matrix products, arithmetic and copies ran while one was open for 0% of the time, Pallas kernels for 14%

profile of v8, /device:TPU:0, one launch (start us, length us, event | category | flops | bytes accessed | tf_op | source)
XLA Modules:
  0.0 25.4 jit_solution(1232723037920120923)
XLA Ops:
  0.6 1.1 %shard_map.59 = (f32[40,256]{1,0:T(8,128)S(1)}, f32[32,32]{1,0:T(8,128)S(1)}) custom-call(bf16[6,4096]{1,0:T(8,128)(2,1)} %features_ref.1, s32[1,256]{1,0:T(1,128)} %bitcast.1, f32[32,256]{1,0:T(8,128)} %unary_ref.1, f32[32,32]{1,0:T(8,128)} %compat_ref.1), custom_call_target="tpu_custom_call" | custom-call | tf_op jit(solution)/shard_map/pallas_call | solution.py:203
  1.7 4.1 %collective-permute-start.2 = (f32[40,256]{1,0:T(8,128)S(1)}, f32[40,256]{1,0:T(8,128)S(1)}, u32[]{:S(2)}, u32[]{:S(2)}) collective-permute-start(f32[40,256]{1,0:T(8,128)S(1)} %get-tuple-element.22.refs_0_.refs_5_.near_ref), channel_id=1, source_target_pairs={{0,2},{1,3},{2,0},{3,1},{4,6},{5,7},{6,4},{7,5},{8,10},{9,11},{10,... | collective-permute-start | bytes 122888 | tf_op jit(solution)/shard_map/ppermute | solution.py:166
  5.8 1.3 %collective-permute-start.1 = (f32[40,256]{1,0:T(8,128)S(1)}, f32[40,256]{1,0:T(8,128)S(1)}, u32[]{:S(2)}, u32[]{:S(2)}) collective-permute-start(f32[40,256]{1,0:T(8,128)S(1)} %get-tuple-element.22.refs_0_.refs_5_.near_ref), channel_id=1, source_target_pairs={{0,3},{1,2},{2,1},{3,0},{4,7},{5,6},{6,5},{7,4},{8,11},{9,10},{10,... | collective-permute-start | bytes 122888 | tf_op jit(solution)/shard_map/ppermute | solution.py:166
  7.1 0.2 collective-permute-start
  7.4 0.8 %collective-permute-done.2.refs_3_.refs_8_ = f32[40,256]{1,0:T(8,128)S(1)} collective-permute-done((f32[40,256]{1,0:T(8,128)S(1)}, f32[40,256]{1,0:T(8,128)S(1)}, u32[]{:S(2)}, u32[]{:S(2)}) %collective-permute-start.2) | collective-permute-done | bytes 40992 | tf_op jit(solution)/shard_map/ppermute | solution.py:166
  8.2 3.4 %collective-permute-done.1.refs_2_.refs_7_ = f32[40,256]{1,0:T(8,128)S(1)} collective-permute-done((f32[40,256]{1,0:T(8,128)S(1)}, f32[40,256]{1,0:T(8,128)S(1)}, u32[]{:S(2)}, u32[]{:S(2)}) %collective-permute-start.1) | collective-permute-done | bytes 40992 | tf_op jit(solution)/shard_map/ppermute | solution.py:166
  11.6 0.0 collective-permute-done.refs_1_.refs_6_
  11.6 0.1 shard_map.60
  11.7 0.1 collective-permute-start.4
  11.7 1.6 %collective-permute-start.3 = (bf16[4,40,256]{2,1,0:T(8,128)(2,1)S(1)}, bf16[4,40,256]{2,1,0:T(8,128)(2,1)S(1)}, u32[]{:S(2)}, u32[]{:S(2)}) collective-permute-start(bf16[4,40,256]{2,1,0:T(8,128)(2,1)S(1)} %get-tuple-element.24.packed_ref.refs_3_), channel_id=1, source_target_pairs={{0,8},{4,12},{8,0},{12,4},{1,9},{5,13},{9,1},{13,5},{2,10},{6,14},... | collective-permute-start | bytes 245768 | tf_op jit(solution)/shard_map/ppermute | solution.py:166
  13.3 1.1 %shard_map.61 = (f32[32,1024]{1,0:T(8,128)S(1)}, bf16[256,1024]{1,0:T(8,128)(2,1)S(1)}) custom-call(bf16[16,1024]{1,0:T(8,128)(2,1)S(1)} %get-tuple-element.23.rows_ref.refs_0_, bf16[4,40,256]{2,1,0:T(8,128)(2,1)S(1)} %get-tuple-element.24.packed_ref.refs_3_), custom_call_target="tpu_custom_call" | custom-call | tf_op jit(solution)/shard_map/pallas_call | solution.py:203
  14.4 1.1 %shard_map.62 = (f32[32,1024]{1,0:T(8,128)S(1)}, bf16[256,1024]{1,0:T(8,128)(2,1)S(1)}) custom-call(bf16[16,1024]{1,0:T(8,128)(2,1)S(1)} %get-tuple-element.23.rows_ref.refs_0_, bf16[4,40,256]{2,1,0:T(8,128)(2,1)S(1)} %collective-permute-done.4.packed_ref, f32[32,1024]{1,0:T(8,128)S(1)} %get-tuple-element.25.sum_ref), custom_call_target="tpu_custom_call" | custom-call | tf_op jit(solution)/shard_map/pallas_call | solution.py:203
  15.4 1.2 %collective-permute-done.3.packed_ref = bf16[4,40,256]{2,1,0:T(8,128)(2,1)S(1)} collective-permute-done((bf16[4,40,256]{2,1,0:T(8,128)(2,1)S(1)}, bf16[4,40,256]{2,1,0:T(8,128)(2,1)S(1)}, u32[]{:S(2)}, u32[]{:S(2)}) %collective-permute-start.3) | collective-permute-done | bytes 81952 | tf_op jit(solution)/shard_map/ppermute | solution.py:166
  16.6 1.1 %shard_map.63 = (f32[32,1024]{1,0:T(8,128)S(1)}, bf16[256,1024]{1,0:T(8,128)(2,1)S(1)}) custom-call(bf16[16,1024]{1,0:T(8,128)(2,1)S(1)} %get-tuple-element.23.rows_ref.refs_0_, bf16[4,40,256]{2,1,0:T(8,128)(2,1)S(1)} %collective-permute-done.3.packed_ref, f32[32,1024]{1,0:T(8,128)S(1)} %get-tuple-element.26.sum_ref), custom_call_target="tpu_custom_call" | custom-call | tf_op jit(solution)/shard_map/pallas_call | solution.py:203
  17.7 0.2 collective-permute-done.5.refs_1_
  17.9 1.3 %shard_map.64 = (bf16[32,1024]{1,0:T(8,128)(2,1)S(1)}, bf16[256,1024]{1,0:T(8,128)(2,1)S(1)}) custom-call(bf16[16,1024]{1,0:T(8,128)(2,1)S(1)} %get-tuple-element.23.rows_ref.refs_0_, bf16[4,40,256]{2,1,0:T(8,128)(2,1)S(1)} %collective-permute-done.5.refs_1_, f32[32,1024]{1,0:T(8,128)S(1)} %get-tuple-element.28.refs_2_, ...), custom_call_target="tpu_custom_call" | custom-call | tf_op jit(solution)/shard_map/pallas_call | solution.py:203
  19.2 0.4 %shard_map.65 = (f32[32,256]{1,0:T(8,128)S(1)}, f32[32,256]{1,0:T(8,128)S(1)}) custom-call(bf16[32,1024]{1,0:T(8,128)(2,1)S(1)} %get-tuple-element.35.q_ref, bf16[256,1024]{1,0:T(8,128)(2,1)S(1)} %get-tuple-element.31.refs_0_, bf16[256,1024]{1,0:T(8,128)(2,1)S(1)} %get-tuple-element.32.refs_1_), custom_call_target="tpu_custom_call" | custom-call | tf_op jit(solution)/shard_map/pallas_call | solution.py:203
  19.6 1.5 %collective-permute-start.7 = (f32[32,256]{1,0:T(8,128)S(1)}, f32[32,256]{1,0:T(8,128)S(1)}, u32[]{:S(2)}, u32[]{:S(2)}) collective-permute-start(f32[32,256]{1,0:T(8,128)S(1)} %get-tuple-element.40), channel_id=1, source_target_pairs={{0,8},{4,12},{8,0},{12,4},{1,9},{5,13},{9,1},{13,5},{2,10},{6,14},... | collective-permute-start | bytes 98312 | tf_op jit(solution)/shard_map/ppermute | solution.py:166
  21.1 0.1 collective-permute-start.8
  21.2 0.4 %shard_map.66 = (f32[32,256]{1,0:T(8,128)S(1)}, f32[32,256]{1,0:T(8,128)S(1)}) custom-call(bf16[32,1024]{1,0:T(8,128)(2,1)S(1)} %get-tuple-element.35.q_ref, bf16[256,1024]{1,0:T(8,128)(2,1)S(1)} %get-tuple-element.36.refs_0_, bf16[256,1024]{1,0:T(8,128)(2,1)S(1)} %get-tuple-element.37.refs_1_), custom_call_target="tpu_custom_call" | custom-call | tf_op jit(solution)/shard_map/pallas_call | solution.py:203
  21.6 0.5 %collective-permute-start.6 = (f32[32,256]{1,0:T(8,128)S(1)}, f32[32,256]{1,0:T(8,128)S(1)}, u32[]{:S(2)}, u32[]{:S(2)}) collective-permute-start(f32[32,256]{1,0:T(8,128)S(1)} %get-tuple-element.39), channel_id=1, source_target_pairs={{0,4},{4,0},{8,12},{12,8},{1,5},{5,1},{9,13},{13,9},{2,6},{6,2},{1... | collective-permute-start | bytes 98312 | tf_op jit(solution)/shard_map/ppermute | solution.py:166
  22.1 1.3 %collective-permute-done.7.refs_2_ = f32[32,256]{1,0:T(8,128)S(1)} collective-permute-done((f32[32,256]{1,0:T(8,128)S(1)}, f32[32,256]{1,0:T(8,128)S(1)}, u32[]{:S(2)}, u32[]{:S(2)}) %collective-permute-start.7) | collective-permute-done | bytes 32800 | tf_op jit(solution)/shard_map/ppermute | solution.py:166
  23.5 1.1 %collective-permute-done.8.refs_3_ = f32[32,256]{1,0:T(8,128)S(1)} collective-permute-done((f32[32,256]{1,0:T(8,128)S(1)}, f32[32,256]{1,0:T(8,128)S(1)}, u32[]{:S(2)}, u32[]{:S(2)}) %collective-permute-start.8) | collective-permute-done | bytes 32800 | tf_op jit(solution)/shard_map/ppermute | solution.py:166
  24.6 0.8 %shard_map.67 = (f32[32,256]{1,0:T(8,128)}, f32[32,256]{1,0:T(8,128)}) custom-call(bf16[32,1024]{1,0:T(8,128)(2,1)S(1)} %get-tuple-element.35.q_ref, f32[40,256]{1,0:T(8,128)S(1)} %get-tuple-element.22.refs_0_.refs_5_.near_ref, f32[32,32]{1,0:T(8,128)S(1)} %get-tuple-element.29.refs_4_.compat_ref, f32[32,256]{1,0:T(8,128)S(1)} %get-tuple-element.38.refs_0_, ...), custom_call_target="tpu_custom_call" | custom-call | tf_op jit(solution)/shard_map/pallas_call | solution.py:203
  (3 shorter events, 0.0 us)
Async XLA Ops:
  1.7 6.5 %collective-permute-start.2 = (f32[40,256]{1,0:T(8,128)S(1)}, f32[40,256]{1,0:T(8,128)S(1)}, u32[]{:S(2)}, u32[]{:S(2)}) collective-permute-start(f32[40,256]{1,0:T(8,128)S(1)} %get-tuple-element.22.refs_0_.refs_5_.near_ref), channel_id=1, source_target_pairs={{0,2},{1,3},{2,0},{3,1},{4,6},{5,7},{6,4},{7,5},{8,10},{9,11},{10,... | collective-permute-start | bytes 122888 | tf_op jit(solution)/shard_map/ppermute | solution.py:166
  5.8 5.8 %collective-permute-start.1 = (f32[40,256]{1,0:T(8,128)S(1)}, f32[40,256]{1,0:T(8,128)S(1)}, u32[]{:S(2)}, u32[]{:S(2)}) collective-permute-start(f32[40,256]{1,0:T(8,128)S(1)} %get-tuple-element.22.refs_0_.refs_5_.near_ref), channel_id=1, source_target_pairs={{0,3},{1,2},{2,1},{3,0},{4,7},{5,6},{6,5},{7,4},{8,11},{9,10},{10,... | collective-permute-start | bytes 122888 | tf_op jit(solution)/shard_map/ppermute | solution.py:166
  7.1 4.5 %collective-permute-start = (f32[40,256]{1,0:T(8,128)S(1)}, f32[40,256]{1,0:T(8,128)S(1)}, u32[]{:S(2)}, u32[]{:S(2)}) collective-permute-start(f32[40,256]{1,0:T(8,128)S(1)} %get-tuple-element.22.refs_0_.refs_5_.near_ref), channel_id=1, source_target_pairs={{0,1},{1,0},{2,3},{3,2},{4,5},{5,4},{6,7},{7,6},{8,9},{9,8},{10,11... | collective-permute-start | bytes 122888 | tf_op jit(solution)/shard_map/ppermute | solution.py:166
  11.7 2.7 %collective-permute-start.4 = (bf16[4,40,256]{2,1,0:T(8,128)(2,1)S(1)}, bf16[4,40,256]{2,1,0:T(8,128)(2,1)S(1)}, u32[]{:S(2)}, u32[]{:S(2)}) collective-permute-start(bf16[4,40,256]{2,1,0:T(8,128)(2,1)S(1)} %get-tuple-element.24.packed_ref.refs_3_), channel_id=1, source_target_pairs={{0,4},{4,0},{8,12},{12,8},{1,5},{5,1},{9,13},{13,9},{2,6},{6,2},{1... | collective-permute-start | bytes 245768 | tf_op jit(solution)/shard_map/ppermute | solution.py:166
  11.7 4.9 %collective-permute-start.3 = (bf16[4,40,256]{2,1,0:T(8,128)(2,1)S(1)}, bf16[4,40,256]{2,1,0:T(8,128)(2,1)S(1)}, u32[]{:S(2)}, u32[]{:S(2)}) collective-permute-start(bf16[4,40,256]{2,1,0:T(8,128)(2,1)S(1)} %get-tuple-element.24.packed_ref.refs_3_), channel_id=1, source_target_pairs={{0,8},{4,12},{8,0},{12,4},{1,9},{5,13},{9,1},{13,5},{2,10},{6,14},... | collective-permute-start | bytes 245768 | tf_op jit(solution)/shard_map/ppermute | solution.py:166
  16.6 1.3 %collective-permute-start.5 = (bf16[4,40,256]{2,1,0:T(8,128)(2,1)S(1)}, bf16[4,40,256]{2,1,0:T(8,128)(2,1)S(1)}, u32[]{:S(2)}, u32[]{:S(2)}) collective-permute-start(bf16[4,40,256]{2,1,0:T(8,128)(2,1)S(1)} %collective-permute-done.3.packed_ref), channel_id=1, source_target_pairs={{0,4},{4,0},{8,12},{12,8},{1,5},{5,1},{9,13},{13,9},{2,6},{6,2},{1... | collective-permute-start | bytes 245768 | tf_op jit(solution)/shard_map/ppermute | solution.py:166
  19.6 3.9 %collective-permute-start.7 = (f32[32,256]{1,0:T(8,128)S(1)}, f32[32,256]{1,0:T(8,128)S(1)}, u32[]{:S(2)}, u32[]{:S(2)}) collective-permute-start(f32[32,256]{1,0:T(8,128)S(1)} %get-tuple-element.40), channel_id=1, source_target_pairs={{0,8},{4,12},{8,0},{12,4},{1,9},{5,13},{9,1},{13,5},{2,10},{6,14},... | collective-permute-start | bytes 98312 | tf_op jit(solution)/shard_map/ppermute | solution.py:166
  21.1 3.5 %collective-permute-start.8 = (f32[32,256]{1,0:T(8,128)S(1)}, f32[32,256]{1,0:T(8,128)S(1)}, u32[]{:S(2)}, u32[]{:S(2)}) collective-permute-start(f32[32,256]{1,0:T(8,128)S(1)} %get-tuple-element.41), channel_id=1, source_target_pairs={{0,12},{4,8},{8,4},{12,0},{1,13},{5,9},{9,5},{13,1},{2,14},{6,10},... | collective-permute-start | bytes 98312 | tf_op jit(solution)/shard_map/ppermute | solution.py:166
  21.6 2.9 %collective-permute-start.6 = (f32[32,256]{1,0:T(8,128)S(1)}, f32[32,256]{1,0:T(8,128)S(1)}, u32[]{:S(2)}, u32[]{:S(2)}) collective-permute-start(f32[32,256]{1,0:T(8,128)S(1)} %get-tuple-element.39), channel_id=1, source_target_pairs={{0,4},{4,0},{8,12},{12,8},{1,5},{5,1},{9,13},{13,9},{2,6},{6,2},{1... | collective-permute-start | bytes 98312 | tf_op jit(solution)/shard_map/ppermute | solution.py:166

commit v9 on v8

--- a/solution.py
+++ b/solution.py
@@ -12,6 +12,7 @@
 LANES = 128
 VMEM_LIMIT = 56 * 1024 * 1024
 KEPT_BYTES = 4 * 1024 * 1024
+SCHEDULE_COST = 10 ** 10
 
 
 def normalize(logits):
@@ -90,8 +91,8 @@
     return normalize(-unary - pairwise), pairwise
 
 
-def first_part(labels, rows_ref, packed_ref, total, tile_ref):
-    blocks, _, own = packed_ref.shape
+def first_part(labels, rows_ref, packed_ref, total, tile_ref=None, begin=0, end=None):
+    blocks = range(begin, packed_ref.shape[0] if end is None else end)
     rows = rows_ref[...]
 
     def exponents(index):
@@ -100,13 +101,13 @@
             columns, rows, (((0,), (0,)), ((), ())), preferred_element_type=jnp.float32
         )
 
-    ahead = exponents(0)
-    for index in range(blocks):
+    ahead = exponents(begin)
+    for index in blocks:
         exponent = ahead
-        if index + 1 < blocks:
+        if index + 1 < blocks.stop:
             ahead = exponents(index + 1)
         tile = jnp.exp(exponent).astype(jnp.bfloat16)
-        if index == 0:
+        if index == 0 and tile_ref is not None:
             tile_ref[...] = tile
         total = total + jnp.dot(
             packed_ref[index][:labels], tile, preferred_element_type=jnp.float32
@@ -116,7 +117,11 @@
 
 def first_opening(labels, rows_ref, packed_ref, total_ref, tile_ref):
     start = jnp.zeros(total_ref.shape, jnp.float32)
-    total_ref[...] = first_part(labels, rows_ref, packed_ref, start, tile_ref)
+    total_ref[...] = first_part(labels, rows_ref, packed_ref, start, tile_ref, end=1)
+
+
+def first_rest(labels, rows_ref, packed_ref, sum_ref, total_ref):
+    total_ref[...] = first_part(labels, rows_ref, packed_ref, sum_ref[...], begin=1)
 
 
 def first_middle(labels, rows_ref, packed_ref, sum_ref, total_ref, tile_ref):
@@ -177,16 +182,18 @@
     return count & (count - 1) == 0
 
 
-def block_partners(value, use_early):
+def block_partners(value, use_own, use_beside):
     count = lax.axis_size("blk")
     if not paired("blk"):
         stacks = [value] + [swap(value, "blk", steps) for steps in range(1, count)]
-        use_early(stacks[:2])
+        use_own(value)
+        use_beside(stacks[1])
         return stacks, list(range(count))
     steps = list(range(2, count, 2))
     far = [swap(value, "blk", step) for step in steps]
-    beside = swap(value, "blk", 1)
-    *far, _ = lax.optimization_barrier((*far, use_early([value, beside])))
+    sent, _ = lax.optimization_barrier((value, use_own(value)))
+    beside = swap(sent, "blk", 1)
+    *far, _ = lax.optimization_barrier((*far, use_beside(beside)))
     stacks = [value, beside] + far + [swap(stack, "blk", 1) for stack in far]
     return stacks, [0, 1] + steps + [step + 1 for step in steps]
 
@@ -203,6 +210,7 @@
     return pl.pallas_call(
         kernel,
         out_shape=tuple(out_shapes),
+        cost_estimate=pl.CostEstimate(flops=SCHEDULE_COST, transcendentals=0, bytes_accessed=SCHEDULE_COST),
         compiler_params=pltpu.CompilerParams(vmem_limit_bytes=VMEM_LIMIT),
     )(*operands)
 
@@ -240,32 +248,37 @@
     tile_kind = kept((own, nears * own), jnp.bfloat16, parts)
     tiles, totals = [], []
 
-    def first(place, last, stack):
-        if last:
-            q_near, tile = call(
-                functools.partial(first_closing, labels, nears),
-                [kept((labels, nears * own), jnp.bfloat16), tile_kind],
-                *hold(rows, stack, *totals[-1:], packed, held, *near),
-            )
-            tiles.append(tile)
-            return q_near
+    total_kind = kept((labels, nears * own), jnp.float32)
+
+    def first_own(stack):
+        opened, tile = call(
+            functools.partial(first_opening, labels), [total_kind, tile_kind], *hold(rows, stack)
+        )
+        (total,) = call(
+            functools.partial(first_rest, labels), [total_kind], *hold(rows, stack, opened)
+        )
+        tiles.append(tile)
+        totals.append(total)
+        return opened
+
+    def first(stack):
         total, tile = call(
-            functools.partial(first_middle if totals else first_opening, labels),
-            [kept((labels, nears * own), jnp.float32), tile_kind],
-            *hold(rows, stack, *totals[-1:]),
+            functools.partial(first_middle, labels), [total_kind, tile_kind],
+            *hold(rows, stack, totals[-1]),
         )
         tiles.append(tile)
         totals.append(total)
         return total
 
-    def first_early(stacks):
-        for place, stack in enumerate(stacks):
-            result = first(place, place + 1 == parts, stack)
-        return result
-
-    stacks, steps = block_partners(packed, first_early)
-    for place in range(2, parts):
-        q_near = first(place, place + 1 == parts, stacks[place])
+    stacks, steps = block_partners(packed, first_own, first)
+    for stack in stacks[2:-1]:
+        first(stack)
+    q_near, tile = call(
+        functools.partial(first_closing, labels, nears),
+        [kept((labels, nears * own), jnp.bfloat16), tile_kind],
+        *hold(rows, stacks[-1], totals[-1], packed, held, *near),
+    )
+    tiles.append(tile)
 
     if parts * math.prod(tile_kind.shape) * 2 <= KEPT_BYTES:
         tiles = hold(*tiles)

time: 25.5 us -> 25.1 us (0.984)
  waiting for transfers between devices: 8.04 us -> 7.3 us
  Pallas kernels: 7.16 us -> 7.43 us
    ppermute x9, waiting for transfers between devices: 8.04 us -> 7.3 us  [swap(): return lax.ppermute(value, axis, pairs)]
    pallas_call x9 -> x10, Pallas kernels: 7.16 us -> 7.43 us  [call(): pl.pallas_call(kernel, out_shape=tuple(out_shapes), cost_estimate=pl.Cost...]
  transfers between devices with their start and end apart: 9 -> 9, of which waited for: 6 -> 7; matrix products, arithmetic and copies ran while one was open for 0% -> 0% of each run, Pallas kernels for 14% -> 15%
where the time goes in v9:
time: 25.1 us; the launch traced here: 25 us
  starting transfers between devices  9.57 us (38%)
  Pallas kernels  7.43 us (30%)
  waiting for transfers between devices  7.3 us (29%)
  between operations  0.67 us (3%)
    ppermute x9, starting transfers between devices, swap(): return lax.ppermute(value, axis, pairs)  9.57 us
    pallas_call x10, Pallas kernels, call(): pl.pallas_call(kernel, out_shape=tuple(out_shapes), cost_estimate=pl.Cost...  7.43 us
    ppermute x9, waiting for transfers between devices, swap(): return lax.ppermute(value, axis, pairs)  7.3 us
  transfers between devices with their start and end apart: 9, of which 7 were waited for; matrix products, arithmetic and copies ran while one was open for 0% of the time, Pallas kernels for 15%

profile of v9, /device:TPU:0, one launch (start us, length us, event | category | flops | bytes accessed | tf_op | source)
XLA Modules:
  0.0 25.0 jit_solution(15911480618333811)
XLA Ops:
  0.6 1.1 %shard_map.59 = (f32[40,256]{1,0:T(8,128)S(1)}, f32[32,32]{1,0:T(8,128)S(1)}) custom-call(bf16[6,4096]{1,0:T(8,128)(2,1)} %features_ref.1, s32[1,256]{1,0:T(1,128)} %bitcast.1, f32[32,256]{1,0:T(8,128)} %unary_ref.1, f32[32,32]{1,0:T(8,128)} %compat_ref.1), custom_call_target="tpu_custom_call" | custom-call | flops 10000000000 | bytes 10000000000 | tf_op jit(solution)/shard_map/pallas_call | solution.py:210
  1.7 4.1 %collective-permute-start.2 = (f32[40,256]{1,0:T(8,128)S(1)}, f32[40,256]{1,0:T(8,128)S(1)}, u32[]{:S(2)}, u32[]{:S(2)}) collective-permute-start(f32[40,256]{1,0:T(8,128)S(1)} %get-tuple-element.23.refs_0_.refs_5_.near_ref), channel_id=1, source_target_pairs={{0,2},{1,3},{2,0},{3,1},{4,6},{5,7},{6,4},{7,5},{8,10},{9,11},{10,... | collective-permute-start | bytes 122888 | tf_op jit(solution)/shard_map/ppermute | solution.py:171
  5.8 1.3 %collective-permute-start.1 = (f32[40,256]{1,0:T(8,128)S(1)}, f32[40,256]{1,0:T(8,128)S(1)}, u32[]{:S(2)}, u32[]{:S(2)}) collective-permute-start(f32[40,256]{1,0:T(8,128)S(1)} %get-tuple-element.23.refs_0_.refs_5_.near_ref), channel_id=1, source_target_pairs={{0,3},{1,2},{2,1},{3,0},{4,7},{5,6},{6,5},{7,4},{8,11},{9,10},{10,... | collective-permute-start | bytes 122888 | tf_op jit(solution)/shard_map/ppermute | solution.py:171
  7.1 0.2 collective-permute-start
  7.4 0.8 %collective-permute-done.2.refs_3_.refs_8_ = f32[40,256]{1,0:T(8,128)S(1)} collective-permute-done((f32[40,256]{1,0:T(8,128)S(1)}, f32[40,256]{1,0:T(8,128)S(1)}, u32[]{:S(2)}, u32[]{:S(2)}) %collective-permute-start.2) | collective-permute-done | bytes 40992 | tf_op jit(solution)/shard_map/ppermute | solution.py:171
  8.2 3.4 %collective-permute-done.1.refs_2_.refs_7_ = f32[40,256]{1,0:T(8,128)S(1)} collective-permute-done((f32[40,256]{1,0:T(8,128)S(1)}, f32[40,256]{1,0:T(8,128)S(1)}, u32[]{:S(2)}, u32[]{:S(2)}) %collective-permute-start.1) | collective-permute-done | bytes 40992 | tf_op jit(solution)/shard_map/ppermute | solution.py:171
  11.7 1.6 %collective-permute-start.3 = (bf16[4,40,256]{2,1,0:T(8,128)(2,1)S(1)}, bf16[4,40,256]{2,1,0:T(8,128)(2,1)S(1)}, u32[]{:S(2)}, u32[]{:S(2)}) collective-permute-start(bf16[4,40,256]{2,1,0:T(8,128)(2,1)S(1)} %get-tuple-element.27.packed_ref.refs_3_), channel_id=1, source_target_pairs={{0,8},{4,12},{8,0},{12,4},{1,9},{5,13},{9,1},{13,5},{2,10},{6,14},... | collective-permute-start | bytes 245768 | tf_op jit(solution)/shard_map/ppermute | solution.py:171
  13.3 0.5 %shard_map.61 = (f32[32,1024]{1,0:T(8,128)S(1)}, bf16[256,1024]{1,0:T(8,128)(2,1)S(1)}) custom-call(bf16[16,1024]{1,0:T(8,128)(2,1)S(1)} %get-tuple-element.24.rows_ref.refs_0_, bf16[4,40,256]{2,1,0:T(8,128)(2,1)S(1)} %get-tuple-element.27.packed_ref.refs_3_), custom_call_target="tpu_custom_call" | custom-call | flops 10000000000 | bytes 10000000000 | tf_op jit(solution)/shard_map/pallas_call | solution.py:210
  13.7 0.9 %shard_map.62.sum_ref = f32[32,1024]{1,0:T(8,128)S(1)} custom-call(bf16[16,1024]{1,0:T(8,128)(2,1)S(1)} %get-tuple-element.24.rows_ref.refs_0_, bf16[4,40,256]{2,1,0:T(8,128)(2,1)S(1)} %get-tuple-element.27.packed_ref.refs_3_, f32[32,1024]{1,0:T(8,128)S(1)} %get-tuple-element.26.sum_ref), custom_call_target="tpu_custom_call" | custom-call | flops 10000000000 | bytes 10000000000 | tf_op jit(solution)/shard_map/pallas_call | solution.py:210
  14.6 0.4 %collective-permute-done.4.packed_ref = bf16[4,40,256]{2,1,0:T(8,128)(2,1)S(1)} collective-permute-done((bf16[4,40,256]{2,1,0:T(8,128)(2,1)S(1)}, bf16[4,40,256]{2,1,0:T(8,128)(2,1)S(1)}, u32[]{:S(2)}, u32[]{:S(2)}) %collective-permute-start.4) | collective-permute-done | bytes 81952 | tf_op jit(solution)/shard_map/ppermute | solution.py:171
  15.0 1.1 %shard_map.63 = (f32[32,1024]{1,0:T(8,128)S(1)}, bf16[256,1024]{1,0:T(8,128)(2,1)S(1)}) custom-call(bf16[16,1024]{1,0:T(8,128)(2,1)S(1)} %get-tuple-element.24.rows_ref.refs_0_, bf16[4,40,256]{2,1,0:T(8,128)(2,1)S(1)} %collective-permute-done.4.packed_ref, f32[32,1024]{1,0:T(8,128)S(1)} %shard_map.62.sum_ref), custom_call_target="tpu_custom_call" | custom-call | flops 10000000000 | bytes 10000000000 | tf_op jit(solution)/shard_map/pallas_call | solution.py:210
  16.1 0.1 collective-permute-done.3.packed_ref
  16.2 0.1 collective-permute-start.5
  16.3 1.1 %shard_map.64 = (f32[32,1024]{1,0:T(8,128)S(1)}, bf16[256,1024]{1,0:T(8,128)(2,1)S(1)}) custom-call(bf16[16,1024]{1,0:T(8,128)(2,1)S(1)} %get-tuple-element.24.rows_ref.refs_0_, bf16[4,40,256]{2,1,0:T(8,128)(2,1)S(1)} %collective-permute-done.3.packed_ref, f32[32,1024]{1,0:T(8,128)S(1)} %get-tuple-element.28.sum_ref), custom_call_target="tpu_custom_call" | custom-call | flops 10000000000 | bytes 10000000000 | tf_op jit(solution)/shard_map/pallas_call | solution.py:210
  17.3 0.1 collective-permute-done.5.refs_1_
  17.5 1.3 %shard_map.65 = (bf16[32,1024]{1,0:T(8,128)(2,1)S(1)}, bf16[256,1024]{1,0:T(8,128)(2,1)S(1)}) custom-call(bf16[16,1024]{1,0:T(8,128)(2,1)S(1)} %get-tuple-element.24.rows_ref.refs_0_, bf16[4,40,256]{2,1,0:T(8,128)(2,1)S(1)} %collective-permute-done.5.refs_1_, f32[32,1024]{1,0:T(8,128)S(1)} %get-tuple-element.30.refs_2_, ...), custom_call_target="tpu_custom_call" | custom-call | flops 10000000000 | bytes 10000000000 | tf_op jit(solution)/shard_map/pallas_call | solution.py:210
  18.7 0.4 %shard_map.66 = (f32[32,256]{1,0:T(8,128)S(1)}, f32[32,256]{1,0:T(8,128)S(1)}) custom-call(bf16[32,1024]{1,0:T(8,128)(2,1)S(1)} %get-tuple-element.37.q_ref, bf16[256,1024]{1,0:T(8,128)(2,1)S(1)} %get-tuple-element.33.refs_0_, bf16[256,1024]{1,0:T(8,128)(2,1)S(1)} %get-tuple-element.34.refs_1_), custom_call_target="tpu_custom_call" | custom-call | flops 10000000000 | bytes 10000000000 | tf_op jit(solution)/shard_map/pallas_call | solution.py:210
  19.1 1.5 %collective-permute-start.7 = (f32[32,256]{1,0:T(8,128)S(1)}, f32[32,256]{1,0:T(8,128)S(1)}, u32[]{:S(2)}, u32[]{:S(2)}) collective-permute-start(f32[32,256]{1,0:T(8,128)S(1)} %get-tuple-element.42), channel_id=1, source_target_pairs={{0,8},{4,12},{8,0},{12,4},{1,9},{5,13},{9,1},{13,5},{2,10},{6,14},... | collective-permute-start | bytes 98312 | tf_op jit(solution)/shard_map/ppermute | solution.py:171
  20.7 0.1 collective-permute-start.8
  20.8 0.4 %shard_map.67 = (f32[32,256]{1,0:T(8,128)S(1)}, f32[32,256]{1,0:T(8,128)S(1)}) custom-call(bf16[32,1024]{1,0:T(8,128)(2,1)S(1)} %get-tuple-element.37.q_ref, bf16[256,1024]{1,0:T(8,128)(2,1)S(1)} %get-tuple-element.38.refs_0_, bf16[256,1024]{1,0:T(8,128)(2,1)S(1)} %get-tuple-element.39.refs_1_), custom_call_target="tpu_custom_call" | custom-call | flops 10000000000 | bytes 10000000000 | tf_op jit(solution)/shard_map/pallas_call | solution.py:210
  21.2 0.5 %collective-permute-start.6 = (f32[32,256]{1,0:T(8,128)S(1)}, f32[32,256]{1,0:T(8,128)S(1)}, u32[]{:S(2)}, u32[]{:S(2)}) collective-permute-start(f32[32,256]{1,0:T(8,128)S(1)} %get-tuple-element.41), channel_id=1, source_target_pairs={{0,4},{4,0},{8,12},{12,8},{1,5},{5,1},{9,13},{13,9},{2,6},{6,2},{1... | collective-permute-start | bytes 98312 | tf_op jit(solution)/shard_map/ppermute | solution.py:171
  21.7 1.3 %collective-permute-done.7.refs_2_ = f32[32,256]{1,0:T(8,128)S(1)} collective-permute-done((f32[32,256]{1,0:T(8,128)S(1)}, f32[32,256]{1,0:T(8,128)S(1)}, u32[]{:S(2)}, u32[]{:S(2)}) %collective-permute-start.7) | collective-permute-done | bytes 32800 | tf_op jit(solution)/shard_map/ppermute | solution.py:171
  23.1 1.1 %collective-permute-done.8.refs_3_ = f32[32,256]{1,0:T(8,128)S(1)} collective-permute-done((f32[32,256]{1,0:T(8,128)S(1)}, f32[32,256]{1,0:T(8,128)S(1)}, u32[]{:S(2)}, u32[]{:S(2)}) %collective-permute-start.8) | collective-permute-done | bytes 32800 | tf_op jit(solution)/shard_map/ppermute | solution.py:171
  24.2 0.8 %shard_map.68 = (f32[32,256]{1,0:T(8,128)}, f32[32,256]{1,0:T(8,128)}) custom-call(bf16[32,1024]{1,0:T(8,128)(2,1)S(1)} %get-tuple-element.37.q_ref, f32[40,256]{1,0:T(8,128)S(1)} %get-tuple-element.23.refs_0_.refs_5_.near_ref, f32[32,32]{1,0:T(8,128)S(1)} %get-tuple-element.31.refs_4_.compat_ref, f32[32,256]{1,0:T(8,128)S(1)} %get-tuple-element.40.refs_0_, ...), custom_call_target="tpu_custom_call" | custom-call | flops 10000000000 | bytes 10000000000 | tf_op jit(solution)/shard_map/pallas_call | solution.py:210
  (4 shorter events, 0.1 us)
Async XLA Ops:
  1.7 6.5 %collective-permute-start.2 = (f32[40,256]{1,0:T(8,128)S(1)}, f32[40,256]{1,0:T(8,128)S(1)}, u32[]{:S(2)}, u32[]{:S(2)}) collective-permute-start(f32[40,256]{1,0:T(8,128)S(1)} %get-tuple-element.23.refs_0_.refs_5_.near_ref), channel_id=1, source_target_pairs={{0,2},{1,3},{2,0},{3,1},{4,6},{5,7},{6,4},{7,5},{8,10},{9,11},{10,... | collective-permute-start | bytes 122888 | tf_op jit(solution)/shard_map/ppermute | solution.py:171
  5.8 5.8 %collective-permute-start.1 = (f32[40,256]{1,0:T(8,128)S(1)}, f32[40,256]{1,0:T(8,128)S(1)}, u32[]{:S(2)}, u32[]{:S(2)}) collective-permute-start(f32[40,256]{1,0:T(8,128)S(1)} %get-tuple-element.23.refs_0_.refs_5_.near_ref), channel_id=1, source_target_pairs={{0,3},{1,2},{2,1},{3,0},{4,7},{5,6},{6,5},{7,4},{8,11},{9,10},{10,... | collective-permute-start | bytes 122888 | tf_op jit(solution)/shard_map/ppermute | solution.py:171
  7.1 4.5 %collective-permute-start = (f32[40,256]{1,0:T(8,128)S(1)}, f32[40,256]{1,0:T(8,128)S(1)}, u32[]{:S(2)}, u32[]{:S(2)}) collective-permute-start(f32[40,256]{1,0:T(8,128)S(1)} %get-tuple-element.23.refs_0_.refs_5_.near_ref), channel_id=1, source_target_pairs={{0,1},{1,0},{2,3},{3,2},{4,5},{5,4},{6,7},{7,6},{8,9},{9,8},{10,11... | collective-permute-start | bytes 122888 | tf_op jit(solution)/shard_map/ppermute | solution.py:171
  11.7 4.5 %collective-permute-start.3 = (bf16[4,40,256]{2,1,0:T(8,128)(2,1)S(1)}, bf16[4,40,256]{2,1,0:T(8,128)(2,1)S(1)}, u32[]{:S(2)}, u32[]{:S(2)}) collective-permute-start(bf16[4,40,256]{2,1,0:T(8,128)(2,1)S(1)} %get-tuple-element.27.packed_ref.refs_3_), channel_id=1, source_target_pairs={{0,8},{4,12},{8,0},{12,4},{1,9},{5,13},{9,1},{13,5},{2,10},{6,14},... | collective-permute-start | bytes 245768 | tf_op jit(solution)/shard_map/ppermute | solution.py:171
  13.7 1.3 %collective-permute-start.4 = (bf16[4,40,256]{2,1,0:T(8,128)(2,1)S(1)}, bf16[4,40,256]{2,1,0:T(8,128)(2,1)S(1)}, u32[]{:S(2)}, u32[]{:S(2)}) collective-permute-start(bf16[4,40,256]{2,1,0:T(8,128)(2,1)S(1)} %get-tuple-element.27.packed_ref.refs_3_), channel_id=1, source_target_pairs={{0,4},{4,0},{8,12},{12,8},{1,5},{5,1},{9,13},{13,9},{2,6},{6,2},{1... | collective-permute-start | bytes 245768 | tf_op jit(solution)/shard_map/ppermute | solution.py:171
  16.2 1.3 %collective-permute-start.5 = (bf16[4,40,256]{2,1,0:T(8,128)(2,1)S(1)}, bf16[4,40,256]{2,1,0:T(8,128)(2,1)S(1)}, u32[]{:S(2)}, u32[]{:S(2)}) collective-permute-start(bf16[4,40,256]{2,1,0:T(8,128)(2,1)S(1)} %collective-permute-done.3.packed_ref), channel_id=1, source_target_pairs={{0,4},{4,0},{8,12},{12,8},{1,5},{5,1},{9,13},{13,9},{2,6},{6,2},{1... | collective-permute-start | bytes 245768 | tf_op jit(solution)/shard_map/ppermute | solution.py:171
  19.1 3.9 %collective-permute-start.7 = (f32[32,256]{1,0:T(8,128)S(1)}, f32[32,256]{1,0:T(8,128)S(1)}, u32[]{:S(2)}, u32[]{:S(2)}) collective-permute-start(f32[32,256]{1,0:T(8,128)S(1)} %get-tuple-element.42), channel_id=1, source_target_pairs={{0,8},{4,12},{8,0},{12,4},{1,9},{5,13},{9,1},{13,5},{2,10},{6,14},... | collective-permute-start | bytes 98312 | tf_op jit(solution)/shard_map/ppermute | solution.py:171
  20.7 3.5 %collective-permute-start.8 = (f32[32,256]{1,0:T(8,128)S(1)}, f32[32,256]{1,0:T(8,128)S(1)}, u32[]{:S(2)}, u32[]{:S(2)}) collective-permute-start(f32[32,256]{1,0:T(8,128)S(1)} %get-tuple-element.43), channel_id=1, source_target_pairs={{0,12},{4,8},{8,4},{12,0},{1,13},{5,9},{9,5},{13,1},{2,14},{6,10},... | collective-permute-start | bytes 98312 | tf_op jit(solution)/shard_map/ppermute | solution.py:171
  21.2 3.0 %collective-permute-start.6 = (f32[32,256]{1,0:T(8,128)S(1)}, f32[32,256]{1,0:T(8,128)S(1)}, u32[]{:S(2)}, u32[]{:S(2)}) collective-permute-start(f32[32,256]{1,0:T(8,128)S(1)} %get-tuple-element.41), channel_id=1, source_target_pairs={{0,4},{4,0},{8,12},{12,8},{1,5},{5,1},{9,13},{13,9},{2,6},{6,2},{1... | collective-permute-start | bytes 98312 | tf_op jit(solution)/shard_map/ppermute | solution.py:171

commit v10 on v9

--- a/solution.py
+++ b/solution.py
@@ -43,11 +43,15 @@
     return jnp.sum(jnp.where(group == (member // LANES)[None], found, 0.0), axis=0)
 
 
-def prepare_kernel(features_ref, member_ref, unary_ref, compat_ref, sent_ref, held_ref):
-    labels = unary_ref.shape[0]
-    sent_ref[pl.ds(0, labels), :] = unary_ref[...]
-    sent_ref[pl.ds(labels, 8), :] = pick_features(features_ref, member_ref[...])
-    held_ref[...] = compat_ref[...]
+def prepare_kernel(
+    features_ref, member_ref, unary_ref, compat_ref, sent_ref, held_unary_ref, held_compat_ref
+):
+    unary = unary_ref[...]
+    high, low, _ = three_parts(unary)
+    feats = pick_features(features_ref, member_ref[...])
+    sent_ref[...] = jnp.concatenate([high, low, feats], axis=0).astype(jnp.bfloat16)
+    held_unary_ref[...] = unary
+    held_compat_ref[...] = compat_ref[...]
 
 
 def half_norms(feats):
@@ -65,21 +69,16 @@
 
 
 def pack_kernel(labels, *refs):
-    near_refs, packed_ref, rows_ref = refs[:-2], refs[-2], refs[-1]
+    near_refs, packed_ref, rows_ref, unary_ref = refs[:-3], refs[-3], refs[-2], refs[-1]
     for place, near_ref in enumerate(near_refs):
         own = near_ref.shape[1]
-        feats = near_ref[pl.ds(labels, 8), :]
-        probs = normalize(-near_ref[pl.ds(0, labels), :])
-        packed_ref[place] = jnp.concatenate([probs, feats], axis=0).astype(jnp.bfloat16)
+        near = near_ref[...].astype(jnp.float32)
+        unary = near[:labels] + near[labels:2 * labels]
+        feats = near[2 * labels:]
+        packed = jnp.concatenate([normalize(-unary), feats], axis=0)
+        packed_ref[place] = packed.astype(jnp.bfloat16)
         rows_ref[:, pl.ds(place * own, own)] = product_sides(feats)[1]
-
-
-def over_blocks(count, body, start):
-    if count <= 4:
-        for index in range(count):
-            start = body(index, start)
-        return start
-    return lax.fori_loop(0, count, body, start)
+        unary_ref[:, pl.ds(place * own, own)] = unary
 
 
 def finish(message, qb, unary, compat_ref):
@@ -128,15 +127,13 @@
     total_ref[...] = first_part(labels, rows_ref, packed_ref, sum_ref[...], tile_ref)
 
 
-def first_closing(labels, nears, *refs):
-    rows_ref, packed_ref, sum_ref, own_ref, compat_ref = refs[:5]
-    near_refs, q_ref, tile_ref = refs[5:-2], refs[-2], refs[-1]
-    own = own_ref.shape[2]
+def first_closing(
+    labels, rows_ref, packed_ref, sum_ref, own_ref, compat_ref, unary_ref, q_ref, tile_ref
+):
     total = first_part(labels, rows_ref, packed_ref, sum_ref[...], tile_ref)
-    labels_now = [own_ref[near][:labels] for near in range(nears)]
-    unary = [near_ref[pl.ds(0, labels), :] for near_ref in near_refs]
+    labels_now = [own_ref[near][:labels] for near in range(own_ref.shape[0])]
     probs, _ = finish(
-        total, jnp.concatenate(labels_now, axis=1), jnp.concatenate(unary, axis=1), compat_ref
+        total, jnp.concatenate(labels_now, axis=1), unary_ref[...], compat_ref
     )
     q_ref[...] = probs.astype(jnp.bfloat16)
 
@@ -150,14 +147,13 @@
         )
 
 
-def second_closing(q_ref, near_ref, compat_ref, *refs):
+def second_closing(q_ref, unary_ref, compat_ref, *refs):
     probs_ref, pairwise_ref = refs[-2:]
     labels, own = probs_ref.shape
     total = refs[0][...]
     for part_ref in refs[1:-2]:
         total = total + part_ref[...]
-    unary = near_ref[pl.ds(0, labels), :]
-    probs, pairwise = finish(total, q_ref[:, pl.ds(0, own)], unary, compat_ref)
+    probs, pairwise = finish(total, q_ref[:, pl.ds(0, own)], unary_ref[...], compat_ref)
     probs_ref[...] = probs
     pairwise_ref[...] = pairwise
 
@@ -233,16 +229,23 @@
     labels, own = unary.shape
     nears = lax.axis_size("grp")
     count = lax.axis_size("blk") * nears
-    sent, held = call(
+    sent, held_unary, held_compat = call(
         prepare_kernel,
-        [kept((labels + 8, own), jnp.float32), kept(compat.shape, jnp.float32)],
+        [
+            kept((2 * labels + 8, own), jnp.bfloat16),
+            kept(unary.shape, jnp.float32),
+            kept(compat.shape, jnp.float32),
+        ],
         features, member[None], unary, compat,
     )
-    near = group_partners(sent)
-    packed, rows = call(
+    packed, rows, near_unary = call(
         functools.partial(pack_kernel, labels),
-        [kept((nears, labels + 8, own), jnp.bfloat16), kept((AUX, nears * own), jnp.bfloat16)],
-        *hold(*near),
+        [
+            kept((nears, labels + 8, own), jnp.bfloat16),
+            kept((AUX, nears * own), jnp.bfloat16),
+            kept((labels, nears * own), jnp.float32),
+        ],
+        *hold(*group_partners(sent)),
     )
     parts = lax.axis_size("blk")
     tile_kind = kept((own, nears * own), jnp.bfloat16, parts)
@@ -274,9 +277,9 @@
     for stack in stacks[2:-1]:
         first(stack)
     q_near, tile = call(
-        functools.partial(first_closing, labels, nears),
+        functools.partial(first_closing, labels),
         [kept((labels, nears * own), jnp.bfloat16), tile_kind],
-        *hold(rows, stacks[-1], totals[-1], packed, held, *near),
+        *hold(rows, stacks[-1], totals[-1], packed, held_compat, near_unary),
     )
     tiles.append(tile)
 
@@ -291,7 +294,7 @@
     return call(
         second_closing,
         [jax.ShapeDtypeStruct((labels, own), jnp.float32)] * 2,
-        *hold(q_near, sent, held, here, *arrived),
+        *hold(q_near, held_unary, held_compat, here, *arrived),
     )
 
 

time: 25.1 us -> 25.1 us (level)
  no operation moved by 1% of the time
where the time goes in v10:
time: 25.1 us; the launch traced here: 24.9 us
  starting transfers between devices  9.57 us (38%)
  Pallas kernels  7.43 us (30%)
  waiting for transfers between devices  7.26 us (29%)
  between operations  0.67 us (3%)
    ppermute x9, starting transfers between devices, swap(): return lax.ppermute(value, axis, pairs)  9.57 us
    pallas_call x10, Pallas kernels, call(): pl.pallas_call(kernel, out_shape=tuple(out_shapes), cost_estimate=pl.Cost...  7.43 us
    ppermute x9, waiting for transfers between devices, swap(): return lax.ppermute(value, axis, pairs)  7.26 us
  transfers between devices with their start and end apart: 9, of which 7 were waited for; matrix products, arithmetic and copies ran while one was open for 0% of the time, Pallas kernels for 15%

profile of v10, /device:TPU:0, one launch (start us, length us, event | category | flops | bytes accessed | tf_op | source)
XLA Modules:
  0.0 24.9 jit_solution(4176539555346908388)
XLA Ops:
  0.6 1.1 %shard_map.59 = (bf16[72,256]{1,0:T(8,128)(2,1)S(1)}, f32[32,256]{1,0:T(8,128)S(1)}, f32[32,32]{1,0:T(8,128)S(1)}) custom-call(bf16[6,4096]{1,0:T(8,128)(2,1)} %features_ref.1, s32[1,256]{1,0:T(1,128)} %bitcast.1, f32[32,256]{1,0:T(8,128)} %unary_ref.1, f32[32,32]{1,0:T(8,128)} %compat_ref.1), custom_call_target="tpu_custom_call" | custom-call | flops 10000000000 | bytes 10000000000 | tf_op jit(solution)/shard_map/pallas_call | solution.py:206
  1.7 4.1 %collective-permute-start.2 = (bf16[72,256]{1,0:T(8,128)(2,1)S(1)}, bf16[72,256]{1,0:T(8,128)(2,1)S(1)}, u32[]{:S(2)}, u32[]{:S(2)}) collective-permute-start(bf16[72,256]{1,0:T(8,128)(2,1)S(1)} %get-tuple-element.25.refs_0_), channel_id=1, source_target_pairs={{0,2},{1,3},{2,0},{3,1},{4,6},{5,7},{6,4},{7,5},{8,10},{9,11},{10,... | collective-permute-start | bytes 110600 | tf_op jit(solution)/shard_map/ppermute | solution.py:167
  5.8 1.3 %collective-permute-start.1 = (bf16[72,256]{1,0:T(8,128)(2,1)S(1)}, bf16[72,256]{1,0:T(8,128)(2,1)S(1)}, u32[]{:S(2)}, u32[]{:S(2)}) collective-permute-start(bf16[72,256]{1,0:T(8,128)(2,1)S(1)} %get-tuple-element.25.refs_0_), channel_id=1, source_target_pairs={{0,3},{1,2},{2,1},{3,0},{4,7},{5,6},{6,5},{7,4},{8,11},{9,10},{10,... | collective-permute-start | bytes 110600 | tf_op jit(solution)/shard_map/ppermute | solution.py:167
  7.2 0.2 collective-permute-start
  7.4 0.8 %collective-permute-done.2.refs_3_ = bf16[72,256]{1,0:T(8,128)(2,1)S(1)} collective-permute-done((bf16[72,256]{1,0:T(8,128)(2,1)S(1)}, bf16[72,256]{1,0:T(8,128)(2,1)S(1)}, u32[]{:S(2)}, u32[]{:S(2)}) %collective-permute-start.2) | collective-permute-done | bytes 36896 | tf_op jit(solution)/shard_map/ppermute | solution.py:167
  8.1 3.4 %collective-permute-done.1.refs_2_ = bf16[72,256]{1,0:T(8,128)(2,1)S(1)} collective-permute-done((bf16[72,256]{1,0:T(8,128)(2,1)S(1)}, bf16[72,256]{1,0:T(8,128)(2,1)S(1)}, u32[]{:S(2)}, u32[]{:S(2)}) %collective-permute-start.1) | collective-permute-done | bytes 36896 | tf_op jit(solution)/shard_map/ppermute | solution.py:167
  11.6 1.6 %collective-permute-start.3 = (bf16[4,40,256]{2,1,0:T(8,128)(2,1)S(1)}, bf16[4,40,256]{2,1,0:T(8,128)(2,1)S(1)}, u32[]{:S(2)}, u32[]{:S(2)}) collective-permute-start(bf16[4,40,256]{2,1,0:T(8,128)(2,1)S(1)} %get-tuple-element.29.packed_ref.own_ref), channel_id=1, source_target_pairs={{0,8},{4,12},{8,0},{12,4},{1,9},{5,13},{9,1},{13,5},{2,10},{6,14},... | collective-permute-start | bytes 245768 | tf_op jit(solution)/shard_map/ppermute | solution.py:167
  13.2 0.5 %shard_map.61 = (f32[32,1024]{1,0:T(8,128)S(1)}, bf16[256,1024]{1,0:T(8,128)(2,1)S(1)}) custom-call(bf16[16,1024]{1,0:T(8,128)(2,1)S(1)} %get-tuple-element.26.rows_ref, bf16[4,40,256]{2,1,0:T(8,128)(2,1)S(1)} %get-tuple-element.29.packed_ref.own_ref), custom_call_target="tpu_custom_call" | custom-call | flops 10000000000 | bytes 10000000000 | tf_op jit(solution)/shard_map/pallas_call | solution.py:206
  13.7 0.8 %shard_map.62.sum_ref = f32[32,1024]{1,0:T(8,128)S(1)} custom-call(bf16[16,1024]{1,0:T(8,128)(2,1)S(1)} %get-tuple-element.26.rows_ref, bf16[4,40,256]{2,1,0:T(8,128)(2,1)S(1)} %get-tuple-element.29.packed_ref.own_ref, f32[32,1024]{1,0:T(8,128)S(1)} %get-tuple-element.28.sum_ref), custom_call_target="tpu_custom_call" | custom-call | flops 10000000000 | bytes 10000000000 | tf_op jit(solution)/shard_map/pallas_call | solution.py:206
  14.6 0.4 %collective-permute-done.4.packed_ref = bf16[4,40,256]{2,1,0:T(8,128)(2,1)S(1)} collective-permute-done((bf16[4,40,256]{2,1,0:T(8,128)(2,1)S(1)}, bf16[4,40,256]{2,1,0:T(8,128)(2,1)S(1)}, u32[]{:S(2)}, u32[]{:S(2)}) %collective-permute-start.4) | collective-permute-done | bytes 81952 | tf_op jit(solution)/shard_map/ppermute | solution.py:167
  15.0 1.1 %shard_map.63 = (f32[32,1024]{1,0:T(8,128)S(1)}, bf16[256,1024]{1,0:T(8,128)(2,1)S(1)}) custom-call(bf16[16,1024]{1,0:T(8,128)(2,1)S(1)} %get-tuple-element.26.rows_ref, bf16[4,40,256]{2,1,0:T(8,128)(2,1)S(1)} %collective-permute-done.4.packed_ref, f32[32,1024]{1,0:T(8,128)S(1)} %shard_map.62.sum_ref), custom_call_target="tpu_custom_call" | custom-call | flops 10000000000 | bytes 10000000000 | tf_op jit(solution)/shard_map/pallas_call | solution.py:206
  16.0 0.1 collective-permute-done.3.packed_ref
  16.1 0.1 collective-permute-start.5
  16.3 1.1 %shard_map.64 = (f32[32,1024]{1,0:T(8,128)S(1)}, bf16[256,1024]{1,0:T(8,128)(2,1)S(1)}) custom-call(bf16[16,1024]{1,0:T(8,128)(2,1)S(1)} %get-tuple-element.26.rows_ref, bf16[4,40,256]{2,1,0:T(8,128)(2,1)S(1)} %collective-permute-done.3.packed_ref, f32[32,1024]{1,0:T(8,128)S(1)} %get-tuple-element.30.sum_ref), custom_call_target="tpu_custom_call" | custom-call | flops 10000000000 | bytes 10000000000 | tf_op jit(solution)/shard_map/pallas_call | solution.py:206
  17.3 0.1 collective-permute-done.5.packed_ref
  17.4 1.3 %shard_map.65 = (bf16[32,1024]{1,0:T(8,128)(2,1)S(1)}, bf16[256,1024]{1,0:T(8,128)(2,1)S(1)}) custom-call(bf16[16,1024]{1,0:T(8,128)(2,1)S(1)} %get-tuple-element.26.rows_ref, bf16[4,40,256]{2,1,0:T(8,128)(2,1)S(1)} %collective-permute-done.5.packed_ref, f32[32,1024]{1,0:T(8,128)S(1)} %get-tuple-element.32.sum_ref, ...), custom_call_target="tpu_custom_call" | custom-call | flops 10000000000 | bytes 10000000000 | tf_op jit(solution)/shard_map/pallas_call | solution.py:206
  18.7 0.4 %shard_map.66 = (f32[32,256]{1,0:T(8,128)S(1)}, f32[32,256]{1,0:T(8,128)S(1)}) custom-call(bf16[32,1024]{1,0:T(8,128)(2,1)S(1)} %get-tuple-element.40.q_ref, bf16[256,1024]{1,0:T(8,128)(2,1)S(1)} %get-tuple-element.36.refs_0_, bf16[256,1024]{1,0:T(8,128)(2,1)S(1)} %get-tuple-element.37.refs_1_), custom_call_target="tpu_custom_call" | custom-call | flops 10000000000 | bytes 10000000000 | tf_op jit(solution)/shard_map/pallas_call | solution.py:206
  19.1 1.5 %collective-permute-start.7 = (f32[32,256]{1,0:T(8,128)S(1)}, f32[32,256]{1,0:T(8,128)S(1)}, u32[]{:S(2)}, u32[]{:S(2)}) collective-permute-start(f32[32,256]{1,0:T(8,128)S(1)} %get-tuple-element.46), channel_id=1, source_target_pairs={{0,8},{4,12},{8,0},{12,4},{1,9},{5,13},{9,1},{13,5},{2,10},{6,14},... | collective-permute-start | bytes 98312 | tf_op jit(solution)/shard_map/ppermute | solution.py:167
  20.6 0.1 collective-permute-start.8
  20.8 0.4 %shard_map.67 = (f32[32,256]{1,0:T(8,128)S(1)}, f32[32,256]{1,0:T(8,128)S(1)}) custom-call(bf16[32,1024]{1,0:T(8,128)(2,1)S(1)} %get-tuple-element.40.q_ref, bf16[256,1024]{1,0:T(8,128)(2,1)S(1)} %get-tuple-element.42.refs_0_, bf16[256,1024]{1,0:T(8,128)(2,1)S(1)} %get-tuple-element.43.refs_1_), custom_call_target="tpu_custom_call" | custom-call | flops 10000000000 | bytes 10000000000 | tf_op jit(solution)/shard_map/pallas_call | solution.py:206
  21.2 0.5 %collective-permute-start.6 = (f32[32,256]{1,0:T(8,128)S(1)}, f32[32,256]{1,0:T(8,128)S(1)}, u32[]{:S(2)}, u32[]{:S(2)}) collective-permute-start(f32[32,256]{1,0:T(8,128)S(1)} %get-tuple-element.45), channel_id=1, source_target_pairs={{0,4},{4,0},{8,12},{12,8},{1,5},{5,1},{9,13},{13,9},{2,6},{6,2},{1... | collective-permute-start | bytes 98312 | tf_op jit(solution)/shard_map/ppermute | solution.py:167
  21.7 1.4 %collective-permute-done.7.refs_2_ = f32[32,256]{1,0:T(8,128)S(1)} collective-permute-done((f32[32,256]{1,0:T(8,128)S(1)}, f32[32,256]{1,0:T(8,128)S(1)}, u32[]{:S(2)}, u32[]{:S(2)}) %collective-permute-start.7) | collective-permute-done | bytes 32800 | tf_op jit(solution)/shard_map/ppermute | solution.py:167
  23.0 1.1 %collective-permute-done.8.refs_3_ = f32[32,256]{1,0:T(8,128)S(1)} collective-permute-done((f32[32,256]{1,0:T(8,128)S(1)}, f32[32,256]{1,0:T(8,128)S(1)}, u32[]{:S(2)}, u32[]{:S(2)}) %collective-permute-start.8) | collective-permute-done | bytes 32800 | tf_op jit(solution)/shard_map/ppermute | solution.py:167
  24.1 0.8 %shard_map.68 = (f32[32,256]{1,0:T(8,128)}, f32[32,256]{1,0:T(8,128)}) custom-call(bf16[32,1024]{1,0:T(8,128)(2,1)S(1)} %get-tuple-element.40.q_ref, f32[32,256]{1,0:T(8,128)S(1)} %get-tuple-element.41.unary_ref, f32[32,32]{1,0:T(8,128)S(1)} %get-tuple-element.33.compat_ref, f32[32,256]{1,0:T(8,128)S(1)} %get-tuple-element.44.refs_0_, ...), custom_call_target="tpu_custom_call" | custom-call | flops 10000000000 | bytes 10000000000 | tf_op jit(solution)/shard_map/pallas_call | solution.py:206
  (4 shorter events, 0.1 us)
Async XLA Ops:
  1.7 6.4 %collective-permute-start.2 = (bf16[72,256]{1,0:T(8,128)(2,1)S(1)}, bf16[72,256]{1,0:T(8,128)(2,1)S(1)}, u32[]{:S(2)}, u32[]{:S(2)}) collective-permute-start(bf16[72,256]{1,0:T(8,128)(2,1)S(1)} %get-tuple-element.25.refs_0_), channel_id=1, source_target_pairs={{0,2},{1,3},{2,0},{3,1},{4,6},{5,7},{6,4},{7,5},{8,10},{9,11},{10,... | collective-permute-start | bytes 110600 | tf_op jit(solution)/shard_map/ppermute | solution.py:167
  5.8 5.8 %collective-permute-start.1 = (bf16[72,256]{1,0:T(8,128)(2,1)S(1)}, bf16[72,256]{1,0:T(8,128)(2,1)S(1)}, u32[]{:S(2)}, u32[]{:S(2)}) collective-permute-start(bf16[72,256]{1,0:T(8,128)(2,1)S(1)} %get-tuple-element.25.refs_0_), channel_id=1, source_target_pairs={{0,3},{1,2},{2,1},{3,0},{4,7},{5,6},{6,5},{7,4},{8,11},{9,10},{10,... | collective-permute-start | bytes 110600 | tf_op jit(solution)/shard_map/ppermute | solution.py:167
  7.2 4.4 %collective-permute-start = (bf16[72,256]{1,0:T(8,128)(2,1)S(1)}, bf16[72,256]{1,0:T(8,128)(2,1)S(1)}, u32[]{:S(2)}, u32[]{:S(2)}) collective-permute-start(bf16[72,256]{1,0:T(8,128)(2,1)S(1)} %get-tuple-element.25.refs_0_), channel_id=1, source_target_pairs={{0,1},{1,0},{2,3},{3,2},{4,5},{5,4},{6,7},{7,6},{8,9},{9,8},{10,11... | collective-permute-start | bytes 110600 | tf_op jit(solution)/shard_map/ppermute | solution.py:167
  11.6 4.5 %collective-permute-start.3 = (bf16[4,40,256]{2,1,0:T(8,128)(2,1)S(1)}, bf16[4,40,256]{2,1,0:T(8,128)(2,1)S(1)}, u32[]{:S(2)}, u32[]{:S(2)}) collective-permute-start(bf16[4,40,256]{2,1,0:T(8,128)(2,1)S(1)} %get-tuple-element.29.packed_ref.own_ref), channel_id=1, source_target_pairs={{0,8},{4,12},{8,0},{12,4},{1,9},{5,13},{9,1},{13,5},{2,10},{6,14},... | collective-permute-start | bytes 245768 | tf_op jit(solution)/shard_map/ppermute | solution.py:167
  13.7 1.3 %collective-permute-start.4 = (bf16[4,40,256]{2,1,0:T(8,128)(2,1)S(1)}, bf16[4,40,256]{2,1,0:T(8,128)(2,1)S(1)}, u32[]{:S(2)}, u32[]{:S(2)}) collective-permute-start(bf16[4,40,256]{2,1,0:T(8,128)(2,1)S(1)} %get-tuple-element.29.packed_ref.own_ref), channel_id=1, source_target_pairs={{0,4},{4,0},{8,12},{12,8},{1,5},{5,1},{9,13},{13,9},{2,6},{6,2},{1... | collective-permute-start | bytes 245768 | tf_op jit(solution)/shard_map/ppermute | solution.py:167
  16.1 1.3 %collective-permute-start.5 = (bf16[4,40,256]{2,1,0:T(8,128)(2,1)S(1)}, bf16[4,40,256]{2,1,0:T(8,128)(2,1)S(1)}, u32[]{:S(2)}, u32[]{:S(2)}) collective-permute-start(bf16[4,40,256]{2,1,0:T(8,128)(2,1)S(1)} %collective-permute-done.3.packed_ref), channel_id=1, source_target_pairs={{0,4},{4,0},{8,12},{12,8},{1,5},{5,1},{9,13},{13,9},{2,6},{6,2},{1... | collective-permute-start | bytes 245768 | tf_op jit(solution)/shard_map/ppermute | solution.py:167
  19.1 3.9 %collective-permute-start.7 = (f32[32,256]{1,0:T(8,128)S(1)}, f32[32,256]{1,0:T(8,128)S(1)}, u32[]{:S(2)}, u32[]{:S(2)}) collective-permute-start(f32[32,256]{1,0:T(8,128)S(1)} %get-tuple-element.46), channel_id=1, source_target_pairs={{0,8},{4,12},{8,0},{12,4},{1,9},{5,13},{9,1},{13,5},{2,10},{6,14},... | collective-permute-start | bytes 98312 | tf_op jit(solution)/shard_map/ppermute | solution.py:167
  20.6 3.5 %collective-permute-start.8 = (f32[32,256]{1,0:T(8,128)S(1)}, f32[32,256]{1,0:T(8,128)S(1)}, u32[]{:S(2)}, u32[]{:S(2)}) collective-permute-start(f32[32,256]{1,0:T(8,128)S(1)} %get-tuple-element.47), channel_id=1, source_target_pairs={{0,12},{4,8},{8,4},{12,0},{1,13},{5,9},{9,5},{13,1},{2,14},{6,10},... | collective-permute-start | bytes 98312 | tf_op jit(solution)/shard_map/ppermute | solution.py:167
  21.2 2.9 %collective-permute-start.6 = (f32[32,256]{1,0:T(8,128)S(1)}, f32[32,256]{1,0:T(8,128)S(1)}, u32[]{:S(2)}, u32[]{:S(2)}) collective-permute-start(f32[32,256]{1,0:T(8,128)S(1)} %get-tuple-element.45), channel_id=1, source_target_pairs={{0,4},{4,0},{8,12},{12,8},{1,5},{5,1},{9,13},{13,9},{2,6},{6,2},{1... | collective-permute-start | bytes 98312 | tf_op jit(solution)/shard_map/ppermute | solution.py:167

commit v11 on v9

--- a/solution.py
+++ b/solution.py
@@ -12,7 +12,7 @@
 LANES = 128
 VMEM_LIMIT = 56 * 1024 * 1024
 KEPT_BYTES = 4 * 1024 * 1024
-SCHEDULE_COST = 10 ** 10
+HIDING_COST = 10 ** 10
 
 
 def normalize(logits):
@@ -61,7 +61,7 @@
     spare = jnp.zeros((AUX - 8 - 6, own), jnp.float32)
     columns = jnp.concatenate([feats] + norms + [ones, spare], axis=0)
     rows = jnp.concatenate([feats, ones] + norms + [spare], axis=0)
-    return columns.astype(jnp.bfloat16), rows.astype(jnp.bfloat16)
+    return columns.astype(jnp.bfloat16), rows
 
 
 def pack_kernel(labels, *refs):
@@ -71,7 +71,7 @@
         feats = near_ref[pl.ds(labels, 8), :]
         probs = normalize(-near_ref[pl.ds(0, labels), :])
         packed_ref[place] = jnp.concatenate([probs, feats], axis=0).astype(jnp.bfloat16)
-        rows_ref[:, pl.ds(place * own, own)] = product_sides(feats)[1]
+        rows_ref[pl.ds(place * own, own), :] = product_sides(feats)[1].T.astype(jnp.bfloat16)
 
 
 def over_blocks(count, body, start):
@@ -93,26 +93,15 @@
 
 def first_part(labels, rows_ref, packed_ref, total, tile_ref=None, begin=0, end=None):
     blocks = range(begin, packed_ref.shape[0] if end is None else end)
-    rows = rows_ref[...]
-
-    def exponents(index):
-        columns = product_sides(packed_ref[index][labels:].astype(jnp.float32))[0]
-        return lax.dot_general(
-            columns, rows, (((0,), (0,)), ((), ())), preferred_element_type=jnp.float32
-        )
-
-    ahead = exponents(begin)
-    for index in blocks:
-        exponent = ahead
-        if index + 1 < blocks.stop:
-            ahead = exponents(index + 1)
-        tile = jnp.exp(exponent).astype(jnp.bfloat16)
-        if index == 0 and tile_ref is not None:
-            tile_ref[...] = tile
-        total = total + jnp.dot(
-            packed_ref[index][:labels], tile, preferred_element_type=jnp.float32
-        )
-    return total
+    packed = jnp.concatenate([packed_ref[index] for index in blocks], axis=1)
+    columns = product_sides(packed[labels:].astype(jnp.float32))[0]
+    exponent = jnp.dot(rows_ref[...], columns, preferred_element_type=jnp.float32)
+    tile = jnp.exp(exponent).astype(jnp.bfloat16)
+    if tile_ref is not None:
+        tile_ref[...] = tile[:, :packed_ref.shape[2]]
+    return total + lax.dot_general(
+        tile, packed[:labels], (((1,), (1,)), ((), ())), preferred_element_type=jnp.float32
+    )
 
 
 def first_opening(labels, rows_ref, packed_ref, total_ref, tile_ref):
@@ -132,7 +121,7 @@
     rows_ref, packed_ref, sum_ref, own_ref, compat_ref = refs[:5]
     near_refs, q_ref, tile_ref = refs[5:-2], refs[-2], refs[-1]
     own = own_ref.shape[2]
-    total = first_part(labels, rows_ref, packed_ref, sum_ref[...], tile_ref)
+    total = first_part(labels, rows_ref, packed_ref, sum_ref[...], tile_ref).T
     labels_now = [own_ref[near][:labels] for near in range(nears)]
     unary = [near_ref[pl.ds(0, labels), :] for near_ref in near_refs]
     probs, _ = finish(
@@ -144,10 +133,7 @@
 def second_parts(q_ref, *refs):
     count = len(refs) // 2
     for tile_ref, part_ref in zip(refs[:count], refs[count:]):
-        part_ref[...] = lax.dot_general(
-            q_ref[...], tile_ref[...], (((1,), (1,)), ((), ())),
-            preferred_element_type=jnp.float32,
-        )
+        part_ref[...] = jnp.dot(q_ref[...], tile_ref[...], preferred_element_type=jnp.float32)
 
 
 def second_closing(q_ref, near_ref, compat_ref, *refs):
@@ -206,11 +192,11 @@
     return math.prod(dims) * jnp.dtype(kind).itemsize <= KEPT_BYTES
 
 
-def call(kernel, out_shapes, *operands):
+def call(kernel, out_shapes, *operands, cost=1):
     return pl.pallas_call(
         kernel,
         out_shape=tuple(out_shapes),
-        cost_estimate=pl.CostEstimate(flops=SCHEDULE_COST, transcendentals=0, bytes_accessed=SCHEDULE_COST),
+        cost_estimate=pl.CostEstimate(flops=cost, transcendentals=0, bytes_accessed=cost),
         compiler_params=pltpu.CompilerParams(vmem_limit_bytes=VMEM_LIMIT),
     )(*operands)
 
@@ -241,21 +227,22 @@
     near = group_partners(sent)
     packed, rows = call(
         functools.partial(pack_kernel, labels),
-        [kept((nears, labels + 8, own), jnp.bfloat16), kept((AUX, nears * own), jnp.bfloat16)],
+        [kept((nears, labels + 8, own), jnp.bfloat16), kept((nears * own, AUX), jnp.bfloat16)],
         *hold(*near),
     )
     parts = lax.axis_size("blk")
-    tile_kind = kept((own, nears * own), jnp.bfloat16, parts)
+    tile_kind = kept((nears * own, own), jnp.bfloat16, parts)
     tiles, totals = [], []
 
-    total_kind = kept((labels, nears * own), jnp.float32)
+    total_kind = kept((nears * own, labels), jnp.float32)
 
     def first_own(stack):
         opened, tile = call(
-            functools.partial(first_opening, labels), [total_kind, tile_kind], *hold(rows, stack)
+            functools.partial(first_opening, labels), [total_kind, tile_kind], *hold(rows, stack),
         )
         (total,) = call(
-            functools.partial(first_rest, labels), [total_kind], *hold(rows, stack, opened)
+            functools.partial(first_rest, labels), [total_kind], *hold(rows, stack, opened),
+            cost=HIDING_COST,
         )
         tiles.append(tile)
         totals.append(total)

time: 25.1 us -> 27.2 us (1.084)
  waiting for transfers between devices: 7.3 us -> 8.85 us
  Pallas kernels: 7.43 us -> 8.04 us
    ppermute x9, waiting for transfers between devices: 7.3 us -> 8.85 us  [swap(): return lax.ppermute(value, axis, pairs)]
    pallas_call x10, Pallas kernels: 7.43 us -> 8.04 us  [call(): pl.pallas_call(kernel, out_shape=tuple(out_shapes), cost_estimate=pl.Cost...]
  transfers between devices with their start and end apart: 9 -> 9, of which waited for: 7 -> 5; matrix products, arithmetic and copies ran while one was open for 0% -> 0% of each run, Pallas kernels for 15% -> 15%
where the time goes in v11:
time: 27.2 us; the launch traced here: 27.1 us
  starting transfers between devices  9.49 us (35%)
  waiting for transfers between devices  8.85 us (33%)
  Pallas kernels  8.04 us (30%)
  between operations  0.7 us (3%)
    ppermute x9, starting transfers between devices, swap(): return lax.ppermute(value, axis, pairs)  9.49 us
    ppermute x9, waiting for transfers between devices, swap(): return lax.ppermute(value, axis, pairs)  8.85 us
    pallas_call x10, Pallas kernels, call(): pl.pallas_call(kernel, out_shape=tuple(out_shapes), cost_estimate=pl.Cost...  8.04 us
  transfers between devices with their start and end apart: 9, of which 5 were waited for; matrix products, arithmetic and copies ran while one was open for 0% of the time, Pallas kernels for 15%

profile of v11, /device:TPU:0, one launch (start us, length us, event | category | flops | bytes accessed | tf_op | source)
XLA Modules:
  0.0 27.1 jit_solution(1202761899789409192)
XLA Ops:
  0.6 1.1 %shard_map.59 = (f32[40,256]{1,0:T(8,128)S(1)}, f32[32,32]{1,0:T(8,128)S(1)}) custom-call(bf16[6,4096]{1,0:T(8,128)(2,1)} %features_ref.1, s32[1,256]{1,0:T(1,128)} %bitcast.1, f32[32,256]{1,0:T(8,128)} %unary_ref.1, f32[32,32]{1,0:T(8,128)} %compat_ref.1), custom_call_target="tpu_custom_call" | custom-call | flops 1 | bytes 1 | tf_op jit(solution)/shard_map/pallas_call | solution.py:196
  1.7 3.1 %collective-permute-start = (f32[40,256]{1,0:T(8,128)S(1)}, f32[40,256]{1,0:T(8,128)S(1)}, u32[]{:S(2)}, u32[]{:S(2)}) collective-permute-start(f32[40,256]{1,0:T(8,128)S(1)} %get-tuple-element.23.refs_0_.refs_5_.near_ref), channel_id=1, source_target_pairs={{0,1},{1,0},{2,3},{3,2},{4,5},{5,4},{6,7},{7,6},{8,9},{9,8},{10,11... | collective-permute-start | bytes 122888 | tf_op jit(solution)/shard_map/ppermute | solution.py:157
  4.8 2.5 %collective-permute-start.1 = (f32[40,256]{1,0:T(8,128)S(1)}, f32[40,256]{1,0:T(8,128)S(1)}, u32[]{:S(2)}, u32[]{:S(2)}) collective-permute-start(f32[40,256]{1,0:T(8,128)S(1)} %get-tuple-element.23.refs_0_.refs_5_.near_ref), channel_id=1, source_target_pairs={{0,3},{1,2},{2,1},{3,0},{4,7},{5,6},{6,5},{7,4},{8,11},{9,10},{10,... | collective-permute-start | bytes 122888 | tf_op jit(solution)/shard_map/ppermute | solution.py:157
  7.3 0.1 collective-permute-start.2
  7.4 3.7 %collective-permute-done.1.refs_2_.refs_7_ = f32[40,256]{1,0:T(8,128)S(1)} collective-permute-done((f32[40,256]{1,0:T(8,128)S(1)}, f32[40,256]{1,0:T(8,128)S(1)}, u32[]{:S(2)}, u32[]{:S(2)}) %collective-permute-start.1) | collective-permute-done | bytes 40992 | tf_op jit(solution)/shard_map/ppermute | solution.py:157
  11.1 1.5 %collective-permute-done.2.refs_3_.refs_8_ = f32[40,256]{1,0:T(8,128)S(1)} collective-permute-done((f32[40,256]{1,0:T(8,128)S(1)}, f32[40,256]{1,0:T(8,128)S(1)}, u32[]{:S(2)}, u32[]{:S(2)}) %collective-permute-start.2) | collective-permute-done | bytes 40992 | tf_op jit(solution)/shard_map/ppermute | solution.py:157
  12.6 0.2 shard_map.60
  12.8 1.6 %collective-permute-start.3 = (bf16[4,40,256]{2,1,0:T(8,128)(2,1)S(1)}, bf16[4,40,256]{2,1,0:T(8,128)(2,1)S(1)}, u32[]{:S(2)}, u32[]{:S(2)}) collective-permute-start(bf16[4,40,256]{2,1,0:T(8,128)(2,1)S(1)} %get-tuple-element.27.packed_ref.refs_3_), channel_id=1, source_target_pairs={{0,8},{4,12},{8,0},{12,4},{1,9},{5,13},{9,1},{13,5},{2,10},{6,14},... | collective-permute-start | bytes 245768 | tf_op jit(solution)/shard_map/ppermute | solution.py:157
  14.4 0.5 %shard_map.61 = (f32[1024,32]{1,0:T(8,128)S(1)}, bf16[1024,256]{1,0:T(8,128)(2,1)S(1)}) custom-call(bf16[1024,16]{1,0:T(8,128)(2,1)S(1)} %get-tuple-element.24.rows_ref.refs_0_, bf16[4,40,256]{2,1,0:T(8,128)(2,1)S(1)} %get-tuple-element.27.packed_ref.refs_3_), custom_call_target="tpu_custom_call" | custom-call | flops 1 | bytes 1 | tf_op jit(solution)/shard_map/pallas_call | solution.py:196
  14.9 0.1 collective-permute-start.4
  15.0 1.0 %shard_map.62.sum_ref = f32[1024,32]{1,0:T(8,128)S(1)} custom-call(bf16[1024,16]{1,0:T(8,128)(2,1)S(1)} %get-tuple-element.24.rows_ref.refs_0_, bf16[4,40,256]{2,1,0:T(8,128)(2,1)S(1)} %get-tuple-element.27.packed_ref.refs_3_, f32[1024,32]{1,0:T(8,128)S(1)} %get-tuple-element.26.sum_ref), custom_call_target="tpu_custom_call" | custom-call | flops 10000000000 | bytes 10000000000 | tf_op jit(solution)/shard_map/pallas_call | solution.py:196
  15.9 0.3 %collective-permute-done.4.packed_ref = bf16[4,40,256]{2,1,0:T(8,128)(2,1)S(1)} collective-permute-done((bf16[4,40,256]{2,1,0:T(8,128)(2,1)S(1)}, bf16[4,40,256]{2,1,0:T(8,128)(2,1)S(1)}, u32[]{:S(2)}, u32[]{:S(2)}) %collective-permute-start.4) | collective-permute-done | bytes 81952 | tf_op jit(solution)/shard_map/ppermute | solution.py:157
  16.2 1.2 %shard_map.63 = (f32[1024,32]{1,0:T(8,128)S(1)}, bf16[1024,256]{1,0:T(8,128)(2,1)S(1)}) custom-call(bf16[1024,16]{1,0:T(8,128)(2,1)S(1)} %get-tuple-element.24.rows_ref.refs_0_, bf16[4,40,256]{2,1,0:T(8,128)(2,1)S(1)} %collective-permute-done.4.packed_ref, f32[1024,32]{1,0:T(8,128)S(1)} %shard_map.62.sum_ref), custom_call_target="tpu_custom_call" | custom-call | flops 1 | bytes 1 | tf_op jit(solution)/shard_map/pallas_call | solution.py:196
  17.5 0.3 %collective-permute-start.5 = (bf16[4,40,256]{2,1,0:T(8,128)(2,1)S(1)}, bf16[4,40,256]{2,1,0:T(8,128)(2,1)S(1)}, u32[]{:S(2)}, u32[]{:S(2)}) collective-permute-start(bf16[4,40,256]{2,1,0:T(8,128)(2,1)S(1)} %collective-permute-done.3.packed_ref), channel_id=1, source_target_pairs={{0,4},{4,0},{8,12},{12,8},{1,5},{5,1},{9,13},{13,9},{2,6},{6,2},{1... | collective-permute-start | bytes 245768 | tf_op jit(solution)/shard_map/ppermute | solution.py:157
  17.8 1.2 %shard_map.64 = (f32[1024,32]{1,0:T(8,128)S(1)}, bf16[1024,256]{1,0:T(8,128)(2,1)S(1)}) custom-call(bf16[1024,16]{1,0:T(8,128)(2,1)S(1)} %get-tuple-element.24.rows_ref.refs_0_, bf16[4,40,256]{2,1,0:T(8,128)(2,1)S(1)} %collective-permute-done.3.packed_ref, f32[1024,32]{1,0:T(8,128)S(1)} %get-tuple-element.28.sum_ref), custom_call_target="tpu_custom_call" | custom-call | flops 1 | bytes 1 | tf_op jit(solution)/shard_map/pallas_call | solution.py:196
  19.0 1.5 %shard_map.65 = (bf16[32,1024]{1,0:T(8,128)(2,1)S(1)}, bf16[1024,256]{1,0:T(8,128)(2,1)S(1)}) custom-call(bf16[1024,16]{1,0:T(8,128)(2,1)S(1)} %get-tuple-element.24.rows_ref.refs_0_, bf16[4,40,256]{2,1,0:T(8,128)(2,1)S(1)} %collective-permute-done.5.refs_1_, f32[1024,32]{1,0:T(8,128)S(1)} %get-tuple-element.30.refs_2_, ...), custom_call_target="tpu_custom_call" | custom-call | flops 1 | bytes 1 | tf_op jit(solution)/shard_map/pallas_call | solution.py:196
  20.5 0.3 %shard_map.66 = (f32[32,256]{1,0:T(8,128)S(1)}, f32[32,256]{1,0:T(8,128)S(1)}) custom-call(bf16[32,1024]{1,0:T(8,128)(2,1)S(1)} %get-tuple-element.37.q_ref, bf16[1024,256]{1,0:T(8,128)(2,1)S(1)} %get-tuple-element.33.refs_0_, bf16[1024,256]{1,0:T(8,128)(2,1)S(1)} %get-tuple-element.34.refs_1_), custom_call_target="tpu_custom_call" | custom-call | flops 1 | bytes 1 | tf_op jit(solution)/shard_map/pallas_call | solution.py:196
  20.8 0.3 %shard_map.67 = (f32[32,256]{1,0:T(8,128)S(1)}, f32[32,256]{1,0:T(8,128)S(1)}) custom-call(bf16[32,1024]{1,0:T(8,128)(2,1)S(1)} %get-tuple-element.37.q_ref, bf16[1024,256]{1,0:T(8,128)(2,1)S(1)} %get-tuple-element.38.refs_0_, bf16[1024,256]{1,0:T(8,128)(2,1)S(1)} %get-tuple-element.39.refs_1_), custom_call_target="tpu_custom_call" | custom-call | flops 1 | bytes 1 | tf_op jit(solution)/shard_map/pallas_call | solution.py:196
  21.1 0.3 %collective-permute-start.6 = (f32[32,256]{1,0:T(8,128)S(1)}, f32[32,256]{1,0:T(8,128)S(1)}, u32[]{:S(2)}, u32[]{:S(2)}) collective-permute-start(f32[32,256]{1,0:T(8,128)S(1)} %get-tuple-element.41), channel_id=1, source_target_pairs={{0,4},{4,0},{8,12},{12,8},{1,5},{5,1},{9,13},{13,9},{2,6},{6,2},{1... | collective-permute-start | bytes 98312 | tf_op jit(solution)/shard_map/ppermute | solution.py:157
  21.4 1.2 %collective-permute-start.7 = (f32[32,256]{1,0:T(8,128)S(1)}, f32[32,256]{1,0:T(8,128)S(1)}, u32[]{:S(2)}, u32[]{:S(2)}) collective-permute-start(f32[32,256]{1,0:T(8,128)S(1)} %get-tuple-element.42), channel_id=1, source_target_pairs={{0,8},{4,12},{8,0},{12,4},{1,9},{5,13},{9,1},{13,5},{2,10},{6,14},... | collective-permute-start | bytes 98312 | tf_op jit(solution)/shard_map/ppermute | solution.py:157
  22.6 0.3 %collective-permute-start.8 = (f32[32,256]{1,0:T(8,128)S(1)}, f32[32,256]{1,0:T(8,128)S(1)}, u32[]{:S(2)}, u32[]{:S(2)}) collective-permute-start(f32[32,256]{1,0:T(8,128)S(1)} %get-tuple-element.43), channel_id=1, source_target_pairs={{0,12},{4,8},{8,4},{12,0},{1,13},{5,9},{9,5},{13,1},{2,14},{6,10},... | collective-permute-start | bytes 98312 | tf_op jit(solution)/shard_map/ppermute | solution.py:157
  23.0 2.3 %collective-permute-done.7.refs_2_ = f32[32,256]{1,0:T(8,128)S(1)} collective-permute-done((f32[32,256]{1,0:T(8,128)S(1)}, f32[32,256]{1,0:T(8,128)S(1)}, u32[]{:S(2)}, u32[]{:S(2)}) %collective-permute-start.7) | collective-permute-done | bytes 32800 | tf_op jit(solution)/shard_map/ppermute | solution.py:157
  25.3 1.0 %collective-permute-done.8.refs_3_ = f32[32,256]{1,0:T(8,128)S(1)} collective-permute-done((f32[32,256]{1,0:T(8,128)S(1)}, f32[32,256]{1,0:T(8,128)S(1)}, u32[]{:S(2)}, u32[]{:S(2)}) %collective-permute-start.8) | collective-permute-done | bytes 32800 | tf_op jit(solution)/shard_map/ppermute | solution.py:157
  26.3 0.8 %shard_map.68 = (f32[32,256]{1,0:T(8,128)}, f32[32,256]{1,0:T(8,128)}) custom-call(bf16[32,1024]{1,0:T(8,128)(2,1)S(1)} %get-tuple-element.37.q_ref, f32[40,256]{1,0:T(8,128)S(1)} %get-tuple-element.23.refs_0_.refs_5_.near_ref, f32[32,32]{1,0:T(8,128)S(1)} %get-tuple-element.31.refs_4_.compat_ref, f32[32,256]{1,0:T(8,128)S(1)} %get-tuple-element.40.refs_0_, ...), custom_call_target="tpu_custom_call" | custom-call | flops 1 | bytes 1 | tf_op jit(solution)/shard_map/pallas_call | solution.py:196
  (4 shorter events, 0.0 us)
Async XLA Ops:
  1.7 5.7 %collective-permute-start = (f32[40,256]{1,0:T(8,128)S(1)}, f32[40,256]{1,0:T(8,128)S(1)}, u32[]{:S(2)}, u32[]{:S(2)}) collective-permute-start(f32[40,256]{1,0:T(8,128)S(1)} %get-tuple-element.23.refs_0_.refs_5_.near_ref), channel_id=1, source_target_pairs={{0,1},{1,0},{2,3},{3,2},{4,5},{5,4},{6,7},{7,6},{8,9},{9,8},{10,11... | collective-permute-start | bytes 122888 | tf_op jit(solution)/shard_map/ppermute | solution.py:157
  4.8 6.3 %collective-permute-start.1 = (f32[40,256]{1,0:T(8,128)S(1)}, f32[40,256]{1,0:T(8,128)S(1)}, u32[]{:S(2)}, u32[]{:S(2)}) collective-permute-start(f32[40,256]{1,0:T(8,128)S(1)} %get-tuple-element.23.refs_0_.refs_5_.near_ref), channel_id=1, source_target_pairs={{0,3},{1,2},{2,1},{3,0},{4,7},{5,6},{6,5},{7,4},{8,11},{9,10},{10,... | collective-permute-start | bytes 122888 | tf_op jit(solution)/shard_map/ppermute | solution.py:157
  7.3 5.3 %collective-permute-start.2 = (f32[40,256]{1,0:T(8,128)S(1)}, f32[40,256]{1,0:T(8,128)S(1)}, u32[]{:S(2)}, u32[]{:S(2)}) collective-permute-start(f32[40,256]{1,0:T(8,128)S(1)} %get-tuple-element.23.refs_0_.refs_5_.near_ref), channel_id=1, source_target_pairs={{0,2},{1,3},{2,0},{3,1},{4,6},{5,7},{6,4},{7,5},{8,10},{9,11},{10,... | collective-permute-start | bytes 122888 | tf_op jit(solution)/shard_map/ppermute | solution.py:157
  12.8 4.7 %collective-permute-start.3 = (bf16[4,40,256]{2,1,0:T(8,128)(2,1)S(1)}, bf16[4,40,256]{2,1,0:T(8,128)(2,1)S(1)}, u32[]{:S(2)}, u32[]{:S(2)}) collective-permute-start(bf16[4,40,256]{2,1,0:T(8,128)(2,1)S(1)} %get-tuple-element.27.packed_ref.refs_3_), channel_id=1, source_target_pairs={{0,8},{4,12},{8,0},{12,4},{1,9},{5,13},{9,1},{13,5},{2,10},{6,14},... | collective-permute-start | bytes 245768 | tf_op jit(solution)/shard_map/ppermute | solution.py:157
  14.9 1.3 %collective-permute-start.4 = (bf16[4,40,256]{2,1,0:T(8,128)(2,1)S(1)}, bf16[4,40,256]{2,1,0:T(8,128)(2,1)S(1)}, u32[]{:S(2)}, u32[]{:S(2)}) collective-permute-start(bf16[4,40,256]{2,1,0:T(8,128)(2,1)S(1)} %get-tuple-element.27.packed_ref.refs_3_), channel_id=1, source_target_pairs={{0,4},{4,0},{8,12},{12,8},{1,5},{5,1},{9,13},{13,9},{2,6},{6,2},{1... | collective-permute-start | bytes 245768 | tf_op jit(solution)/shard_map/ppermute | solution.py:157
  17.5 1.5 %collective-permute-start.5 = (bf16[4,40,256]{2,1,0:T(8,128)(2,1)S(1)}, bf16[4,40,256]{2,1,0:T(8,128)(2,1)S(1)}, u32[]{:S(2)}, u32[]{:S(2)}) collective-permute-start(bf16[4,40,256]{2,1,0:T(8,128)(2,1)S(1)} %collective-permute-done.3.packed_ref), channel_id=1, source_target_pairs={{0,4},{4,0},{8,12},{12,8},{1,5},{5,1},{9,13},{13,9},{2,6},{6,2},{1... | collective-permute-start | bytes 245768 | tf_op jit(solution)/shard_map/ppermute | solution.py:157
  21.1 1.9 %collective-permute-start.6 = (f32[32,256]{1,0:T(8,128)S(1)}, f32[32,256]{1,0:T(8,128)S(1)}, u32[]{:S(2)}, u32[]{:S(2)}) collective-permute-start(f32[32,256]{1,0:T(8,128)S(1)} %get-tuple-element.41), channel_id=1, source_target_pairs={{0,4},{4,0},{8,12},{12,8},{1,5},{5,1},{9,13},{13,9},{2,6},{6,2},{1... | collective-permute-start | bytes 98312 | tf_op jit(solution)/shard_map/ppermute | solution.py:157
  21.4 3.9 %collective-permute-start.7 = (f32[32,256]{1,0:T(8,128)S(1)}, f32[32,256]{1,0:T(8,128)S(1)}, u32[]{:S(2)}, u32[]{:S(2)}) collective-permute-start(f32[32,256]{1,0:T(8,128)S(1)} %get-tuple-element.42), channel_id=1, source_target_pairs={{0,8},{4,12},{8,0},{12,4},{1,9},{5,13},{9,1},{13,5},{2,10},{6,14},... | collective-permute-start | bytes 98312 | tf_op jit(solution)/shard_map/ppermute | solution.py:157
  22.6 3.7 %collective-permute-start.8 = (f32[32,256]{1,0:T(8,128)S(1)}, f32[32,256]{1,0:T(8,128)S(1)}, u32[]{:S(2)}, u32[]{:S(2)}) collective-permute-start(f32[32,256]{1,0:T(8,128)S(1)} %get-tuple-element.43), channel_id=1, source_target_pairs={{0,12},{4,8},{8,4},{12,0},{1,13},{5,9},{9,5},{13,1},{2,14},{6,10},... | collective-permute-start | bytes 98312 | tf_op jit(solution)/shard_map/ppermute | solution.py:157

commit v12 on v9

--- a/solution.py
+++ b/solution.py
@@ -13,6 +13,14 @@
 VMEM_LIMIT = 56 * 1024 * 1024
 KEPT_BYTES = 4 * 1024 * 1024
 SCHEDULE_COST = 10 ** 10
+EXP_SQUARINGS = 5
+EXP_TERMS = [
+    term / 2.0 ** (EXP_SQUARINGS * power)
+    for power, term in enumerate([
+        1.0000000387843881, 0.9999854684180126, 0.499772553042558,
+        0.16550051010162015, 0.03898878338548839, 0.005403287826230924,
+    ])
+]
 
 
 def normalize(logits):
@@ -91,6 +99,21 @@
     return normalize(-unary - pairwise), pairwise
 
 
+def exp_by_squaring(value):
+    result = jnp.full_like(value, EXP_TERMS[-1])
+    for term in EXP_TERMS[-2::-1]:
+        result = result * value + term
+    for _ in range(EXP_SQUARINGS):
+        result = result * result
+    return result
+
+
+def exp_tile(exponent):
+    count = exponent.shape[0] // 4
+    parts = [jnp.exp(exponent[count:]), exp_by_squaring(exponent[:count])]
+    return jnp.concatenate([parts[1], parts[0]], axis=0).astype(jnp.bfloat16)
+
+
 def first_part(labels, rows_ref, packed_ref, total, tile_ref=None, begin=0, end=None):
     blocks = range(begin, packed_ref.shape[0] if end is None else end)
     rows = rows_ref[...]
@@ -106,7 +129,7 @@
         exponent = ahead
         if index + 1 < blocks.stop:
             ahead = exponents(index + 1)
-        tile = jnp.exp(exponent).astype(jnp.bfloat16)
+        tile = exp_tile(exponent)
         if index == 0 and tile_ref is not None:
             tile_ref[...] = tile
         total = total + jnp.dot(

time: 25.1 us -> 25.5 us (1.016)
  Pallas kernels: 7.43 us -> 8.65 us
  waiting for transfers between devices: 7.3 us -> 6.18 us
    pallas_call x10, Pallas kernels: 7.43 us -> 8.65 us  [call(): pl.pallas_call(kernel, out_shape=tuple(out_shapes), cost_estimate=pl.Cost...]
    ppermute x9, waiting for transfers between devices: 7.3 us -> 6.18 us  [swap(): return lax.ppermute(value, axis, pairs)]
    ppermute x9, starting transfers between devices: 9.57 us -> 9.82 us  [swap(): return lax.ppermute(value, axis, pairs)]
  transfers between devices with their start and end apart: 9 -> 9, of which waited for: 7 -> 5; matrix products, arithmetic and copies ran while one was open for 0% -> 0% of each run, Pallas kernels for 15% -> 19%
where the time goes in v12:
time: 25.5 us; the launch traced here: 25.3 us
  starting transfers between devices  9.82 us (39%)
  Pallas kernels  8.65 us (34%)
  waiting for transfers between devices  6.18 us (24%)
  between operations  0.68 us (3%)
    ppermute x9, starting transfers between devices, swap(): return lax.ppermute(value, axis, pairs)  9.82 us
    pallas_call x10, Pallas kernels, call(): pl.pallas_call(kernel, out_shape=tuple(out_shapes), cost_estimate=pl.Cost...  8.65 us
    ppermute x9, waiting for transfers between devices, swap(): return lax.ppermute(value, axis, pairs)  6.18 us
  transfers between devices with their start and end apart: 9, of which 5 were waited for; matrix products, arithmetic and copies ran while one was open for 0% of the time, Pallas kernels for 19%

profile of v12, /device:TPU:0, one launch (start us, length us, event | category | flops | bytes accessed | tf_op | source)
XLA Modules:
  0.0 25.3 jit_solution(1942729034241467477)
XLA Ops:
  0.6 1.1 %shard_map.59 = (f32[40,256]{1,0:T(8,128)S(1)}, f32[32,32]{1,0:T(8,128)S(1)}) custom-call(bf16[6,4096]{1,0:T(8,128)(2,1)} %features_ref.1, s32[1,256]{1,0:T(1,128)} %bitcast.1, f32[32,256]{1,0:T(8,128)} %unary_ref.1, f32[32,32]{1,0:T(8,128)} %compat_ref.1), custom_call_target="tpu_custom_call" | custom-call | flops 10000000000 | bytes 10000000000 | tf_op jit(solution)/shard_map/pallas_call | solution.py:233
  1.7 4.1 %collective-permute-start.2 = (f32[40,256]{1,0:T(8,128)S(1)}, f32[40,256]{1,0:T(8,128)S(1)}, u32[]{:S(2)}, u32[]{:S(2)}) collective-permute-start(f32[40,256]{1,0:T(8,128)S(1)} %get-tuple-element.23.refs_0_.refs_5_.near_ref), channel_id=1, source_target_pairs={{0,2},{1,3},{2,0},{3,1},{4,6},{5,7},{6,4},{7,5},{8,10},{9,11},{10,... | collective-permute-start | bytes 122888 | tf_op jit(solution)/shard_map/ppermute | solution.py:194
  5.8 1.3 %collective-permute-start.1 = (f32[40,256]{1,0:T(8,128)S(1)}, f32[40,256]{1,0:T(8,128)S(1)}, u32[]{:S(2)}, u32[]{:S(2)}) collective-permute-start(f32[40,256]{1,0:T(8,128)S(1)} %get-tuple-element.23.refs_0_.refs_5_.near_ref), channel_id=1, source_target_pairs={{0,3},{1,2},{2,1},{3,0},{4,7},{5,6},{6,5},{7,4},{8,11},{9,10},{10,... | collective-permute-start | bytes 122888 | tf_op jit(solution)/shard_map/ppermute | solution.py:194
  7.1 0.2 collective-permute-start
  7.4 0.8 %collective-permute-done.2.refs_3_.refs_8_ = f32[40,256]{1,0:T(8,128)S(1)} collective-permute-done((f32[40,256]{1,0:T(8,128)S(1)}, f32[40,256]{1,0:T(8,128)S(1)}, u32[]{:S(2)}, u32[]{:S(2)}) %collective-permute-start.2) | collective-permute-done | bytes 40992 | tf_op jit(solution)/shard_map/ppermute | solution.py:194
  8.2 3.4 %collective-permute-done.1.refs_2_.refs_7_ = f32[40,256]{1,0:T(8,128)S(1)} collective-permute-done((f32[40,256]{1,0:T(8,128)S(1)}, f32[40,256]{1,0:T(8,128)S(1)}, u32[]{:S(2)}, u32[]{:S(2)}) %collective-permute-start.1) | collective-permute-done | bytes 40992 | tf_op jit(solution)/shard_map/ppermute | solution.py:194
  11.6 0.1 shard_map.60
  11.7 1.6 %collective-permute-start.3 = (bf16[4,40,256]{2,1,0:T(8,128)(2,1)S(1)}, bf16[4,40,256]{2,1,0:T(8,128)(2,1)S(1)}, u32[]{:S(2)}, u32[]{:S(2)}) collective-permute-start(bf16[4,40,256]{2,1,0:T(8,128)(2,1)S(1)} %get-tuple-element.27.packed_ref.refs_3_), channel_id=1, source_target_pairs={{0,8},{4,12},{8,0},{12,4},{1,9},{5,13},{9,1},{13,5},{2,10},{6,14},... | collective-permute-start | bytes 245768 | tf_op jit(solution)/shard_map/ppermute | solution.py:194
  13.3 0.5 %shard_map.61 = (f32[32,1024]{1,0:T(8,128)S(1)}, bf16[256,1024]{1,0:T(8,128)(2,1)S(1)}) custom-call(bf16[16,1024]{1,0:T(8,128)(2,1)S(1)} %get-tuple-element.24.rows_ref.refs_0_, bf16[4,40,256]{2,1,0:T(8,128)(2,1)S(1)} %get-tuple-element.27.packed_ref.refs_3_), custom_call_target="tpu_custom_call" | custom-call | flops 10000000000 | bytes 10000000000 | tf_op jit(solution)/shard_map/pallas_call | solution.py:233
  13.8 0.0 collective-permute-start.4
  13.8 1.1 %shard_map.62.sum_ref = f32[32,1024]{1,0:T(8,128)S(1)} custom-call(bf16[16,1024]{1,0:T(8,128)(2,1)S(1)} %get-tuple-element.24.rows_ref.refs_0_, bf16[4,40,256]{2,1,0:T(8,128)(2,1)S(1)} %get-tuple-element.27.packed_ref.refs_3_, f32[32,1024]{1,0:T(8,128)S(1)} %get-tuple-element.26.sum_ref), custom_call_target="tpu_custom_call" | custom-call | flops 10000000000 | bytes 10000000000 | tf_op jit(solution)/shard_map/pallas_call | solution.py:233
  14.9 0.2 collective-permute-done.4.packed_ref
  15.1 1.4 %shard_map.63 = (f32[32,1024]{1,0:T(8,128)S(1)}, bf16[256,1024]{1,0:T(8,128)(2,1)S(1)}) custom-call(bf16[16,1024]{1,0:T(8,128)(2,1)S(1)} %get-tuple-element.24.rows_ref.refs_0_, bf16[4,40,256]{2,1,0:T(8,128)(2,1)S(1)} %collective-permute-done.4.packed_ref, f32[32,1024]{1,0:T(8,128)S(1)} %shard_map.62.sum_ref), custom_call_target="tpu_custom_call" | custom-call | flops 10000000000 | bytes 10000000000 | tf_op jit(solution)/shard_map/pallas_call | solution.py:233
  16.5 0.4 %collective-permute-start.5 = (bf16[4,40,256]{2,1,0:T(8,128)(2,1)S(1)}, bf16[4,40,256]{2,1,0:T(8,128)(2,1)S(1)}, u32[]{:S(2)}, u32[]{:S(2)}) collective-permute-start(bf16[4,40,256]{2,1,0:T(8,128)(2,1)S(1)} %collective-permute-done.3.packed_ref), channel_id=1, source_target_pairs={{0,4},{4,0},{8,12},{12,8},{1,5},{5,1},{9,13},{13,9},{2,6},{6,2},{1... | collective-permute-start | bytes 245768 | tf_op jit(solution)/shard_map/ppermute | solution.py:194
  16.8 1.4 %shard_map.64 = (f32[32,1024]{1,0:T(8,128)S(1)}, bf16[256,1024]{1,0:T(8,128)(2,1)S(1)}) custom-call(bf16[16,1024]{1,0:T(8,128)(2,1)S(1)} %get-tuple-element.24.rows_ref.refs_0_, bf16[4,40,256]{2,1,0:T(8,128)(2,1)S(1)} %collective-permute-done.3.packed_ref, f32[32,1024]{1,0:T(8,128)S(1)} %get-tuple-element.28.sum_ref), custom_call_target="tpu_custom_call" | custom-call | flops 10000000000 | bytes 10000000000 | tf_op jit(solution)/shard_map/pallas_call | solution.py:233
  18.2 1.6 %shard_map.65 = (bf16[32,1024]{1,0:T(8,128)(2,1)S(1)}, bf16[256,1024]{1,0:T(8,128)(2,1)S(1)}) custom-call(bf16[16,1024]{1,0:T(8,128)(2,1)S(1)} %get-tuple-element.24.rows_ref.refs_0_, bf16[4,40,256]{2,1,0:T(8,128)(2,1)S(1)} %collective-permute-done.5.refs_1_, f32[32,1024]{1,0:T(8,128)S(1)} %get-tuple-element.30.refs_2_, ...), custom_call_target="tpu_custom_call" | custom-call | flops 10000000000 | bytes 10000000000 | tf_op jit(solution)/shard_map/pallas_call | solution.py:233
  19.8 0.4 %shard_map.66 = (f32[32,256]{1,0:T(8,128)S(1)}, f32[32,256]{1,0:T(8,128)S(1)}) custom-call(bf16[32,1024]{1,0:T(8,128)(2,1)S(1)} %get-tuple-element.37.q_ref, bf16[256,1024]{1,0:T(8,128)(2,1)S(1)} %get-tuple-element.33.refs_0_, bf16[256,1024]{1,0:T(8,128)(2,1)S(1)} %get-tuple-element.34.refs_1_), custom_call_target="tpu_custom_call" | custom-call | flops 10000000000 | bytes 10000000000 | tf_op jit(solution)/shard_map/pallas_call | solution.py:233
  20.2 0.9 %collective-permute-start.7 = (f32[32,256]{1,0:T(8,128)S(1)}, f32[32,256]{1,0:T(8,128)S(1)}, u32[]{:S(2)}, u32[]{:S(2)}) collective-permute-start(f32[32,256]{1,0:T(8,128)S(1)} %get-tuple-element.42), channel_id=1, source_target_pairs={{0,8},{4,12},{8,0},{12,4},{1,9},{5,13},{9,1},{13,5},{2,10},{6,14},... | collective-permute-start | bytes 98312 | tf_op jit(solution)/shard_map/ppermute | solution.py:194
  21.1 0.7 %collective-permute-start.8 = (f32[32,256]{1,0:T(8,128)S(1)}, f32[32,256]{1,0:T(8,128)S(1)}, u32[]{:S(2)}, u32[]{:S(2)}) collective-permute-start(f32[32,256]{1,0:T(8,128)S(1)} %get-tuple-element.43), channel_id=1, source_target_pairs={{0,12},{4,8},{8,4},{12,0},{1,13},{5,9},{9,5},{13,1},{2,14},{6,10},... | collective-permute-start | bytes 98312 | tf_op jit(solution)/shard_map/ppermute | solution.py:194
  21.8 0.4 %shard_map.67 = (f32[32,256]{1,0:T(8,128)S(1)}, f32[32,256]{1,0:T(8,128)S(1)}) custom-call(bf16[32,1024]{1,0:T(8,128)(2,1)S(1)} %get-tuple-element.37.q_ref, bf16[256,1024]{1,0:T(8,128)(2,1)S(1)} %get-tuple-element.38.refs_0_, bf16[256,1024]{1,0:T(8,128)(2,1)S(1)} %get-tuple-element.39.refs_1_), custom_call_target="tpu_custom_call" | custom-call | flops 10000000000 | bytes 10000000000 | tf_op jit(solution)/shard_map/pallas_call | solution.py:233
  22.2 0.6 %collective-permute-start.6 = (f32[32,256]{1,0:T(8,128)S(1)}, f32[32,256]{1,0:T(8,128)S(1)}, u32[]{:S(2)}, u32[]{:S(2)}) collective-permute-start(f32[32,256]{1,0:T(8,128)S(1)} %get-tuple-element.41), channel_id=1, source_target_pairs={{0,4},{4,0},{8,12},{12,8},{1,5},{5,1},{9,13},{13,9},{2,6},{6,2},{1... | collective-permute-start | bytes 98312 | tf_op jit(solution)/shard_map/ppermute | solution.py:194
  22.8 1.4 %collective-permute-done.7.refs_2_ = f32[32,256]{1,0:T(8,128)S(1)} collective-permute-done((f32[32,256]{1,0:T(8,128)S(1)}, f32[32,256]{1,0:T(8,128)S(1)}, u32[]{:S(2)}, u32[]{:S(2)}) %collective-permute-start.7) | collective-permute-done | bytes 32800 | tf_op jit(solution)/shard_map/ppermute | solution.py:194
  24.2 0.3 %collective-permute-done.8.refs_3_ = f32[32,256]{1,0:T(8,128)S(1)} collective-permute-done((f32[32,256]{1,0:T(8,128)S(1)}, f32[32,256]{1,0:T(8,128)S(1)}, u32[]{:S(2)}, u32[]{:S(2)}) %collective-permute-start.8) | collective-permute-done | bytes 32800 | tf_op jit(solution)/shard_map/ppermute | solution.py:194
  24.5 0.8 %shard_map.68 = (f32[32,256]{1,0:T(8,128)}, f32[32,256]{1,0:T(8,128)}) custom-call(bf16[32,1024]{1,0:T(8,128)(2,1)S(1)} %get-tuple-element.37.q_ref, f32[40,256]{1,0:T(8,128)S(1)} %get-tuple-element.23.refs_0_.refs_5_.near_ref, f32[32,32]{1,0:T(8,128)S(1)} %get-tuple-element.31.refs_4_.compat_ref, f32[32,256]{1,0:T(8,128)S(1)} %get-tuple-element.40.refs_0_, ...), custom_call_target="tpu_custom_call" | custom-call | flops 10000000000 | bytes 10000000000 | tf_op jit(solution)/shard_map/pallas_call | solution.py:233
  (4 shorter events, 0.0 us)
Async XLA Ops:
  1.7 6.5 %collective-permute-start.2 = (f32[40,256]{1,0:T(8,128)S(1)}, f32[40,256]{1,0:T(8,128)S(1)}, u32[]{:S(2)}, u32[]{:S(2)}) collective-permute-start(f32[40,256]{1,0:T(8,128)S(1)} %get-tuple-element.23.refs_0_.refs_5_.near_ref), channel_id=1, source_target_pairs={{0,2},{1,3},{2,0},{3,1},{4,6},{5,7},{6,4},{7,5},{8,10},{9,11},{10,... | collective-permute-start | bytes 122888 | tf_op jit(solution)/shard_map/ppermute | solution.py:194
  5.8 5.8 %collective-permute-start.1 = (f32[40,256]{1,0:T(8,128)S(1)}, f32[40,256]{1,0:T(8,128)S(1)}, u32[]{:S(2)}, u32[]{:S(2)}) collective-permute-start(f32[40,256]{1,0:T(8,128)S(1)} %get-tuple-element.23.refs_0_.refs_5_.near_ref), channel_id=1, source_target_pairs={{0,3},{1,2},{2,1},{3,0},{4,7},{5,6},{6,5},{7,4},{8,11},{9,10},{10,... | collective-permute-start | bytes 122888 | tf_op jit(solution)/shard_map/ppermute | solution.py:194
  7.1 4.5 %collective-permute-start = (f32[40,256]{1,0:T(8,128)S(1)}, f32[40,256]{1,0:T(8,128)S(1)}, u32[]{:S(2)}, u32[]{:S(2)}) collective-permute-start(f32[40,256]{1,0:T(8,128)S(1)} %get-tuple-element.23.refs_0_.refs_5_.near_ref), channel_id=1, source_target_pairs={{0,1},{1,0},{2,3},{3,2},{4,5},{5,4},{6,7},{7,6},{8,9},{9,8},{10,11... | collective-permute-start | bytes 122888 | tf_op jit(solution)/shard_map/ppermute | solution.py:194
  11.7 4.8 %collective-permute-start.3 = (bf16[4,40,256]{2,1,0:T(8,128)(2,1)S(1)}, bf16[4,40,256]{2,1,0:T(8,128)(2,1)S(1)}, u32[]{:S(2)}, u32[]{:S(2)}) collective-permute-start(bf16[4,40,256]{2,1,0:T(8,128)(2,1)S(1)} %get-tuple-element.27.packed_ref.refs_3_), channel_id=1, source_target_pairs={{0,8},{4,12},{8,0},{12,4},{1,9},{5,13},{9,1},{13,5},{2,10},{6,14},... | collective-permute-start | bytes 245768 | tf_op jit(solution)/shard_map/ppermute | solution.py:194
  13.8 1.3 %collective-permute-start.4 = (bf16[4,40,256]{2,1,0:T(8,128)(2,1)S(1)}, bf16[4,40,256]{2,1,0:T(8,128)(2,1)S(1)}, u32[]{:S(2)}, u32[]{:S(2)}) collective-permute-start(bf16[4,40,256]{2,1,0:T(8,128)(2,1)S(1)} %get-tuple-element.27.packed_ref.refs_3_), channel_id=1, source_target_pairs={{0,4},{4,0},{8,12},{12,8},{1,5},{5,1},{9,13},{13,9},{2,6},{6,2},{1... | collective-permute-start | bytes 245768 | tf_op jit(solution)/shard_map/ppermute | solution.py:194
  16.5 1.7 %collective-permute-start.5 = (bf16[4,40,256]{2,1,0:T(8,128)(2,1)S(1)}, bf16[4,40,256]{2,1,0:T(8,128)(2,1)S(1)}, u32[]{:S(2)}, u32[]{:S(2)}) collective-permute-start(bf16[4,40,256]{2,1,0:T(8,128)(2,1)S(1)} %collective-permute-done.3.packed_ref), channel_id=1, source_target_pairs={{0,4},{4,0},{8,12},{12,8},{1,5},{5,1},{9,13},{13,9},{2,6},{6,2},{1... | collective-permute-start | bytes 245768 | tf_op jit(solution)/shard_map/ppermute | solution.py:194
  20.2 4.0 %collective-permute-start.7 = (f32[32,256]{1,0:T(8,128)S(1)}, f32[32,256]{1,0:T(8,128)S(1)}, u32[]{:S(2)}, u32[]{:S(2)}) collective-permute-start(f32[32,256]{1,0:T(8,128)S(1)} %get-tuple-element.42), channel_id=1, source_target_pairs={{0,8},{4,12},{8,0},{12,4},{1,9},{5,13},{9,1},{13,5},{2,10},{6,14},... | collective-permute-start | bytes 98312 | tf_op jit(solution)/shard_map/ppermute | solution.py:194
  21.1 3.4 %collective-permute-start.8 = (f32[32,256]{1,0:T(8,128)S(1)}, f32[32,256]{1,0:T(8,128)S(1)}, u32[]{:S(2)}, u32[]{:S(2)}) collective-permute-start(f32[32,256]{1,0:T(8,128)S(1)} %get-tuple-element.43), channel_id=1, source_target_pairs={{0,12},{4,8},{8,4},{12,0},{1,13},{5,9},{9,5},{13,1},{2,14},{6,10},... | collective-permute-start | bytes 98312 | tf_op jit(solution)/shard_map/ppermute | solution.py:194
  22.2 2.3 %collective-permute-start.6 = (f32[32,256]{1,0:T(8,128)S(1)}, f32[32,256]{1,0:T(8,128)S(1)}, u32[]{:S(2)}, u32[]{:S(2)}) collective-permute-start(f32[32,256]{1,0:T(8,128)S(1)} %get-tuple-element.41), channel_id=1, source_target_pairs={{0,4},{4,0},{8,12},{12,8},{1,5},{5,1},{9,13},{13,9},{2,6},{6,2},{1... | collective-permute-start | bytes 98312 | tf_op jit(solution)/shard_map/ppermute | solution.py:194

commit v13 on v9

--- a/solution.py
+++ b/solution.py
@@ -8,7 +8,8 @@
 from jax.experimental.pallas import tpu as pltpu
 from jax.sharding import PartitionSpec as P
 
-AUX = 16
+AUX = 32
+LOG2E = math.log2(math.e)
 LANES = 128
 VMEM_LIMIT = 56 * 1024 * 1024
 KEPT_BYTES = 4 * 1024 * 1024
@@ -50,17 +51,13 @@
     held_ref[...] = compat_ref[...]
 
 
-def half_norms(feats):
-    return three_parts(-0.5 * jnp.sum(feats * feats, axis=0, keepdims=True))
-
-
 def product_sides(feats):
     own = feats.shape[1]
-    norms = half_norms(feats)
+    norms = three_parts(-0.5 * LOG2E * jnp.sum(feats * feats, axis=0, keepdims=True))
     ones = jnp.ones((3, own), jnp.float32)
-    spare = jnp.zeros((AUX - 8 - 6, own), jnp.float32)
-    columns = jnp.concatenate([feats] + norms + [ones, spare], axis=0)
-    rows = jnp.concatenate([feats, ones] + norms + [spare], axis=0)
+    spare = jnp.zeros((AUX - 3 * 8 - 6, own), jnp.float32)
+    columns = jnp.concatenate([feats] * 3 + norms + [ones, spare], axis=0)
+    rows = jnp.concatenate(three_parts(LOG2E * feats) + [ones] + norms + [spare], axis=0)
     return columns.astype(jnp.bfloat16), rows.astype(jnp.bfloat16)
 
 
@@ -106,7 +103,7 @@
         exponent = ahead
         if index + 1 < blocks.stop:
             ahead = exponents(index + 1)
-        tile = jnp.exp(exponent).astype(jnp.bfloat16)
+        tile = jnp.exp2(exponent).astype(jnp.bfloat16)
         if index == 0 and tile_ref is not None:
             tile_ref[...] = tile
         total = total + jnp.dot(

time: 25.1 us -> 25.1 us (level)
  no operation moved by 1% of the time
where the time goes in v13:
time: 25.1 us; the launch traced here: 25 us
  starting transfers between devices  9.57 us (38%)
  Pallas kernels  7.43 us (30%)
  waiting for transfers between devices  7.31 us (29%)
  between operations  0.67 us (3%)
    ppermute x9, starting transfers between devices, swap(): return lax.ppermute(value, axis, pairs)  9.57 us
    pallas_call x10, Pallas kernels, call(): pl.pallas_call(kernel, out_shape=tuple(out_shapes), cost_estimate=pl.Cost...  7.43 us
    ppermute x9, waiting for transfers between devices, swap(): return lax.ppermute(value, axis, pairs)  7.31 us
  transfers between devices with their start and end apart: 9, of which 7 were waited for; matrix products, arithmetic and copies ran while one was open for 0% of the time, Pallas kernels for 15%

profile of v13, /device:TPU:0, one launch (start us, length us, event | category | flops | bytes accessed | tf_op | source)
XLA Modules:
  0.0 25.0 jit_solution(15222247745466200997)
XLA Ops:
  0.6 1.1 %shard_map.59 = (f32[40,256]{1,0:T(8,128)S(1)}, f32[32,32]{1,0:T(8,128)S(1)}) custom-call(bf16[6,4096]{1,0:T(8,128)(2,1)} %features_ref.1, s32[1,256]{1,0:T(1,128)} %bitcast.1, f32[32,256]{1,0:T(8,128)} %unary_ref.1, f32[32,32]{1,0:T(8,128)} %compat_ref.1), custom_call_target="tpu_custom_call" | custom-call | flops 10000000000 | bytes 10000000000 | tf_op jit(solution)/shard_map/pallas_call | solution.py:207
  1.7 4.1 %collective-permute-start.2 = (f32[40,256]{1,0:T(8,128)S(1)}, f32[40,256]{1,0:T(8,128)S(1)}, u32[]{:S(2)}, u32[]{:S(2)}) collective-permute-start(f32[40,256]{1,0:T(8,128)S(1)} %get-tuple-element.23.refs_0_.refs_5_.near_ref), channel_id=1, source_target_pairs={{0,2},{1,3},{2,0},{3,1},{4,6},{5,7},{6,4},{7,5},{8,10},{9,11},{10,... | collective-permute-start | bytes 122888 | tf_op jit(solution)/shard_map/ppermute | solution.py:168
  5.8 1.3 %collective-permute-start.1 = (f32[40,256]{1,0:T(8,128)S(1)}, f32[40,256]{1,0:T(8,128)S(1)}, u32[]{:S(2)}, u32[]{:S(2)}) collective-permute-start(f32[40,256]{1,0:T(8,128)S(1)} %get-tuple-element.23.refs_0_.refs_5_.near_ref), channel_id=1, source_target_pairs={{0,3},{1,2},{2,1},{3,0},{4,7},{5,6},{6,5},{7,4},{8,11},{9,10},{10,... | collective-permute-start | bytes 122888 | tf_op jit(solution)/shard_map/ppermute | solution.py:168
  7.1 0.2 collective-permute-start
  7.4 0.8 %collective-permute-done.2.refs_3_.refs_8_ = f32[40,256]{1,0:T(8,128)S(1)} collective-permute-done((f32[40,256]{1,0:T(8,128)S(1)}, f32[40,256]{1,0:T(8,128)S(1)}, u32[]{:S(2)}, u32[]{:S(2)}) %collective-permute-start.2) | collective-permute-done | bytes 40992 | tf_op jit(solution)/shard_map/ppermute | solution.py:168
  8.2 3.4 %collective-permute-done.1.refs_2_.refs_7_ = f32[40,256]{1,0:T(8,128)S(1)} collective-permute-done((f32[40,256]{1,0:T(8,128)S(1)}, f32[40,256]{1,0:T(8,128)S(1)}, u32[]{:S(2)}, u32[]{:S(2)}) %collective-permute-start.1) | collective-permute-done | bytes 40992 | tf_op jit(solution)/shard_map/ppermute | solution.py:168
  11.7 1.6 %collective-permute-start.3 = (bf16[4,40,256]{2,1,0:T(8,128)(2,1)S(1)}, bf16[4,40,256]{2,1,0:T(8,128)(2,1)S(1)}, u32[]{:S(2)}, u32[]{:S(2)}) collective-permute-start(bf16[4,40,256]{2,1,0:T(8,128)(2,1)S(1)} %get-tuple-element.27.packed_ref.refs_3_), channel_id=1, source_target_pairs={{0,8},{4,12},{8,0},{12,4},{1,9},{5,13},{9,1},{13,5},{2,10},{6,14},... | collective-permute-start | bytes 245768 | tf_op jit(solution)/shard_map/ppermute | solution.py:168
  13.3 0.5 %shard_map.61 = (f32[32,1024]{1,0:T(8,128)S(1)}, bf16[256,1024]{1,0:T(8,128)(2,1)S(1)}) custom-call(bf16[32,1024]{1,0:T(8,128)(2,1)S(1)} %get-tuple-element.24.rows_ref.refs_0_, bf16[4,40,256]{2,1,0:T(8,128)(2,1)S(1)} %get-tuple-element.27.packed_ref.refs_3_), custom_call_target="tpu_custom_call" | custom-call | flops 10000000000 | bytes 10000000000 | tf_op jit(solution)/shard_map/pallas_call | solution.py:207
  13.7 0.8 %shard_map.62.sum_ref = f32[32,1024]{1,0:T(8,128)S(1)} custom-call(bf16[32,1024]{1,0:T(8,128)(2,1)S(1)} %get-tuple-element.24.rows_ref.refs_0_, bf16[4,40,256]{2,1,0:T(8,128)(2,1)S(1)} %get-tuple-element.27.packed_ref.refs_3_, f32[32,1024]{1,0:T(8,128)S(1)} %get-tuple-element.26.sum_ref), custom_call_target="tpu_custom_call" | custom-call | flops 10000000000 | bytes 10000000000 | tf_op jit(solution)/shard_map/pallas_call | solution.py:207
  14.6 0.4 %collective-permute-done.4.packed_ref = bf16[4,40,256]{2,1,0:T(8,128)(2,1)S(1)} collective-permute-done((bf16[4,40,256]{2,1,0:T(8,128)(2,1)S(1)}, bf16[4,40,256]{2,1,0:T(8,128)(2,1)S(1)}, u32[]{:S(2)}, u32[]{:S(2)}) %collective-permute-start.4) | collective-permute-done | bytes 81952 | tf_op jit(solution)/shard_map/ppermute | solution.py:168
  15.0 1.1 %shard_map.63 = (f32[32,1024]{1,0:T(8,128)S(1)}, bf16[256,1024]{1,0:T(8,128)(2,1)S(1)}) custom-call(bf16[32,1024]{1,0:T(8,128)(2,1)S(1)} %get-tuple-element.24.rows_ref.refs_0_, bf16[4,40,256]{2,1,0:T(8,128)(2,1)S(1)} %collective-permute-done.4.packed_ref, f32[32,1024]{1,0:T(8,128)S(1)} %shard_map.62.sum_ref), custom_call_target="tpu_custom_call" | custom-call | flops 10000000000 | bytes 10000000000 | tf_op jit(solution)/shard_map/pallas_call | solution.py:207
  16.1 0.1 collective-permute-done.3.packed_ref
  16.2 0.1 collective-permute-start.5
  16.3 1.1 %shard_map.64 = (f32[32,1024]{1,0:T(8,128)S(1)}, bf16[256,1024]{1,0:T(8,128)(2,1)S(1)}) custom-call(bf16[32,1024]{1,0:T(8,128)(2,1)S(1)} %get-tuple-element.24.rows_ref.refs_0_, bf16[4,40,256]{2,1,0:T(8,128)(2,1)S(1)} %collective-permute-done.3.packed_ref, f32[32,1024]{1,0:T(8,128)S(1)} %get-tuple-element.28.sum_ref), custom_call_target="tpu_custom_call" | custom-call | flops 10000000000 | bytes 10000000000 | tf_op jit(solution)/shard_map/pallas_call | solution.py:207
  17.4 0.1 collective-permute-done.5.refs_1_
  17.5 1.3 %shard_map.65 = (bf16[32,1024]{1,0:T(8,128)(2,1)S(1)}, bf16[256,1024]{1,0:T(8,128)(2,1)S(1)}) custom-call(bf16[32,1024]{1,0:T(8,128)(2,1)S(1)} %get-tuple-element.24.rows_ref.refs_0_, bf16[4,40,256]{2,1,0:T(8,128)(2,1)S(1)} %collective-permute-done.5.refs_1_, f32[32,1024]{1,0:T(8,128)S(1)} %get-tuple-element.30.refs_2_, ...), custom_call_target="tpu_custom_call" | custom-call | flops 10000000000 | bytes 10000000000 | tf_op jit(solution)/shard_map/pallas_call | solution.py:207
  18.7 0.4 %shard_map.66 = (f32[32,256]{1,0:T(8,128)S(1)}, f32[32,256]{1,0:T(8,128)S(1)}) custom-call(bf16[32,1024]{1,0:T(8,128)(2,1)S(1)} %get-tuple-element.37.q_ref, bf16[256,1024]{1,0:T(8,128)(2,1)S(1)} %get-tuple-element.33.refs_0_, bf16[256,1024]{1,0:T(8,128)(2,1)S(1)} %get-tuple-element.34.refs_1_), custom_call_target="tpu_custom_call" | custom-call | flops 10000000000 | bytes 10000000000 | tf_op jit(solution)/shard_map/pallas_call | solution.py:207
  19.1 1.5 %collective-permute-start.7 = (f32[32,256]{1,0:T(8,128)S(1)}, f32[32,256]{1,0:T(8,128)S(1)}, u32[]{:S(2)}, u32[]{:S(2)}) collective-permute-start(f32[32,256]{1,0:T(8,128)S(1)} %get-tuple-element.42), channel_id=1, source_target_pairs={{0,8},{4,12},{8,0},{12,4},{1,9},{5,13},{9,1},{13,5},{2,10},{6,14},... | collective-permute-start | bytes 98312 | tf_op jit(solution)/shard_map/ppermute | solution.py:168
  20.7 0.1 collective-permute-start.8
  20.8 0.4 %shard_map.67 = (f32[32,256]{1,0:T(8,128)S(1)}, f32[32,256]{1,0:T(8,128)S(1)}) custom-call(bf16[32,1024]{1,0:T(8,128)(2,1)S(1)} %get-tuple-element.37.q_ref, bf16[256,1024]{1,0:T(8,128)(2,1)S(1)} %get-tuple-element.38.refs_0_, bf16[256,1024]{1,0:T(8,128)(2,1)S(1)} %get-tuple-element.39.refs_1_), custom_call_target="tpu_custom_call" | custom-call | flops 10000000000 | bytes 10000000000 | tf_op jit(solution)/shard_map/pallas_call | solution.py:207
  21.2 0.5 %collective-permute-start.6 = (f32[32,256]{1,0:T(8,128)S(1)}, f32[32,256]{1,0:T(8,128)S(1)}, u32[]{:S(2)}, u32[]{:S(2)}) collective-permute-start(f32[32,256]{1,0:T(8,128)S(1)} %get-tuple-element.41), channel_id=1, source_target_pairs={{0,4},{4,0},{8,12},{12,8},{1,5},{5,1},{9,13},{13,9},{2,6},{6,2},{1... | collective-permute-start | bytes 98312 | tf_op jit(solution)/shard_map/ppermute | solution.py:168
  21.7 1.4 %collective-permute-done.7.refs_2_ = f32[32,256]{1,0:T(8,128)S(1)} collective-permute-done((f32[32,256]{1,0:T(8,128)S(1)}, f32[32,256]{1,0:T(8,128)S(1)}, u32[]{:S(2)}, u32[]{:S(2)}) %collective-permute-start.7) | collective-permute-done | bytes 32800 | tf_op jit(solution)/shard_map/ppermute | solution.py:168
  23.1 1.1 %collective-permute-done.8.refs_3_ = f32[32,256]{1,0:T(8,128)S(1)} collective-permute-done((f32[32,256]{1,0:T(8,128)S(1)}, f32[32,256]{1,0:T(8,128)S(1)}, u32[]{:S(2)}, u32[]{:S(2)}) %collective-permute-start.8) | collective-permute-done | bytes 32800 | tf_op jit(solution)/shard_map/ppermute | solution.py:168
  24.2 0.8 %shard_map.68 = (f32[32,256]{1,0:T(8,128)}, f32[32,256]{1,0:T(8,128)}) custom-call(bf16[32,1024]{1,0:T(8,128)(2,1)S(1)} %get-tuple-element.37.q_ref, f32[40,256]{1,0:T(8,128)S(1)} %get-tuple-element.23.refs_0_.refs_5_.near_ref, f32[32,32]{1,0:T(8,128)S(1)} %get-tuple-element.31.refs_4_.compat_ref, f32[32,256]{1,0:T(8,128)S(1)} %get-tuple-element.40.refs_0_, ...), custom_call_target="tpu_custom_call" | custom-call | flops 10000000000 | bytes 10000000000 | tf_op jit(solution)/shard_map/pallas_call | solution.py:207
  (4 shorter events, 0.1 us)
Async XLA Ops:
  1.7 6.5 %collective-permute-start.2 = (f32[40,256]{1,0:T(8,128)S(1)}, f32[40,256]{1,0:T(8,128)S(1)}, u32[]{:S(2)}, u32[]{:S(2)}) collective-permute-start(f32[40,256]{1,0:T(8,128)S(1)} %get-tuple-element.23.refs_0_.refs_5_.near_ref), channel_id=1, source_target_pairs={{0,2},{1,3},{2,0},{3,1},{4,6},{5,7},{6,4},{7,5},{8,10},{9,11},{10,... | collective-permute-start | bytes 122888 | tf_op jit(solution)/shard_map/ppermute | solution.py:168
  5.8 5.8 %collective-permute-start.1 = (f32[40,256]{1,0:T(8,128)S(1)}, f32[40,256]{1,0:T(8,128)S(1)}, u32[]{:S(2)}, u32[]{:S(2)}) collective-permute-start(f32[40,256]{1,0:T(8,128)S(1)} %get-tuple-element.23.refs_0_.refs_5_.near_ref), channel_id=1, source_target_pairs={{0,3},{1,2},{2,1},{3,0},{4,7},{5,6},{6,5},{7,4},{8,11},{9,10},{10,... | collective-permute-start | bytes 122888 | tf_op jit(solution)/shard_map/ppermute | solution.py:168
  7.1 4.5 %collective-permute-start = (f32[40,256]{1,0:T(8,128)S(1)}, f32[40,256]{1,0:T(8,128)S(1)}, u32[]{:S(2)}, u32[]{:S(2)}) collective-permute-start(f32[40,256]{1,0:T(8,128)S(1)} %get-tuple-element.23.refs_0_.refs_5_.near_ref), channel_id=1, source_target_pairs={{0,1},{1,0},{2,3},{3,2},{4,5},{5,4},{6,7},{7,6},{8,9},{9,8},{10,11... | collective-permute-start | bytes 122888 | tf_op jit(solution)/shard_map/ppermute | solution.py:168
  11.7 4.5 %collective-permute-start.3 = (bf16[4,40,256]{2,1,0:T(8,128)(2,1)S(1)}, bf16[4,40,256]{2,1,0:T(8,128)(2,1)S(1)}, u32[]{:S(2)}, u32[]{:S(2)}) collective-permute-start(bf16[4,40,256]{2,1,0:T(8,128)(2,1)S(1)} %get-tuple-element.27.packed_ref.refs_3_), channel_id=1, source_target_pairs={{0,8},{4,12},{8,0},{12,4},{1,9},{5,13},{9,1},{13,5},{2,10},{6,14},... | collective-permute-start | bytes 245768 | tf_op jit(solution)/shard_map/ppermute | solution.py:168
  13.7 1.3 %collective-permute-start.4 = (bf16[4,40,256]{2,1,0:T(8,128)(2,1)S(1)}, bf16[4,40,256]{2,1,0:T(8,128)(2,1)S(1)}, u32[]{:S(2)}, u32[]{:S(2)}) collective-permute-start(bf16[4,40,256]{2,1,0:T(8,128)(2,1)S(1)} %get-tuple-element.27.packed_ref.refs_3_), channel_id=1, source_target_pairs={{0,4},{4,0},{8,12},{12,8},{1,5},{5,1},{9,13},{13,9},{2,6},{6,2},{1... | collective-permute-start | bytes 245768 | tf_op jit(solution)/shard_map/ppermute | solution.py:168
  16.2 1.3 %collective-permute-start.5 = (bf16[4,40,256]{2,1,0:T(8,128)(2,1)S(1)}, bf16[4,40,256]{2,1,0:T(8,128)(2,1)S(1)}, u32[]{:S(2)}, u32[]{:S(2)}) collective-permute-start(bf16[4,40,256]{2,1,0:T(8,128)(2,1)S(1)} %collective-permute-done.3.packed_ref), channel_id=1, source_target_pairs={{0,4},{4,0},{8,12},{12,8},{1,5},{5,1},{9,13},{13,9},{2,6},{6,2},{1... | collective-permute-start | bytes 245768 | tf_op jit(solution)/shard_map/ppermute | solution.py:168
  19.1 3.9 %collective-permute-start.7 = (f32[32,256]{1,0:T(8,128)S(1)}, f32[32,256]{1,0:T(8,128)S(1)}, u32[]{:S(2)}, u32[]{:S(2)}) collective-permute-start(f32[32,256]{1,0:T(8,128)S(1)} %get-tuple-element.42), channel_id=1, source_target_pairs={{0,8},{4,12},{8,0},{12,4},{1,9},{5,13},{9,1},{13,5},{2,10},{6,14},... | collective-permute-start | bytes 98312 | tf_op jit(solution)/shard_map/ppermute | solution.py:168
  20.7 3.5 %collective-permute-start.8 = (f32[32,256]{1,0:T(8,128)S(1)}, f32[32,256]{1,0:T(8,128)S(1)}, u32[]{:S(2)}, u32[]{:S(2)}) collective-permute-start(f32[32,256]{1,0:T(8,128)S(1)} %get-tuple-element.43), channel_id=1, source_target_pairs={{0,12},{4,8},{8,4},{12,0},{1,13},{5,9},{9,5},{13,1},{2,14},{6,10},... | collective-permute-start | bytes 98312 | tf_op jit(solution)/shard_map/ppermute | solution.py:168
  21.2 3.0 %collective-permute-start.6 = (f32[32,256]{1,0:T(8,128)S(1)}, f32[32,256]{1,0:T(8,128)S(1)}, u32[]{:S(2)}, u32[]{:S(2)}) collective-permute-start(f32[32,256]{1,0:T(8,128)S(1)} %get-tuple-element.41), channel_id=1, source_target_pairs={{0,4},{4,0},{8,12},{12,8},{1,5},{5,1},{9,13},{13,9},{2,6},{6,2},{1... | collective-permute-start | bytes 98312 | tf_op jit(solution)/shard_map/ppermute | solution.py:168

commit v14 on v8

--- a/solution.py
+++ b/solution.py
@@ -12,6 +12,7 @@
 LANES = 128
 VMEM_LIMIT = 56 * 1024 * 1024
 KEPT_BYTES = 4 * 1024 * 1024
+SCHEDULE_COST = 10 ** 10
 
 
 def normalize(logits):
@@ -123,10 +124,15 @@
     total_ref[...] = first_part(labels, rows_ref, packed_ref, sum_ref[...], tile_ref)
 
 
+def copy_kernel(stack_ref, copy_ref):
+    copy_ref[...] = stack_ref[...]
+
+
 def first_closing(labels, nears, *refs):
     rows_ref, packed_ref, sum_ref, own_ref, compat_ref = refs[:5]
-    near_refs, q_ref, tile_ref = refs[5:-2], refs[-2], refs[-1]
-    own = own_ref.shape[2]
+    near_refs, refs = refs[5:5 + nears], refs[5 + nears:]
+    count = len(refs) // 2
+    far_refs, (q_ref, tile_ref, *part_refs) = refs[:count - 1], refs[count - 1:]
     total = first_part(labels, rows_ref, packed_ref, sum_ref[...], tile_ref)
     labels_now = [own_ref[near][:labels] for near in range(nears)]
     unary = [near_ref[pl.ds(0, labels), :] for near_ref in near_refs]
@@ -134,6 +140,7 @@
         total, jnp.concatenate(labels_now, axis=1), jnp.concatenate(unary, axis=1), compat_ref
     )
     q_ref[...] = probs.astype(jnp.bfloat16)
+    second_parts(q_ref, *far_refs, tile_ref, *part_refs)
 
 
 def second_parts(q_ref, *refs):
@@ -177,16 +184,18 @@
     return count & (count - 1) == 0
 
 
-def block_partners(value, use_early):
+def block_partners(value, copied, use):
     count = lax.axis_size("blk")
     if not paired("blk"):
         stacks = [value] + [swap(value, "blk", steps) for steps in range(1, count)]
-        use_early(stacks[:2])
+        use(value)
+        use(stacks[1])
         return stacks, list(range(count))
     steps = list(range(2, count, 2))
     far = [swap(value, "blk", step) for step in steps]
-    beside = swap(value, "blk", 1)
-    *far, _ = lax.optimization_barrier((*far, use_early([value, beside])))
+    beside = swap(copied, "blk", 1)
+    use(value)
+    *far, _ = lax.optimization_barrier((*far, use(beside)))
     stacks = [value, beside] + far + [swap(stack, "blk", 1) for stack in far]
     return stacks, [0, 1] + steps + [step + 1 for step in steps]
 
@@ -203,6 +212,7 @@
     return pl.pallas_call(
         kernel,
         out_shape=tuple(out_shapes),
+        cost_estimate=pl.CostEstimate(flops=SCHEDULE_COST, transcendentals=0, bytes_accessed=SCHEDULE_COST),
         compiler_params=pltpu.CompilerParams(vmem_limit_bytes=VMEM_LIMIT),
     )(*operands)
 
@@ -240,37 +250,31 @@
     tile_kind = kept((own, nears * own), jnp.bfloat16, parts)
     tiles, totals = [], []
 
-    def first(place, last, stack):
-        if last:
-            q_near, tile = call(
-                functools.partial(first_closing, labels, nears),
-                [kept((labels, nears * own), jnp.bfloat16), tile_kind],
-                *hold(rows, stack, *totals[-1:], packed, held, *near),
-            )
-            tiles.append(tile)
-            return q_near
+    total_kind = kept((labels, nears * own), jnp.float32)
+
+    def first(stack):
+        kernel = first_middle if totals else first_opening
         total, tile = call(
-            functools.partial(first_middle if totals else first_opening, labels),
-            [kept((labels, nears * own), jnp.float32), tile_kind],
+            functools.partial(kernel, labels), [total_kind, tile_kind],
             *hold(rows, stack, *totals[-1:]),
         )
         tiles.append(tile)
         totals.append(total)
         return total
 
-    def first_early(stacks):
-        for place, stack in enumerate(stacks):
-            result = first(place, place + 1 == parts, stack)
-        return result
-
-    stacks, steps = block_partners(packed, first_early)
-    for place in range(2, parts):
-        q_near = first(place, place + 1 == parts, stacks[place])
-
+    (copied,) = call(copy_kernel, [kept(packed.shape, jnp.bfloat16)], *hold(packed))
+    stacks, steps = block_partners(packed, copied, first)
+    for stack in stacks[2:-1]:
+        first(stack)
+    far_tiles = tiles[2:]
     if parts * math.prod(tile_kind.shape) * 2 <= KEPT_BYTES:
-        tiles = hold(*tiles)
+        tiles, far_tiles = hold(*tiles), hold(*far_tiles)
     part_kind = kept((labels, own), jnp.float32)
-    far = call(second_parts, [part_kind] * (parts - 2), *hold(q_near), *tiles[2:])
+    q_near, _, *far = call(
+        functools.partial(first_closing, labels, nears),
+        [kept((labels, nears * own), jnp.bfloat16), tile_kind] + [part_kind] * (parts - 2),
+        *hold(rows, stacks[-1], totals[-1], packed, held, *near), *far_tiles,
+    )
     if far:
         q_near, *far = lax.optimization_barrier((q_near, *far))
     here, beside = call(second_parts, [part_kind] * 2, *hold(q_near), *tiles[:2])

time: 25.5 us -> 25.6 us (level)
  Pallas kernels: 7.16 us -> 7.68 us
  waiting for transfers between devices: 8.04 us -> 7.7 us
    pallas_call x9, Pallas kernels: 7.16 us -> 7.68 us  [call(): pl.pallas_call(kernel, out_shape=tuple(out_shapes), cost_estimate=pl.Cost...]
    ppermute x9, waiting for transfers between devices: 8.04 us -> 7.7 us  [swap(): return lax.ppermute(value, axis, pairs)]
  transfers between devices with their start and end apart: 9 -> 9, of which waited for: 6 -> 7; matrix products, arithmetic and copies ran while one was open for 0% -> 0% of each run, Pallas kernels for 14% -> 14%
where the time goes in v14:
time: 25.6 us; the launch traced here: 25.5 us
  starting transfers between devices  9.43 us (37%)
  waiting for transfers between devices  7.7 us (30%)
  Pallas kernels  7.68 us (30%)
  between operations  0.66 us (3%)
    ppermute x9, starting transfers between devices, swap(): return lax.ppermute(value, axis, pairs)  9.43 us
    ppermute x9, waiting for transfers between devices, swap(): return lax.ppermute(value, axis, pairs)  7.7 us
    pallas_call x9, Pallas kernels, call(): pl.pallas_call(kernel, out_shape=tuple(out_shapes), cost_estimate=pl.Cost...  7.68 us
  transfers between devices with their start and end apart: 9, of which 7 were waited for; matrix products, arithmetic and copies ran while one was open for 0% of the time, Pallas kernels for 14%

profile of v14, /device:TPU:0, one launch (start us, length us, event | category | flops | bytes accessed | tf_op | source)
XLA Modules:
  0.0 25.5 jit_solution(7334596943818309701)
XLA Ops:
  0.6 1.1 %shard_map.59 = (f32[40,256]{1,0:T(8,128)S(1)}, f32[32,32]{1,0:T(8,128)S(1)}) custom-call(bf16[6,4096]{1,0:T(8,128)(2,1)} %features_ref.1, s32[1,256]{1,0:T(1,128)} %bitcast.1, f32[32,256]{1,0:T(8,128)} %unary_ref.1, f32[32,32]{1,0:T(8,128)} %compat_ref.1), custom_call_target="tpu_custom_call" | custom-call | flops 10000000000 | bytes 10000000000 | tf_op jit(solution)/shard_map/pallas_call | solution.py:212
  1.7 4.1 %collective-permute-start.2 = (f32[40,256]{1,0:T(8,128)S(1)}, f32[40,256]{1,0:T(8,128)S(1)}, u32[]{:S(2)}, u32[]{:S(2)}) collective-permute-start(f32[40,256]{1,0:T(8,128)S(1)} %get-tuple-element.21.refs_0_.refs_5_.near_ref), channel_id=1, source_target_pairs={{0,2},{1,3},{2,0},{3,1},{4,6},{5,7},{6,4},{7,5},{8,10},{9,11},{10,... | collective-permute-start | bytes 122888 | tf_op jit(solution)/shard_map/ppermute | solution.py:173
  5.8 1.3 %collective-permute-start.1 = (f32[40,256]{1,0:T(8,128)S(1)}, f32[40,256]{1,0:T(8,128)S(1)}, u32[]{:S(2)}, u32[]{:S(2)}) collective-permute-start(f32[40,256]{1,0:T(8,128)S(1)} %get-tuple-element.21.refs_0_.refs_5_.near_ref), channel_id=1, source_target_pairs={{0,3},{1,2},{2,1},{3,0},{4,7},{5,6},{6,5},{7,4},{8,11},{9,10},{10,... | collective-permute-start | bytes 122888 | tf_op jit(solution)/shard_map/ppermute | solution.py:173
  7.1 0.2 collective-permute-start
  7.4 0.8 %collective-permute-done.2.refs_3_.refs_8_ = f32[40,256]{1,0:T(8,128)S(1)} collective-permute-done((f32[40,256]{1,0:T(8,128)S(1)}, f32[40,256]{1,0:T(8,128)S(1)}, u32[]{:S(2)}, u32[]{:S(2)}) %collective-permute-start.2) | collective-permute-done | bytes 40992 | tf_op jit(solution)/shard_map/ppermute | solution.py:173
  8.2 3.4 %collective-permute-done.1.refs_2_.refs_7_ = f32[40,256]{1,0:T(8,128)S(1)} collective-permute-done((f32[40,256]{1,0:T(8,128)S(1)}, f32[40,256]{1,0:T(8,128)S(1)}, u32[]{:S(2)}, u32[]{:S(2)}) %collective-permute-start.1) | collective-permute-done | bytes 40992 | tf_op jit(solution)/shard_map/ppermute | solution.py:173
  11.6 0.0 collective-permute-done.refs_1_.refs_6_
  11.6 0.1 shard_map.60
  11.7 1.6 %collective-permute-start.3 = (bf16[4,40,256]{2,1,0:T(8,128)(2,1)S(1)}, bf16[4,40,256]{2,1,0:T(8,128)(2,1)S(1)}, u32[]{:S(2)}, u32[]{:S(2)}) collective-permute-start(bf16[4,40,256]{2,1,0:T(8,128)(2,1)S(1)} %get-tuple-element.23.stack_ref.packed_ref.refs_3_), channel_id=1, source_target_pairs={{0,8},{4,12},{8,0},{12,4},{1,9},{5,13},{9,1},{13,5},{2,10},{6,14},... | collective-permute-start | bytes 245768 | tf_op jit(solution)/shard_map/ppermute | solution.py:173
  13.3 0.0 collective-permute-start.4
  13.3 1.0 %shard_map.62 = (f32[32,1024]{1,0:T(8,128)S(1)}, bf16[256,1024]{1,0:T(8,128)(2,1)S(1)}) custom-call(bf16[16,1024]{1,0:T(8,128)(2,1)S(1)} %get-tuple-element.22.rows_ref.refs_0_, bf16[4,40,256]{2,1,0:T(8,128)(2,1)S(1)} %get-tuple-element.23.stack_ref.packed_ref.refs_3_), custom_call_target="tpu_custom_call" | custom-call | flops 10000000000 | bytes 10000000000 | tf_op jit(solution)/shard_map/pallas_call | solution.py:212
  14.3 0.2 collective-permute-done.4.packed_ref
  14.5 1.1 %shard_map.63 = (f32[32,1024]{1,0:T(8,128)S(1)}, bf16[256,1024]{1,0:T(8,128)(2,1)S(1)}) custom-call(bf16[16,1024]{1,0:T(8,128)(2,1)S(1)} %get-tuple-element.22.rows_ref.refs_0_, bf16[4,40,256]{2,1,0:T(8,128)(2,1)S(1)} %collective-permute-done.4.packed_ref, f32[32,1024]{1,0:T(8,128)S(1)} %get-tuple-element.24.sum_ref), custom_call_target="tpu_custom_call" | custom-call | flops 10000000000 | bytes 10000000000 | tf_op jit(solution)/shard_map/pallas_call | solution.py:212
  15.6 0.6 %collective-permute-done.3.packed_ref = bf16[4,40,256]{2,1,0:T(8,128)(2,1)S(1)} collective-permute-done((bf16[4,40,256]{2,1,0:T(8,128)(2,1)S(1)}, bf16[4,40,256]{2,1,0:T(8,128)(2,1)S(1)}, u32[]{:S(2)}, u32[]{:S(2)}) %collective-permute-start.3) | collective-permute-done | bytes 81952 | tf_op jit(solution)/shard_map/ppermute | solution.py:173
  16.2 1.0 %shard_map.64 = (f32[32,1024]{1,0:T(8,128)S(1)}, bf16[256,1024]{1,0:T(8,128)(2,1)S(1)}) custom-call(bf16[16,1024]{1,0:T(8,128)(2,1)S(1)} %get-tuple-element.22.rows_ref.refs_0_, bf16[4,40,256]{2,1,0:T(8,128)(2,1)S(1)} %collective-permute-done.3.packed_ref, f32[32,1024]{1,0:T(8,128)S(1)} %get-tuple-element.25.sum_ref), custom_call_target="tpu_custom_call" | custom-call | flops 10000000000 | bytes 10000000000 | tf_op jit(solution)/shard_map/pallas_call | solution.py:212
  17.2 0.2 collective-permute-done.5.refs_1_
  17.5 2.2 %shard_map.65 = (bf16[32,1024]{1,0:T(8,128)(2,1)S(1)}, bf16[256,1024]{1,0:T(8,128)(2,1)}, f32[32,256]{1,0:T(8,128)S(1)}, f32[32,256]{1,0:T(8,128)S(1)}) custom-call(bf16[16,1024]{1,0:T(8,128)(2,1)S(1)} %get-tuple-element.22.rows_ref.refs_0_, bf16[4,40,256]{2,1,0:T(8,128)(2,1)S(1)} %collective-permute-done.5.refs_1_, ...), custom_call_target="tpu_custom_call" | custom-call | flops 10000000000 | bytes 10000000000 | tf_op jit(solution)/shard_map/pallas_call | solution.py:212
  19.7 1.5 %collective-permute-start.7 = (f32[32,256]{1,0:T(8,128)S(1)}, f32[32,256]{1,0:T(8,128)S(1)}, u32[]{:S(2)}, u32[]{:S(2)}) collective-permute-start(f32[32,256]{1,0:T(8,128)S(1)} %get-tuple-element.38), channel_id=1, source_target_pairs={{0,8},{4,12},{8,0},{12,4},{1,9},{5,13},{9,1},{13,5},{2,10},{6,14},... | collective-permute-start | bytes 98312 | tf_op jit(solution)/shard_map/ppermute | solution.py:173
  21.2 0.1 collective-permute-start.8
  21.3 0.4 %shard_map.66 = (f32[32,256]{1,0:T(8,128)S(1)}, f32[32,256]{1,0:T(8,128)S(1)}) custom-call(bf16[32,1024]{1,0:T(8,128)(2,1)S(1)} %get-tuple-element.33.q_ref, bf16[256,1024]{1,0:T(8,128)(2,1)S(1)} %get-tuple-element.34.refs_0_, bf16[256,1024]{1,0:T(8,128)(2,1)S(1)} %get-tuple-element.35.refs_1_), custom_call_target="tpu_custom_call" | custom-call | flops 10000000000 | bytes 10000000000 | tf_op jit(solution)/shard_map/pallas_call | solution.py:212
  21.7 0.5 %collective-permute-start.6 = (f32[32,256]{1,0:T(8,128)S(1)}, f32[32,256]{1,0:T(8,128)S(1)}, u32[]{:S(2)}, u32[]{:S(2)}) collective-permute-start(f32[32,256]{1,0:T(8,128)S(1)} %get-tuple-element.37), channel_id=1, source_target_pairs={{0,4},{4,0},{8,12},{12,8},{1,5},{5,1},{9,13},{13,9},{2,6},{6,2},{1... | collective-permute-start | bytes 98312 | tf_op jit(solution)/shard_map/ppermute | solution.py:173
  22.2 1.4 %collective-permute-done.7.refs_2_ = f32[32,256]{1,0:T(8,128)S(1)} collective-permute-done((f32[32,256]{1,0:T(8,128)S(1)}, f32[32,256]{1,0:T(8,128)S(1)}, u32[]{:S(2)}, u32[]{:S(2)}) %collective-permute-start.7) | collective-permute-done | bytes 32800 | tf_op jit(solution)/shard_map/ppermute | solution.py:173
  23.6 1.1 %collective-permute-done.8.refs_3_ = f32[32,256]{1,0:T(8,128)S(1)} collective-permute-done((f32[32,256]{1,0:T(8,128)S(1)}, f32[32,256]{1,0:T(8,128)S(1)}, u32[]{:S(2)}, u32[]{:S(2)}) %collective-permute-start.8) | collective-permute-done | bytes 32800 | tf_op jit(solution)/shard_map/ppermute | solution.py:173
  24.7 0.8 %shard_map.67 = (f32[32,256]{1,0:T(8,128)}, f32[32,256]{1,0:T(8,128)}) custom-call(bf16[32,1024]{1,0:T(8,128)(2,1)S(1)} %get-tuple-element.33.q_ref, f32[40,256]{1,0:T(8,128)S(1)} %get-tuple-element.21.refs_0_.refs_5_.near_ref, f32[32,32]{1,0:T(8,128)S(1)} %get-tuple-element.28.refs_4_.compat_ref, f32[32,256]{1,0:T(8,128)S(1)} %get-tuple-element.36.refs_0_, ...), custom_call_target="tpu_custom_call" | custom-call | flops 10000000000 | bytes 10000000000 | tf_op jit(solution)/shard_map/pallas_call | solution.py:212
  (3 shorter events, 0.0 us)
Async XLA Ops:
  1.7 6.5 %collective-permute-start.2 = (f32[40,256]{1,0:T(8,128)S(1)}, f32[40,256]{1,0:T(8,128)S(1)}, u32[]{:S(2)}, u32[]{:S(2)}) collective-permute-start(f32[40,256]{1,0:T(8,128)S(1)} %get-tuple-element.21.refs_0_.refs_5_.near_ref), channel_id=1, source_target_pairs={{0,2},{1,3},{2,0},{3,1},{4,6},{5,7},{6,4},{7,5},{8,10},{9,11},{10,... | collective-permute-start | bytes 122888 | tf_op jit(solution)/shard_map/ppermute | solution.py:173
  5.8 5.8 %collective-permute-start.1 = (f32[40,256]{1,0:T(8,128)S(1)}, f32[40,256]{1,0:T(8,128)S(1)}, u32[]{:S(2)}, u32[]{:S(2)}) collective-permute-start(f32[40,256]{1,0:T(8,128)S(1)} %get-tuple-element.21.refs_0_.refs_5_.near_ref), channel_id=1, source_target_pairs={{0,3},{1,2},{2,1},{3,0},{4,7},{5,6},{6,5},{7,4},{8,11},{9,10},{10,... | collective-permute-start | bytes 122888 | tf_op jit(solution)/shard_map/ppermute | solution.py:173
  7.1 4.5 %collective-permute-start = (f32[40,256]{1,0:T(8,128)S(1)}, f32[40,256]{1,0:T(8,128)S(1)}, u32[]{:S(2)}, u32[]{:S(2)}) collective-permute-start(f32[40,256]{1,0:T(8,128)S(1)} %get-tuple-element.21.refs_0_.refs_5_.near_ref), channel_id=1, source_target_pairs={{0,1},{1,0},{2,3},{3,2},{4,5},{5,4},{6,7},{7,6},{8,9},{9,8},{10,11... | collective-permute-start | bytes 122888 | tf_op jit(solution)/shard_map/ppermute | solution.py:173
  11.7 4.5 %collective-permute-start.3 = (bf16[4,40,256]{2,1,0:T(8,128)(2,1)S(1)}, bf16[4,40,256]{2,1,0:T(8,128)(2,1)S(1)}, u32[]{:S(2)}, u32[]{:S(2)}) collective-permute-start(bf16[4,40,256]{2,1,0:T(8,128)(2,1)S(1)} %get-tuple-element.23.stack_ref.packed_ref.refs_3_), channel_id=1, source_target_pairs={{0,8},{4,12},{8,0},{12,4},{1,9},{5,13},{9,1},{13,5},{2,10},{6,14},... | collective-permute-start | bytes 245768 | tf_op jit(solution)/shard_map/ppermute | solution.py:173
  13.3 1.3 %collective-permute-start.4 = (bf16[4,40,256]{2,1,0:T(8,128)(2,1)S(1)}, bf16[4,40,256]{2,1,0:T(8,128)(2,1)S(1)}, u32[]{:S(2)}, u32[]{:S(2)}) collective-permute-start(bf16[4,40,256]{2,1,0:T(8,128)(2,1)S(1)} %shard_map.61), channel_id=1, source_target_pairs={{0,4},{4,0},{8,12},{12,8},{1,5},{5,1},{9,13},{13,9},{2,6},{6,2},{1... | collective-permute-start | bytes 245768 | tf_op jit(solution)/shard_map/ppermute | solution.py:173
  16.2 1.3 %collective-permute-start.5 = (bf16[4,40,256]{2,1,0:T(8,128)(2,1)S(1)}, bf16[4,40,256]{2,1,0:T(8,128)(2,1)S(1)}, u32[]{:S(2)}, u32[]{:S(2)}) collective-permute-start(bf16[4,40,256]{2,1,0:T(8,128)(2,1)S(1)} %collective-permute-done.3.packed_ref), channel_id=1, source_target_pairs={{0,4},{4,0},{8,12},{12,8},{1,5},{5,1},{9,13},{13,9},{2,6},{6,2},{1... | collective-permute-start | bytes 245768 | tf_op jit(solution)/shard_map/ppermute | solution.py:173
  19.7 3.9 %collective-permute-start.7 = (f32[32,256]{1,0:T(8,128)S(1)}, f32[32,256]{1,0:T(8,128)S(1)}, u32[]{:S(2)}, u32[]{:S(2)}) collective-permute-start(f32[32,256]{1,0:T(8,128)S(1)} %get-tuple-element.38), channel_id=1, source_target_pairs={{0,8},{4,12},{8,0},{12,4},{1,9},{5,13},{9,1},{13,5},{2,10},{6,14},... | collective-permute-start | bytes 98312 | tf_op jit(solution)/shard_map/ppermute | solution.py:173
  21.2 3.5 %collective-permute-start.8 = (f32[32,256]{1,0:T(8,128)S(1)}, f32[32,256]{1,0:T(8,128)S(1)}, u32[]{:S(2)}, u32[]{:S(2)}) collective-permute-start(f32[32,256]{1,0:T(8,128)S(1)} %get-tuple-element.39), channel_id=1, source_target_pairs={{0,12},{4,8},{8,4},{12,0},{1,13},{5,9},{9,5},{13,1},{2,14},{6,10},... | collective-permute-start | bytes 98312 | tf_op jit(solution)/shard_map/ppermute | solution.py:173
  21.7 3.0 %collective-permute-start.6 = (f32[32,256]{1,0:T(8,128)S(1)}, f32[32,256]{1,0:T(8,128)S(1)}, u32[]{:S(2)}, u32[]{:S(2)}) collective-permute-start(f32[32,256]{1,0:T(8,128)S(1)} %get-tuple-element.37), channel_id=1, source_target_pairs={{0,4},{4,0},{8,12},{12,8},{1,5},{5,1},{9,13},{13,9},{2,6},{6,2},{1... | collective-permute-start | bytes 98312 | tf_op jit(solution)/shard_map/ppermute | solution.py:173

commit v15 on v14

--- a/solution.py
+++ b/solution.py
@@ -132,7 +132,7 @@
     rows_ref, packed_ref, sum_ref, own_ref, compat_ref = refs[:5]
     near_refs, refs = refs[5:5 + nears], refs[5 + nears:]
     count = len(refs) // 2
-    far_refs, (q_ref, tile_ref, *part_refs) = refs[:count - 1], refs[count - 1:]
+    far_refs, (q_ref, *part_refs, tile_ref) = refs[:count - 1], refs[count - 1:]
     total = first_part(labels, rows_ref, packed_ref, sum_ref[...], tile_ref)
     labels_now = [own_ref[near][:labels] for near in range(nears)]
     unary = [near_ref[pl.ds(0, labels), :] for near_ref in near_refs]
@@ -208,10 +208,11 @@
     return math.prod(dims) * jnp.dtype(kind).itemsize <= KEPT_BYTES
 
 
-def call(kernel, out_shapes, *operands):
+def call(kernel, out_shapes, *operands, scratch=()):
     return pl.pallas_call(
         kernel,
         out_shape=tuple(out_shapes),
+        scratch_shapes=scratch,
         cost_estimate=pl.CostEstimate(flops=SCHEDULE_COST, transcendentals=0, bytes_accessed=SCHEDULE_COST),
         compiler_params=pltpu.CompilerParams(vmem_limit_bytes=VMEM_LIMIT),
     )(*operands)
@@ -270,10 +271,11 @@
     if parts * math.prod(tile_kind.shape) * 2 <= KEPT_BYTES:
         tiles, far_tiles = hold(*tiles), hold(*far_tiles)
     part_kind = kept((labels, own), jnp.float32)
-    q_near, _, *far = call(
+    q_near, *far = call(
         functools.partial(first_closing, labels, nears),
-        [kept((labels, nears * own), jnp.bfloat16), tile_kind] + [part_kind] * (parts - 2),
+        [kept((labels, nears * own), jnp.bfloat16)] + [part_kind] * (parts - 2),
         *hold(rows, stacks[-1], totals[-1], packed, held, *near), *far_tiles,
+        scratch=[pltpu.VMEM((own, nears * own), jnp.bfloat16)],
     )
     if far:
         q_near, *far = lax.optimization_barrier((q_near, *far))

time: 25.6 us -> 26.9 us (1.051)
  waiting for transfers between devices: 7.7 us -> 9.82 us
  Pallas kernels: 7.68 us -> 7.06 us
  starting transfers between devices: 9.43 us -> 9.16 us
    ppermute x9, waiting for transfers between devices: 7.7 us -> 9.82 us  [swap(): return lax.ppermute(value, axis, pairs)]
    pallas_call x9, Pallas kernels: 7.68 us -> 7.06 us  [call(): pl.pallas_call(kernel, out_shape=tuple(out_shapes), scratch_shapes=scratc...]
  transfers between devices with their start and end apart: 9 -> 9, of which waited for: 7 -> 7; matrix products, arithmetic and copies ran while one was open for 0% -> 0% of each run, Pallas kernels for 14% -> 12%
where the time goes in v15:
time: 26.9 us; the launch traced here: 26.7 us
  waiting for transfers between devices  9.82 us (37%)
  starting transfers between devices  9.16 us (34%)
  Pallas kernels  7.06 us (26%)
  between operations  0.66 us (2%)
    ppermute x9, waiting for transfers between devices, swap(): return lax.ppermute(value, axis, pairs)  9.82 us
    ppermute x9, starting transfers between devices, swap(): return lax.ppermute(value, axis, pairs)  9.16 us
    pallas_call x9, Pallas kernels, call(): pl.pallas_call(kernel, out_shape=tuple(out_shapes), scratch_shapes=scratc...  7.06 us
  transfers between devices with their start and end apart: 9, of which 7 were waited for; matrix products, arithmetic and copies ran while one was open for 0% of the time, Pallas kernels for 12%

profile of v15, /device:TPU:0, one launch (start us, length us, event | category | flops | bytes accessed | tf_op | source)
XLA Modules:
  0.0 26.7 jit_solution(1059438178717992055)
XLA Ops:
  0.6 1.1 %shard_map.59 = (f32[40,256]{1,0:T(8,128)S(1)}, f32[32,32]{1,0:T(8,128)S(1)}) custom-call(bf16[6,4096]{1,0:T(8,128)(2,1)} %features_ref.1, s32[1,256]{1,0:T(1,128)} %bitcast.1, f32[32,256]{1,0:T(8,128)} %unary_ref.1, f32[32,32]{1,0:T(8,128)} %compat_ref.1), custom_call_target="tpu_custom_call" | custom-call | flops 10000000000 | bytes 10000000000 | tf_op jit(solution)/shard_map/pallas_call | solution.py:212
  1.7 3.1 %collective-permute-start = (f32[40,256]{1,0:T(8,128)S(1)}, f32[40,256]{1,0:T(8,128)S(1)}, u32[]{:S(2)}, u32[]{:S(2)}) collective-permute-start(f32[40,256]{1,0:T(8,128)S(1)} %get-tuple-element.18.refs_0_.refs_5_.near_ref), channel_id=1, source_target_pairs={{0,1},{1,0},{2,3},{3,2},{4,5},{5,4},{6,7},{7,6},{8,9},{9,8},{10,11... | collective-permute-start | bytes 122888 | tf_op jit(solution)/shard_map/ppermute | solution.py:173
  4.8 2.5 %collective-permute-start.1 = (f32[40,256]{1,0:T(8,128)S(1)}, f32[40,256]{1,0:T(8,128)S(1)}, u32[]{:S(2)}, u32[]{:S(2)}) collective-permute-start(f32[40,256]{1,0:T(8,128)S(1)} %get-tuple-element.18.refs_0_.refs_5_.near_ref), channel_id=1, source_target_pairs={{0,3},{1,2},{2,1},{3,0},{4,7},{5,6},{6,5},{7,4},{8,11},{9,10},{10,... | collective-permute-start | bytes 122888 | tf_op jit(solution)/shard_map/ppermute | solution.py:173
  7.3 0.1 collective-permute-start.2
  7.4 0.0 collective-permute-done.refs_1_.refs_6_
  7.4 3.7 %collective-permute-done.1.refs_2_.refs_7_ = f32[40,256]{1,0:T(8,128)S(1)} collective-permute-done((f32[40,256]{1,0:T(8,128)S(1)}, f32[40,256]{1,0:T(8,128)S(1)}, u32[]{:S(2)}, u32[]{:S(2)}) %collective-permute-start.1) | collective-permute-done | bytes 40992 | tf_op jit(solution)/shard_map/ppermute | solution.py:173
  11.1 1.5 %collective-permute-done.2.refs_3_.refs_8_ = f32[40,256]{1,0:T(8,128)S(1)} collective-permute-done((f32[40,256]{1,0:T(8,128)S(1)}, f32[40,256]{1,0:T(8,128)S(1)}, u32[]{:S(2)}, u32[]{:S(2)}) %collective-permute-start.2) | collective-permute-done | bytes 40992 | tf_op jit(solution)/shard_map/ppermute | solution.py:173
  12.6 0.1 shard_map.60
  12.7 1.6 %collective-permute-start.3 = (bf16[4,40,256]{2,1,0:T(8,128)(2,1)S(1)}, bf16[4,40,256]{2,1,0:T(8,128)(2,1)S(1)}, u32[]{:S(2)}, u32[]{:S(2)}) collective-permute-start(bf16[4,40,256]{2,1,0:T(8,128)(2,1)S(1)} %get-tuple-element.20.stack_ref.packed_ref.refs_3_), channel_id=1, source_target_pairs={{0,8},{4,12},{8,0},{12,4},{1,9},{5,13},{9,1},{13,5},{2,10},{6,14},... | collective-permute-start | bytes 245768 | tf_op jit(solution)/shard_map/ppermute | solution.py:173
  14.3 0.0 collective-permute-start.4
  14.3 1.1 %shard_map.62 = (f32[32,1024]{1,0:T(8,128)S(1)}, bf16[256,1024]{1,0:T(8,128)(2,1)S(1)}) custom-call(bf16[16,1024]{1,0:T(8,128)(2,1)S(1)} %get-tuple-element.19.rows_ref.refs_0_, bf16[4,40,256]{2,1,0:T(8,128)(2,1)S(1)} %get-tuple-element.20.stack_ref.packed_ref.refs_3_), custom_call_target="tpu_custom_call" | custom-call | flops 10000000000 | bytes 10000000000 | tf_op jit(solution)/shard_map/pallas_call | solution.py:212
  15.3 0.2 collective-permute-done.4.packed_ref
  15.5 1.0 %shard_map.63 = (f32[32,1024]{1,0:T(8,128)S(1)}, bf16[256,1024]{1,0:T(8,128)(2,1)S(1)}) custom-call(bf16[16,1024]{1,0:T(8,128)(2,1)S(1)} %get-tuple-element.19.rows_ref.refs_0_, bf16[4,40,256]{2,1,0:T(8,128)(2,1)S(1)} %collective-permute-done.4.packed_ref, f32[32,1024]{1,0:T(8,128)S(1)} %get-tuple-element.21.sum_ref), custom_call_target="tpu_custom_call" | custom-call | flops 10000000000 | bytes 10000000000 | tf_op jit(solution)/shard_map/pallas_call | solution.py:212
  16.6 0.6 %collective-permute-done.3.packed_ref = bf16[4,40,256]{2,1,0:T(8,128)(2,1)S(1)} collective-permute-done((bf16[4,40,256]{2,1,0:T(8,128)(2,1)S(1)}, bf16[4,40,256]{2,1,0:T(8,128)(2,1)S(1)}, u32[]{:S(2)}, u32[]{:S(2)}) %collective-permute-start.3) | collective-permute-done | bytes 81952 | tf_op jit(solution)/shard_map/ppermute | solution.py:173
  17.2 1.1 %shard_map.64 = (f32[32,1024]{1,0:T(8,128)S(1)}, bf16[256,1024]{1,0:T(8,128)(2,1)S(1)}) custom-call(bf16[16,1024]{1,0:T(8,128)(2,1)S(1)} %get-tuple-element.19.rows_ref.refs_0_, bf16[4,40,256]{2,1,0:T(8,128)(2,1)S(1)} %collective-permute-done.3.packed_ref, f32[32,1024]{1,0:T(8,128)S(1)} %get-tuple-element.22.sum_ref), custom_call_target="tpu_custom_call" | custom-call | flops 10000000000 | bytes 10000000000 | tf_op jit(solution)/shard_map/pallas_call | solution.py:212
  18.2 0.2 collective-permute-done.5.refs_1_
  18.5 1.5 %shard_map.65 = (bf16[32,1024]{1,0:T(8,128)(2,1)S(1)}, f32[32,256]{1,0:T(8,128)S(1)}, f32[32,256]{1,0:T(8,128)S(1)}) custom-call(bf16[16,1024]{1,0:T(8,128)(2,1)S(1)} %get-tuple-element.19.rows_ref.refs_0_, bf16[4,40,256]{2,1,0:T(8,128)(2,1)S(1)} %collective-permute-done.5.refs_1_, f32[32,1024]{1,0:T(8,128)S(1)} %get-tuple-element.24.refs_2_, ...), custom_call_target="tpu_custom_call" | custom-call | flops 10000000000 | bytes 10000000000 | tf_op jit(solution)/shard_map/pallas_call | solution.py:212
  20.0 0.4 %shard_map.66 = (f32[32,256]{1,0:T(8,128)S(1)}, f32[32,256]{1,0:T(8,128)S(1)}) custom-call(bf16[32,1024]{1,0:T(8,128)(2,1)S(1)} %get-tuple-element.27.q_ref, bf16[256,1024]{1,0:T(8,128)(2,1)S(1)} %get-tuple-element.28.refs_0_, bf16[256,1024]{1,0:T(8,128)(2,1)S(1)} %get-tuple-element.29.refs_1_), custom_call_target="tpu_custom_call" | custom-call | flops 10000000000 | bytes 10000000000 | tf_op jit(solution)/shard_map/pallas_call | solution.py:212
  20.4 0.3 %collective-permute-start.6 = (f32[32,256]{1,0:T(8,128)S(1)}, f32[32,256]{1,0:T(8,128)S(1)}, u32[]{:S(2)}, u32[]{:S(2)}) collective-permute-start(f32[32,256]{1,0:T(8,128)S(1)} %get-tuple-element.31), channel_id=1, source_target_pairs={{0,4},{4,0},{8,12},{12,8},{1,5},{5,1},{9,13},{13,9},{2,6},{6,2},{1... | collective-permute-start | bytes 98312 | tf_op jit(solution)/shard_map/ppermute | solution.py:173
  20.8 1.5 %collective-permute-start.7 = (f32[32,256]{1,0:T(8,128)S(1)}, f32[32,256]{1,0:T(8,128)S(1)}, u32[]{:S(2)}, u32[]{:S(2)}) collective-permute-start(f32[32,256]{1,0:T(8,128)S(1)} %get-tuple-element.32), channel_id=1, source_target_pairs={{0,8},{4,12},{8,0},{12,4},{1,9},{5,13},{9,1},{13,5},{2,10},{6,14},... | collective-permute-start | bytes 98312 | tf_op jit(solution)/shard_map/ppermute | solution.py:173
  22.3 0.0 collective-permute-start.8
  22.3 2.3 %collective-permute-done.7.refs_2_ = f32[32,256]{1,0:T(8,128)S(1)} collective-permute-done((f32[32,256]{1,0:T(8,128)S(1)}, f32[32,256]{1,0:T(8,128)S(1)}, u32[]{:S(2)}, u32[]{:S(2)}) %collective-permute-start.7) | collective-permute-done | bytes 32800 | tf_op jit(solution)/shard_map/ppermute | solution.py:173
  24.7 1.2 %collective-permute-done.8.refs_3_ = f32[32,256]{1,0:T(8,128)S(1)} collective-permute-done((f32[32,256]{1,0:T(8,128)S(1)}, f32[32,256]{1,0:T(8,128)S(1)}, u32[]{:S(2)}, u32[]{:S(2)}) %collective-permute-start.8) | collective-permute-done | bytes 32800 | tf_op jit(solution)/shard_map/ppermute | solution.py:173
  25.9 0.8 %shard_map.67 = (f32[32,256]{1,0:T(8,128)}, f32[32,256]{1,0:T(8,128)}) custom-call(bf16[32,1024]{1,0:T(8,128)(2,1)S(1)} %get-tuple-element.27.q_ref, f32[40,256]{1,0:T(8,128)S(1)} %get-tuple-element.18.refs_0_.refs_5_.near_ref, f32[32,32]{1,0:T(8,128)S(1)} %get-tuple-element.25.refs_4_.compat_ref, f32[32,256]{1,0:T(8,128)S(1)} %get-tuple-element.30.refs_0_, ...), custom_call_target="tpu_custom_call" | custom-call | flops 10000000000 | bytes 10000000000 | tf_op jit(solution)/shard_map/pallas_call | solution.py:212
  (3 shorter events, 0.0 us)
Async XLA Ops:
  1.7 5.7 %collective-permute-start = (f32[40,256]{1,0:T(8,128)S(1)}, f32[40,256]{1,0:T(8,128)S(1)}, u32[]{:S(2)}, u32[]{:S(2)}) collective-permute-start(f32[40,256]{1,0:T(8,128)S(1)} %get-tuple-element.18.refs_0_.refs_5_.near_ref), channel_id=1, source_target_pairs={{0,1},{1,0},{2,3},{3,2},{4,5},{5,4},{6,7},{7,6},{8,9},{9,8},{10,11... | collective-permute-start | bytes 122888 | tf_op jit(solution)/shard_map/ppermute | solution.py:173
  4.8 6.3 %collective-permute-start.1 = (f32[40,256]{1,0:T(8,128)S(1)}, f32[40,256]{1,0:T(8,128)S(1)}, u32[]{:S(2)}, u32[]{:S(2)}) collective-permute-start(f32[40,256]{1,0:T(8,128)S(1)} %get-tuple-element.18.refs_0_.refs_5_.near_ref), channel_id=1, source_target_pairs={{0,3},{1,2},{2,1},{3,0},{4,7},{5,6},{6,5},{7,4},{8,11},{9,10},{10,... | collective-permute-start | bytes 122888 | tf_op jit(solution)/shard_map/ppermute | solution.py:173
  7.3 5.3 %collective-permute-start.2 = (f32[40,256]{1,0:T(8,128)S(1)}, f32[40,256]{1,0:T(8,128)S(1)}, u32[]{:S(2)}, u32[]{:S(2)}) collective-permute-start(f32[40,256]{1,0:T(8,128)S(1)} %get-tuple-element.18.refs_0_.refs_5_.near_ref), channel_id=1, source_target_pairs={{0,2},{1,3},{2,0},{3,1},{4,6},{5,7},{6,4},{7,5},{8,10},{9,11},{10,... | collective-permute-start | bytes 122888 | tf_op jit(solution)/shard_map/ppermute | solution.py:173
  12.7 4.5 %collective-permute-start.3 = (bf16[4,40,256]{2,1,0:T(8,128)(2,1)S(1)}, bf16[4,40,256]{2,1,0:T(8,128)(2,1)S(1)}, u32[]{:S(2)}, u32[]{:S(2)}) collective-permute-start(bf16[4,40,256]{2,1,0:T(8,128)(2,1)S(1)} %get-tuple-element.20.stack_ref.packed_ref.refs_3_), channel_id=1, source_target_pairs={{0,8},{4,12},{8,0},{12,4},{1,9},{5,13},{9,1},{13,5},{2,10},{6,14},... | collective-permute-start | bytes 245768 | tf_op jit(solution)/shard_map/ppermute | solution.py:173
  14.3 1.3 %collective-permute-start.4 = (bf16[4,40,256]{2,1,0:T(8,128)(2,1)S(1)}, bf16[4,40,256]{2,1,0:T(8,128)(2,1)S(1)}, u32[]{:S(2)}, u32[]{:S(2)}) collective-permute-start(bf16[4,40,256]{2,1,0:T(8,128)(2,1)S(1)} %shard_map.61), channel_id=1, source_target_pairs={{0,4},{4,0},{8,12},{12,8},{1,5},{5,1},{9,13},{13,9},{2,6},{6,2},{1... | collective-permute-start | bytes 245768 | tf_op jit(solution)/shard_map/ppermute | solution.py:173
  17.2 1.3 %collective-permute-start.5 = (bf16[4,40,256]{2,1,0:T(8,128)(2,1)S(1)}, bf16[4,40,256]{2,1,0:T(8,128)(2,1)S(1)}, u32[]{:S(2)}, u32[]{:S(2)}) collective-permute-start(bf16[4,40,256]{2,1,0:T(8,128)(2,1)S(1)} %collective-permute-done.3.packed_ref), channel_id=1, source_target_pairs={{0,4},{4,0},{8,12},{12,8},{1,5},{5,1},{9,13},{13,9},{2,6},{6,2},{1... | collective-permute-start | bytes 245768 | tf_op jit(solution)/shard_map/ppermute | solution.py:173
  20.4 1.9 %collective-permute-start.6 = (f32[32,256]{1,0:T(8,128)S(1)}, f32[32,256]{1,0:T(8,128)S(1)}, u32[]{:S(2)}, u32[]{:S(2)}) collective-permute-start(f32[32,256]{1,0:T(8,128)S(1)} %get-tuple-element.31), channel_id=1, source_target_pairs={{0,4},{4,0},{8,12},{12,8},{1,5},{5,1},{9,13},{13,9},{2,6},{6,2},{1... | collective-permute-start | bytes 98312 | tf_op jit(solution)/shard_map/ppermute | solution.py:173
  20.8 3.9 %collective-permute-start.7 = (f32[32,256]{1,0:T(8,128)S(1)}, f32[32,256]{1,0:T(8,128)S(1)}, u32[]{:S(2)}, u32[]{:S(2)}) collective-permute-start(f32[32,256]{1,0:T(8,128)S(1)} %get-tuple-element.32), channel_id=1, source_target_pairs={{0,8},{4,12},{8,0},{12,4},{1,9},{5,13},{9,1},{13,5},{2,10},{6,14},... | collective-permute-start | bytes 98312 | tf_op jit(solution)/shard_map/ppermute | solution.py:173
  22.3 3.6 %collective-permute-start.8 = (f32[32,256]{1,0:T(8,128)S(1)}, f32[32,256]{1,0:T(8,128)S(1)}, u32[]{:S(2)}, u32[]{:S(2)}) collective-permute-start(f32[32,256]{1,0:T(8,128)S(1)} %get-tuple-element.33), channel_id=1, source_target_pairs={{0,12},{4,8},{8,4},{12,0},{1,13},{5,9},{9,5},{13,1},{2,14},{6,10},... | collective-permute-start | bytes 98312 | tf_op jit(solution)/shard_map/ppermute | solution.py:173

commit v16 on v8

--- a/solution.py
+++ b/solution.py
@@ -12,6 +12,7 @@
 LANES = 128
 VMEM_LIMIT = 56 * 1024 * 1024
 KEPT_BYTES = 4 * 1024 * 1024
+SCHEDULE_COST = 10 ** 10
 
 
 def normalize(logits):
@@ -73,12 +74,12 @@
         rows_ref[:, pl.ds(place * own, own)] = product_sides(feats)[1]
 
 
-def over_blocks(count, body, start):
-    if count <= 4:
-        for index in range(count):
-            start = body(index, start)
-        return start
-    return lax.fori_loop(0, count, body, start)
+def join_kernel(*refs):
+    joined_ref = refs[-1]
+    base = 0
+    for ref in refs[:-1]:
+        joined_ref[pl.ds(base, ref.shape[0])] = ref[...]
+        base += ref.shape[0]
 
 
 def finish(message, qb, unary, compat_ref):
@@ -90,45 +91,47 @@
     return normalize(-unary - pairwise), pairwise
 
 
-def first_part(labels, rows_ref, packed_ref, total, tile_ref):
-    blocks, _, own = packed_ref.shape
-    rows = rows_ref[...]
-
-    def exponents(index):
-        columns = product_sides(packed_ref[index][labels:].astype(jnp.float32))[0]
+def first_part(labels, row_refs, stack_refs, total, tile_ref):
+    blocks = [(ref, index) for ref in stack_refs for index in range(ref.shape[0])]
+    rows = jnp.concatenate([ref[...] for ref in row_refs], axis=1)
+
+    def exponents(place):
+        ref, index = blocks[place]
+        columns = product_sides(ref[index][labels:].astype(jnp.float32))[0]
         return lax.dot_general(
             columns, rows, (((0,), (0,)), ((), ())), preferred_element_type=jnp.float32
         )
 
     ahead = exponents(0)
-    for index in range(blocks):
+    for place, (ref, index) in enumerate(blocks):
         exponent = ahead
-        if index + 1 < blocks:
-            ahead = exponents(index + 1)
+        if place + 1 < len(blocks):
+            ahead = exponents(place + 1)
         tile = jnp.exp(exponent).astype(jnp.bfloat16)
-        if index == 0:
+        if place == 0:
             tile_ref[...] = tile
-        total = total + jnp.dot(
-            packed_ref[index][:labels], tile, preferred_element_type=jnp.float32
-        )
+        total = total + jnp.dot(ref[index][:labels], tile, preferred_element_type=jnp.float32)
     return total
 
 
-def first_opening(labels, rows_ref, packed_ref, total_ref, tile_ref):
+def first_opening(labels, *refs):
+    total_ref, tile_ref = refs[-2:]
     start = jnp.zeros(total_ref.shape, jnp.float32)
-    total_ref[...] = first_part(labels, rows_ref, packed_ref, start, tile_ref)
-
-
-def first_middle(labels, rows_ref, packed_ref, sum_ref, total_ref, tile_ref):
-    total_ref[...] = first_part(labels, rows_ref, packed_ref, sum_ref[...], tile_ref)
-
-
-def first_closing(labels, nears, *refs):
-    rows_ref, packed_ref, sum_ref, own_ref, compat_ref = refs[:5]
-    near_refs, q_ref, tile_ref = refs[5:-2], refs[-2], refs[-1]
-    own = own_ref.shape[2]
-    total = first_part(labels, rows_ref, packed_ref, sum_ref[...], tile_ref)
-    labels_now = [own_ref[near][:labels] for near in range(nears)]
+    total_ref[...] = first_part(labels, refs[:2], refs[2:-2], start, tile_ref)
+
+
+def first_middle(labels, *refs):
+    sum_ref, total_ref, tile_ref = refs[-3:]
+    total_ref[...] = first_part(labels, refs[:2], refs[2:-3], sum_ref[...], tile_ref)
+
+
+def first_closing(labels, nears, stacks, *refs):
+    row_refs, refs = refs[:2], refs[2:]
+    stack_refs, (sum_ref, compat_ref, *refs) = refs[:stacks], refs[stacks:]
+    near_refs, refs = refs[:nears], refs[nears:]
+    own_refs, (q_ref, tile_ref) = refs[:-2], refs[-2:]
+    total = first_part(labels, row_refs, stack_refs, sum_ref[...], tile_ref)
+    labels_now = [ref[index][:labels] for ref in own_refs for index in range(ref.shape[0])]
     unary = [near_ref[pl.ds(0, labels), :] for near_ref in near_refs]
     probs, _ = finish(
         total, jnp.concatenate(labels_now, axis=1), jnp.concatenate(unary, axis=1), compat_ref
@@ -168,27 +171,13 @@
 
 def group_partners(value):
     count = lax.axis_size("grp")
-    order = sorted(range(1, count), key=lambda steps: (steps != count // 2, -steps))
-    return [value] + [swap(value, "grp", steps) for steps in reversed(order)]
+    order = sorted(range(1, count), key=lambda steps: (steps != count // 2, steps))
+    return [value] + [swap(value, "grp", steps) for steps in order]
 
 
 def paired(axis):
     count = lax.axis_size(axis)
     return count & (count - 1) == 0
-
-
-def block_partners(value, use_early):
-    count = lax.axis_size("blk")
-    if not paired("blk"):
-        stacks = [value] + [swap(value, "blk", steps) for steps in range(1, count)]
-        use_early(stacks[:2])
-        return stacks, list(range(count))
-    steps = list(range(2, count, 2))
-    far = [swap(value, "blk", step) for step in steps]
-    beside = swap(value, "blk", 1)
-    *far, _ = lax.optimization_barrier((*far, use_early([value, beside])))
-    stacks = [value, beside] + far + [swap(stack, "blk", 1) for stack in far]
-    return stacks, [0, 1] + steps + [step + 1 for step in steps]
 
 
 def send_back(value, steps):
@@ -203,6 +192,7 @@
     return pl.pallas_call(
         kernel,
         out_shape=tuple(out_shapes),
+        cost_estimate=pl.CostEstimate(flops=SCHEDULE_COST, transcendentals=0, bytes_accessed=SCHEDULE_COST),
         compiler_params=pltpu.CompilerParams(vmem_limit_bytes=VMEM_LIMIT),
     )(*operands)
 
@@ -231,41 +221,62 @@
         features, member[None], unary, compat,
     )
     near = group_partners(sent)
-    packed, rows = call(
-        functools.partial(pack_kernel, labels),
-        [kept((nears, labels + 8, own), jnp.bfloat16), kept((AUX, nears * own), jnp.bfloat16)],
-        *hold(*near),
-    )
+    half = max(1, nears // 2)
+    halves = [
+        call(
+            functools.partial(pack_kernel, labels),
+            [
+                kept((len(some), labels + 8, own), jnp.bfloat16),
+                kept((AUX, len(some) * own), jnp.bfloat16),
+            ],
+            *hold(*some),
+        )
+        for some in (near[:half], near[half:])
+    ]
+    packed, rows = zip(*halves)
     parts = lax.axis_size("blk")
     tile_kind = kept((own, nears * own), jnp.bfloat16, parts)
+    total_kind = kept((labels, nears * own), jnp.float32)
     tiles, totals = [], []
 
-    def first(place, last, stack):
-        if last:
-            q_near, tile = call(
-                functools.partial(first_closing, labels, nears),
-                [kept((labels, nears * own), jnp.bfloat16), tile_kind],
-                *hold(rows, stack, *totals[-1:], packed, held, *near),
-            )
-            tiles.append(tile)
-            return q_near
+    def first(*stack):
         total, tile = call(
             functools.partial(first_middle if totals else first_opening, labels),
-            [kept((labels, nears * own), jnp.float32), tile_kind],
-            *hold(rows, stack, *totals[-1:]),
+            [total_kind, tile_kind], *hold(*rows, *stack, *totals[-1:]),
         )
         tiles.append(tile)
         totals.append(total)
         return total
 
-    def first_early(stacks):
-        for place, stack in enumerate(stacks):
-            result = first(place, place + 1 == parts, stack)
-        return result
-
-    stacks, steps = block_partners(packed, first_early)
-    for place in range(2, parts):
-        q_near = first(place, place + 1 == parts, stacks[place])
+    (joined,) = call(
+        join_kernel, [kept((nears, labels + 8, own), jnp.bfloat16)], *hold(*packed)
+    )
+    if paired("blk"):
+        steps = list(range(2, parts, 2))
+        far = [[swap(some, "blk", step) for step in steps] for some in packed]
+        beside = swap(joined, "blk", 1)
+        opened = first(*packed)
+        early, late = far
+        *early, _ = lax.optimization_barrier((*early, opened))
+        relayed = [swap(some, "blk", 1) for some in early]
+        *late, _ = lax.optimization_barrier((*late, first(beside)))
+        stacks = list(zip(early, late))
+        stacks += list(zip(relayed, [swap(some, "blk", 1) for some in late]))
+        steps = [0, 1] + steps + [step + 1 for step in steps]
+    else:
+        steps = list(range(parts))
+        stacks = [[swap(joined, "blk", step)] for step in steps[1:]]
+        first(*packed)
+        first(*stacks.pop(0))
+    *middle, last = stacks
+    for stack in middle:
+        first(*stack)
+    q_near, tile = call(
+        functools.partial(first_closing, labels, nears, len(last)),
+        [kept((labels, nears * own), jnp.bfloat16), tile_kind],
+        *hold(*rows, *last, totals[-1], held, *near, *packed),
+    )
+    tiles.append(tile)
 
     if parts * math.prod(tile_kind.shape) * 2 <= KEPT_BYTES:
         tiles = hold(*tiles)

time: 25.5 us -> 24.6 us (0.965)
  waiting for transfers between devices: 8.04 us -> 4.64 us
  starting transfers between devices: 9.52 us -> 11.9 us
    ppermute x9 -> x11, waiting for transfers between devices: 8.04 us -> 4.64 us  [swap(): return lax.ppermute(value, axis, pairs)]
    ppermute x9 -> x11, starting transfers between devices: 9.52 us -> 11.9 us  [swap(): return lax.ppermute(value, axis, pairs)]
    pallas_call x9 -> x11, Pallas kernels: 7.16 us -> 7.17 us  [call(): pl.pallas_call(kernel, out_shape=tuple(out_shapes), cost_estimate=pl.Cost...]
  transfers between devices with their start and end apart: 9 -> 11, of which waited for: 6 -> 5; matrix products, arithmetic and copies ran while one was open for 0% -> 0% of each run, Pallas kernels for 14% -> 15%
where the time goes in v16:
time: 24.6 us; the launch traced here: 24.4 us
  starting transfers between devices  11.9 us (48%)
  Pallas kernels  7.17 us (29%)
  waiting for transfers between devices  4.64 us (19%)
  between operations  0.69 us (3%)
    ppermute x11, starting transfers between devices, swap(): return lax.ppermute(value, axis, pairs)  11.9 us
    pallas_call x11, Pallas kernels, call(): pl.pallas_call(kernel, out_shape=tuple(out_shapes), cost_estimate=pl.Cost...  7.17 us
    ppermute x11, waiting for transfers between devices, swap(): return lax.ppermute(value, axis, pairs)  4.64 us
  transfers between devices with their start and end apart: 11, of which 5 were waited for; matrix products, arithmetic and copies ran while one was open for 0% of the time, Pallas kernels for 15%

profile of v16, /device:TPU:0, one launch (start us, length us, event | category | flops | bytes accessed | tf_op | source)
XLA Modules:
  0.0 24.4 jit_solution(1579602977337594379)
XLA Ops:
  0.6 1.1 %shard_map.59 = (f32[40,256]{1,0:T(8,128)S(1)}, f32[32,32]{1,0:T(8,128)S(1)}) custom-call(bf16[6,4096]{1,0:T(8,128)(2,1)} %features_ref.1, s32[1,256]{1,0:T(1,128)} %bitcast.1, f32[32,256]{1,0:T(8,128)} %unary_ref.1, f32[32,32]{1,0:T(8,128)} %compat_ref.1), custom_call_target="tpu_custom_call" | custom-call | flops 10000000000 | bytes 10000000000 | tf_op jit(solution)/shard_map/pallas_call | solution.py:192
  1.7 4.1 %collective-permute-start = (f32[40,256]{1,0:T(8,128)S(1)}, f32[40,256]{1,0:T(8,128)S(1)}, u32[]{:S(2)}, u32[]{:S(2)}) collective-permute-start(f32[40,256]{1,0:T(8,128)S(1)} %get-tuple-element.25.refs_0_.refs_6_.near_ref), channel_id=1, source_target_pairs={{0,2},{1,3},{2,0},{3,1},{4,6},{5,7},{6,4},{7,5},{8,10},{9,11},{10,... | collective-permute-start | bytes 122888 | tf_op jit(solution)/shard_map/ppermute | solution.py:169
  5.8 1.3 %collective-permute-start.2 = (f32[40,256]{1,0:T(8,128)S(1)}, f32[40,256]{1,0:T(8,128)S(1)}, u32[]{:S(2)}, u32[]{:S(2)}) collective-permute-start(f32[40,256]{1,0:T(8,128)S(1)} %get-tuple-element.25.refs_0_.refs_6_.near_ref), channel_id=1, source_target_pairs={{0,3},{1,2},{2,1},{3,0},{4,7},{5,6},{6,5},{7,4},{8,11},{9,10},{10,... | collective-permute-start | bytes 122888 | tf_op jit(solution)/shard_map/ppermute | solution.py:169
  7.1 0.2 collective-permute-start.1
  7.4 0.8 %collective-permute-done.refs_1_.refs_7_ = f32[40,256]{1,0:T(8,128)S(1)} collective-permute-done((f32[40,256]{1,0:T(8,128)S(1)}, f32[40,256]{1,0:T(8,128)S(1)}, u32[]{:S(2)}, u32[]{:S(2)}) %collective-permute-start) | collective-permute-done | bytes 40992 | tf_op jit(solution)/shard_map/ppermute | solution.py:169
  8.3 1.8 %collective-permute-start.3 = (bf16[2,40,256]{2,1,0:T(8,128)(2,1)S(1)}, bf16[2,40,256]{2,1,0:T(8,128)(2,1)S(1)}, u32[]{:S(2)}, u32[]{:S(2)}) collective-permute-start(bf16[2,40,256]{2,1,0:T(8,128)(2,1)S(1)} %get-tuple-element.28.refs_2_.refs_0_.refs_10_), channel_id=1, source_target_pairs={{0,8},{4,12},{8,0},{12,4},{1,9},{5,13},{9,1},{13,5},{2,10},{6,14},... | collective-permute-start | bytes 122888 | tf_op jit(solution)/shard_map/ppermute | solution.py:169
  10.1 1.5 %collective-permute-done.2.refs_1_.refs_9_ = f32[40,256]{1,0:T(8,128)S(1)} collective-permute-done((f32[40,256]{1,0:T(8,128)S(1)}, f32[40,256]{1,0:T(8,128)S(1)}, u32[]{:S(2)}, u32[]{:S(2)}) %collective-permute-start.2) | collective-permute-done | bytes 40992 | tf_op jit(solution)/shard_map/ppermute | solution.py:169
  11.6 1.6 %collective-permute-start.5 = (bf16[2,40,256]{2,1,0:T(8,128)(2,1)S(1)}, bf16[2,40,256]{2,1,0:T(8,128)(2,1)S(1)}, u32[]{:S(2)}, u32[]{:S(2)}) collective-permute-start(bf16[2,40,256]{2,1,0:T(8,128)(2,1)S(1)} %get-tuple-element.29.refs_3_.refs_1_.refs_11_), channel_id=1, source_target_pairs={{0,8},{4,12},{8,0},{12,4},{1,9},{5,13},{9,1},{13,5},{2,10},{6,14},... | collective-permute-start | bytes 122888 | tf_op jit(solution)/shard_map/ppermute | solution.py:169
  13.2 1.1 %shard_map.62 = (f32[32,1024]{1,0:T(8,128)S(1)}, bf16[256,1024]{1,0:T(8,128)(2,1)S(1)}) custom-call(bf16[16,512]{1,0:T(8,128)(2,1)S(1)} %get-tuple-element.26.refs_0_, bf16[16,512]{1,0:T(8,128)(2,1)S(1)} %get-tuple-element.27.refs_1_, bf16[2,40,256]{2,1,0:T(8,128)(2,1)S(1)} %get-tuple-element.28.refs_2_.refs_0_.refs_10_, ...), custom_call_target="tpu_custom_call" | custom-call | flops 10000000000 | bytes 10000000000 | tf_op jit(solution)/shard_map/pallas_call | solution.py:192
  14.3 0.6 %collective-permute-start.4 = (bf16[2,40,256]{2,1,0:T(8,128)(2,1)S(1)}, bf16[2,40,256]{2,1,0:T(8,128)(2,1)S(1)}, u32[]{:S(2)}, u32[]{:S(2)}) collective-permute-start(bf16[2,40,256]{2,1,0:T(8,128)(2,1)S(1)} %collective-permute-done.3.refs_2_), channel_id=1, source_target_pairs={{0,4},{4,0},{8,12},{12,8},{1,5},{5,1},{9,13},{13,9},{2,6},{6,2},{1... | collective-permute-start | bytes 122888 | tf_op jit(solution)/shard_map/ppermute | solution.py:169
  14.9 1.0 %shard_map.64 = (f32[32,1024]{1,0:T(8,128)S(1)}, bf16[256,1024]{1,0:T(8,128)(2,1)S(1)}) custom-call(bf16[16,512]{1,0:T(8,128)(2,1)S(1)} %get-tuple-element.26.refs_0_, bf16[16,512]{1,0:T(8,128)(2,1)S(1)} %get-tuple-element.27.refs_1_, bf16[4,40,256]{2,1,0:T(8,128)(2,1)S(1)} %collective-permute-done.6.refs_2_, f32[32,1024]{1,0:T(8,128)S(1)} %get-tuple-element.30.refs_3_), custom_call_target="tpu_custom_call" | custom-call | flops 10000000000 | bytes 10000000000 | tf_op jit(solution)/shard_map/pallas_call | solution.py:192
  15.9 0.0 collective-permute-done.5.refs_3_
  15.9 0.1 collective-permute-start.7
  16.0 1.1 %shard_map.65 = (f32[32,1024]{1,0:T(8,128)S(1)}, bf16[256,1024]{1,0:T(8,128)(2,1)S(1)}) custom-call(bf16[16,512]{1,0:T(8,128)(2,1)S(1)} %get-tuple-element.26.refs_0_, bf16[16,512]{1,0:T(8,128)(2,1)S(1)} %get-tuple-element.27.refs_1_, bf16[2,40,256]{2,1,0:T(8,128)(2,1)S(1)} %collective-permute-done.3.refs_2_, ...), custom_call_target="tpu_custom_call" | custom-call | flops 10000000000 | bytes 10000000000 | tf_op jit(solution)/shard_map/pallas_call | solution.py:192
  17.1 0.1 collective-permute-done.7.refs_3_
  17.2 1.3 %shard_map.66 = (bf16[32,1024]{1,0:T(8,128)(2,1)S(1)}, bf16[256,1024]{1,0:T(8,128)(2,1)S(1)}) custom-call(bf16[16,512]{1,0:T(8,128)(2,1)S(1)} %get-tuple-element.26.refs_0_, bf16[16,512]{1,0:T(8,128)(2,1)S(1)} %get-tuple-element.27.refs_1_, bf16[2,40,256]{2,1,0:T(8,128)(2,1)S(1)} %collective-permute-done.4.refs_2_, ...), custom_call_target="tpu_custom_call" | custom-call | flops 10000000000 | bytes 10000000000 | tf_op jit(solution)/shard_map/pallas_call | solution.py:192
  18.5 0.4 %shard_map.67 = (f32[32,256]{1,0:T(8,128)S(1)}, f32[32,256]{1,0:T(8,128)S(1)}) custom-call(bf16[32,1024]{1,0:T(8,128)(2,1)S(1)} %get-tuple-element.41.q_ref, bf16[256,1024]{1,0:T(8,128)(2,1)S(1)} %get-tuple-element.37.refs_0_, bf16[256,1024]{1,0:T(8,128)(2,1)S(1)} %get-tuple-element.38.refs_1_), custom_call_target="tpu_custom_call" | custom-call | flops 10000000000 | bytes 10000000000 | tf_op jit(solution)/shard_map/pallas_call | solution.py:192
  18.9 1.3 %collective-permute-start.9 = (f32[32,256]{1,0:T(8,128)S(1)}, f32[32,256]{1,0:T(8,128)S(1)}, u32[]{:S(2)}, u32[]{:S(2)}) collective-permute-start(f32[32,256]{1,0:T(8,128)S(1)} %get-tuple-element.46), channel_id=1, source_target_pairs={{0,8},{4,12},{8,0},{12,4},{1,9},{5,13},{9,1},{13,5},{2,10},{6,14},... | collective-permute-start | bytes 98312 | tf_op jit(solution)/shard_map/ppermute | solution.py:169
  20.2 0.5 %collective-permute-start.10 = (f32[32,256]{1,0:T(8,128)S(1)}, f32[32,256]{1,0:T(8,128)S(1)}, u32[]{:S(2)}, u32[]{:S(2)}) collective-permute-start(f32[32,256]{1,0:T(8,128)S(1)} %get-tuple-element.47), channel_id=1, source_target_pairs={{0,12},{4,8},{8,4},{12,0},{1,13},{5,9},{9,5},{13,1},{2,14},{6,10},... | collective-permute-start | bytes 98312 | tf_op jit(solution)/shard_map/ppermute | solution.py:169
  20.6 0.4 %shard_map.68 = (f32[32,256]{1,0:T(8,128)S(1)}, f32[32,256]{1,0:T(8,128)S(1)}) custom-call(bf16[32,1024]{1,0:T(8,128)(2,1)S(1)} %get-tuple-element.41.q_ref, bf16[256,1024]{1,0:T(8,128)(2,1)S(1)} %get-tuple-element.42.refs_0_, bf16[256,1024]{1,0:T(8,128)(2,1)S(1)} %get-tuple-element.43.refs_1_), custom_call_target="tpu_custom_call" | custom-call | flops 10000000000 | bytes 10000000000 | tf_op jit(solution)/shard_map/pallas_call | solution.py:192
  21.0 0.5 %collective-permute-start.8 = (f32[32,256]{1,0:T(8,128)S(1)}, f32[32,256]{1,0:T(8,128)S(1)}, u32[]{:S(2)}, u32[]{:S(2)}) collective-permute-start(f32[32,256]{1,0:T(8,128)S(1)} %get-tuple-element.45), channel_id=1, source_target_pairs={{0,4},{4,0},{8,12},{12,8},{1,5},{5,1},{9,13},{13,9},{2,6},{6,2},{1... | collective-permute-start | bytes 98312 | tf_op jit(solution)/shard_map/ppermute | solution.py:169
  21.5 1.4 %collective-permute-done.9.refs_2_ = f32[32,256]{1,0:T(8,128)S(1)} collective-permute-done((f32[32,256]{1,0:T(8,128)S(1)}, f32[32,256]{1,0:T(8,128)S(1)}, u32[]{:S(2)}, u32[]{:S(2)}) %collective-permute-start.9) | collective-permute-done | bytes 32800 | tf_op jit(solution)/shard_map/ppermute | solution.py:169
  22.8 0.8 %collective-permute-done.10.refs_3_ = f32[32,256]{1,0:T(8,128)S(1)} collective-permute-done((f32[32,256]{1,0:T(8,128)S(1)}, f32[32,256]{1,0:T(8,128)S(1)}, u32[]{:S(2)}, u32[]{:S(2)}) %collective-permute-start.10) | collective-permute-done | bytes 32800 | tf_op jit(solution)/shard_map/ppermute | solution.py:169
  23.6 0.8 %shard_map.69 = (f32[32,256]{1,0:T(8,128)}, f32[32,256]{1,0:T(8,128)}) custom-call(bf16[32,1024]{1,0:T(8,128)(2,1)S(1)} %get-tuple-element.41.q_ref, f32[40,256]{1,0:T(8,128)S(1)} %get-tuple-element.25.refs_0_.refs_6_.near_ref, f32[32,32]{1,0:T(8,128)S(1)} %get-tuple-element.35.refs_5_.compat_ref, f32[32,256]{1,0:T(8,128)S(1)} %get-tuple-element.44.refs_0_, ...), custom_call_target="tpu_custom_call" | custom-call | flops 10000000000 | bytes 10000000000 | tf_op jit(solution)/shard_map/pallas_call | solution.py:192
  (9 shorter events, 0.1 us)
Async XLA Ops:
  1.7 6.5 %collective-permute-start = (f32[40,256]{1,0:T(8,128)S(1)}, f32[40,256]{1,0:T(8,128)S(1)}, u32[]{:S(2)}, u32[]{:S(2)}) collective-permute-start(f32[40,256]{1,0:T(8,128)S(1)} %get-tuple-element.25.refs_0_.refs_6_.near_ref), channel_id=1, source_target_pairs={{0,2},{1,3},{2,0},{3,1},{4,6},{5,7},{6,4},{7,5},{8,10},{9,11},{10,... | collective-permute-start | bytes 122888 | tf_op jit(solution)/shard_map/ppermute | solution.py:169
  5.8 5.8 %collective-permute-start.2 = (f32[40,256]{1,0:T(8,128)S(1)}, f32[40,256]{1,0:T(8,128)S(1)}, u32[]{:S(2)}, u32[]{:S(2)}) collective-permute-start(f32[40,256]{1,0:T(8,128)S(1)} %get-tuple-element.25.refs_0_.refs_6_.near_ref), channel_id=1, source_target_pairs={{0,3},{1,2},{2,1},{3,0},{4,7},{5,6},{6,5},{7,4},{8,11},{9,10},{10,... | collective-permute-start | bytes 122888 | tf_op jit(solution)/shard_map/ppermute | solution.py:169
  7.1 4.5 %collective-permute-start.1 = (f32[40,256]{1,0:T(8,128)S(1)}, f32[40,256]{1,0:T(8,128)S(1)}, u32[]{:S(2)}, u32[]{:S(2)}) collective-permute-start(f32[40,256]{1,0:T(8,128)S(1)} %get-tuple-element.25.refs_0_.refs_6_.near_ref), channel_id=1, source_target_pairs={{0,1},{1,0},{2,3},{3,2},{4,5},{5,4},{6,7},{7,6},{8,9},{9,8},{10,11... | collective-permute-start | bytes 122888 | tf_op jit(solution)/shard_map/ppermute | solution.py:169
  8.3 6.0 %collective-permute-start.3 = (bf16[2,40,256]{2,1,0:T(8,128)(2,1)S(1)}, bf16[2,40,256]{2,1,0:T(8,128)(2,1)S(1)}, u32[]{:S(2)}, u32[]{:S(2)}) collective-permute-start(bf16[2,40,256]{2,1,0:T(8,128)(2,1)S(1)} %get-tuple-element.28.refs_2_.refs_0_.refs_10_), channel_id=1, source_target_pairs={{0,8},{4,12},{8,0},{12,4},{1,9},{5,13},{9,1},{13,5},{2,10},{6,14},... | collective-permute-start | bytes 122888 | tf_op jit(solution)/shard_map/ppermute | solution.py:169
  11.6 4.3 %collective-permute-start.5 = (bf16[2,40,256]{2,1,0:T(8,128)(2,1)S(1)}, bf16[2,40,256]{2,1,0:T(8,128)(2,1)S(1)}, u32[]{:S(2)}, u32[]{:S(2)}) collective-permute-start(bf16[2,40,256]{2,1,0:T(8,128)(2,1)S(1)} %get-tuple-element.29.refs_3_.refs_1_.refs_11_), channel_id=1, source_target_pairs={{0,8},{4,12},{8,0},{12,4},{1,9},{5,13},{9,1},{13,5},{2,10},{6,14},... | collective-permute-start | bytes 122888 | tf_op jit(solution)/shard_map/ppermute | solution.py:169
  13.2 1.6 %collective-permute-start.6 = (bf16[4,40,256]{2,1,0:T(8,128)(2,1)S(1)}, bf16[4,40,256]{2,1,0:T(8,128)(2,1)S(1)}, u32[]{:S(2)}, u32[]{:S(2)}) collective-permute-start(bf16[4,40,256]{2,1,0:T(8,128)(2,1)S(1)} %shard_map.63), channel_id=1, source_target_pairs={{0,4},{4,0},{8,12},{12,8},{1,5},{5,1},{9,13},{13,9},{2,6},{6,2},{1... | collective-permute-start | bytes 245768 | tf_op jit(solution)/shard_map/ppermute | solution.py:169
  14.3 2.8 %collective-permute-start.4 = (bf16[2,40,256]{2,1,0:T(8,128)(2,1)S(1)}, bf16[2,40,256]{2,1,0:T(8,128)(2,1)S(1)}, u32[]{:S(2)}, u32[]{:S(2)}) collective-permute-start(bf16[2,40,256]{2,1,0:T(8,128)(2,1)S(1)} %collective-permute-done.3.refs_2_), channel_id=1, source_target_pairs={{0,4},{4,0},{8,12},{12,8},{1,5},{5,1},{9,13},{13,9},{2,6},{6,2},{1... | collective-permute-start | bytes 122888 | tf_op jit(solution)/shard_map/ppermute | solution.py:169
  15.9 1.3 %collective-permute-start.7 = (bf16[2,40,256]{2,1,0:T(8,128)(2,1)S(1)}, bf16[2,40,256]{2,1,0:T(8,128)(2,1)S(1)}, u32[]{:S(2)}, u32[]{:S(2)}) collective-permute-start(bf16[2,40,256]{2,1,0:T(8,128)(2,1)S(1)} %collective-permute-done.5.refs_3_), channel_id=1, source_target_pairs={{0,4},{4,0},{8,12},{12,8},{1,5},{5,1},{9,13},{13,9},{2,6},{6,2},{1... | collective-permute-start | bytes 122888 | tf_op jit(solution)/shard_map/ppermute | solution.py:169
  18.9 3.9 %collective-permute-start.9 = (f32[32,256]{1,0:T(8,128)S(1)}, f32[32,256]{1,0:T(8,128)S(1)}, u32[]{:S(2)}, u32[]{:S(2)}) collective-permute-start(f32[32,256]{1,0:T(8,128)S(1)} %get-tuple-element.46), channel_id=1, source_target_pairs={{0,8},{4,12},{8,0},{12,4},{1,9},{5,13},{9,1},{13,5},{2,10},{6,14},... | collective-permute-start | bytes 98312 | tf_op jit(solution)/shard_map/ppermute | solution.py:169
  20.2 3.4 %collective-permute-start.10 = (f32[32,256]{1,0:T(8,128)S(1)}, f32[32,256]{1,0:T(8,128)S(1)}, u32[]{:S(2)}, u32[]{:S(2)}) collective-permute-start(f32[32,256]{1,0:T(8,128)S(1)} %get-tuple-element.47), channel_id=1, source_target_pairs={{0,12},{4,8},{8,4},{12,0},{1,13},{5,9},{9,5},{13,1},{2,14},{6,10},... | collective-permute-start | bytes 98312 | tf_op jit(solution)/shard_map/ppermute | solution.py:169
  21.0 2.6 %collective-permute-start.8 = (f32[32,256]{1,0:T(8,128)S(1)}, f32[32,256]{1,0:T(8,128)S(1)}, u32[]{:S(2)}, u32[]{:S(2)}) collective-permute-start(f32[32,256]{1,0:T(8,128)S(1)} %get-tuple-element.45), channel_id=1, source_target_pairs={{0,4},{4,0},{8,12},{12,8},{1,5},{5,1},{9,13},{13,9},{2,6},{6,2},{1... | collective-permute-start | bytes 98312 | tf_op jit(solution)/shard_map/ppermute | solution.py:169

commit v17 on v16

--- a/solution.py
+++ b/solution.py
@@ -160,19 +160,25 @@
     pairwise_ref[...] = pairwise
 
 
-def swap(value, axis, steps):
-    count = lax.axis_size(axis)
+def swap(value, blk_steps, grp_steps=0):
+    blks, grps = lax.axis_size("blk"), lax.axis_size("grp")
     pairs = [
-        (source, source ^ steps if paired(axis) else (source + steps) % count)
-        for source in range(count)
+        (
+            blk * grps + grp,
+            (blk ^ blk_steps if paired("blk") else (blk + blk_steps) % blks) * grps
+            + (grp ^ grp_steps if paired("grp") else (grp + grp_steps) % grps),
+        )
+        for blk in range(blks)
+        for grp in range(grps)
     ]
-    return lax.ppermute(value, axis, pairs)
+    return lax.ppermute(value, ("blk", "grp"), pairs)
 
 
 def group_partners(value):
     count = lax.axis_size("grp")
     order = sorted(range(1, count), key=lambda steps: (steps != count // 2, steps))
-    return [value] + [swap(value, "grp", steps) for steps in order]
+    crossed = paired("blk") and paired("grp") and lax.axis_size("blk") > 1
+    return [value] + [swap(value, steps % 2 if crossed else 0, steps) for steps in order]
 
 
 def paired(axis):
@@ -181,7 +187,7 @@
 
 
 def send_back(value, steps):
-    return swap(value, "blk", steps if paired("blk") else lax.axis_size("blk") - steps)
+    return swap(value, steps if paired("blk") else lax.axis_size("blk") - steps)
 
 
 def small(dims, kind):
@@ -252,20 +258,20 @@
         join_kernel, [kept((nears, labels + 8, own), jnp.bfloat16)], *hold(*packed)
     )
     if paired("blk"):
-        steps = list(range(2, parts, 2))
-        far = [[swap(some, "blk", step) for step in steps] for some in packed]
-        beside = swap(joined, "blk", 1)
+        steps = list(range(3, parts, 2))
+        far = [[swap(some, step) for step in steps] for some in packed]
+        beside = swap(joined, 1)
         opened = first(*packed)
         early, late = far
         *early, _ = lax.optimization_barrier((*early, opened))
-        relayed = [swap(some, "blk", 1) for some in early]
+        relayed = [swap(some, 1) for some in early]
         *late, _ = lax.optimization_barrier((*late, first(beside)))
         stacks = list(zip(early, late))
-        stacks += list(zip(relayed, [swap(some, "blk", 1) for some in late]))
-        steps = [0, 1] + steps + [step + 1 for step in steps]
+        stacks += list(zip(relayed, [swap(some, 1) for some in late]))
+        steps = [0, 1] + steps + [step - 1 for step in steps]
     else:
         steps = list(range(parts))
-        stacks = [[swap(joined, "blk", step)] for step in steps[1:]]
+        stacks = [[swap(joined, step)] for step in steps[1:]]
         first(*packed)
         first(*stacks.pop(0))
     *middle, last = stacks
@@ -285,7 +291,8 @@
     if far:
         q_near, *far = lax.optimization_barrier((q_near, *far))
     here, beside = call(second_parts, [part_kind] * 2, *hold(q_near), *tiles[:2])
-    arrived = [send_back(part, step) for part, step in zip([beside, *far], steps[1:])]
+    sent_parts = dict(zip(steps[1:], [beside, *far]))
+    arrived = [send_back(sent_parts[step], step) for step in range(1, parts)]
     return call(
         second_closing,
         [jax.ShapeDtypeStruct((labels, own), jnp.float32)] * 2,

time: 24.6 us -> 24.3 us (0.988)
  starting transfers between devices: 11.9 us -> 9.86 us
  waiting for transfers between devices: 4.64 us -> 6.45 us
    ppermute x11, starting transfers between devices: 11.9 us -> 9.86 us  [swap(): return lax.ppermute(value, ('blk', 'grp'), pairs)]
    ppermute x11, waiting for transfers between devices: 4.64 us -> 6.45 us  [swap(): return lax.ppermute(value, ('blk', 'grp'), pairs)]
where the time goes in v17:
time: 24.3 us; the launch traced here: 24.2 us
  starting transfers between devices  9.86 us (41%)
  Pallas kernels  7.16 us (29%)
  waiting for transfers between devices  6.45 us (27%)
  between operations  0.68 us (3%)
    ppermute x11, starting transfers between devices, swap(): return lax.ppermute(value, ('blk', 'grp'), pairs)  9.86 us
    pallas_call x11, Pallas kernels, call(): pl.pallas_call(kernel, out_shape=tuple(out_shapes), cost_estimate=pl.Cost...  7.16 us
    ppermute x11, waiting for transfers between devices, swap(): return lax.ppermute(value, ('blk', 'grp'), pairs)  6.45 us
  transfers between devices with their start and end apart: 11, of which 5 were waited for; matrix products, arithmetic and copies ran while one was open for 0% of the time, Pallas kernels for 15%

profile of v17, /device:TPU:0, one launch (start us, length us, event | category | flops | bytes accessed | tf_op | source)
XLA Modules:
  0.0 24.2 jit_solution(5924988934769521207)
XLA Ops:
  0.6 1.1 %shard_map.59 = (f32[40,256]{1,0:T(8,128)S(1)}, f32[32,32]{1,0:T(8,128)S(1)}) custom-call(bf16[6,4096]{1,0:T(8,128)(2,1)} %features_ref.1, s32[1,256]{1,0:T(1,128)} %bitcast.1, f32[32,256]{1,0:T(8,128)} %unary_ref.1, f32[32,32]{1,0:T(8,128)} %compat_ref.1), custom_call_target="tpu_custom_call" | custom-call | flops 10000000000 | bytes 10000000000 | tf_op jit(solution)/shard_map/pallas_call | solution.py:198
  1.7 4.1 %collective-permute-start = (f32[40,256]{1,0:T(8,128)S(1)}, f32[40,256]{1,0:T(8,128)S(1)}, u32[]{:S(2)}, u32[]{:S(2)}) collective-permute-start(f32[40,256]{1,0:T(8,128)S(1)} %get-tuple-element.25.refs_0_.refs_6_.near_ref), channel_id=1, source_target_pairs={{0,2},{1,3},{2,0},{3,1},{4,6},{5,7},{6,4},{7,5},{8,10},{9,11},{10,... | collective-permute-start | bytes 122888 | tf_op jit(solution)/shard_map/ppermute | solution.py:174
  5.8 0.5 %collective-permute-start.2 = (f32[40,256]{1,0:T(8,128)S(1)}, f32[40,256]{1,0:T(8,128)S(1)}, u32[]{:S(2)}, u32[]{:S(2)}) collective-permute-start(f32[40,256]{1,0:T(8,128)S(1)} %get-tuple-element.25.refs_0_.refs_6_.near_ref), channel_id=1, source_target_pairs={{0,7},{1,6},{2,5},{3,4},{4,3},{5,2},{6,1},{7,0},{8,15},{9,14},{10,... | collective-permute-start | bytes 122888 | tf_op jit(solution)/shard_map/ppermute | solution.py:174
  6.3 0.2 collective-permute-start.1
  6.5 1.7 %collective-permute-done.refs_1_.refs_7_ = f32[40,256]{1,0:T(8,128)S(1)} collective-permute-done((f32[40,256]{1,0:T(8,128)S(1)}, f32[40,256]{1,0:T(8,128)S(1)}, u32[]{:S(2)}, u32[]{:S(2)}) %collective-permute-start) | collective-permute-done | bytes 40992 | tf_op jit(solution)/shard_map/ppermute | solution.py:174
  8.3 0.5 %collective-permute-start.3 = (bf16[2,40,256]{2,1,0:T(8,128)(2,1)S(1)}, bf16[2,40,256]{2,1,0:T(8,128)(2,1)S(1)}, u32[]{:S(2)}, u32[]{:S(2)}) collective-permute-start(bf16[2,40,256]{2,1,0:T(8,128)(2,1)S(1)} %get-tuple-element.28.refs_2_.refs_0_.refs_10_), channel_id=1, source_target_pairs={{0,12},{1,13},{2,14},{3,15},{4,8},{5,9},{6,10},{7,11},{8,4},{9,5},... | collective-permute-start | bytes 122888 | tf_op jit(solution)/shard_map/ppermute | solution.py:174
  8.7 2.7 %collective-permute-done.2.refs_1_.refs_9_ = f32[40,256]{1,0:T(8,128)S(1)} collective-permute-done((f32[40,256]{1,0:T(8,128)S(1)}, f32[40,256]{1,0:T(8,128)S(1)}, u32[]{:S(2)}, u32[]{:S(2)}) %collective-permute-start.2) | collective-permute-done | bytes 40992 | tf_op jit(solution)/shard_map/ppermute | solution.py:174
  11.4 1.6 %collective-permute-start.5 = (bf16[2,40,256]{2,1,0:T(8,128)(2,1)S(1)}, bf16[2,40,256]{2,1,0:T(8,128)(2,1)S(1)}, u32[]{:S(2)}, u32[]{:S(2)}) collective-permute-start(bf16[2,40,256]{2,1,0:T(8,128)(2,1)S(1)} %get-tuple-element.29.refs_3_.refs_1_.refs_11_), channel_id=1, source_target_pairs={{0,12},{1,13},{2,14},{3,15},{4,8},{5,9},{6,10},{7,11},{8,4},{9,5},... | collective-permute-start | bytes 122888 | tf_op jit(solution)/shard_map/ppermute | solution.py:174
  13.1 0.1 collective-permute-start.6
  13.1 1.1 %shard_map.62 = (f32[32,1024]{1,0:T(8,128)S(1)}, bf16[256,1024]{1,0:T(8,128)(2,1)S(1)}) custom-call(bf16[16,512]{1,0:T(8,128)(2,1)S(1)} %get-tuple-element.26.refs_0_, bf16[16,512]{1,0:T(8,128)(2,1)S(1)} %get-tuple-element.27.refs_1_, bf16[2,40,256]{2,1,0:T(8,128)(2,1)S(1)} %get-tuple-element.28.refs_2_.refs_0_.refs_10_, ...), custom_call_target="tpu_custom_call" | custom-call | flops 10000000000 | bytes 10000000000 | tf_op jit(solution)/shard_map/pallas_call | solution.py:198
  14.2 0.5 %collective-permute-start.4 = (bf16[2,40,256]{2,1,0:T(8,128)(2,1)S(1)}, bf16[2,40,256]{2,1,0:T(8,128)(2,1)S(1)}, u32[]{:S(2)}, u32[]{:S(2)}) collective-permute-start(bf16[2,40,256]{2,1,0:T(8,128)(2,1)S(1)} %collective-permute-done.3.refs_2_), channel_id=1, source_target_pairs={{0,4},{1,5},{2,6},{3,7},{4,0},{5,1},{6,2},{7,3},{8,12},{9,13},{10,... | collective-permute-start | bytes 122888 | tf_op jit(solution)/shard_map/ppermute | solution.py:174
  14.7 1.0 %shard_map.64 = (f32[32,1024]{1,0:T(8,128)S(1)}, bf16[256,1024]{1,0:T(8,128)(2,1)S(1)}) custom-call(bf16[16,512]{1,0:T(8,128)(2,1)S(1)} %get-tuple-element.26.refs_0_, bf16[16,512]{1,0:T(8,128)(2,1)S(1)} %get-tuple-element.27.refs_1_, bf16[4,40,256]{2,1,0:T(8,128)(2,1)S(1)} %collective-permute-done.6.refs_2_, f32[32,1024]{1,0:T(8,128)S(1)} %get-tuple-element.30.refs_3_), custom_call_target="tpu_custom_call" | custom-call | flops 10000000000 | bytes 10000000000 | tf_op jit(solution)/shard_map/pallas_call | solution.py:198
  15.8 0.1 collective-permute-start.7
  15.9 1.1 %shard_map.65 = (f32[32,1024]{1,0:T(8,128)S(1)}, bf16[256,1024]{1,0:T(8,128)(2,1)S(1)}) custom-call(bf16[16,512]{1,0:T(8,128)(2,1)S(1)} %get-tuple-element.26.refs_0_, bf16[16,512]{1,0:T(8,128)(2,1)S(1)} %get-tuple-element.27.refs_1_, bf16[2,40,256]{2,1,0:T(8,128)(2,1)S(1)} %collective-permute-done.3.refs_2_, ...), custom_call_target="tpu_custom_call" | custom-call | flops 10000000000 | bytes 10000000000 | tf_op jit(solution)/shard_map/pallas_call | solution.py:198
  17.0 0.1 collective-permute-done.7.refs_3_
  17.1 1.3 %shard_map.66 = (bf16[32,1024]{1,0:T(8,128)(2,1)S(1)}, bf16[256,1024]{1,0:T(8,128)(2,1)S(1)}) custom-call(bf16[16,512]{1,0:T(8,128)(2,1)S(1)} %get-tuple-element.26.refs_0_, bf16[16,512]{1,0:T(8,128)(2,1)S(1)} %get-tuple-element.27.refs_1_, bf16[2,40,256]{2,1,0:T(8,128)(2,1)S(1)} %collective-permute-done.4.refs_2_, ...), custom_call_target="tpu_custom_call" | custom-call | flops 10000000000 | bytes 10000000000 | tf_op jit(solution)/shard_map/pallas_call | solution.py:198
  18.3 0.4 %shard_map.67 = (f32[32,256]{1,0:T(8,128)S(1)}, f32[32,256]{1,0:T(8,128)S(1)}) custom-call(bf16[32,1024]{1,0:T(8,128)(2,1)S(1)} %get-tuple-element.41.q_ref, bf16[256,1024]{1,0:T(8,128)(2,1)S(1)} %get-tuple-element.37.refs_0_, bf16[256,1024]{1,0:T(8,128)(2,1)S(1)} %get-tuple-element.38.refs_1_), custom_call_target="tpu_custom_call" | custom-call | flops 10000000000 | bytes 10000000000 | tf_op jit(solution)/shard_map/pallas_call | solution.py:198
  18.7 0.9 %collective-permute-start.9 = (f32[32,256]{1,0:T(8,128)S(1)}, f32[32,256]{1,0:T(8,128)S(1)}, u32[]{:S(2)}, u32[]{:S(2)}) collective-permute-start(f32[32,256]{1,0:T(8,128)S(1)} %get-tuple-element.46), channel_id=1, source_target_pairs={{0,8},{1,9},{2,10},{3,11},{4,12},{5,13},{6,14},{7,15},{8,0},{9,1},... | collective-permute-start | bytes 98312 | tf_op jit(solution)/shard_map/ppermute | solution.py:174
  19.7 0.8 %collective-permute-start.10 = (f32[32,256]{1,0:T(8,128)S(1)}, f32[32,256]{1,0:T(8,128)S(1)}, u32[]{:S(2)}, u32[]{:S(2)}) collective-permute-start(f32[32,256]{1,0:T(8,128)S(1)} %get-tuple-element.47), channel_id=1, source_target_pairs={{0,12},{1,13},{2,14},{3,15},{4,8},{5,9},{6,10},{7,11},{8,4},{9,5},... | collective-permute-start | bytes 98312 | tf_op jit(solution)/shard_map/ppermute | solution.py:174
  20.5 0.4 %shard_map.68 = (f32[32,256]{1,0:T(8,128)S(1)}, f32[32,256]{1,0:T(8,128)S(1)}) custom-call(bf16[32,1024]{1,0:T(8,128)(2,1)S(1)} %get-tuple-element.41.q_ref, bf16[256,1024]{1,0:T(8,128)(2,1)S(1)} %get-tuple-element.42.refs_0_, bf16[256,1024]{1,0:T(8,128)(2,1)S(1)} %get-tuple-element.43.refs_1_), custom_call_target="tpu_custom_call" | custom-call | flops 10000000000 | bytes 10000000000 | tf_op jit(solution)/shard_map/pallas_call | solution.py:198
  20.9 0.5 %collective-permute-start.8 = (f32[32,256]{1,0:T(8,128)S(1)}, f32[32,256]{1,0:T(8,128)S(1)}, u32[]{:S(2)}, u32[]{:S(2)}) collective-permute-start(f32[32,256]{1,0:T(8,128)S(1)} %get-tuple-element.45), channel_id=1, source_target_pairs={{0,4},{1,5},{2,6},{3,7},{4,0},{5,1},{6,2},{7,3},{8,12},{9,13},{10,... | collective-permute-start | bytes 98312 | tf_op jit(solution)/shard_map/ppermute | solution.py:174
  21.3 1.4 %collective-permute-done.9.refs_2_ = f32[32,256]{1,0:T(8,128)S(1)} collective-permute-done((f32[32,256]{1,0:T(8,128)S(1)}, f32[32,256]{1,0:T(8,128)S(1)}, u32[]{:S(2)}, u32[]{:S(2)}) %collective-permute-start.9) | collective-permute-done | bytes 32800 | tf_op jit(solution)/shard_map/ppermute | solution.py:174
  22.7 0.6 %collective-permute-done.10.refs_3_ = f32[32,256]{1,0:T(8,128)S(1)} collective-permute-done((f32[32,256]{1,0:T(8,128)S(1)}, f32[32,256]{1,0:T(8,128)S(1)}, u32[]{:S(2)}, u32[]{:S(2)}) %collective-permute-start.10) | collective-permute-done | bytes 32800 | tf_op jit(solution)/shard_map/ppermute | solution.py:174
  23.4 0.8 %shard_map.69 = (f32[32,256]{1,0:T(8,128)}, f32[32,256]{1,0:T(8,128)}) custom-call(bf16[32,1024]{1,0:T(8,128)(2,1)S(1)} %get-tuple-element.41.q_ref, f32[40,256]{1,0:T(8,128)S(1)} %get-tuple-element.25.refs_0_.refs_6_.near_ref, f32[32,32]{1,0:T(8,128)S(1)} %get-tuple-element.35.refs_5_.compat_ref, f32[32,256]{1,0:T(8,128)S(1)} %get-tuple-element.44.refs_0_, ...), custom_call_target="tpu_custom_call" | custom-call | flops 10000000000 | bytes 10000000000 | tf_op jit(solution)/shard_map/pallas_call | solution.py:198
  (9 shorter events, 0.1 us)
Async XLA Ops:
  1.7 6.5 %collective-permute-start = (f32[40,256]{1,0:T(8,128)S(1)}, f32[40,256]{1,0:T(8,128)S(1)}, u32[]{:S(2)}, u32[]{:S(2)}) collective-permute-start(f32[40,256]{1,0:T(8,128)S(1)} %get-tuple-element.25.refs_0_.refs_6_.near_ref), channel_id=1, source_target_pairs={{0,2},{1,3},{2,0},{3,1},{4,6},{5,7},{6,4},{7,5},{8,10},{9,11},{10,... | collective-permute-start | bytes 122888 | tf_op jit(solution)/shard_map/ppermute | solution.py:174
  5.8 5.6 %collective-permute-start.2 = (f32[40,256]{1,0:T(8,128)S(1)}, f32[40,256]{1,0:T(8,128)S(1)}, u32[]{:S(2)}, u32[]{:S(2)}) collective-permute-start(f32[40,256]{1,0:T(8,128)S(1)} %get-tuple-element.25.refs_0_.refs_6_.near_ref), channel_id=1, source_target_pairs={{0,7},{1,6},{2,5},{3,4},{4,3},{5,2},{6,1},{7,0},{8,15},{9,14},{10,... | collective-permute-start | bytes 122888 | tf_op jit(solution)/shard_map/ppermute | solution.py:174
  6.3 5.1 %collective-permute-start.1 = (f32[40,256]{1,0:T(8,128)S(1)}, f32[40,256]{1,0:T(8,128)S(1)}, u32[]{:S(2)}, u32[]{:S(2)}) collective-permute-start(f32[40,256]{1,0:T(8,128)S(1)} %get-tuple-element.25.refs_0_.refs_6_.near_ref), channel_id=1, source_target_pairs={{0,5},{1,4},{2,7},{3,6},{4,1},{5,0},{6,3},{7,2},{8,13},{9,12},{10,... | collective-permute-start | bytes 122888 | tf_op jit(solution)/shard_map/ppermute | solution.py:174
  8.3 5.9 %collective-permute-start.3 = (bf16[2,40,256]{2,1,0:T(8,128)(2,1)S(1)}, bf16[2,40,256]{2,1,0:T(8,128)(2,1)S(1)}, u32[]{:S(2)}, u32[]{:S(2)}) collective-permute-start(bf16[2,40,256]{2,1,0:T(8,128)(2,1)S(1)} %get-tuple-element.28.refs_2_.refs_0_.refs_10_), channel_id=1, source_target_pairs={{0,12},{1,13},{2,14},{3,15},{4,8},{5,9},{6,10},{7,11},{8,4},{9,5},... | collective-permute-start | bytes 122888 | tf_op jit(solution)/shard_map/ppermute | solution.py:174
  11.4 4.4 %collective-permute-start.5 = (bf16[2,40,256]{2,1,0:T(8,128)(2,1)S(1)}, bf16[2,40,256]{2,1,0:T(8,128)(2,1)S(1)}, u32[]{:S(2)}, u32[]{:S(2)}) collective-permute-start(bf16[2,40,256]{2,1,0:T(8,128)(2,1)S(1)} %get-tuple-element.29.refs_3_.refs_1_.refs_11_), channel_id=1, source_target_pairs={{0,12},{1,13},{2,14},{3,15},{4,8},{5,9},{6,10},{7,11},{8,4},{9,5},... | collective-permute-start | bytes 122888 | tf_op jit(solution)/shard_map/ppermute | solution.py:174
  13.1 1.6 %collective-permute-start.6 = (bf16[4,40,256]{2,1,0:T(8,128)(2,1)S(1)}, bf16[4,40,256]{2,1,0:T(8,128)(2,1)S(1)}, u32[]{:S(2)}, u32[]{:S(2)}) collective-permute-start(bf16[4,40,256]{2,1,0:T(8,128)(2,1)S(1)} %shard_map.63), channel_id=1, source_target_pairs={{0,4},{1,5},{2,6},{3,7},{4,0},{5,1},{6,2},{7,3},{8,12},{9,13},{10,... | collective-permute-start | bytes 245768 | tf_op jit(solution)/shard_map/ppermute | solution.py:174
  14.2 2.8 %collective-permute-start.4 = (bf16[2,40,256]{2,1,0:T(8,128)(2,1)S(1)}, bf16[2,40,256]{2,1,0:T(8,128)(2,1)S(1)}, u32[]{:S(2)}, u32[]{:S(2)}) collective-permute-start(bf16[2,40,256]{2,1,0:T(8,128)(2,1)S(1)} %collective-permute-done.3.refs_2_), channel_id=1, source_target_pairs={{0,4},{1,5},{2,6},{3,7},{4,0},{5,1},{6,2},{7,3},{8,12},{9,13},{10,... | collective-permute-start | bytes 122888 | tf_op jit(solution)/shard_map/ppermute | solution.py:174
  15.8 1.3 %collective-permute-start.7 = (bf16[2,40,256]{2,1,0:T(8,128)(2,1)S(1)}, bf16[2,40,256]{2,1,0:T(8,128)(2,1)S(1)}, u32[]{:S(2)}, u32[]{:S(2)}) collective-permute-start(bf16[2,40,256]{2,1,0:T(8,128)(2,1)S(1)} %collective-permute-done.5.refs_3_), channel_id=1, source_target_pairs={{0,4},{1,5},{2,6},{3,7},{4,0},{5,1},{6,2},{7,3},{8,12},{9,13},{10,... | collective-permute-start | bytes 122888 | tf_op jit(solution)/shard_map/ppermute | solution.py:174
  18.7 4.0 %collective-permute-start.9 = (f32[32,256]{1,0:T(8,128)S(1)}, f32[32,256]{1,0:T(8,128)S(1)}, u32[]{:S(2)}, u32[]{:S(2)}) collective-permute-start(f32[32,256]{1,0:T(8,128)S(1)} %get-tuple-element.46), channel_id=1, source_target_pairs={{0,8},{1,9},{2,10},{3,11},{4,12},{5,13},{6,14},{7,15},{8,0},{9,1},... | collective-permute-start | bytes 98312 | tf_op jit(solution)/shard_map/ppermute | solution.py:174
  19.7 3.7 %collective-permute-start.10 = (f32[32,256]{1,0:T(8,128)S(1)}, f32[32,256]{1,0:T(8,128)S(1)}, u32[]{:S(2)}, u32[]{:S(2)}) collective-permute-start(f32[32,256]{1,0:T(8,128)S(1)} %get-tuple-element.47), channel_id=1, source_target_pairs={{0,12},{1,13},{2,14},{3,15},{4,8},{5,9},{6,10},{7,11},{8,4},{9,5},... | collective-permute-start | bytes 98312 | tf_op jit(solution)/shard_map/ppermute | solution.py:174
  20.9 2.5 %collective-permute-start.8 = (f32[32,256]{1,0:T(8,128)S(1)}, f32[32,256]{1,0:T(8,128)S(1)}, u32[]{:S(2)}, u32[]{:S(2)}) collective-permute-start(f32[32,256]{1,0:T(8,128)S(1)} %get-tuple-element.45), channel_id=1, source_target_pairs={{0,4},{1,5},{2,6},{3,7},{4,0},{5,1},{6,2},{7,3},{8,12},{9,13},{10,... | collective-permute-start | bytes 98312 | tf_op jit(solution)/shard_map/ppermute | solution.py:174

commit v18 on v17

--- a/solution.py
+++ b/solution.py
@@ -254,20 +254,20 @@
         totals.append(total)
         return total
 
-    (joined,) = call(
-        join_kernel, [kept((nears, labels + 8, own), jnp.bfloat16)], *hold(*packed)
-    )
+    def join(some):
+        kind = kept((nears, labels + 8, own), jnp.bfloat16)
+        return call(join_kernel, [kind], *hold(*some))[0]
+
+    joined = join(packed)
     if paired("blk"):
         steps = list(range(3, parts, 2))
         far = [[swap(some, step) for step in steps] for some in packed]
         beside = swap(joined, 1)
-        opened = first(*packed)
+        first(*packed)
         early, late = far
-        *early, _ = lax.optimization_barrier((*early, opened))
-        relayed = [swap(some, 1) for some in early]
         *late, _ = lax.optimization_barrier((*late, first(beside)))
         stacks = list(zip(early, late))
-        stacks += list(zip(relayed, [swap(some, 1) for some in late]))
+        stacks += [(swap(join(some), 1),) for some in stacks]
         steps = [0, 1] + steps + [step - 1 for step in steps]
     else:
         steps = list(range(parts))

time: 24.3 us -> 24.3 us (level)
  starting transfers between devices: 9.86 us -> 9.56 us
  waiting for transfers between devices: 6.45 us -> 6.71 us
    ppermute x11 -> x10, starting transfers between devices: 9.86 us -> 9.56 us  [swap(): return lax.ppermute(value, ('blk', 'grp'), pairs)]
    ppermute x11 -> x10, waiting for transfers between devices: 6.45 us -> 6.71 us  [swap(): return lax.ppermute(value, ('blk', 'grp'), pairs)]
    pallas_call x11 -> x12, Pallas kernels: 7.16 us -> 7.18 us  [call(): pl.pallas_call(kernel, out_shape=tuple(out_shapes), cost_estimate=pl.Cost...]
  transfers between devices with their start and end apart: 11 -> 10, of which waited for: 5 -> 5; matrix products, arithmetic and copies ran while one was open for 0% -> 0% of each run, Pallas kernels for 15% -> 15%
where the time goes in v18:
time: 24.3 us; the launch traced here: 24.1 us
  starting transfers between devices  9.56 us (39%)
  Pallas kernels  7.18 us (30%)
  waiting for transfers between devices  6.71 us (28%)
  between operations  0.7 us (3%)
    ppermute x10, starting transfers between devices, swap(): return lax.ppermute(value, ('blk', 'grp'), pairs)  9.56 us
    pallas_call x12, Pallas kernels, call(): pl.pallas_call(kernel, out_shape=tuple(out_shapes), cost_estimate=pl.Cost...  7.18 us
    ppermute x10, waiting for transfers between devices, swap(): return lax.ppermute(value, ('blk', 'grp'), pairs)  6.71 us
  transfers between devices with their start and end apart: 10, of which 5 were waited for; matrix products, arithmetic and copies ran while one was open for 0% of the time, Pallas kernels for 15%

profile of v18, /device:TPU:0, one launch (start us, length us, event | category | flops | bytes accessed | tf_op | source)
XLA Modules:
  0.0 24.1 jit_solution(4008861656746375765)
XLA Ops:
  0.6 1.1 %shard_map.59 = (f32[40,256]{1,0:T(8,128)S(1)}, f32[32,32]{1,0:T(8,128)S(1)}) custom-call(bf16[6,4096]{1,0:T(8,128)(2,1)} %features_ref.1, s32[1,256]{1,0:T(1,128)} %bitcast.1, f32[32,256]{1,0:T(8,128)} %unary_ref.1, f32[32,32]{1,0:T(8,128)} %compat_ref.1), custom_call_target="tpu_custom_call" | custom-call | flops 10000000000 | bytes 10000000000 | tf_op jit(solution)/shard_map/pallas_call | solution.py:198
  1.7 4.1 %collective-permute-start = (f32[40,256]{1,0:T(8,128)S(1)}, f32[40,256]{1,0:T(8,128)S(1)}, u32[]{:S(2)}, u32[]{:S(2)}) collective-permute-start(f32[40,256]{1,0:T(8,128)S(1)} %get-tuple-element.24.refs_0_.refs_5_.near_ref), channel_id=1, source_target_pairs={{0,2},{1,3},{2,0},{3,1},{4,6},{5,7},{6,4},{7,5},{8,10},{9,11},{10,... | collective-permute-start | bytes 122888 | tf_op jit(solution)/shard_map/ppermute | solution.py:174
  5.8 0.5 %collective-permute-start.2 = (f32[40,256]{1,0:T(8,128)S(1)}, f32[40,256]{1,0:T(8,128)S(1)}, u32[]{:S(2)}, u32[]{:S(2)}) collective-permute-start(f32[40,256]{1,0:T(8,128)S(1)} %get-tuple-element.24.refs_0_.refs_5_.near_ref), channel_id=1, source_target_pairs={{0,7},{1,6},{2,5},{3,4},{4,3},{5,2},{6,1},{7,0},{8,15},{9,14},{10,... | collective-permute-start | bytes 122888 | tf_op jit(solution)/shard_map/ppermute | solution.py:174
  6.3 0.2 collective-permute-start.1
  6.5 1.7 %collective-permute-done.refs_1_.refs_6_ = f32[40,256]{1,0:T(8,128)S(1)} collective-permute-done((f32[40,256]{1,0:T(8,128)S(1)}, f32[40,256]{1,0:T(8,128)S(1)}, u32[]{:S(2)}, u32[]{:S(2)}) %collective-permute-start) | collective-permute-done | bytes 40992 | tf_op jit(solution)/shard_map/ppermute | solution.py:174
  8.3 0.5 %collective-permute-start.3 = (bf16[2,40,256]{2,1,0:T(8,128)(2,1)S(1)}, bf16[2,40,256]{2,1,0:T(8,128)(2,1)S(1)}, u32[]{:S(2)}, u32[]{:S(2)}) collective-permute-start(bf16[2,40,256]{2,1,0:T(8,128)(2,1)S(1)} %get-tuple-element.27.refs_0_.refs_2_.refs_9_), channel_id=1, source_target_pairs={{0,12},{1,13},{2,14},{3,15},{4,8},{5,9},{6,10},{7,11},{8,4},{9,5},... | collective-permute-start | bytes 122888 | tf_op jit(solution)/shard_map/ppermute | solution.py:174
  8.7 2.7 %collective-permute-done.2.refs_1_.refs_8_ = f32[40,256]{1,0:T(8,128)S(1)} collective-permute-done((f32[40,256]{1,0:T(8,128)S(1)}, f32[40,256]{1,0:T(8,128)S(1)}, u32[]{:S(2)}, u32[]{:S(2)}) %collective-permute-start.2) | collective-permute-done | bytes 40992 | tf_op jit(solution)/shard_map/ppermute | solution.py:174
  11.4 1.6 %collective-permute-start.4 = (bf16[2,40,256]{2,1,0:T(8,128)(2,1)S(1)}, bf16[2,40,256]{2,1,0:T(8,128)(2,1)S(1)}, u32[]{:S(2)}, u32[]{:S(2)}) collective-permute-start(bf16[2,40,256]{2,1,0:T(8,128)(2,1)S(1)} %get-tuple-element.28.refs_1_.refs_3_.refs_10_), channel_id=1, source_target_pairs={{0,12},{1,13},{2,14},{3,15},{4,8},{5,9},{6,10},{7,11},{8,4},{9,5},... | collective-permute-start | bytes 122888 | tf_op jit(solution)/shard_map/ppermute | solution.py:174
  13.1 0.1 collective-permute-start.5
  13.1 1.1 %shard_map.63 = (f32[32,1024]{1,0:T(8,128)S(1)}, bf16[256,1024]{1,0:T(8,128)(2,1)S(1)}) custom-call(bf16[16,512]{1,0:T(8,128)(2,1)S(1)} %get-tuple-element.25.refs_0_, bf16[16,512]{1,0:T(8,128)(2,1)S(1)} %get-tuple-element.26.refs_1_, bf16[2,40,256]{2,1,0:T(8,128)(2,1)S(1)} %get-tuple-element.27.refs_0_.refs_2_.refs_9_, ...), custom_call_target="tpu_custom_call" | custom-call | flops 10000000000 | bytes 10000000000 | tf_op jit(solution)/shard_map/pallas_call | solution.py:198
  14.2 0.2 collective-permute-done.5.refs_2_
  14.4 1.0 %shard_map.64 = (f32[32,1024]{1,0:T(8,128)S(1)}, bf16[256,1024]{1,0:T(8,128)(2,1)S(1)}) custom-call(bf16[16,512]{1,0:T(8,128)(2,1)S(1)} %get-tuple-element.25.refs_0_, bf16[16,512]{1,0:T(8,128)(2,1)S(1)} %get-tuple-element.26.refs_1_, bf16[4,40,256]{2,1,0:T(8,128)(2,1)S(1)} %collective-permute-done.5.refs_2_, f32[32,1024]{1,0:T(8,128)S(1)} %get-tuple-element.29.refs_3_), custom_call_target="tpu_custom_call" | custom-call | flops 10000000000 | bytes 10000000000 | tf_op jit(solution)/shard_map/pallas_call | solution.py:198
  15.4 0.0 collective-permute-done.4.refs_1_.refs_3_
  15.4 0.4 %collective-permute-start.6 = (bf16[4,40,256]{2,1,0:T(8,128)(2,1)S(1)}, bf16[4,40,256]{2,1,0:T(8,128)(2,1)S(1)}, u32[]{:S(2)}, u32[]{:S(2)}) collective-permute-start(bf16[4,40,256]{2,1,0:T(8,128)(2,1)S(1)} %shard_map.65), channel_id=1, source_target_pairs={{0,4},{1,5},{2,6},{3,7},{4,0},{5,1},{6,2},{7,3},{8,12},{9,13},{10,... | collective-permute-start | bytes 245768 | tf_op jit(solution)/shard_map/ppermute | solution.py:174
  15.8 1.1 %shard_map.66 = (f32[32,1024]{1,0:T(8,128)S(1)}, bf16[256,1024]{1,0:T(8,128)(2,1)S(1)}) custom-call(bf16[16,512]{1,0:T(8,128)(2,1)S(1)} %get-tuple-element.25.refs_0_, bf16[16,512]{1,0:T(8,128)(2,1)S(1)} %get-tuple-element.26.refs_1_, bf16[2,40,256]{2,1,0:T(8,128)(2,1)S(1)} %collective-permute-done.3.refs_0_.refs_2_, ...), custom_call_target="tpu_custom_call" | custom-call | flops 10000000000 | bytes 10000000000 | tf_op jit(solution)/shard_map/pallas_call | solution.py:198
  16.9 1.3 %shard_map.67 = (bf16[32,1024]{1,0:T(8,128)(2,1)S(1)}, bf16[256,1024]{1,0:T(8,128)(2,1)S(1)}) custom-call(bf16[16,512]{1,0:T(8,128)(2,1)S(1)} %get-tuple-element.25.refs_0_, bf16[16,512]{1,0:T(8,128)(2,1)S(1)} %get-tuple-element.26.refs_1_, bf16[4,40,256]{2,1,0:T(8,128)(2,1)S(1)} %collective-permute-done.6.refs_2_, ...), custom_call_target="tpu_custom_call" | custom-call | flops 10000000000 | bytes 10000000000 | tf_op jit(solution)/shard_map/pallas_call | solution.py:198
  18.2 0.4 %shard_map.68 = (f32[32,256]{1,0:T(8,128)S(1)}, f32[32,256]{1,0:T(8,128)S(1)}) custom-call(bf16[32,1024]{1,0:T(8,128)(2,1)S(1)} %get-tuple-element.39.q_ref, bf16[256,1024]{1,0:T(8,128)(2,1)S(1)} %get-tuple-element.35.refs_0_, bf16[256,1024]{1,0:T(8,128)(2,1)S(1)} %get-tuple-element.36.refs_1_), custom_call_target="tpu_custom_call" | custom-call | flops 10000000000 | bytes 10000000000 | tf_op jit(solution)/shard_map/pallas_call | solution.py:198
  18.6 1.2 %collective-permute-start.8 = (f32[32,256]{1,0:T(8,128)S(1)}, f32[32,256]{1,0:T(8,128)S(1)}, u32[]{:S(2)}, u32[]{:S(2)}) collective-permute-start(f32[32,256]{1,0:T(8,128)S(1)} %get-tuple-element.44), channel_id=1, source_target_pairs={{0,8},{1,9},{2,10},{3,11},{4,12},{5,13},{6,14},{7,15},{8,0},{9,1},... | collective-permute-start | bytes 98312 | tf_op jit(solution)/shard_map/ppermute | solution.py:174
  19.7 0.4 %collective-permute-start.9 = (f32[32,256]{1,0:T(8,128)S(1)}, f32[32,256]{1,0:T(8,128)S(1)}, u32[]{:S(2)}, u32[]{:S(2)}) collective-permute-start(f32[32,256]{1,0:T(8,128)S(1)} %get-tuple-element.45), channel_id=1, source_target_pairs={{0,12},{1,13},{2,14},{3,15},{4,8},{5,9},{6,10},{7,11},{8,4},{9,5},... | collective-permute-start | bytes 98312 | tf_op jit(solution)/shard_map/ppermute | solution.py:174
  20.2 0.4 %shard_map.69 = (f32[32,256]{1,0:T(8,128)S(1)}, f32[32,256]{1,0:T(8,128)S(1)}) custom-call(bf16[32,1024]{1,0:T(8,128)(2,1)S(1)} %get-tuple-element.39.q_ref, bf16[256,1024]{1,0:T(8,128)(2,1)S(1)} %get-tuple-element.40.refs_0_, bf16[256,1024]{1,0:T(8,128)(2,1)S(1)} %get-tuple-element.41.refs_1_), custom_call_target="tpu_custom_call" | custom-call | flops 10000000000 | bytes 10000000000 | tf_op jit(solution)/shard_map/pallas_call | solution.py:198
  20.6 0.6 %collective-permute-start.7 = (f32[32,256]{1,0:T(8,128)S(1)}, f32[32,256]{1,0:T(8,128)S(1)}, u32[]{:S(2)}, u32[]{:S(2)}) collective-permute-start(f32[32,256]{1,0:T(8,128)S(1)} %get-tuple-element.43), channel_id=1, source_target_pairs={{0,4},{1,5},{2,6},{3,7},{4,0},{5,1},{6,2},{7,3},{8,12},{9,13},{10,... | collective-permute-start | bytes 98312 | tf_op jit(solution)/shard_map/ppermute | solution.py:174
  21.2 1.4 %collective-permute-done.8.refs_2_ = f32[32,256]{1,0:T(8,128)S(1)} collective-permute-done((f32[32,256]{1,0:T(8,128)S(1)}, f32[32,256]{1,0:T(8,128)S(1)}, u32[]{:S(2)}, u32[]{:S(2)}) %collective-permute-start.8) | collective-permute-done | bytes 32800 | tf_op jit(solution)/shard_map/ppermute | solution.py:174
  22.5 0.8 %collective-permute-done.9.refs_3_ = f32[32,256]{1,0:T(8,128)S(1)} collective-permute-done((f32[32,256]{1,0:T(8,128)S(1)}, f32[32,256]{1,0:T(8,128)S(1)}, u32[]{:S(2)}, u32[]{:S(2)}) %collective-permute-start.9) | collective-permute-done | bytes 32800 | tf_op jit(solution)/shard_map/ppermute | solution.py:174
  23.3 0.8 %shard_map.70 = (f32[32,256]{1,0:T(8,128)}, f32[32,256]{1,0:T(8,128)}) custom-call(bf16[32,1024]{1,0:T(8,128)(2,1)S(1)} %get-tuple-element.39.q_ref, f32[40,256]{1,0:T(8,128)S(1)} %get-tuple-element.24.refs_0_.refs_5_.near_ref, f32[32,32]{1,0:T(8,128)S(1)} %get-tuple-element.33.refs_4_.compat_ref, f32[32,256]{1,0:T(8,128)S(1)} %get-tuple-element.42.refs_0_, ...), custom_call_target="tpu_custom_call" | custom-call | flops 10000000000 | bytes 10000000000 | tf_op jit(solution)/shard_map/pallas_call | solution.py:198
  (8 shorter events, 0.1 us)
Async XLA Ops:
  1.7 6.5 %collective-permute-start = (f32[40,256]{1,0:T(8,128)S(1)}, f32[40,256]{1,0:T(8,128)S(1)}, u32[]{:S(2)}, u32[]{:S(2)}) collective-permute-start(f32[40,256]{1,0:T(8,128)S(1)} %get-tuple-element.24.refs_0_.refs_5_.near_ref), channel_id=1, source_target_pairs={{0,2},{1,3},{2,0},{3,1},{4,6},{5,7},{6,4},{7,5},{8,10},{9,11},{10,... | collective-permute-start | bytes 122888 | tf_op jit(solution)/shard_map/ppermute | solution.py:174
  5.8 5.6 %collective-permute-start.2 = (f32[40,256]{1,0:T(8,128)S(1)}, f32[40,256]{1,0:T(8,128)S(1)}, u32[]{:S(2)}, u32[]{:S(2)}) collective-permute-start(f32[40,256]{1,0:T(8,128)S(1)} %get-tuple-element.24.refs_0_.refs_5_.near_ref), channel_id=1, source_target_pairs={{0,7},{1,6},{2,5},{3,4},{4,3},{5,2},{6,1},{7,0},{8,15},{9,14},{10,... | collective-permute-start | bytes 122888 | tf_op jit(solution)/shard_map/ppermute | solution.py:174
  6.3 5.1 %collective-permute-start.1 = (f32[40,256]{1,0:T(8,128)S(1)}, f32[40,256]{1,0:T(8,128)S(1)}, u32[]{:S(2)}, u32[]{:S(2)}) collective-permute-start(f32[40,256]{1,0:T(8,128)S(1)} %get-tuple-element.24.refs_0_.refs_5_.near_ref), channel_id=1, source_target_pairs={{0,5},{1,4},{2,7},{3,6},{4,1},{5,0},{6,3},{7,2},{8,13},{9,12},{10,... | collective-permute-start | bytes 122888 | tf_op jit(solution)/shard_map/ppermute | solution.py:174
  8.3 7.2 %collective-permute-start.3 = (bf16[2,40,256]{2,1,0:T(8,128)(2,1)S(1)}, bf16[2,40,256]{2,1,0:T(8,128)(2,1)S(1)}, u32[]{:S(2)}, u32[]{:S(2)}) collective-permute-start(bf16[2,40,256]{2,1,0:T(8,128)(2,1)S(1)} %get-tuple-element.27.refs_0_.refs_2_.refs_9_), channel_id=1, source_target_pairs={{0,12},{1,13},{2,14},{3,15},{4,8},{5,9},{6,10},{7,11},{8,4},{9,5},... | collective-permute-start | bytes 122888 | tf_op jit(solution)/shard_map/ppermute | solution.py:174
  11.4 4.0 %collective-permute-start.4 = (bf16[2,40,256]{2,1,0:T(8,128)(2,1)S(1)}, bf16[2,40,256]{2,1,0:T(8,128)(2,1)S(1)}, u32[]{:S(2)}, u32[]{:S(2)}) collective-permute-start(bf16[2,40,256]{2,1,0:T(8,128)(2,1)S(1)} %get-tuple-element.28.refs_1_.refs_3_.refs_10_), channel_id=1, source_target_pairs={{0,12},{1,13},{2,14},{3,15},{4,8},{5,9},{6,10},{7,11},{8,4},{9,5},... | collective-permute-start | bytes 122888 | tf_op jit(solution)/shard_map/ppermute | solution.py:174
  13.1 1.3 %collective-permute-start.5 = (bf16[4,40,256]{2,1,0:T(8,128)(2,1)S(1)}, bf16[4,40,256]{2,1,0:T(8,128)(2,1)S(1)}, u32[]{:S(2)}, u32[]{:S(2)}) collective-permute-start(bf16[4,40,256]{2,1,0:T(8,128)(2,1)S(1)} %shard_map.62), channel_id=1, source_target_pairs={{0,4},{1,5},{2,6},{3,7},{4,0},{5,1},{6,2},{7,3},{8,12},{9,13},{10,... | collective-permute-start | bytes 245768 | tf_op jit(solution)/shard_map/ppermute | solution.py:174
  15.4 1.4 %collective-permute-start.6 = (bf16[4,40,256]{2,1,0:T(8,128)(2,1)S(1)}, bf16[4,40,256]{2,1,0:T(8,128)(2,1)S(1)}, u32[]{:S(2)}, u32[]{:S(2)}) collective-permute-start(bf16[4,40,256]{2,1,0:T(8,128)(2,1)S(1)} %shard_map.65), channel_id=1, source_target_pairs={{0,4},{1,5},{2,6},{3,7},{4,0},{5,1},{6,2},{7,3},{8,12},{9,13},{10,... | collective-permute-start | bytes 245768 | tf_op jit(solution)/shard_map/ppermute | solution.py:174
  18.6 3.9 %collective-permute-start.8 = (f32[32,256]{1,0:T(8,128)S(1)}, f32[32,256]{1,0:T(8,128)S(1)}, u32[]{:S(2)}, u32[]{:S(2)}) collective-permute-start(f32[32,256]{1,0:T(8,128)S(1)} %get-tuple-element.44), channel_id=1, source_target_pairs={{0,8},{1,9},{2,10},{3,11},{4,12},{5,13},{6,14},{7,15},{8,0},{9,1},... | collective-permute-start | bytes 98312 | tf_op jit(solution)/shard_map/ppermute | solution.py:174
  19.7 3.6 %collective-permute-start.9 = (f32[32,256]{1,0:T(8,128)S(1)}, f32[32,256]{1,0:T(8,128)S(1)}, u32[]{:S(2)}, u32[]{:S(2)}) collective-permute-start(f32[32,256]{1,0:T(8,128)S(1)} %get-tuple-element.45), channel_id=1, source_target_pairs={{0,12},{1,13},{2,14},{3,15},{4,8},{5,9},{6,10},{7,11},{8,4},{9,5},... | collective-permute-start | bytes 98312 | tf_op jit(solution)/shard_map/ppermute | solution.py:174
  20.6 2.8 %collective-permute-start.7 = (f32[32,256]{1,0:T(8,128)S(1)}, f32[32,256]{1,0:T(8,128)S(1)}, u32[]{:S(2)}, u32[]{:S(2)}) collective-permute-start(f32[32,256]{1,0:T(8,128)S(1)} %get-tuple-element.43), channel_id=1, source_target_pairs={{0,4},{1,5},{2,6},{3,7},{4,0},{5,1},{6,2},{7,3},{8,12},{9,13},{10,... | collective-permute-start | bytes 98312 | tf_op jit(solution)/shard_map/ppermute | solution.py:174

commit v19 on v18

--- a/solution.py
+++ b/solution.py
@@ -143,9 +143,9 @@
     count = len(refs) // 2
     for tile_ref, part_ref in zip(refs[:count], refs[count:]):
         part_ref[...] = lax.dot_general(
-            q_ref[...], tile_ref[...], (((1,), (1,)), ((), ())),
+            tile_ref[...], q_ref[...], (((1,), (1,)), ((), ())),
             preferred_element_type=jnp.float32,
-        )
+        ).T
 
 
 def second_closing(q_ref, near_ref, compat_ref, *refs):

time: 24.3 us -> 24.4 us (level)
  no operation moved by 1% of the time
where the time goes in v19:
time: 24.4 us; the launch traced here: 24.2 us
  starting transfers between devices  9.64 us (40%)
  Pallas kernels  7.3 us (30%)
  waiting for transfers between devices  6.62 us (27%)
  between operations  0.7 us (3%)
    ppermute x10, starting transfers between devices, swap(): return lax.ppermute(value, ('blk', 'grp'), pairs)  9.64 us
    pallas_call x12, Pallas kernels, call(): pl.pallas_call(kernel, out_shape=tuple(out_shapes), cost_estimate=pl.Cost...  7.3 us
    ppermute x10, waiting for transfers between devices, swap(): return lax.ppermute(value, ('blk', 'grp'), pairs)  6.62 us
  transfers between devices with their start and end apart: 10, of which 5 were waited for; matrix products, arithmetic and copies ran while one was open for 0% of the time, Pallas kernels for 15%

profile of v19, /device:TPU:0, one launch (start us, length us, event | category | flops | bytes accessed | tf_op | source)
XLA Modules:
  0.0 24.2 jit_solution(12171889535415679108)
XLA Ops:
  0.6 1.1 %shard_map.59 = (f32[40,256]{1,0:T(8,128)S(1)}, f32[32,32]{1,0:T(8,128)S(1)}) custom-call(bf16[6,4096]{1,0:T(8,128)(2,1)} %features_ref.1, s32[1,256]{1,0:T(1,128)} %bitcast.1, f32[32,256]{1,0:T(8,128)} %unary_ref.1, f32[32,32]{1,0:T(8,128)} %compat_ref.1), custom_call_target="tpu_custom_call" | custom-call | flops 10000000000 | bytes 10000000000 | tf_op jit(solution)/shard_map/pallas_call | solution.py:198
  1.7 4.1 %collective-permute-start = (f32[40,256]{1,0:T(8,128)S(1)}, f32[40,256]{1,0:T(8,128)S(1)}, u32[]{:S(2)}, u32[]{:S(2)}) collective-permute-start(f32[40,256]{1,0:T(8,128)S(1)} %get-tuple-element.24.refs_0_.refs_5_.near_ref), channel_id=1, source_target_pairs={{0,2},{1,3},{2,0},{3,1},{4,6},{5,7},{6,4},{7,5},{8,10},{9,11},{10,... | collective-permute-start | bytes 122888 | tf_op jit(solution)/shard_map/ppermute | solution.py:174
  5.8 0.5 %collective-permute-start.2 = (f32[40,256]{1,0:T(8,128)S(1)}, f32[40,256]{1,0:T(8,128)S(1)}, u32[]{:S(2)}, u32[]{:S(2)}) collective-permute-start(f32[40,256]{1,0:T(8,128)S(1)} %get-tuple-element.24.refs_0_.refs_5_.near_ref), channel_id=1, source_target_pairs={{0,7},{1,6},{2,5},{3,4},{4,3},{5,2},{6,1},{7,0},{8,15},{9,14},{10,... | collective-permute-start | bytes 122888 | tf_op jit(solution)/shard_map/ppermute | solution.py:174
  6.3 0.2 collective-permute-start.1
  6.5 1.7 %collective-permute-done.refs_1_.refs_6_ = f32[40,256]{1,0:T(8,128)S(1)} collective-permute-done((f32[40,256]{1,0:T(8,128)S(1)}, f32[40,256]{1,0:T(8,128)S(1)}, u32[]{:S(2)}, u32[]{:S(2)}) %collective-permute-start) | collective-permute-done | bytes 40992 | tf_op jit(solution)/shard_map/ppermute | solution.py:174
  8.3 0.5 %collective-permute-start.3 = (bf16[2,40,256]{2,1,0:T(8,128)(2,1)S(1)}, bf16[2,40,256]{2,1,0:T(8,128)(2,1)S(1)}, u32[]{:S(2)}, u32[]{:S(2)}) collective-permute-start(bf16[2,40,256]{2,1,0:T(8,128)(2,1)S(1)} %get-tuple-element.27.refs_0_.refs_2_.refs_9_), channel_id=1, source_target_pairs={{0,12},{1,13},{2,14},{3,15},{4,8},{5,9},{6,10},{7,11},{8,4},{9,5},... | collective-permute-start | bytes 122888 | tf_op jit(solution)/shard_map/ppermute | solution.py:174
  8.7 2.7 %collective-permute-done.2.refs_1_.refs_8_ = f32[40,256]{1,0:T(8,128)S(1)} collective-permute-done((f32[40,256]{1,0:T(8,128)S(1)}, f32[40,256]{1,0:T(8,128)S(1)}, u32[]{:S(2)}, u32[]{:S(2)}) %collective-permute-start.2) | collective-permute-done | bytes 40992 | tf_op jit(solution)/shard_map/ppermute | solution.py:174
  11.4 1.6 %collective-permute-start.4 = (bf16[2,40,256]{2,1,0:T(8,128)(2,1)S(1)}, bf16[2,40,256]{2,1,0:T(8,128)(2,1)S(1)}, u32[]{:S(2)}, u32[]{:S(2)}) collective-permute-start(bf16[2,40,256]{2,1,0:T(8,128)(2,1)S(1)} %get-tuple-element.28.refs_1_.refs_3_.refs_10_), channel_id=1, source_target_pairs={{0,12},{1,13},{2,14},{3,15},{4,8},{5,9},{6,10},{7,11},{8,4},{9,5},... | collective-permute-start | bytes 122888 | tf_op jit(solution)/shard_map/ppermute | solution.py:174
  13.1 0.1 collective-permute-start.5
  13.1 1.1 %shard_map.63 = (f32[32,1024]{1,0:T(8,128)S(1)}, bf16[256,1024]{1,0:T(8,128)(2,1)S(1)}) custom-call(bf16[16,512]{1,0:T(8,128)(2,1)S(1)} %get-tuple-element.25.refs_0_, bf16[16,512]{1,0:T(8,128)(2,1)S(1)} %get-tuple-element.26.refs_1_, bf16[2,40,256]{2,1,0:T(8,128)(2,1)S(1)} %get-tuple-element.27.refs_0_.refs_2_.refs_9_, ...), custom_call_target="tpu_custom_call" | custom-call | flops 10000000000 | bytes 10000000000 | tf_op jit(solution)/shard_map/pallas_call | solution.py:198
  14.2 0.2 collective-permute-done.5.refs_2_
  14.4 1.0 %shard_map.64 = (f32[32,1024]{1,0:T(8,128)S(1)}, bf16[256,1024]{1,0:T(8,128)(2,1)S(1)}) custom-call(bf16[16,512]{1,0:T(8,128)(2,1)S(1)} %get-tuple-element.25.refs_0_, bf16[16,512]{1,0:T(8,128)(2,1)S(1)} %get-tuple-element.26.refs_1_, bf16[4,40,256]{2,1,0:T(8,128)(2,1)S(1)} %collective-permute-done.5.refs_2_, f32[32,1024]{1,0:T(8,128)S(1)} %get-tuple-element.29.refs_3_), custom_call_target="tpu_custom_call" | custom-call | flops 10000000000 | bytes 10000000000 | tf_op jit(solution)/shard_map/pallas_call | solution.py:198
  15.4 0.0 collective-permute-done.4.refs_1_.refs_3_
  15.4 0.4 %collective-permute-start.6 = (bf16[4,40,256]{2,1,0:T(8,128)(2,1)S(1)}, bf16[4,40,256]{2,1,0:T(8,128)(2,1)S(1)}, u32[]{:S(2)}, u32[]{:S(2)}) collective-permute-start(bf16[4,40,256]{2,1,0:T(8,128)(2,1)S(1)} %shard_map.65), channel_id=1, source_target_pairs={{0,4},{1,5},{2,6},{3,7},{4,0},{5,1},{6,2},{7,3},{8,12},{9,13},{10,... | collective-permute-start | bytes 245768 | tf_op jit(solution)/shard_map/ppermute | solution.py:174
  15.8 1.1 %shard_map.66 = (f32[32,1024]{1,0:T(8,128)S(1)}, bf16[256,1024]{1,0:T(8,128)(2,1)S(1)}) custom-call(bf16[16,512]{1,0:T(8,128)(2,1)S(1)} %get-tuple-element.25.refs_0_, bf16[16,512]{1,0:T(8,128)(2,1)S(1)} %get-tuple-element.26.refs_1_, bf16[2,40,256]{2,1,0:T(8,128)(2,1)S(1)} %collective-permute-done.3.refs_0_.refs_2_, ...), custom_call_target="tpu_custom_call" | custom-call | flops 10000000000 | bytes 10000000000 | tf_op jit(solution)/shard_map/pallas_call | solution.py:198
  16.9 1.3 %shard_map.67 = (bf16[32,1024]{1,0:T(8,128)(2,1)S(1)}, bf16[256,1024]{1,0:T(8,128)(2,1)S(1)}) custom-call(bf16[16,512]{1,0:T(8,128)(2,1)S(1)} %get-tuple-element.25.refs_0_, bf16[16,512]{1,0:T(8,128)(2,1)S(1)} %get-tuple-element.26.refs_1_, bf16[4,40,256]{2,1,0:T(8,128)(2,1)S(1)} %collective-permute-done.6.refs_2_, ...), custom_call_target="tpu_custom_call" | custom-call | flops 10000000000 | bytes 10000000000 | tf_op jit(solution)/shard_map/pallas_call | solution.py:198
  18.2 0.5 %shard_map.68 = (f32[32,256]{1,0:T(8,128)S(1)}, f32[32,256]{1,0:T(8,128)S(1)}) custom-call(bf16[32,1024]{1,0:T(8,128)(2,1)S(1)} %get-tuple-element.39.q_ref, bf16[256,1024]{1,0:T(8,128)(2,1)S(1)} %get-tuple-element.35.refs_0_, bf16[256,1024]{1,0:T(8,128)(2,1)S(1)} %get-tuple-element.36.refs_1_), custom_call_target="tpu_custom_call" | custom-call | flops 10000000000 | bytes 10000000000 | tf_op jit(solution)/shard_map/pallas_call | solution.py:198
  18.6 1.2 %collective-permute-start.8 = (f32[32,256]{1,0:T(8,128)S(1)}, f32[32,256]{1,0:T(8,128)S(1)}, u32[]{:S(2)}, u32[]{:S(2)}) collective-permute-start(f32[32,256]{1,0:T(8,128)S(1)} %get-tuple-element.44), channel_id=1, source_target_pairs={{0,8},{1,9},{2,10},{3,11},{4,12},{5,13},{6,14},{7,15},{8,0},{9,1},... | collective-permute-start | bytes 98312 | tf_op jit(solution)/shard_map/ppermute | solution.py:174
  19.8 0.4 %collective-permute-start.9 = (f32[32,256]{1,0:T(8,128)S(1)}, f32[32,256]{1,0:T(8,128)S(1)}, u32[]{:S(2)}, u32[]{:S(2)}) collective-permute-start(f32[32,256]{1,0:T(8,128)S(1)} %get-tuple-element.45), channel_id=1, source_target_pairs={{0,12},{1,13},{2,14},{3,15},{4,8},{5,9},{6,10},{7,11},{8,4},{9,5},... | collective-permute-start | bytes 98312 | tf_op jit(solution)/shard_map/ppermute | solution.py:174
  20.3 0.5 %shard_map.69 = (f32[32,256]{1,0:T(8,128)S(1)}, f32[32,256]{1,0:T(8,128)S(1)}) custom-call(bf16[32,1024]{1,0:T(8,128)(2,1)S(1)} %get-tuple-element.39.q_ref, bf16[256,1024]{1,0:T(8,128)(2,1)S(1)} %get-tuple-element.40.refs_0_, bf16[256,1024]{1,0:T(8,128)(2,1)S(1)} %get-tuple-element.41.refs_1_), custom_call_target="tpu_custom_call" | custom-call | flops 10000000000 | bytes 10000000000 | tf_op jit(solution)/shard_map/pallas_call | solution.py:198
  20.7 0.6 %collective-permute-start.7 = (f32[32,256]{1,0:T(8,128)S(1)}, f32[32,256]{1,0:T(8,128)S(1)}, u32[]{:S(2)}, u32[]{:S(2)}) collective-permute-start(f32[32,256]{1,0:T(8,128)S(1)} %get-tuple-element.43), channel_id=1, source_target_pairs={{0,4},{1,5},{2,6},{3,7},{4,0},{5,1},{6,2},{7,3},{8,12},{9,13},{10,... | collective-permute-start | bytes 98312 | tf_op jit(solution)/shard_map/ppermute | solution.py:174
  21.4 1.3 %collective-permute-done.8.refs_2_ = f32[32,256]{1,0:T(8,128)S(1)} collective-permute-done((f32[32,256]{1,0:T(8,128)S(1)}, f32[32,256]{1,0:T(8,128)S(1)}, u32[]{:S(2)}, u32[]{:S(2)}) %collective-permute-start.8) | collective-permute-done | bytes 32800 | tf_op jit(solution)/shard_map/ppermute | solution.py:174
  22.6 0.8 %collective-permute-done.9.refs_3_ = f32[32,256]{1,0:T(8,128)S(1)} collective-permute-done((f32[32,256]{1,0:T(8,128)S(1)}, f32[32,256]{1,0:T(8,128)S(1)}, u32[]{:S(2)}, u32[]{:S(2)}) %collective-permute-start.9) | collective-permute-done | bytes 32800 | tf_op jit(solution)/shard_map/ppermute | solution.py:174
  23.4 0.8 %shard_map.70 = (f32[32,256]{1,0:T(8,128)}, f32[32,256]{1,0:T(8,128)}) custom-call(bf16[32,1024]{1,0:T(8,128)(2,1)S(1)} %get-tuple-element.39.q_ref, f32[40,256]{1,0:T(8,128)S(1)} %get-tuple-element.24.refs_0_.refs_5_.near_ref, f32[32,32]{1,0:T(8,128)S(1)} %get-tuple-element.33.refs_4_.compat_ref, f32[32,256]{1,0:T(8,128)S(1)} %get-tuple-element.42.refs_0_, ...), custom_call_target="tpu_custom_call" | custom-call | flops 10000000000 | bytes 10000000000 | tf_op jit(solution)/shard_map/pallas_call | solution.py:198
  (8 shorter events, 0.1 us)
Async XLA Ops:
  1.7 6.5 %collective-permute-start = (f32[40,256]{1,0:T(8,128)S(1)}, f32[40,256]{1,0:T(8,128)S(1)}, u32[]{:S(2)}, u32[]{:S(2)}) collective-permute-start(f32[40,256]{1,0:T(8,128)S(1)} %get-tuple-element.24.refs_0_.refs_5_.near_ref), channel_id=1, source_target_pairs={{0,2},{1,3},{2,0},{3,1},{4,6},{5,7},{6,4},{7,5},{8,10},{9,11},{10,... | collective-permute-start | bytes 122888 | tf_op jit(solution)/shard_map/ppermute | solution.py:174
  5.8 5.6 %collective-permute-start.2 = (f32[40,256]{1,0:T(8,128)S(1)}, f32[40,256]{1,0:T(8,128)S(1)}, u32[]{:S(2)}, u32[]{:S(2)}) collective-permute-start(f32[40,256]{1,0:T(8,128)S(1)} %get-tuple-element.24.refs_0_.refs_5_.near_ref), channel_id=1, source_target_pairs={{0,7},{1,6},{2,5},{3,4},{4,3},{5,2},{6,1},{7,0},{8,15},{9,14},{10,... | collective-permute-start | bytes 122888 | tf_op jit(solution)/shard_map/ppermute | solution.py:174
  6.3 5.1 %collective-permute-start.1 = (f32[40,256]{1,0:T(8,128)S(1)}, f32[40,256]{1,0:T(8,128)S(1)}, u32[]{:S(2)}, u32[]{:S(2)}) collective-permute-start(f32[40,256]{1,0:T(8,128)S(1)} %get-tuple-element.24.refs_0_.refs_5_.near_ref), channel_id=1, source_target_pairs={{0,5},{1,4},{2,7},{3,6},{4,1},{5,0},{6,3},{7,2},{8,13},{9,12},{10,... | collective-permute-start | bytes 122888 | tf_op jit(solution)/shard_map/ppermute | solution.py:174
  8.3 7.2 %collective-permute-start.3 = (bf16[2,40,256]{2,1,0:T(8,128)(2,1)S(1)}, bf16[2,40,256]{2,1,0:T(8,128)(2,1)S(1)}, u32[]{:S(2)}, u32[]{:S(2)}) collective-permute-start(bf16[2,40,256]{2,1,0:T(8,128)(2,1)S(1)} %get-tuple-element.27.refs_0_.refs_2_.refs_9_), channel_id=1, source_target_pairs={{0,12},{1,13},{2,14},{3,15},{4,8},{5,9},{6,10},{7,11},{8,4},{9,5},... | collective-permute-start | bytes 122888 | tf_op jit(solution)/shard_map/ppermute | solution.py:174
  11.4 4.0 %collective-permute-start.4 = (bf16[2,40,256]{2,1,0:T(8,128)(2,1)S(1)}, bf16[2,40,256]{2,1,0:T(8,128)(2,1)S(1)}, u32[]{:S(2)}, u32[]{:S(2)}) collective-permute-start(bf16[2,40,256]{2,1,0:T(8,128)(2,1)S(1)} %get-tuple-element.28.refs_1_.refs_3_.refs_10_), channel_id=1, source_target_pairs={{0,12},{1,13},{2,14},{3,15},{4,8},{5,9},{6,10},{7,11},{8,4},{9,5},... | collective-permute-start | bytes 122888 | tf_op jit(solution)/shard_map/ppermute | solution.py:174
  13.1 1.3 %collective-permute-start.5 = (bf16[4,40,256]{2,1,0:T(8,128)(2,1)S(1)}, bf16[4,40,256]{2,1,0:T(8,128)(2,1)S(1)}, u32[]{:S(2)}, u32[]{:S(2)}) collective-permute-start(bf16[4,40,256]{2,1,0:T(8,128)(2,1)S(1)} %shard_map.62), channel_id=1, source_target_pairs={{0,4},{1,5},{2,6},{3,7},{4,0},{5,1},{6,2},{7,3},{8,12},{9,13},{10,... | collective-permute-start | bytes 245768 | tf_op jit(solution)/shard_map/ppermute | solution.py:174
  15.4 1.4 %collective-permute-start.6 = (bf16[4,40,256]{2,1,0:T(8,128)(2,1)S(1)}, bf16[4,40,256]{2,1,0:T(8,128)(2,1)S(1)}, u32[]{:S(2)}, u32[]{:S(2)}) collective-permute-start(bf16[4,40,256]{2,1,0:T(8,128)(2,1)S(1)} %shard_map.65), channel_id=1, source_target_pairs={{0,4},{1,5},{2,6},{3,7},{4,0},{5,1},{6,2},{7,3},{8,12},{9,13},{10,... | collective-permute-start | bytes 245768 | tf_op jit(solution)/shard_map/ppermute | solution.py:174
  18.6 4.0 %collective-permute-start.8 = (f32[32,256]{1,0:T(8,128)S(1)}, f32[32,256]{1,0:T(8,128)S(1)}, u32[]{:S(2)}, u32[]{:S(2)}) collective-permute-start(f32[32,256]{1,0:T(8,128)S(1)} %get-tuple-element.44), channel_id=1, source_target_pairs={{0,8},{1,9},{2,10},{3,11},{4,12},{5,13},{6,14},{7,15},{8,0},{9,1},... | collective-permute-start | bytes 98312 | tf_op jit(solution)/shard_map/ppermute | solution.py:174
  19.8 3.6 %collective-permute-start.9 = (f32[32,256]{1,0:T(8,128)S(1)}, f32[32,256]{1,0:T(8,128)S(1)}, u32[]{:S(2)}, u32[]{:S(2)}) collective-permute-start(f32[32,256]{1,0:T(8,128)S(1)} %get-tuple-element.45), channel_id=1, source_target_pairs={{0,12},{1,13},{2,14},{3,15},{4,8},{5,9},{6,10},{7,11},{8,4},{9,5},... | collective-permute-start | bytes 98312 | tf_op jit(solution)/shard_map/ppermute | solution.py:174
  20.7 2.7 %collective-permute-start.7 = (f32[32,256]{1,0:T(8,128)S(1)}, f32[32,256]{1,0:T(8,128)S(1)}, u32[]{:S(2)}, u32[]{:S(2)}) collective-permute-start(f32[32,256]{1,0:T(8,128)S(1)} %get-tuple-element.43), channel_id=1, source_target_pairs={{0,4},{1,5},{2,6},{3,7},{4,0},{5,1},{6,2},{7,3},{8,12},{9,13},{10,... | collective-permute-start | bytes 98312 | tf_op jit(solution)/shard_map/ppermute | solution.py:174

commit v20 on v19

--- a/solution.py
+++ b/solution.py
@@ -139,13 +139,27 @@
     q_ref[...] = probs.astype(jnp.bfloat16)
 
 
+def partial_message(q_ref, tile_ref):
+    return lax.dot_general(
+        q_ref[...], tile_ref[...], (((1,), (1,)), ((), ())), preferred_element_type=jnp.float32
+    )
+
+
 def second_parts(q_ref, *refs):
     count = len(refs) // 2
     for tile_ref, part_ref in zip(refs[:count], refs[count:]):
-        part_ref[...] = lax.dot_general(
-            tile_ref[...], q_ref[...], (((1,), (1,)), ((), ())),
-            preferred_element_type=jnp.float32,
-        ).T
+        part_ref[...] = partial_message(q_ref, tile_ref)
+
+
+def second_stacked(q_ref, *refs):
+    for index, tile_ref in enumerate(refs[:-1]):
+        refs[-1][index] = partial_message(q_ref, tile_ref)
+
+
+def second_sums(given_ref, *refs):
+    count = len(refs) // 2
+    for index in range(count):
+        refs[count + index][...] = refs[index][...] + given_ref[index + 1]
 
 
 def second_closing(q_ref, near_ref, compat_ref, *refs):
@@ -153,7 +167,7 @@
     labels, own = probs_ref.shape
     total = refs[0][...]
     for part_ref in refs[1:-2]:
-        total = total + part_ref[...]
+        total = total + (part_ref[0] if len(part_ref.shape) == 3 else part_ref[...])
     unary = near_ref[pl.ds(0, labels), :]
     probs, pairwise = finish(total, q_ref[:, pl.ds(0, own)], unary, compat_ref)
     probs_ref[...] = probs
@@ -184,10 +198,6 @@
 def paired(axis):
     count = lax.axis_size(axis)
     return count & (count - 1) == 0
-
-
-def send_back(value, steps):
-    return swap(value, steps if paired("blk") else lax.axis_size("blk") - steps)
 
 
 def small(dims, kind):
@@ -287,12 +297,27 @@
     if parts * math.prod(tile_kind.shape) * 2 <= KEPT_BYTES:
         tiles = hold(*tiles)
     part_kind = kept((labels, own), jnp.float32)
-    far = call(second_parts, [part_kind] * (parts - 2), *hold(q_near), *tiles[2:])
-    if far:
-        q_near, *far = lax.optimization_barrier((q_near, *far))
-    here, beside = call(second_parts, [part_kind] * 2, *hold(q_near), *tiles[:2])
-    sent_parts = dict(zip(steps[1:], [beside, *far]))
-    arrived = [send_back(sent_parts[step], step) for step in range(1, parts)]
+    tile_of = dict(zip(steps, tiles))
+    if paired("blk"):
+        even = [1] + list(range(2, parts, 2))
+        odd = list(range(3, parts, 2))
+        (stacked,) = call(
+            second_stacked, [kept((len(even), labels, own), jnp.float32)],
+            *hold(q_near), *[tile_of[step] for step in even],
+        )
+        q_near, stacked = lax.optimization_barrier((q_near, stacked))
+        here, *mine = call(
+            second_parts, [part_kind] * (1 + len(odd)),
+            *hold(q_near), *[tile_of[step] for step in [0] + odd],
+        )
+        given = swap(stacked, 1)
+        sums = call(second_sums, [part_kind] * len(odd), *hold(given, *mine))
+        arrived = [given] + [swap(part, step) for part, step in zip(sums, odd)]
+    else:
+        here, *away = call(
+            second_parts, [part_kind] * parts, *hold(q_near), *[tile_of[step] for step in steps]
+        )
+        arrived = [swap(part, parts - step) for part, step in zip(away, steps[1:])]
     return call(
         second_closing,
         [jax.ShapeDtypeStruct((labels, own), jnp.float32)] * 2,

time: 24.4 us -> 24.2 us (level)
  starting transfers between devices: 9.64 us -> 8.57 us
  waiting for transfers between devices: 6.62 us -> 7.55 us
    ppermute x10 -> x9, starting transfers between devices: 9.64 us -> 8.57 us  [swap(): return lax.ppermute(value, ('blk', 'grp'), pairs)]
    ppermute x10 -> x9, waiting for transfers between devices: 6.62 us -> 7.55 us  [swap(): return lax.ppermute(value, ('blk', 'grp'), pairs)]
    pallas_call x12 -> x13, Pallas kernels: 7.3 us -> 7.18 us  [call(): pl.pallas_call(kernel, out_shape=tuple(out_shapes), cost_estimate=pl.Cost...]
  transfers between devices with their start and end apart: 10 -> 9, of which waited for: 5 -> 5; matrix products, arithmetic and copies ran while one was open for 0% -> 0% of each run, Pallas kernels for 15% -> 15%
where the time goes in v20:
time: 24.2 us; the launch traced here: 24 us
  starting transfers between devices  8.57 us (35%)
  waiting for transfers between devices  7.55 us (31%)
  Pallas kernels  7.18 us (30%)
  between operations  0.7 us (3%)
    ppermute x9, starting transfers between devices, swap(): return lax.ppermute(value, ('blk', 'grp'), pairs)  8.57 us
    ppermute x9, waiting for transfers between devices, swap(): return lax.ppermute(value, ('blk', 'grp'), pairs)  7.55 us
    pallas_call x13, Pallas kernels, call(): pl.pallas_call(kernel, out_shape=tuple(out_shapes), cost_estimate=pl.Cost...  7.18 us
  transfers between devices with their start and end apart: 9, of which 5 were waited for; matrix products, arithmetic and copies ran while one was open for 0% of the time, Pallas kernels for 15%

profile of v20, /device:TPU:0, one launch (start us, length us, event | category | flops | bytes accessed | tf_op | source)
XLA Modules:
  0.0 24.0 jit_solution(13516296858642938976)
XLA Ops:
  0.6 1.1 %shard_map.59 = (f32[40,256]{1,0:T(8,128)S(1)}, f32[32,32]{1,0:T(8,128)S(1)}) custom-call(bf16[6,4096]{1,0:T(8,128)(2,1)} %features_ref.1, s32[1,256]{1,0:T(1,128)} %bitcast.1, f32[32,256]{1,0:T(8,128)} %unary_ref.1, f32[32,32]{1,0:T(8,128)} %compat_ref.1), custom_call_target="tpu_custom_call" | custom-call | flops 10000000000 | bytes 10000000000 | tf_op jit(solution)/shard_map/pallas_call | solution.py:208
  1.7 4.1 %collective-permute-start = (f32[40,256]{1,0:T(8,128)S(1)}, f32[40,256]{1,0:T(8,128)S(1)}, u32[]{:S(2)}, u32[]{:S(2)}) collective-permute-start(f32[40,256]{1,0:T(8,128)S(1)} %get-tuple-element.21.refs_0_.refs_5_.near_ref), channel_id=1, source_target_pairs={{0,2},{1,3},{2,0},{3,1},{4,6},{5,7},{6,4},{7,5},{8,10},{9,11},{10,... | collective-permute-start | bytes 122888 | tf_op jit(solution)/shard_map/ppermute | solution.py:188
  5.8 0.5 %collective-permute-start.2 = (f32[40,256]{1,0:T(8,128)S(1)}, f32[40,256]{1,0:T(8,128)S(1)}, u32[]{:S(2)}, u32[]{:S(2)}) collective-permute-start(f32[40,256]{1,0:T(8,128)S(1)} %get-tuple-element.21.refs_0_.refs_5_.near_ref), channel_id=1, source_target_pairs={{0,7},{1,6},{2,5},{3,4},{4,3},{5,2},{6,1},{7,0},{8,15},{9,14},{10,... | collective-permute-start | bytes 122888 | tf_op jit(solution)/shard_map/ppermute | solution.py:188
  6.3 0.2 collective-permute-start.1
  6.5 1.7 %collective-permute-done.refs_1_.refs_6_ = f32[40,256]{1,0:T(8,128)S(1)} collective-permute-done((f32[40,256]{1,0:T(8,128)S(1)}, f32[40,256]{1,0:T(8,128)S(1)}, u32[]{:S(2)}, u32[]{:S(2)}) %collective-permute-start) | collective-permute-done | bytes 40992 | tf_op jit(solution)/shard_map/ppermute | solution.py:188
  8.3 0.5 %collective-permute-start.3 = (bf16[2,40,256]{2,1,0:T(8,128)(2,1)S(1)}, bf16[2,40,256]{2,1,0:T(8,128)(2,1)S(1)}, u32[]{:S(2)}, u32[]{:S(2)}) collective-permute-start(bf16[2,40,256]{2,1,0:T(8,128)(2,1)S(1)} %get-tuple-element.24.refs_0_.refs_2_.refs_9_), channel_id=1, source_target_pairs={{0,12},{1,13},{2,14},{3,15},{4,8},{5,9},{6,10},{7,11},{8,4},{9,5},... | collective-permute-start | bytes 122888 | tf_op jit(solution)/shard_map/ppermute | solution.py:188
  8.7 2.7 %collective-permute-done.2.refs_1_.refs_8_ = f32[40,256]{1,0:T(8,128)S(1)} collective-permute-done((f32[40,256]{1,0:T(8,128)S(1)}, f32[40,256]{1,0:T(8,128)S(1)}, u32[]{:S(2)}, u32[]{:S(2)}) %collective-permute-start.2) | collective-permute-done | bytes 40992 | tf_op jit(solution)/shard_map/ppermute | solution.py:188
  11.4 1.6 %collective-permute-start.4 = (bf16[2,40,256]{2,1,0:T(8,128)(2,1)S(1)}, bf16[2,40,256]{2,1,0:T(8,128)(2,1)S(1)}, u32[]{:S(2)}, u32[]{:S(2)}) collective-permute-start(bf16[2,40,256]{2,1,0:T(8,128)(2,1)S(1)} %get-tuple-element.25.refs_1_.refs_3_.refs_10_), channel_id=1, source_target_pairs={{0,12},{1,13},{2,14},{3,15},{4,8},{5,9},{6,10},{7,11},{8,4},{9,5},... | collective-permute-start | bytes 122888 | tf_op jit(solution)/shard_map/ppermute | solution.py:188
  13.1 0.1 collective-permute-start.5
  13.1 1.1 %shard_map.63 = (f32[32,1024]{1,0:T(8,128)S(1)}, bf16[256,1024]{1,0:T(8,128)(2,1)S(1)}) custom-call(bf16[16,512]{1,0:T(8,128)(2,1)S(1)} %get-tuple-element.22.refs_0_, bf16[16,512]{1,0:T(8,128)(2,1)S(1)} %get-tuple-element.23.refs_1_, bf16[2,40,256]{2,1,0:T(8,128)(2,1)S(1)} %get-tuple-element.24.refs_0_.refs_2_.refs_9_, ...), custom_call_target="tpu_custom_call" | custom-call | flops 10000000000 | bytes 10000000000 | tf_op jit(solution)/shard_map/pallas_call | solution.py:208
  14.2 0.2 collective-permute-done.5.refs_2_
  14.4 1.0 %shard_map.64 = (f32[32,1024]{1,0:T(8,128)S(1)}, bf16[256,1024]{1,0:T(8,128)(2,1)S(1)}) custom-call(bf16[16,512]{1,0:T(8,128)(2,1)S(1)} %get-tuple-element.22.refs_0_, bf16[16,512]{1,0:T(8,128)(2,1)S(1)} %get-tuple-element.23.refs_1_, bf16[4,40,256]{2,1,0:T(8,128)(2,1)S(1)} %collective-permute-done.5.refs_2_, f32[32,1024]{1,0:T(8,128)S(1)} %get-tuple-element.26.refs_3_), custom_call_target="tpu_custom_call" | custom-call | flops 10000000000 | bytes 10000000000 | tf_op jit(solution)/shard_map/pallas_call | solution.py:208
  15.4 0.0 collective-permute-done.4.refs_1_.refs_3_
  15.4 0.4 %collective-permute-start.6 = (bf16[4,40,256]{2,1,0:T(8,128)(2,1)S(1)}, bf16[4,40,256]{2,1,0:T(8,128)(2,1)S(1)}, u32[]{:S(2)}, u32[]{:S(2)}) collective-permute-start(bf16[4,40,256]{2,1,0:T(8,128)(2,1)S(1)} %shard_map.65), channel_id=1, source_target_pairs={{0,4},{1,5},{2,6},{3,7},{4,0},{5,1},{6,2},{7,3},{8,12},{9,13},{10,... | collective-permute-start | bytes 245768 | tf_op jit(solution)/shard_map/ppermute | solution.py:188
  15.8 1.1 %shard_map.66 = (f32[32,1024]{1,0:T(8,128)S(1)}, bf16[256,1024]{1,0:T(8,128)(2,1)S(1)}) custom-call(bf16[16,512]{1,0:T(8,128)(2,1)S(1)} %get-tuple-element.22.refs_0_, bf16[16,512]{1,0:T(8,128)(2,1)S(1)} %get-tuple-element.23.refs_1_, bf16[2,40,256]{2,1,0:T(8,128)(2,1)S(1)} %collective-permute-done.3.refs_0_.refs_2_, ...), custom_call_target="tpu_custom_call" | custom-call | flops 10000000000 | bytes 10000000000 | tf_op jit(solution)/shard_map/pallas_call | solution.py:208
  16.9 0.0 collective-permute-done.6.refs_2_
  16.9 1.3 %shard_map.67 = (bf16[32,1024]{1,0:T(8,128)(2,1)S(1)}, bf16[256,1024]{1,0:T(8,128)(2,1)S(1)}) custom-call(bf16[16,512]{1,0:T(8,128)(2,1)S(1)} %get-tuple-element.22.refs_0_, bf16[16,512]{1,0:T(8,128)(2,1)S(1)} %get-tuple-element.23.refs_1_, bf16[4,40,256]{2,1,0:T(8,128)(2,1)S(1)} %collective-permute-done.6.refs_2_, ...), custom_call_target="tpu_custom_call" | custom-call | flops 10000000000 | bytes 10000000000 | tf_op jit(solution)/shard_map/pallas_call | solution.py:208
  18.2 0.4 %shard_map.68 = f32[2,32,256]{2,1,0:T(8,128)S(1)} custom-call(bf16[32,1024]{1,0:T(8,128)(2,1)S(1)} %get-tuple-element.34.q_ref, bf16[256,1024]{1,0:T(8,128)(2,1)S(1)} %get-tuple-element.32.refs_0_, bf16[256,1024]{1,0:T(8,128)(2,1)S(1)} %get-tuple-element.33.refs_1_), custom_call_target="tpu_custom_call" | custom-call | flops 10000000000 | bytes 10000000000 | tf_op jit(solution)/shard_map/pallas_call | solution.py:208
  18.6 0.2 collective-permute-start.7
  18.8 0.4 %shard_map.69 = (f32[32,256]{1,0:T(8,128)S(1)}, f32[32,256]{1,0:T(8,128)S(1)}) custom-call(bf16[32,1024]{1,0:T(8,128)(2,1)S(1)} %get-tuple-element.34.q_ref, bf16[256,1024]{1,0:T(8,128)(2,1)S(1)} %get-tuple-element.35.refs_0_, bf16[256,1024]{1,0:T(8,128)(2,1)S(1)} %get-tuple-element.36.refs_1_), custom_call_target="tpu_custom_call" | custom-call | flops 10000000000 | bytes 10000000000 | tf_op jit(solution)/shard_map/pallas_call | solution.py:208
  19.2 0.6 %collective-permute-done.7.given_ref.refs_1_ = f32[2,32,256]{2,1,0:T(8,128)S(1)} collective-permute-done((f32[2,32,256]{2,1,0:T(8,128)S(1)}, f32[2,32,256]{2,1,0:T(8,128)S(1)}, u32[]{:S(2)}, u32[]{:S(2)}) %collective-permute-start.7) | collective-permute-done | bytes 65568 | tf_op jit(solution)/shard_map/ppermute | solution.py:188
  19.8 1.0 %collective-permute-start.8 = (f32[32,256]{1,0:T(8,128)S(1)}, f32[32,256]{1,0:T(8,128)S(1)}, u32[]{:S(2)}, u32[]{:S(2)}) collective-permute-start(f32[32,256]{1,0:T(8,128)S(1)} %shard_map.70), channel_id=1, source_target_pairs={{0,12},{1,13},{2,14},{3,15},{4,8},{5,9},{6,10},{7,11},{8,4},{9,5},... | collective-permute-start | bytes 98312 | tf_op jit(solution)/shard_map/ppermute | solution.py:188
  20.8 2.4 %collective-permute-done.8.refs_2_ = f32[32,256]{1,0:T(8,128)S(1)} collective-permute-done((f32[32,256]{1,0:T(8,128)S(1)}, f32[32,256]{1,0:T(8,128)S(1)}, u32[]{:S(2)}, u32[]{:S(2)}) %collective-permute-start.8) | collective-permute-done | bytes 32800 | tf_op jit(solution)/shard_map/ppermute | solution.py:188
  23.2 0.8 %shard_map.71 = (f32[32,256]{1,0:T(8,128)}, f32[32,256]{1,0:T(8,128)}) custom-call(bf16[32,1024]{1,0:T(8,128)(2,1)S(1)} %get-tuple-element.34.q_ref, f32[40,256]{1,0:T(8,128)S(1)} %get-tuple-element.21.refs_0_.refs_5_.near_ref, f32[32,32]{1,0:T(8,128)S(1)} %get-tuple-element.30.refs_4_.compat_ref, f32[32,256]{1,0:T(8,128)S(1)} %get-tuple-element.37.refs_0_, ...), custom_call_target="tpu_custom_call" | custom-call | flops 10000000000 | bytes 10000000000 | tf_op jit(solution)/shard_map/pallas_call | solution.py:208
  (7 shorter events, 0.1 us)
Async XLA Ops:
  1.7 6.5 %collective-permute-start = (f32[40,256]{1,0:T(8,128)S(1)}, f32[40,256]{1,0:T(8,128)S(1)}, u32[]{:S(2)}, u32[]{:S(2)}) collective-permute-start(f32[40,256]{1,0:T(8,128)S(1)} %get-tuple-element.21.refs_0_.refs_5_.near_ref), channel_id=1, source_target_pairs={{0,2},{1,3},{2,0},{3,1},{4,6},{5,7},{6,4},{7,5},{8,10},{9,11},{10,... | collective-permute-start | bytes 122888 | tf_op jit(solution)/shard_map/ppermute | solution.py:188
  5.8 5.6 %collective-permute-start.2 = (f32[40,256]{1,0:T(8,128)S(1)}, f32[40,256]{1,0:T(8,128)S(1)}, u32[]{:S(2)}, u32[]{:S(2)}) collective-permute-start(f32[40,256]{1,0:T(8,128)S(1)} %get-tuple-element.21.refs_0_.refs_5_.near_ref), channel_id=1, source_target_pairs={{0,7},{1,6},{2,5},{3,4},{4,3},{5,2},{6,1},{7,0},{8,15},{9,14},{10,... | collective-permute-start | bytes 122888 | tf_op jit(solution)/shard_map/ppermute | solution.py:188
  6.3 5.1 %collective-permute-start.1 = (f32[40,256]{1,0:T(8,128)S(1)}, f32[40,256]{1,0:T(8,128)S(1)}, u32[]{:S(2)}, u32[]{:S(2)}) collective-permute-start(f32[40,256]{1,0:T(8,128)S(1)} %get-tuple-element.21.refs_0_.refs_5_.near_ref), channel_id=1, source_target_pairs={{0,5},{1,4},{2,7},{3,6},{4,1},{5,0},{6,3},{7,2},{8,13},{9,12},{10,... | collective-permute-start | bytes 122888 | tf_op jit(solution)/shard_map/ppermute | solution.py:188
  8.3 7.2 %collective-permute-start.3 = (bf16[2,40,256]{2,1,0:T(8,128)(2,1)S(1)}, bf16[2,40,256]{2,1,0:T(8,128)(2,1)S(1)}, u32[]{:S(2)}, u32[]{:S(2)}) collective-permute-start(bf16[2,40,256]{2,1,0:T(8,128)(2,1)S(1)} %get-tuple-element.24.refs_0_.refs_2_.refs_9_), channel_id=1, source_target_pairs={{0,12},{1,13},{2,14},{3,15},{4,8},{5,9},{6,10},{7,11},{8,4},{9,5},... | collective-permute-start | bytes 122888 | tf_op jit(solution)/shard_map/ppermute | solution.py:188
  11.4 4.0 %collective-permute-start.4 = (bf16[2,40,256]{2,1,0:T(8,128)(2,1)S(1)}, bf16[2,40,256]{2,1,0:T(8,128)(2,1)S(1)}, u32[]{:S(2)}, u32[]{:S(2)}) collective-permute-start(bf16[2,40,256]{2,1,0:T(8,128)(2,1)S(1)} %get-tuple-element.25.refs_1_.refs_3_.refs_10_), channel_id=1, source_target_pairs={{0,12},{1,13},{2,14},{3,15},{4,8},{5,9},{6,10},{7,11},{8,4},{9,5},... | collective-permute-start | bytes 122888 | tf_op jit(solution)/shard_map/ppermute | solution.py:188
  13.1 1.3 %collective-permute-start.5 = (bf16[4,40,256]{2,1,0:T(8,128)(2,1)S(1)}, bf16[4,40,256]{2,1,0:T(8,128)(2,1)S(1)}, u32[]{:S(2)}, u32[]{:S(2)}) collective-permute-start(bf16[4,40,256]{2,1,0:T(8,128)(2,1)S(1)} %shard_map.62), channel_id=1, source_target_pairs={{0,4},{1,5},{2,6},{3,7},{4,0},{5,1},{6,2},{7,3},{8,12},{9,13},{10,... | collective-permute-start | bytes 245768 | tf_op jit(solution)/shard_map/ppermute | solution.py:188
  15.4 1.4 %collective-permute-start.6 = (bf16[4,40,256]{2,1,0:T(8,128)(2,1)S(1)}, bf16[4,40,256]{2,1,0:T(8,128)(2,1)S(1)}, u32[]{:S(2)}, u32[]{:S(2)}) collective-permute-start(bf16[4,40,256]{2,1,0:T(8,128)(2,1)S(1)} %shard_map.65), channel_id=1, source_target_pairs={{0,4},{1,5},{2,6},{3,7},{4,0},{5,1},{6,2},{7,3},{8,12},{9,13},{10,... | collective-permute-start | bytes 245768 | tf_op jit(solution)/shard_map/ppermute | solution.py:188
  18.6 1.3 %collective-permute-start.7 = (f32[2,32,256]{2,1,0:T(8,128)S(1)}, f32[2,32,256]{2,1,0:T(8,128)S(1)}, u32[]{:S(2)}, u32[]{:S(2)}) collective-permute-start(f32[2,32,256]{2,1,0:T(8,128)S(1)} %shard_map.68), channel_id=1, source_target_pairs={{0,4},{1,5},{2,6},{3,7},{4,0},{5,1},{6,2},{7,3},{8,12},{9,13},{10,... | collective-permute-start | bytes 196616 | tf_op jit(solution)/shard_map/ppermute | solution.py:188
  19.8 3.3 %collective-permute-start.8 = (f32[32,256]{1,0:T(8,128)S(1)}, f32[32,256]{1,0:T(8,128)S(1)}, u32[]{:S(2)}, u32[]{:S(2)}) collective-permute-start(f32[32,256]{1,0:T(8,128)S(1)} %shard_map.70), channel_id=1, source_target_pairs={{0,12},{1,13},{2,14},{3,15},{4,8},{5,9},{6,10},{7,11},{8,4},{9,5},... | collective-permute-start | bytes 98312 | tf_op jit(solution)/shard_map/ppermute | solution.py:188

commit v21 on v18

--- a/solution.py
+++ b/solution.py
@@ -178,7 +178,9 @@
     count = lax.axis_size("grp")
     order = sorted(range(1, count), key=lambda steps: (steps != count // 2, steps))
     crossed = paired("blk") and paired("grp") and lax.axis_size("blk") > 1
-    return [value] + [swap(value, steps % 2 if crossed else 0, steps) for steps in order]
+    return [value] + [
+        swap(value, 2 * steps // count if crossed else 0, steps) for steps in order
+    ]
 
 
 def paired(axis):

time: 24.3 us -> 24.2 us (level)
  waiting for transfers between devices: 6.71 us -> 4.98 us
  starting transfers between devices: 9.56 us -> 11.2 us
    ppermute x10, waiting for transfers between devices: 6.71 us -> 4.98 us  [swap(): return lax.ppermute(value, ('blk', 'grp'), pairs)]
    ppermute x10, starting transfers between devices: 9.56 us -> 11.2 us  [swap(): return lax.ppermute(value, ('blk', 'grp'), pairs)]
where the time goes in v21:
time: 24.2 us; the launch traced here: 24 us
  starting transfers between devices  11.2 us (46%)
  Pallas kernels  7.18 us (30%)
  waiting for transfers between devices  4.98 us (21%)
  between operations  0.69 us (3%)
    ppermute x10, starting transfers between devices, swap(): return lax.ppermute(value, ('blk', 'grp'), pairs)  11.2 us
    pallas_call x12, Pallas kernels, call(): pl.pallas_call(kernel, out_shape=tuple(out_shapes), cost_estimate=pl.Cost...  7.18 us
    ppermute x10, waiting for transfers between devices, swap(): return lax.ppermute(value, ('blk', 'grp'), pairs)  4.98 us
  transfers between devices with their start and end apart: 10, of which 5 were waited for; matrix products, arithmetic and copies ran while one was open for 0% of the time, Pallas kernels for 15%

profile of v21, /device:TPU:0, one launch (start us, length us, event | category | flops | bytes accessed | tf_op | source)
XLA Modules:
  0.0 24.0 jit_solution(12307117112940747061)
XLA Ops:
  0.6 1.1 %shard_map.59 = (f32[40,256]{1,0:T(8,128)S(1)}, f32[32,32]{1,0:T(8,128)S(1)}) custom-call(bf16[6,4096]{1,0:T(8,128)(2,1)} %features_ref.1, s32[1,256]{1,0:T(1,128)} %bitcast.1, f32[32,256]{1,0:T(8,128)} %unary_ref.1, f32[32,32]{1,0:T(8,128)} %compat_ref.1), custom_call_target="tpu_custom_call" | custom-call | flops 10000000000 | bytes 10000000000 | tf_op jit(solution)/shard_map/pallas_call | solution.py:200
  1.7 3.5 %collective-permute-start = (f32[40,256]{1,0:T(8,128)S(1)}, f32[40,256]{1,0:T(8,128)S(1)}, u32[]{:S(2)}, u32[]{:S(2)}) collective-permute-start(f32[40,256]{1,0:T(8,128)S(1)} %get-tuple-element.24.refs_0_.refs_5_.near_ref), channel_id=1, source_target_pairs={{0,6},{1,7},{2,4},{3,5},{4,2},{5,3},{6,0},{7,1},{8,14},{9,15},{10,... | collective-permute-start | bytes 122888 | tf_op jit(solution)/shard_map/ppermute | solution.py:174
  5.2 1.6 %collective-permute-start.2 = (f32[40,256]{1,0:T(8,128)S(1)}, f32[40,256]{1,0:T(8,128)S(1)}, u32[]{:S(2)}, u32[]{:S(2)}) collective-permute-start(f32[40,256]{1,0:T(8,128)S(1)} %get-tuple-element.24.refs_0_.refs_5_.near_ref), channel_id=1, source_target_pairs={{0,7},{1,6},{2,5},{3,4},{4,3},{5,2},{6,1},{7,0},{8,15},{9,14},{10,... | collective-permute-start | bytes 122888 | tf_op jit(solution)/shard_map/ppermute | solution.py:174
  6.9 0.3 %collective-permute-done.refs_1_.refs_6_ = f32[40,256]{1,0:T(8,128)S(1)} collective-permute-done((f32[40,256]{1,0:T(8,128)S(1)}, f32[40,256]{1,0:T(8,128)S(1)}, u32[]{:S(2)}, u32[]{:S(2)}) %collective-permute-start) | collective-permute-done | bytes 40992 | tf_op jit(solution)/shard_map/ppermute | solution.py:174
  7.2 1.8 %collective-permute-start.3 = (bf16[2,40,256]{2,1,0:T(8,128)(2,1)S(1)}, bf16[2,40,256]{2,1,0:T(8,128)(2,1)S(1)}, u32[]{:S(2)}, u32[]{:S(2)}) collective-permute-start(bf16[2,40,256]{2,1,0:T(8,128)(2,1)S(1)} %get-tuple-element.27.refs_0_.refs_2_.refs_9_), channel_id=1, source_target_pairs={{0,12},{1,13},{2,14},{3,15},{4,8},{5,9},{6,10},{7,11},{8,4},{9,5},... | collective-permute-start | bytes 122888 | tf_op jit(solution)/shard_map/ppermute | solution.py:174
  9.1 1.4 %collective-permute-done.2.refs_1_.refs_8_ = f32[40,256]{1,0:T(8,128)S(1)} collective-permute-done((f32[40,256]{1,0:T(8,128)S(1)}, f32[40,256]{1,0:T(8,128)S(1)}, u32[]{:S(2)}, u32[]{:S(2)}) %collective-permute-start.2) | collective-permute-done | bytes 40992 | tf_op jit(solution)/shard_map/ppermute | solution.py:174
  10.5 0.8 %collective-permute-done.1.refs_0_.refs_7_ = f32[40,256]{1,0:T(8,128)S(1)} collective-permute-done((f32[40,256]{1,0:T(8,128)S(1)}, f32[40,256]{1,0:T(8,128)S(1)}, u32[]{:S(2)}, u32[]{:S(2)}) %collective-permute-start.1) | collective-permute-done | bytes 40992 | tf_op jit(solution)/shard_map/ppermute | solution.py:174
  11.3 1.1 %collective-permute-start.4 = (bf16[2,40,256]{2,1,0:T(8,128)(2,1)S(1)}, bf16[2,40,256]{2,1,0:T(8,128)(2,1)S(1)}, u32[]{:S(2)}, u32[]{:S(2)}) collective-permute-start(bf16[2,40,256]{2,1,0:T(8,128)(2,1)S(1)} %get-tuple-element.28.refs_1_.refs_3_.refs_10_), channel_id=1, source_target_pairs={{0,12},{1,13},{2,14},{3,15},{4,8},{5,9},{6,10},{7,11},{8,4},{9,5},... | collective-permute-start | bytes 122888 | tf_op jit(solution)/shard_map/ppermute | solution.py:174
  12.4 0.6 %collective-permute-start.5 = (bf16[4,40,256]{2,1,0:T(8,128)(2,1)S(1)}, bf16[4,40,256]{2,1,0:T(8,128)(2,1)S(1)}, u32[]{:S(2)}, u32[]{:S(2)}) collective-permute-start(bf16[4,40,256]{2,1,0:T(8,128)(2,1)S(1)} %shard_map.62), channel_id=1, source_target_pairs={{0,4},{1,5},{2,6},{3,7},{4,0},{5,1},{6,2},{7,3},{8,12},{9,13},{10,... | collective-permute-start | bytes 245768 | tf_op jit(solution)/shard_map/ppermute | solution.py:174
  13.0 1.1 %shard_map.63 = (f32[32,1024]{1,0:T(8,128)S(1)}, bf16[256,1024]{1,0:T(8,128)(2,1)S(1)}) custom-call(bf16[16,512]{1,0:T(8,128)(2,1)S(1)} %get-tuple-element.25.refs_0_, bf16[16,512]{1,0:T(8,128)(2,1)S(1)} %get-tuple-element.26.refs_1_, bf16[2,40,256]{2,1,0:T(8,128)(2,1)S(1)} %get-tuple-element.27.refs_0_.refs_2_.refs_9_, ...), custom_call_target="tpu_custom_call" | custom-call | flops 10000000000 | bytes 10000000000 | tf_op jit(solution)/shard_map/pallas_call | solution.py:200
  14.1 1.1 %shard_map.64 = (f32[32,1024]{1,0:T(8,128)S(1)}, bf16[256,1024]{1,0:T(8,128)(2,1)S(1)}) custom-call(bf16[16,512]{1,0:T(8,128)(2,1)S(1)} %get-tuple-element.25.refs_0_, bf16[16,512]{1,0:T(8,128)(2,1)S(1)} %get-tuple-element.26.refs_1_, bf16[4,40,256]{2,1,0:T(8,128)(2,1)S(1)} %collective-permute-done.5.refs_2_, f32[32,1024]{1,0:T(8,128)S(1)} %get-tuple-element.29.refs_3_), custom_call_target="tpu_custom_call" | custom-call | flops 10000000000 | bytes 10000000000 | tf_op jit(solution)/shard_map/pallas_call | solution.py:200
  15.1 0.0 collective-permute-done.4.refs_1_.refs_3_
  15.2 0.3 %collective-permute-start.6 = (bf16[4,40,256]{2,1,0:T(8,128)(2,1)S(1)}, bf16[4,40,256]{2,1,0:T(8,128)(2,1)S(1)}, u32[]{:S(2)}, u32[]{:S(2)}) collective-permute-start(bf16[4,40,256]{2,1,0:T(8,128)(2,1)S(1)} %shard_map.65), channel_id=1, source_target_pairs={{0,4},{1,5},{2,6},{3,7},{4,0},{5,1},{6,2},{7,3},{8,12},{9,13},{10,... | collective-permute-start | bytes 245768 | tf_op jit(solution)/shard_map/ppermute | solution.py:174
  15.5 1.1 %shard_map.66 = (f32[32,1024]{1,0:T(8,128)S(1)}, bf16[256,1024]{1,0:T(8,128)(2,1)S(1)}) custom-call(bf16[16,512]{1,0:T(8,128)(2,1)S(1)} %get-tuple-element.25.refs_0_, bf16[16,512]{1,0:T(8,128)(2,1)S(1)} %get-tuple-element.26.refs_1_, bf16[2,40,256]{2,1,0:T(8,128)(2,1)S(1)} %collective-permute-done.3.refs_0_.refs_2_, ...), custom_call_target="tpu_custom_call" | custom-call | flops 10000000000 | bytes 10000000000 | tf_op jit(solution)/shard_map/pallas_call | solution.py:200
  16.5 0.0 collective-permute-done.6.refs_2_
  16.5 1.3 %shard_map.67 = (bf16[32,1024]{1,0:T(8,128)(2,1)S(1)}, bf16[256,1024]{1,0:T(8,128)(2,1)S(1)}) custom-call(bf16[16,512]{1,0:T(8,128)(2,1)S(1)} %get-tuple-element.25.refs_0_, bf16[16,512]{1,0:T(8,128)(2,1)S(1)} %get-tuple-element.26.refs_1_, bf16[4,40,256]{2,1,0:T(8,128)(2,1)S(1)} %collective-permute-done.6.refs_2_, ...), custom_call_target="tpu_custom_call" | custom-call | flops 10000000000 | bytes 10000000000 | tf_op jit(solution)/shard_map/pallas_call | solution.py:200
  17.8 0.4 %shard_map.68 = (f32[32,256]{1,0:T(8,128)S(1)}, f32[32,256]{1,0:T(8,128)S(1)}) custom-call(bf16[32,1024]{1,0:T(8,128)(2,1)S(1)} %get-tuple-element.39.q_ref, bf16[256,1024]{1,0:T(8,128)(2,1)S(1)} %get-tuple-element.35.refs_0_, bf16[256,1024]{1,0:T(8,128)(2,1)S(1)} %get-tuple-element.36.refs_1_), custom_call_target="tpu_custom_call" | custom-call | flops 10000000000 | bytes 10000000000 | tf_op jit(solution)/shard_map/pallas_call | solution.py:200
  18.2 1.5 %collective-permute-start.8 = (f32[32,256]{1,0:T(8,128)S(1)}, f32[32,256]{1,0:T(8,128)S(1)}, u32[]{:S(2)}, u32[]{:S(2)}) collective-permute-start(f32[32,256]{1,0:T(8,128)S(1)} %get-tuple-element.44), channel_id=1, source_target_pairs={{0,8},{1,9},{2,10},{3,11},{4,12},{5,13},{6,14},{7,15},{8,0},{9,1},... | collective-permute-start | bytes 98312 | tf_op jit(solution)/shard_map/ppermute | solution.py:174
  19.7 0.2 collective-permute-start.9
  19.9 0.4 %shard_map.69 = (f32[32,256]{1,0:T(8,128)S(1)}, f32[32,256]{1,0:T(8,128)S(1)}) custom-call(bf16[32,1024]{1,0:T(8,128)(2,1)S(1)} %get-tuple-element.39.q_ref, bf16[256,1024]{1,0:T(8,128)(2,1)S(1)} %get-tuple-element.40.refs_0_, bf16[256,1024]{1,0:T(8,128)(2,1)S(1)} %get-tuple-element.41.refs_1_), custom_call_target="tpu_custom_call" | custom-call | flops 10000000000 | bytes 10000000000 | tf_op jit(solution)/shard_map/pallas_call | solution.py:200
  20.3 0.5 %collective-permute-start.7 = (f32[32,256]{1,0:T(8,128)S(1)}, f32[32,256]{1,0:T(8,128)S(1)}, u32[]{:S(2)}, u32[]{:S(2)}) collective-permute-start(f32[32,256]{1,0:T(8,128)S(1)} %get-tuple-element.43), channel_id=1, source_target_pairs={{0,4},{1,5},{2,6},{3,7},{4,0},{5,1},{6,2},{7,3},{8,12},{9,13},{10,... | collective-permute-start | bytes 98312 | tf_op jit(solution)/shard_map/ppermute | solution.py:174
  20.8 1.4 %collective-permute-done.8.refs_2_ = f32[32,256]{1,0:T(8,128)S(1)} collective-permute-done((f32[32,256]{1,0:T(8,128)S(1)}, f32[32,256]{1,0:T(8,128)S(1)}, u32[]{:S(2)}, u32[]{:S(2)}) %collective-permute-start.8) | collective-permute-done | bytes 32800 | tf_op jit(solution)/shard_map/ppermute | solution.py:174
  22.1 1.1 %collective-permute-done.9.refs_3_ = f32[32,256]{1,0:T(8,128)S(1)} collective-permute-done((f32[32,256]{1,0:T(8,128)S(1)}, f32[32,256]{1,0:T(8,128)S(1)}, u32[]{:S(2)}, u32[]{:S(2)}) %collective-permute-start.9) | collective-permute-done | bytes 32800 | tf_op jit(solution)/shard_map/ppermute | solution.py:174
  23.2 0.8 %shard_map.70 = (f32[32,256]{1,0:T(8,128)}, f32[32,256]{1,0:T(8,128)}) custom-call(bf16[32,1024]{1,0:T(8,128)(2,1)S(1)} %get-tuple-element.39.q_ref, f32[40,256]{1,0:T(8,128)S(1)} %get-tuple-element.24.refs_0_.refs_5_.near_ref, f32[32,32]{1,0:T(8,128)S(1)} %get-tuple-element.33.refs_4_.compat_ref, f32[32,256]{1,0:T(8,128)S(1)} %get-tuple-element.42.refs_0_, ...), custom_call_target="tpu_custom_call" | custom-call | flops 10000000000 | bytes 10000000000 | tf_op jit(solution)/shard_map/pallas_call | solution.py:200
  (8 shorter events, 0.1 us)
Async XLA Ops:
  1.7 5.5 %collective-permute-start = (f32[40,256]{1,0:T(8,128)S(1)}, f32[40,256]{1,0:T(8,128)S(1)}, u32[]{:S(2)}, u32[]{:S(2)}) collective-permute-start(f32[40,256]{1,0:T(8,128)S(1)} %get-tuple-element.24.refs_0_.refs_5_.near_ref), channel_id=1, source_target_pairs={{0,6},{1,7},{2,4},{3,5},{4,2},{5,3},{6,0},{7,1},{8,14},{9,15},{10,... | collective-permute-start | bytes 122888 | tf_op jit(solution)/shard_map/ppermute | solution.py:174
  5.2 5.3 %collective-permute-start.2 = (f32[40,256]{1,0:T(8,128)S(1)}, f32[40,256]{1,0:T(8,128)S(1)}, u32[]{:S(2)}, u32[]{:S(2)}) collective-permute-start(f32[40,256]{1,0:T(8,128)S(1)} %get-tuple-element.24.refs_0_.refs_5_.near_ref), channel_id=1, source_target_pairs={{0,7},{1,6},{2,5},{3,4},{4,3},{5,2},{6,1},{7,0},{8,15},{9,14},{10,... | collective-permute-start | bytes 122888 | tf_op jit(solution)/shard_map/ppermute | solution.py:174
  6.9 4.4 %collective-permute-start.1 = (f32[40,256]{1,0:T(8,128)S(1)}, f32[40,256]{1,0:T(8,128)S(1)}, u32[]{:S(2)}, u32[]{:S(2)}) collective-permute-start(f32[40,256]{1,0:T(8,128)S(1)} %get-tuple-element.24.refs_0_.refs_5_.near_ref), channel_id=1, source_target_pairs={{0,1},{1,0},{2,3},{3,2},{4,5},{5,4},{6,7},{7,6},{8,9},{9,8},{10,11... | collective-permute-start | bytes 122888 | tf_op jit(solution)/shard_map/ppermute | solution.py:174
  7.2 7.9 %collective-permute-start.3 = (bf16[2,40,256]{2,1,0:T(8,128)(2,1)S(1)}, bf16[2,40,256]{2,1,0:T(8,128)(2,1)S(1)}, u32[]{:S(2)}, u32[]{:S(2)}) collective-permute-start(bf16[2,40,256]{2,1,0:T(8,128)(2,1)S(1)} %get-tuple-element.27.refs_0_.refs_2_.refs_9_), channel_id=1, source_target_pairs={{0,12},{1,13},{2,14},{3,15},{4,8},{5,9},{6,10},{7,11},{8,4},{9,5},... | collective-permute-start | bytes 122888 | tf_op jit(solution)/shard_map/ppermute | solution.py:174
  11.3 3.8 %collective-permute-start.4 = (bf16[2,40,256]{2,1,0:T(8,128)(2,1)S(1)}, bf16[2,40,256]{2,1,0:T(8,128)(2,1)S(1)}, u32[]{:S(2)}, u32[]{:S(2)}) collective-permute-start(bf16[2,40,256]{2,1,0:T(8,128)(2,1)S(1)} %get-tuple-element.28.refs_1_.refs_3_.refs_10_), channel_id=1, source_target_pairs={{0,12},{1,13},{2,14},{3,15},{4,8},{5,9},{6,10},{7,11},{8,4},{9,5},... | collective-permute-start | bytes 122888 | tf_op jit(solution)/shard_map/ppermute | solution.py:174
  12.4 1.6 %collective-permute-start.5 = (bf16[4,40,256]{2,1,0:T(8,128)(2,1)S(1)}, bf16[4,40,256]{2,1,0:T(8,128)(2,1)S(1)}, u32[]{:S(2)}, u32[]{:S(2)}) collective-permute-start(bf16[4,40,256]{2,1,0:T(8,128)(2,1)S(1)} %shard_map.62), channel_id=1, source_target_pairs={{0,4},{1,5},{2,6},{3,7},{4,0},{5,1},{6,2},{7,3},{8,12},{9,13},{10,... | collective-permute-start | bytes 245768 | tf_op jit(solution)/shard_map/ppermute | solution.py:174
  15.2 1.3 %collective-permute-start.6 = (bf16[4,40,256]{2,1,0:T(8,128)(2,1)S(1)}, bf16[4,40,256]{2,1,0:T(8,128)(2,1)S(1)}, u32[]{:S(2)}, u32[]{:S(2)}) collective-permute-start(bf16[4,40,256]{2,1,0:T(8,128)(2,1)S(1)} %shard_map.65), channel_id=1, source_target_pairs={{0,4},{1,5},{2,6},{3,7},{4,0},{5,1},{6,2},{7,3},{8,12},{9,13},{10,... | collective-permute-start | bytes 245768 | tf_op jit(solution)/shard_map/ppermute | solution.py:174
  18.2 3.9 %collective-permute-start.8 = (f32[32,256]{1,0:T(8,128)S(1)}, f32[32,256]{1,0:T(8,128)S(1)}, u32[]{:S(2)}, u32[]{:S(2)}) collective-permute-start(f32[32,256]{1,0:T(8,128)S(1)} %get-tuple-element.44), channel_id=1, source_target_pairs={{0,8},{1,9},{2,10},{3,11},{4,12},{5,13},{6,14},{7,15},{8,0},{9,1},... | collective-permute-start | bytes 98312 | tf_op jit(solution)/shard_map/ppermute | solution.py:174
  19.7 3.5 %collective-permute-start.9 = (f32[32,256]{1,0:T(8,128)S(1)}, f32[32,256]{1,0:T(8,128)S(1)}, u32[]{:S(2)}, u32[]{:S(2)}) collective-permute-start(f32[32,256]{1,0:T(8,128)S(1)} %get-tuple-element.45), channel_id=1, source_target_pairs={{0,12},{1,13},{2,14},{3,15},{4,8},{5,9},{6,10},{7,11},{8,4},{9,5},... | collective-permute-start | bytes 98312 | tf_op jit(solution)/shard_map/ppermute | solution.py:174
  20.3 2.9 %collective-permute-start.7 = (f32[32,256]{1,0:T(8,128)S(1)}, f32[32,256]{1,0:T(8,128)S(1)}, u32[]{:S(2)}, u32[]{:S(2)}) collective-permute-start(f32[32,256]{1,0:T(8,128)S(1)} %get-tuple-element.43), channel_id=1, source_target_pairs={{0,4},{1,5},{2,6},{3,7},{4,0},{5,1},{6,2},{7,3},{8,12},{9,13},{10,... | collective-permute-start | bytes 98312 | tf_op jit(solution)/shard_map/ppermute | solution.py:174

commit v22 on v20

--- a/solution.py
+++ b/solution.py
@@ -159,7 +159,7 @@
 def second_sums(given_ref, *refs):
     count = len(refs) // 2
     for index in range(count):
-        refs[count + index][...] = refs[index][...] + given_ref[index + 1]
+        refs[count + index][...] = refs[index][...] + given_ref[index]
 
 
 def second_closing(q_ref, near_ref, compat_ref, *refs):
@@ -167,7 +167,7 @@
     labels, own = probs_ref.shape
     total = refs[0][...]
     for part_ref in refs[1:-2]:
-        total = total + (part_ref[0] if len(part_ref.shape) == 3 else part_ref[...])
+        total = total + part_ref[...]
     unary = near_ref[pl.ds(0, labels), :]
     probs, pairwise = finish(total, q_ref[:, pl.ds(0, own)], unary, compat_ref)
     probs_ref[...] = probs
@@ -192,7 +192,9 @@
     count = lax.axis_size("grp")
     order = sorted(range(1, count), key=lambda steps: (steps != count // 2, steps))
     crossed = paired("blk") and paired("grp") and lax.axis_size("blk") > 1
-    return [value] + [swap(value, steps % 2 if crossed else 0, steps) for steps in order]
+    return [value] + [
+        swap(value, 2 * steps // count if crossed else 0, steps) for steps in order
+    ]
 
 
 def paired(axis):
@@ -299,20 +301,20 @@
     part_kind = kept((labels, own), jnp.float32)
     tile_of = dict(zip(steps, tiles))
     if paired("blk"):
-        even = [1] + list(range(2, parts, 2))
-        odd = list(range(3, parts, 2))
+        even, odd = list(range(2, parts, 2)), list(range(3, parts, 2))
         (stacked,) = call(
             second_stacked, [kept((len(even), labels, own), jnp.float32)],
             *hold(q_near), *[tile_of[step] for step in even],
         )
         q_near, stacked = lax.optimization_barrier((q_near, stacked))
-        here, *mine = call(
-            second_parts, [part_kind] * (1 + len(odd)),
-            *hold(q_near), *[tile_of[step] for step in [0] + odd],
-        )
-        given = swap(stacked, 1)
-        sums = call(second_sums, [part_kind] * len(odd), *hold(given, *mine))
-        arrived = [given] + [swap(part, step) for part, step in zip(sums, odd)]
+        here, beside, *mine = call(
+            second_parts, [part_kind] * (2 + len(odd)),
+            *hold(q_near), *[tile_of[step] for step in [0, 1] + odd],
+        )
+        sums = call(second_sums, [part_kind] * len(odd), *hold(swap(stacked, 1), *mine))
+        beside, *sums = lax.optimization_barrier((beside, *sums))
+        arrived = [swap(part, step) for part, step in zip(sums, odd)]
+        arrived.append(swap(beside, 1))
     else:
         here, *away = call(
             second_parts, [part_kind] * parts, *hold(q_near), *[tile_of[step] for step in steps]

time: 24.2 us -> 23.6 us (0.975)
  waiting for transfers between devices: 7.55 us -> 4.66 us
  starting transfers between devices: 8.57 us -> 10.9 us
    ppermute x9 -> x10, waiting for transfers between devices: 7.55 us -> 4.66 us  [swap(): return lax.ppermute(value, ('blk', 'grp'), pairs)]
    ppermute x9 -> x10, starting transfers between devices: 8.57 us -> 10.9 us  [swap(): return lax.ppermute(value, ('blk', 'grp'), pairs)]
  transfers between devices with their start and end apart: 9 -> 10, of which waited for: 5 -> 5; matrix products, arithmetic and copies ran while one was open for 0% -> 0% of each run, Pallas kernels for 15% -> 16%
where the time goes in v22:
time: 23.6 us; the launch traced here: 23.4 us
  starting transfers between devices  10.9 us (46%)
  Pallas kernels  7.14 us (30%)
  waiting for transfers between devices  4.66 us (20%)
  between operations  0.69 us (3%)
    ppermute x10, starting transfers between devices, swap(): return lax.ppermute(value, ('blk', 'grp'), pairs)  10.9 us
    pallas_call x13, Pallas kernels, call(): pl.pallas_call(kernel, out_shape=tuple(out_shapes), cost_estimate=pl.Cost...  7.14 us
    ppermute x10, waiting for transfers between devices, swap(): return lax.ppermute(value, ('blk', 'grp'), pairs)  4.66 us
  transfers between devices with their start and end apart: 10, of which 5 were waited for; matrix products, arithmetic and copies ran while one was open for 0% of the time, Pallas kernels for 16%

profile of v22, /device:TPU:0, one launch (start us, length us, event | category | flops | bytes accessed | tf_op | source)
XLA Modules:
  0.0 23.4 jit_solution(4399335232151655765)
XLA Ops:
  0.6 1.1 %shard_map.59 = (f32[40,256]{1,0:T(8,128)S(1)}, f32[32,32]{1,0:T(8,128)S(1)}) custom-call(bf16[6,4096]{1,0:T(8,128)(2,1)} %features_ref.1, s32[1,256]{1,0:T(1,128)} %bitcast.1, f32[32,256]{1,0:T(8,128)} %unary_ref.1, f32[32,32]{1,0:T(8,128)} %compat_ref.1), custom_call_target="tpu_custom_call" | custom-call | flops 10000000000 | bytes 10000000000 | tf_op jit(solution)/shard_map/pallas_call | solution.py:210
  1.7 3.5 %collective-permute-start = (f32[40,256]{1,0:T(8,128)S(1)}, f32[40,256]{1,0:T(8,128)S(1)}, u32[]{:S(2)}, u32[]{:S(2)}) collective-permute-start(f32[40,256]{1,0:T(8,128)S(1)} %get-tuple-element.24.refs_0_.refs_5_.near_ref), channel_id=1, source_target_pairs={{0,6},{1,7},{2,4},{3,5},{4,2},{5,3},{6,0},{7,1},{8,14},{9,15},{10,... | collective-permute-start | bytes 122888 | tf_op jit(solution)/shard_map/ppermute | solution.py:188
  5.2 1.6 %collective-permute-start.2 = (f32[40,256]{1,0:T(8,128)S(1)}, f32[40,256]{1,0:T(8,128)S(1)}, u32[]{:S(2)}, u32[]{:S(2)}) collective-permute-start(f32[40,256]{1,0:T(8,128)S(1)} %get-tuple-element.24.refs_0_.refs_5_.near_ref), channel_id=1, source_target_pairs={{0,7},{1,6},{2,5},{3,4},{4,3},{5,2},{6,1},{7,0},{8,15},{9,14},{10,... | collective-permute-start | bytes 122888 | tf_op jit(solution)/shard_map/ppermute | solution.py:188
  6.9 0.3 %collective-permute-done.refs_1_.refs_6_ = f32[40,256]{1,0:T(8,128)S(1)} collective-permute-done((f32[40,256]{1,0:T(8,128)S(1)}, f32[40,256]{1,0:T(8,128)S(1)}, u32[]{:S(2)}, u32[]{:S(2)}) %collective-permute-start) | collective-permute-done | bytes 40992 | tf_op jit(solution)/shard_map/ppermute | solution.py:188
  7.2 1.8 %collective-permute-start.3 = (bf16[2,40,256]{2,1,0:T(8,128)(2,1)S(1)}, bf16[2,40,256]{2,1,0:T(8,128)(2,1)S(1)}, u32[]{:S(2)}, u32[]{:S(2)}) collective-permute-start(bf16[2,40,256]{2,1,0:T(8,128)(2,1)S(1)} %get-tuple-element.27.refs_0_.refs_2_.refs_9_), channel_id=1, source_target_pairs={{0,12},{1,13},{2,14},{3,15},{4,8},{5,9},{6,10},{7,11},{8,4},{9,5},... | collective-permute-start | bytes 122888 | tf_op jit(solution)/shard_map/ppermute | solution.py:188
  9.1 1.4 %collective-permute-done.2.refs_1_.refs_8_ = f32[40,256]{1,0:T(8,128)S(1)} collective-permute-done((f32[40,256]{1,0:T(8,128)S(1)}, f32[40,256]{1,0:T(8,128)S(1)}, u32[]{:S(2)}, u32[]{:S(2)}) %collective-permute-start.2) | collective-permute-done | bytes 40992 | tf_op jit(solution)/shard_map/ppermute | solution.py:188
  10.5 0.8 %collective-permute-done.1.refs_0_.refs_7_ = f32[40,256]{1,0:T(8,128)S(1)} collective-permute-done((f32[40,256]{1,0:T(8,128)S(1)}, f32[40,256]{1,0:T(8,128)S(1)}, u32[]{:S(2)}, u32[]{:S(2)}) %collective-permute-start.1) | collective-permute-done | bytes 40992 | tf_op jit(solution)/shard_map/ppermute | solution.py:188
  11.3 1.1 %collective-permute-start.4 = (bf16[2,40,256]{2,1,0:T(8,128)(2,1)S(1)}, bf16[2,40,256]{2,1,0:T(8,128)(2,1)S(1)}, u32[]{:S(2)}, u32[]{:S(2)}) collective-permute-start(bf16[2,40,256]{2,1,0:T(8,128)(2,1)S(1)} %get-tuple-element.28.refs_1_.refs_3_.refs_10_), channel_id=1, source_target_pairs={{0,12},{1,13},{2,14},{3,15},{4,8},{5,9},{6,10},{7,11},{8,4},{9,5},... | collective-permute-start | bytes 122888 | tf_op jit(solution)/shard_map/ppermute | solution.py:188
  12.4 0.6 %collective-permute-start.5 = (bf16[4,40,256]{2,1,0:T(8,128)(2,1)S(1)}, bf16[4,40,256]{2,1,0:T(8,128)(2,1)S(1)}, u32[]{:S(2)}, u32[]{:S(2)}) collective-permute-start(bf16[4,40,256]{2,1,0:T(8,128)(2,1)S(1)} %shard_map.62), channel_id=1, source_target_pairs={{0,4},{1,5},{2,6},{3,7},{4,0},{5,1},{6,2},{7,3},{8,12},{9,13},{10,... | collective-permute-start | bytes 245768 | tf_op jit(solution)/shard_map/ppermute | solution.py:188
  13.0 1.1 %shard_map.63 = (f32[32,1024]{1,0:T(8,128)S(1)}, bf16[256,1024]{1,0:T(8,128)(2,1)S(1)}) custom-call(bf16[16,512]{1,0:T(8,128)(2,1)S(1)} %get-tuple-element.25.refs_0_, bf16[16,512]{1,0:T(8,128)(2,1)S(1)} %get-tuple-element.26.refs_1_, bf16[2,40,256]{2,1,0:T(8,128)(2,1)S(1)} %get-tuple-element.27.refs_0_.refs_2_.refs_9_, ...), custom_call_target="tpu_custom_call" | custom-call | flops 10000000000 | bytes 10000000000 | tf_op jit(solution)/shard_map/pallas_call | solution.py:210
  14.1 1.1 %shard_map.64 = (f32[32,1024]{1,0:T(8,128)S(1)}, bf16[256,1024]{1,0:T(8,128)(2,1)S(1)}) custom-call(bf16[16,512]{1,0:T(8,128)(2,1)S(1)} %get-tuple-element.25.refs_0_, bf16[16,512]{1,0:T(8,128)(2,1)S(1)} %get-tuple-element.26.refs_1_, bf16[4,40,256]{2,1,0:T(8,128)(2,1)S(1)} %collective-permute-done.5.refs_2_, f32[32,1024]{1,0:T(8,128)S(1)} %get-tuple-element.29.refs_3_), custom_call_target="tpu_custom_call" | custom-call | flops 10000000000 | bytes 10000000000 | tf_op jit(solution)/shard_map/pallas_call | solution.py:210
  15.1 0.0 collective-permute-done.4.refs_1_.refs_3_
  15.2 0.3 %collective-permute-start.6 = (bf16[4,40,256]{2,1,0:T(8,128)(2,1)S(1)}, bf16[4,40,256]{2,1,0:T(8,128)(2,1)S(1)}, u32[]{:S(2)}, u32[]{:S(2)}) collective-permute-start(bf16[4,40,256]{2,1,0:T(8,128)(2,1)S(1)} %shard_map.65), channel_id=1, source_target_pairs={{0,4},{1,5},{2,6},{3,7},{4,0},{5,1},{6,2},{7,3},{8,12},{9,13},{10,... | collective-permute-start | bytes 245768 | tf_op jit(solution)/shard_map/ppermute | solution.py:188
  15.5 1.1 %shard_map.66 = (f32[32,1024]{1,0:T(8,128)S(1)}, bf16[256,1024]{1,0:T(8,128)(2,1)S(1)}) custom-call(bf16[16,512]{1,0:T(8,128)(2,1)S(1)} %get-tuple-element.25.refs_0_, bf16[16,512]{1,0:T(8,128)(2,1)S(1)} %get-tuple-element.26.refs_1_, bf16[2,40,256]{2,1,0:T(8,128)(2,1)S(1)} %collective-permute-done.3.refs_0_.refs_2_, ...), custom_call_target="tpu_custom_call" | custom-call | flops 10000000000 | bytes 10000000000 | tf_op jit(solution)/shard_map/pallas_call | solution.py:210
  16.5 0.0 collective-permute-done.6.refs_2_
  16.5 1.3 %shard_map.67 = (bf16[32,1024]{1,0:T(8,128)(2,1)S(1)}, bf16[256,1024]{1,0:T(8,128)(2,1)S(1)}) custom-call(bf16[16,512]{1,0:T(8,128)(2,1)S(1)} %get-tuple-element.25.refs_0_, bf16[16,512]{1,0:T(8,128)(2,1)S(1)} %get-tuple-element.26.refs_1_, bf16[4,40,256]{2,1,0:T(8,128)(2,1)S(1)} %collective-permute-done.6.refs_2_, ...), custom_call_target="tpu_custom_call" | custom-call | flops 10000000000 | bytes 10000000000 | tf_op jit(solution)/shard_map/pallas_call | solution.py:210
  17.8 0.2 shard_map.68
  18.0 0.3 %collective-permute-start.7 = (f32[1,32,256]{2,1,0:T(8,128)S(1)}, f32[1,32,256]{2,1,0:T(8,128)S(1)}, u32[]{:S(2)}, u32[]{:S(2)}) collective-permute-start(f32[1,32,256]{2,1,0:T(8,128)S(1)} %shard_map.68), channel_id=1, source_target_pairs={{0,4},{1,5},{2,6},{3,7},{4,0},{5,1},{6,2},{7,3},{8,12},{9,13},{10,... | collective-permute-start | bytes 98312 | tf_op jit(solution)/shard_map/ppermute | solution.py:188
  18.4 0.5 %shard_map.69 = (f32[32,256]{1,0:T(8,128)S(1)}, f32[32,256]{1,0:T(8,128)S(1)}, f32[32,256]{1,0:T(8,128)S(1)}) custom-call(bf16[32,1024]{1,0:T(8,128)(2,1)S(1)} %get-tuple-element.36.q_ref, bf16[256,1024]{1,0:T(8,128)(2,1)S(1)} %get-tuple-element.37.refs_0_, bf16[256,1024]{1,0:T(8,128)(2,1)S(1)} %get-tuple-element.38.refs_1_, ...), custom_call_target="tpu_custom_call" | custom-call | flops 10000000000 | bytes 10000000000 | tf_op jit(solution)/shard_map/pallas_call | solution.py:210
  18.9 0.4 %collective-permute-done.7.given_ref = f32[1,32,256]{2,1,0:T(8,128)S(1)} collective-permute-done((f32[1,32,256]{2,1,0:T(8,128)S(1)}, f32[1,32,256]{2,1,0:T(8,128)S(1)}, u32[]{:S(2)}, u32[]{:S(2)}) %collective-permute-start.7) | collective-permute-done | bytes 32800 | tf_op jit(solution)/shard_map/ppermute | solution.py:188
  19.3 1.4 %collective-permute-start.8 = (f32[32,256]{1,0:T(8,128)S(1)}, f32[32,256]{1,0:T(8,128)S(1)}, u32[]{:S(2)}, u32[]{:S(2)}) collective-permute-start(f32[32,256]{1,0:T(8,128)S(1)} %shard_map.70), channel_id=1, source_target_pairs={{0,12},{1,13},{2,14},{3,15},{4,8},{5,9},{6,10},{7,11},{8,4},{9,5},... | collective-permute-start | bytes 98312 | tf_op jit(solution)/shard_map/ppermute | solution.py:188
  20.7 0.2 collective-permute-start.9
  20.9 1.7 %collective-permute-done.8.refs_1_ = f32[32,256]{1,0:T(8,128)S(1)} collective-permute-done((f32[32,256]{1,0:T(8,128)S(1)}, f32[32,256]{1,0:T(8,128)S(1)}, u32[]{:S(2)}, u32[]{:S(2)}) %collective-permute-start.8) | collective-permute-done | bytes 32800 | tf_op jit(solution)/shard_map/ppermute | solution.py:188
  22.6 0.8 %shard_map.71 = (f32[32,256]{1,0:T(8,128)}, f32[32,256]{1,0:T(8,128)}) custom-call(bf16[32,1024]{1,0:T(8,128)(2,1)S(1)} %get-tuple-element.36.q_ref, f32[40,256]{1,0:T(8,128)S(1)} %get-tuple-element.24.refs_0_.refs_5_.near_ref, f32[32,32]{1,0:T(8,128)S(1)} %get-tuple-element.33.refs_4_.compat_ref, f32[32,256]{1,0:T(8,128)S(1)} %get-tuple-element.40.refs_0_, ...), custom_call_target="tpu_custom_call" | custom-call | flops 10000000000 | bytes 10000000000 | tf_op jit(solution)/shard_map/pallas_call | solution.py:210
  (9 shorter events, 0.1 us)
Async XLA Ops:
  1.7 5.5 %collective-permute-start = (f32[40,256]{1,0:T(8,128)S(1)}, f32[40,256]{1,0:T(8,128)S(1)}, u32[]{:S(2)}, u32[]{:S(2)}) collective-permute-start(f32[40,256]{1,0:T(8,128)S(1)} %get-tuple-element.24.refs_0_.refs_5_.near_ref), channel_id=1, source_target_pairs={{0,6},{1,7},{2,4},{3,5},{4,2},{5,3},{6,0},{7,1},{8,14},{9,15},{10,... | collective-permute-start | bytes 122888 | tf_op jit(solution)/shard_map/ppermute | solution.py:188
  5.2 5.3 %collective-permute-start.2 = (f32[40,256]{1,0:T(8,128)S(1)}, f32[40,256]{1,0:T(8,128)S(1)}, u32[]{:S(2)}, u32[]{:S(2)}) collective-permute-start(f32[40,256]{1,0:T(8,128)S(1)} %get-tuple-element.24.refs_0_.refs_5_.near_ref), channel_id=1, source_target_pairs={{0,7},{1,6},{2,5},{3,4},{4,3},{5,2},{6,1},{7,0},{8,15},{9,14},{10,... | collective-permute-start | bytes 122888 | tf_op jit(solution)/shard_map/ppermute | solution.py:188
  6.9 4.4 %collective-permute-start.1 = (f32[40,256]{1,0:T(8,128)S(1)}, f32[40,256]{1,0:T(8,128)S(1)}, u32[]{:S(2)}, u32[]{:S(2)}) collective-permute-start(f32[40,256]{1,0:T(8,128)S(1)} %get-tuple-element.24.refs_0_.refs_5_.near_ref), channel_id=1, source_target_pairs={{0,1},{1,0},{2,3},{3,2},{4,5},{5,4},{6,7},{7,6},{8,9},{9,8},{10,11... | collective-permute-start | bytes 122888 | tf_op jit(solution)/shard_map/ppermute | solution.py:188
  7.2 7.9 %collective-permute-start.3 = (bf16[2,40,256]{2,1,0:T(8,128)(2,1)S(1)}, bf16[2,40,256]{2,1,0:T(8,128)(2,1)S(1)}, u32[]{:S(2)}, u32[]{:S(2)}) collective-permute-start(bf16[2,40,256]{2,1,0:T(8,128)(2,1)S(1)} %get-tuple-element.27.refs_0_.refs_2_.refs_9_), channel_id=1, source_target_pairs={{0,12},{1,13},{2,14},{3,15},{4,8},{5,9},{6,10},{7,11},{8,4},{9,5},... | collective-permute-start | bytes 122888 | tf_op jit(solution)/shard_map/ppermute | solution.py:188
  11.3 3.8 %collective-permute-start.4 = (bf16[2,40,256]{2,1,0:T(8,128)(2,1)S(1)}, bf16[2,40,256]{2,1,0:T(8,128)(2,1)S(1)}, u32[]{:S(2)}, u32[]{:S(2)}) collective-permute-start(bf16[2,40,256]{2,1,0:T(8,128)(2,1)S(1)} %get-tuple-element.28.refs_1_.refs_3_.refs_10_), channel_id=1, source_target_pairs={{0,12},{1,13},{2,14},{3,15},{4,8},{5,9},{6,10},{7,11},{8,4},{9,5},... | collective-permute-start | bytes 122888 | tf_op jit(solution)/shard_map/ppermute | solution.py:188
  12.4 1.6 %collective-permute-start.5 = (bf16[4,40,256]{2,1,0:T(8,128)(2,1)S(1)}, bf16[4,40,256]{2,1,0:T(8,128)(2,1)S(1)}, u32[]{:S(2)}, u32[]{:S(2)}) collective-permute-start(bf16[4,40,256]{2,1,0:T(8,128)(2,1)S(1)} %shard_map.62), channel_id=1, source_target_pairs={{0,4},{1,5},{2,6},{3,7},{4,0},{5,1},{6,2},{7,3},{8,12},{9,13},{10,... | collective-permute-start | bytes 245768 | tf_op jit(solution)/shard_map/ppermute | solution.py:188
  15.2 1.3 %collective-permute-start.6 = (bf16[4,40,256]{2,1,0:T(8,128)(2,1)S(1)}, bf16[4,40,256]{2,1,0:T(8,128)(2,1)S(1)}, u32[]{:S(2)}, u32[]{:S(2)}) collective-permute-start(bf16[4,40,256]{2,1,0:T(8,128)(2,1)S(1)} %shard_map.65), channel_id=1, source_target_pairs={{0,4},{1,5},{2,6},{3,7},{4,0},{5,1},{6,2},{7,3},{8,12},{9,13},{10,... | collective-permute-start | bytes 245768 | tf_op jit(solution)/shard_map/ppermute | solution.py:188
  18.0 1.2 %collective-permute-start.7 = (f32[1,32,256]{2,1,0:T(8,128)S(1)}, f32[1,32,256]{2,1,0:T(8,128)S(1)}, u32[]{:S(2)}, u32[]{:S(2)}) collective-permute-start(f32[1,32,256]{2,1,0:T(8,128)S(1)} %shard_map.68), channel_id=1, source_target_pairs={{0,4},{1,5},{2,6},{3,7},{4,0},{5,1},{6,2},{7,3},{8,12},{9,13},{10,... | collective-permute-start | bytes 98312 | tf_op jit(solution)/shard_map/ppermute | solution.py:188
  19.3 3.3 %collective-permute-start.8 = (f32[32,256]{1,0:T(8,128)S(1)}, f32[32,256]{1,0:T(8,128)S(1)}, u32[]{:S(2)}, u32[]{:S(2)}) collective-permute-start(f32[32,256]{1,0:T(8,128)S(1)} %shard_map.70), channel_id=1, source_target_pairs={{0,12},{1,13},{2,14},{3,15},{4,8},{5,9},{6,10},{7,11},{8,4},{9,5},... | collective-permute-start | bytes 98312 | tf_op jit(solution)/shard_map/ppermute | solution.py:188
  20.7 1.9 %collective-permute-start.9 = (f32[32,256]{1,0:T(8,128)S(1)}, f32[32,256]{1,0:T(8,128)S(1)}, u32[]{:S(2)}, u32[]{:S(2)}) collective-permute-start(f32[32,256]{1,0:T(8,128)S(1)} %get-tuple-element.45), channel_id=1, source_target_pairs={{0,4},{1,5},{2,6},{3,7},{4,0},{5,1},{6,2},{7,3},{8,12},{9,13},{10,... | collective-permute-start | bytes 98312 | tf_op jit(solution)/shard_map/ppermute | solution.py:188

commit v23 on v22

--- a/solution.py
+++ b/solution.py
@@ -190,7 +190,7 @@
 
 def group_partners(value):
     count = lax.axis_size("grp")
-    order = sorted(range(1, count), key=lambda steps: (steps != count // 2, steps))
+    order = sorted(range(1, count), key=lambda steps: (steps != count - 1, steps))
     crossed = paired("blk") and paired("grp") and lax.axis_size("blk") > 1
     return [value] + [
         swap(value, 2 * steps // count if crossed else 0, steps) for steps in order

time: 23.6 us -> 23.4 us (level)
  starting transfers between devices: 10.9 us -> 10.6 us
    ppermute x10, starting transfers between devices: 10.9 us -> 10.6 us  [swap(): return lax.ppermute(value, ('blk', 'grp'), pairs)]
where the time goes in v23:
time: 23.4 us; the launch traced here: 23.2 us
  starting transfers between devices  10.6 us (45%)
  Pallas kernels  7.16 us (31%)
  waiting for transfers between devices  4.76 us (20%)
  between operations  0.7 us (3%)
    ppermute x10, starting transfers between devices, swap(): return lax.ppermute(value, ('blk', 'grp'), pairs)  10.6 us
    pallas_call x13, Pallas kernels, call(): pl.pallas_call(kernel, out_shape=tuple(out_shapes), cost_estimate=pl.Cost...  7.16 us
    ppermute x10, waiting for transfers between devices, swap(): return lax.ppermute(value, ('blk', 'grp'), pairs)  4.76 us
  transfers between devices with their start and end apart: 10, of which 5 were waited for; matrix products, arithmetic and copies ran while one was open for 0% of the time, Pallas kernels for 16%

profile of v23, /device:TPU:0, one launch (start us, length us, event | category | flops | bytes accessed | tf_op | source)
XLA Modules:
  0.0 23.2 jit_solution(7867195072451027033)
XLA Ops:
  0.6 1.1 %shard_map.59 = (f32[40,256]{1,0:T(8,128)S(1)}, f32[32,32]{1,0:T(8,128)S(1)}) custom-call(bf16[6,4096]{1,0:T(8,128)(2,1)} %features_ref.1, s32[1,256]{1,0:T(1,128)} %bitcast.1, f32[32,256]{1,0:T(8,128)} %unary_ref.1, f32[32,32]{1,0:T(8,128)} %compat_ref.1), custom_call_target="tpu_custom_call" | custom-call | flops 10000000000 | bytes 10000000000 | tf_op jit(solution)/shard_map/pallas_call | solution.py:210
  1.7 4.6 %collective-permute-start = (f32[40,256]{1,0:T(8,128)S(1)}, f32[40,256]{1,0:T(8,128)S(1)}, u32[]{:S(2)}, u32[]{:S(2)}) collective-permute-start(f32[40,256]{1,0:T(8,128)S(1)} %get-tuple-element.24.refs_0_.refs_5_.near_ref), channel_id=1, source_target_pairs={{0,7},{1,6},{2,5},{3,4},{4,3},{5,2},{6,1},{7,0},{8,15},{9,14},{10,... | collective-permute-start | bytes 122888 | tf_op jit(solution)/shard_map/ppermute | solution.py:188
  6.3 0.6 %collective-permute-start.1 = (f32[40,256]{1,0:T(8,128)S(1)}, f32[40,256]{1,0:T(8,128)S(1)}, u32[]{:S(2)}, u32[]{:S(2)}) collective-permute-start(f32[40,256]{1,0:T(8,128)S(1)} %get-tuple-element.24.refs_0_.refs_5_.near_ref), channel_id=1, source_target_pairs={{0,1},{1,0},{2,3},{3,2},{4,5},{5,4},{6,7},{7,6},{8,9},{9,8},{10,11... | collective-permute-start | bytes 122888 | tf_op jit(solution)/shard_map/ppermute | solution.py:188
  6.9 1.3 %collective-permute-done.refs_1_.refs_6_ = f32[40,256]{1,0:T(8,128)S(1)} collective-permute-done((f32[40,256]{1,0:T(8,128)S(1)}, f32[40,256]{1,0:T(8,128)S(1)}, u32[]{:S(2)}, u32[]{:S(2)}) %collective-permute-start) | collective-permute-done | bytes 40992 | tf_op jit(solution)/shard_map/ppermute | solution.py:188
  8.2 1.8 %collective-permute-start.3 = (bf16[2,40,256]{2,1,0:T(8,128)(2,1)S(1)}, bf16[2,40,256]{2,1,0:T(8,128)(2,1)S(1)}, u32[]{:S(2)}, u32[]{:S(2)}) collective-permute-start(bf16[2,40,256]{2,1,0:T(8,128)(2,1)S(1)} %get-tuple-element.27.refs_0_.refs_2_.refs_9_), channel_id=1, source_target_pairs={{0,12},{1,13},{2,14},{3,15},{4,8},{5,9},{6,10},{7,11},{8,4},{9,5},... | collective-permute-start | bytes 122888 | tf_op jit(solution)/shard_map/ppermute | solution.py:188
  10.0 0.8 %collective-permute-done.2.refs_1_.refs_8_ = f32[40,256]{1,0:T(8,128)S(1)} collective-permute-done((f32[40,256]{1,0:T(8,128)S(1)}, f32[40,256]{1,0:T(8,128)S(1)}, u32[]{:S(2)}, u32[]{:S(2)}) %collective-permute-start.2) | collective-permute-done | bytes 40992 | tf_op jit(solution)/shard_map/ppermute | solution.py:188
  10.9 1.6 %collective-permute-start.4 = (bf16[2,40,256]{2,1,0:T(8,128)(2,1)S(1)}, bf16[2,40,256]{2,1,0:T(8,128)(2,1)S(1)}, u32[]{:S(2)}, u32[]{:S(2)}) collective-permute-start(bf16[2,40,256]{2,1,0:T(8,128)(2,1)S(1)} %get-tuple-element.28.refs_1_.refs_3_.refs_10_), channel_id=1, source_target_pairs={{0,12},{1,13},{2,14},{3,15},{4,8},{5,9},{6,10},{7,11},{8,4},{9,5},... | collective-permute-start | bytes 122888 | tf_op jit(solution)/shard_map/ppermute | solution.py:188
  12.5 0.1 collective-permute-start.5
  12.6 1.1 %shard_map.63 = (f32[32,1024]{1,0:T(8,128)S(1)}, bf16[256,1024]{1,0:T(8,128)(2,1)S(1)}) custom-call(bf16[16,512]{1,0:T(8,128)(2,1)S(1)} %get-tuple-element.25.refs_0_, bf16[16,512]{1,0:T(8,128)(2,1)S(1)} %get-tuple-element.26.refs_1_, bf16[2,40,256]{2,1,0:T(8,128)(2,1)S(1)} %get-tuple-element.27.refs_0_.refs_2_.refs_9_, ...), custom_call_target="tpu_custom_call" | custom-call | flops 10000000000 | bytes 10000000000 | tf_op jit(solution)/shard_map/pallas_call | solution.py:210
  13.7 0.1 collective-permute-done.5.refs_2_
  13.8 1.1 %shard_map.64 = (f32[32,1024]{1,0:T(8,128)S(1)}, bf16[256,1024]{1,0:T(8,128)(2,1)S(1)}) custom-call(bf16[16,512]{1,0:T(8,128)(2,1)S(1)} %get-tuple-element.25.refs_0_, bf16[16,512]{1,0:T(8,128)(2,1)S(1)} %get-tuple-element.26.refs_1_, bf16[4,40,256]{2,1,0:T(8,128)(2,1)S(1)} %collective-permute-done.5.refs_2_, f32[32,1024]{1,0:T(8,128)S(1)} %get-tuple-element.29.refs_3_), custom_call_target="tpu_custom_call" | custom-call | flops 10000000000 | bytes 10000000000 | tf_op jit(solution)/shard_map/pallas_call | solution.py:210
  14.8 0.0 collective-permute-done.4.refs_1_.refs_3_
  14.9 0.4 %collective-permute-start.6 = (bf16[4,40,256]{2,1,0:T(8,128)(2,1)S(1)}, bf16[4,40,256]{2,1,0:T(8,128)(2,1)S(1)}, u32[]{:S(2)}, u32[]{:S(2)}) collective-permute-start(bf16[4,40,256]{2,1,0:T(8,128)(2,1)S(1)} %shard_map.65), channel_id=1, source_target_pairs={{0,4},{1,5},{2,6},{3,7},{4,0},{5,1},{6,2},{7,3},{8,12},{9,13},{10,... | collective-permute-start | bytes 245768 | tf_op jit(solution)/shard_map/ppermute | solution.py:188
  15.2 1.1 %shard_map.66 = (f32[32,1024]{1,0:T(8,128)S(1)}, bf16[256,1024]{1,0:T(8,128)(2,1)S(1)}) custom-call(bf16[16,512]{1,0:T(8,128)(2,1)S(1)} %get-tuple-element.25.refs_0_, bf16[16,512]{1,0:T(8,128)(2,1)S(1)} %get-tuple-element.26.refs_1_, bf16[2,40,256]{2,1,0:T(8,128)(2,1)S(1)} %collective-permute-done.3.refs_0_.refs_2_, ...), custom_call_target="tpu_custom_call" | custom-call | flops 10000000000 | bytes 10000000000 | tf_op jit(solution)/shard_map/pallas_call | solution.py:210
  16.3 0.0 collective-permute-done.6.refs_2_
  16.3 1.3 %shard_map.67 = (bf16[32,1024]{1,0:T(8,128)(2,1)S(1)}, bf16[256,1024]{1,0:T(8,128)(2,1)S(1)}) custom-call(bf16[16,512]{1,0:T(8,128)(2,1)S(1)} %get-tuple-element.25.refs_0_, bf16[16,512]{1,0:T(8,128)(2,1)S(1)} %get-tuple-element.26.refs_1_, bf16[4,40,256]{2,1,0:T(8,128)(2,1)S(1)} %collective-permute-done.6.refs_2_, ...), custom_call_target="tpu_custom_call" | custom-call | flops 10000000000 | bytes 10000000000 | tf_op jit(solution)/shard_map/pallas_call | solution.py:210
  17.6 0.2 %shard_map.68 = f32[1,32,256]{2,1,0:T(8,128)S(1)} custom-call(bf16[32,1024]{1,0:T(8,128)(2,1)S(1)} %get-tuple-element.36.q_ref, bf16[256,1024]{1,0:T(8,128)(2,1)S(1)} %get-tuple-element.35.refs_0_), custom_call_target="tpu_custom_call" | custom-call | flops 10000000000 | bytes 10000000000 | tf_op jit(solution)/shard_map/pallas_call | solution.py:210
  17.8 0.3 %collective-permute-start.7 = (f32[1,32,256]{2,1,0:T(8,128)S(1)}, f32[1,32,256]{2,1,0:T(8,128)S(1)}, u32[]{:S(2)}, u32[]{:S(2)}) collective-permute-start(f32[1,32,256]{2,1,0:T(8,128)S(1)} %shard_map.68), channel_id=1, source_target_pairs={{0,4},{1,5},{2,6},{3,7},{4,0},{5,1},{6,2},{7,3},{8,12},{9,13},{10,... | collective-permute-start | bytes 98312 | tf_op jit(solution)/shard_map/ppermute | solution.py:188
  18.1 0.5 %shard_map.69 = (f32[32,256]{1,0:T(8,128)S(1)}, f32[32,256]{1,0:T(8,128)S(1)}, f32[32,256]{1,0:T(8,128)S(1)}) custom-call(bf16[32,1024]{1,0:T(8,128)(2,1)S(1)} %get-tuple-element.36.q_ref, bf16[256,1024]{1,0:T(8,128)(2,1)S(1)} %get-tuple-element.37.refs_0_, bf16[256,1024]{1,0:T(8,128)(2,1)S(1)} %get-tuple-element.38.refs_1_, ...), custom_call_target="tpu_custom_call" | custom-call | flops 10000000000 | bytes 10000000000 | tf_op jit(solution)/shard_map/pallas_call | solution.py:210
  18.6 0.4 %collective-permute-done.7.given_ref = f32[1,32,256]{2,1,0:T(8,128)S(1)} collective-permute-done((f32[1,32,256]{2,1,0:T(8,128)S(1)}, f32[1,32,256]{2,1,0:T(8,128)S(1)}, u32[]{:S(2)}, u32[]{:S(2)}) %collective-permute-start.7) | collective-permute-done | bytes 32800 | tf_op jit(solution)/shard_map/ppermute | solution.py:188
  19.1 1.0 %collective-permute-start.8 = (f32[32,256]{1,0:T(8,128)S(1)}, f32[32,256]{1,0:T(8,128)S(1)}, u32[]{:S(2)}, u32[]{:S(2)}) collective-permute-start(f32[32,256]{1,0:T(8,128)S(1)} %shard_map.70), channel_id=1, source_target_pairs={{0,12},{1,13},{2,14},{3,15},{4,8},{5,9},{6,10},{7,11},{8,4},{9,5},... | collective-permute-start | bytes 98312 | tf_op jit(solution)/shard_map/ppermute | solution.py:188
  20.0 0.3 %collective-permute-start.9 = (f32[32,256]{1,0:T(8,128)S(1)}, f32[32,256]{1,0:T(8,128)S(1)}, u32[]{:S(2)}, u32[]{:S(2)}) collective-permute-start(f32[32,256]{1,0:T(8,128)S(1)} %get-tuple-element.45), channel_id=1, source_target_pairs={{0,4},{1,5},{2,6},{3,7},{4,0},{5,1},{6,2},{7,3},{8,12},{9,13},{10,... | collective-permute-start | bytes 98312 | tf_op jit(solution)/shard_map/ppermute | solution.py:188
  20.3 2.1 %collective-permute-done.8.refs_1_ = f32[32,256]{1,0:T(8,128)S(1)} collective-permute-done((f32[32,256]{1,0:T(8,128)S(1)}, f32[32,256]{1,0:T(8,128)S(1)}, u32[]{:S(2)}, u32[]{:S(2)}) %collective-permute-start.8) | collective-permute-done | bytes 32800 | tf_op jit(solution)/shard_map/ppermute | solution.py:188
  22.4 0.8 %shard_map.71 = (f32[32,256]{1,0:T(8,128)}, f32[32,256]{1,0:T(8,128)}) custom-call(bf16[32,1024]{1,0:T(8,128)(2,1)S(1)} %get-tuple-element.36.q_ref, f32[40,256]{1,0:T(8,128)S(1)} %get-tuple-element.24.refs_0_.refs_5_.near_ref, f32[32,32]{1,0:T(8,128)S(1)} %get-tuple-element.33.refs_4_.compat_ref, f32[32,256]{1,0:T(8,128)S(1)} %get-tuple-element.40.refs_0_, ...), custom_call_target="tpu_custom_call" | custom-call | flops 10000000000 | bytes 10000000000 | tf_op jit(solution)/shard_map/pallas_call | solution.py:210
  (9 shorter events, 0.1 us)
Async XLA Ops:
  1.7 6.5 %collective-permute-start = (f32[40,256]{1,0:T(8,128)S(1)}, f32[40,256]{1,0:T(8,128)S(1)}, u32[]{:S(2)}, u32[]{:S(2)}) collective-permute-start(f32[40,256]{1,0:T(8,128)S(1)} %get-tuple-element.24.refs_0_.refs_5_.near_ref), channel_id=1, source_target_pairs={{0,7},{1,6},{2,5},{3,4},{4,3},{5,2},{6,1},{7,0},{8,15},{9,14},{10,... | collective-permute-start | bytes 122888 | tf_op jit(solution)/shard_map/ppermute | solution.py:188
  6.2 4.6 %collective-permute-start.2 = (f32[40,256]{1,0:T(8,128)S(1)}, f32[40,256]{1,0:T(8,128)S(1)}, u32[]{:S(2)}, u32[]{:S(2)}) collective-permute-start(f32[40,256]{1,0:T(8,128)S(1)} %get-tuple-element.24.refs_0_.refs_5_.near_ref), channel_id=1, source_target_pairs={{0,6},{1,7},{2,4},{3,5},{4,2},{5,3},{6,0},{7,1},{8,14},{9,15},{10,... | collective-permute-start | bytes 122888 | tf_op jit(solution)/shard_map/ppermute | solution.py:188
  6.3 4.6 %collective-permute-start.1 = (f32[40,256]{1,0:T(8,128)S(1)}, f32[40,256]{1,0:T(8,128)S(1)}, u32[]{:S(2)}, u32[]{:S(2)}) collective-permute-start(f32[40,256]{1,0:T(8,128)S(1)} %get-tuple-element.24.refs_0_.refs_5_.near_ref), channel_id=1, source_target_pairs={{0,1},{1,0},{2,3},{3,2},{4,5},{5,4},{6,7},{7,6},{8,9},{9,8},{10,11... | collective-permute-start | bytes 122888 | tf_op jit(solution)/shard_map/ppermute | solution.py:188
  8.2 6.6 %collective-permute-start.3 = (bf16[2,40,256]{2,1,0:T(8,128)(2,1)S(1)}, bf16[2,40,256]{2,1,0:T(8,128)(2,1)S(1)}, u32[]{:S(2)}, u32[]{:S(2)}) collective-permute-start(bf16[2,40,256]{2,1,0:T(8,128)(2,1)S(1)} %get-tuple-element.27.refs_0_.refs_2_.refs_9_), channel_id=1, source_target_pairs={{0,12},{1,13},{2,14},{3,15},{4,8},{5,9},{6,10},{7,11},{8,4},{9,5},... | collective-permute-start | bytes 122888 | tf_op jit(solution)/shard_map/ppermute | solution.py:188
  10.9 3.9 %collective-permute-start.4 = (bf16[2,40,256]{2,1,0:T(8,128)(2,1)S(1)}, bf16[2,40,256]{2,1,0:T(8,128)(2,1)S(1)}, u32[]{:S(2)}, u32[]{:S(2)}) collective-permute-start(bf16[2,40,256]{2,1,0:T(8,128)(2,1)S(1)} %get-tuple-element.28.refs_1_.refs_3_.refs_10_), channel_id=1, source_target_pairs={{0,12},{1,13},{2,14},{3,15},{4,8},{5,9},{6,10},{7,11},{8,4},{9,5},... | collective-permute-start | bytes 122888 | tf_op jit(solution)/shard_map/ppermute | solution.py:188
  12.5 1.3 %collective-permute-start.5 = (bf16[4,40,256]{2,1,0:T(8,128)(2,1)S(1)}, bf16[4,40,256]{2,1,0:T(8,128)(2,1)S(1)}, u32[]{:S(2)}, u32[]{:S(2)}) collective-permute-start(bf16[4,40,256]{2,1,0:T(8,128)(2,1)S(1)} %shard_map.62), channel_id=1, source_target_pairs={{0,4},{1,5},{2,6},{3,7},{4,0},{5,1},{6,2},{7,3},{8,12},{9,13},{10,... | collective-permute-start | bytes 245768 | tf_op jit(solution)/shard_map/ppermute | solution.py:188
  14.9 1.4 %collective-permute-start.6 = (bf16[4,40,256]{2,1,0:T(8,128)(2,1)S(1)}, bf16[4,40,256]{2,1,0:T(8,128)(2,1)S(1)}, u32[]{:S(2)}, u32[]{:S(2)}) collective-permute-start(bf16[4,40,256]{2,1,0:T(8,128)(2,1)S(1)} %shard_map.65), channel_id=1, source_target_pairs={{0,4},{1,5},{2,6},{3,7},{4,0},{5,1},{6,2},{7,3},{8,12},{9,13},{10,... | collective-permute-start | bytes 245768 | tf_op jit(solution)/shard_map/ppermute | solution.py:188
  17.8 1.2 %collective-permute-start.7 = (f32[1,32,256]{2,1,0:T(8,128)S(1)}, f32[1,32,256]{2,1,0:T(8,128)S(1)}, u32[]{:S(2)}, u32[]{:S(2)}) collective-permute-start(f32[1,32,256]{2,1,0:T(8,128)S(1)} %shard_map.68), channel_id=1, source_target_pairs={{0,4},{1,5},{2,6},{3,7},{4,0},{5,1},{6,2},{7,3},{8,12},{9,13},{10,... | collective-permute-start | bytes 98312 | tf_op jit(solution)/shard_map/ppermute | solution.py:188
  19.1 3.3 %collective-permute-start.8 = (f32[32,256]{1,0:T(8,128)S(1)}, f32[32,256]{1,0:T(8,128)S(1)}, u32[]{:S(2)}, u32[]{:S(2)}) collective-permute-start(f32[32,256]{1,0:T(8,128)S(1)} %shard_map.70), channel_id=1, source_target_pairs={{0,12},{1,13},{2,14},{3,15},{4,8},{5,9},{6,10},{7,11},{8,4},{9,5},... | collective-permute-start | bytes 98312 | tf_op jit(solution)/shard_map/ppermute | solution.py:188
  20.0 2.4 %collective-permute-start.9 = (f32[32,256]{1,0:T(8,128)S(1)}, f32[32,256]{1,0:T(8,128)S(1)}, u32[]{:S(2)}, u32[]{:S(2)}) collective-permute-start(f32[32,256]{1,0:T(8,128)S(1)} %get-tuple-element.45), channel_id=1, source_target_pairs={{0,4},{1,5},{2,6},{3,7},{4,0},{5,1},{6,2},{7,3},{8,12},{9,13},{10,... | collective-permute-start | bytes 98312 | tf_op jit(solution)/shard_map/ppermute | solution.py:188

commit v24 on v23

--- a/solution.py
+++ b/solution.py
@@ -190,7 +190,7 @@
 
 def group_partners(value):
     count = lax.axis_size("grp")
-    order = sorted(range(1, count), key=lambda steps: (steps != count - 1, steps))
+    order = sorted(range(1, count), reverse=True)
     crossed = paired("blk") and paired("grp") and lax.axis_size("blk") > 1
     return [value] + [
         swap(value, 2 * steps // count if crossed else 0, steps) for steps in order

time: 23.4 us -> 23.4 us (level)
  no operation moved by 1% of the time
where the time goes in v24:
time: 23.4 us; the launch traced here: 23.2 us
  starting transfers between devices  10.4 us (44%)
  Pallas kernels  7.13 us (30%)
  waiting for transfers between devices  4.94 us (21%)
  between operations  0.7 us (3%)
    ppermute x10, starting transfers between devices, swap(): return lax.ppermute(value, ('blk', 'grp'), pairs)  10.4 us
    pallas_call x13, Pallas kernels, call(): pl.pallas_call(kernel, out_shape=tuple(out_shapes), cost_estimate=pl.Cost...  7.13 us
    ppermute x10, waiting for transfers between devices, swap(): return lax.ppermute(value, ('blk', 'grp'), pairs)  4.94 us
  transfers between devices with their start and end apart: 10, of which 5 were waited for; matrix products, arithmetic and copies ran while one was open for 0% of the time, Pallas kernels for 16%

profile of v24, /device:TPU:0, one launch (start us, length us, event | category | flops | bytes accessed | tf_op | source)
XLA Modules:
  0.0 23.2 jit_solution(16353677359715249731)
XLA Ops:
  0.6 1.1 %shard_map.59 = (f32[40,256]{1,0:T(8,128)S(1)}, f32[32,32]{1,0:T(8,128)S(1)}) custom-call(bf16[6,4096]{1,0:T(8,128)(2,1)} %features_ref.1, s32[1,256]{1,0:T(1,128)} %bitcast.1, f32[32,256]{1,0:T(8,128)} %unary_ref.1, f32[32,32]{1,0:T(8,128)} %compat_ref.1), custom_call_target="tpu_custom_call" | custom-call | flops 10000000000 | bytes 10000000000 | tf_op jit(solution)/shard_map/pallas_call | solution.py:210
  1.7 4.6 %collective-permute-start = (f32[40,256]{1,0:T(8,128)S(1)}, f32[40,256]{1,0:T(8,128)S(1)}, u32[]{:S(2)}, u32[]{:S(2)}) collective-permute-start(f32[40,256]{1,0:T(8,128)S(1)} %get-tuple-element.24.refs_0_.refs_5_.near_ref), channel_id=1, source_target_pairs={{0,7},{1,6},{2,5},{3,4},{4,3},{5,2},{6,1},{7,0},{8,15},{9,14},{10,... | collective-permute-start | bytes 122888 | tf_op jit(solution)/shard_map/ppermute | solution.py:188
  6.3 0.4 %collective-permute-start.1 = (f32[40,256]{1,0:T(8,128)S(1)}, f32[40,256]{1,0:T(8,128)S(1)}, u32[]{:S(2)}, u32[]{:S(2)}) collective-permute-start(f32[40,256]{1,0:T(8,128)S(1)} %get-tuple-element.24.refs_0_.refs_5_.near_ref), channel_id=1, source_target_pairs={{0,6},{1,7},{2,4},{3,5},{4,2},{5,3},{6,0},{7,1},{8,14},{9,15},{10,... | collective-permute-start | bytes 122888 | tf_op jit(solution)/shard_map/ppermute | solution.py:188
  6.6 1.6 %collective-permute-done.refs_1_.refs_6_ = f32[40,256]{1,0:T(8,128)S(1)} collective-permute-done((f32[40,256]{1,0:T(8,128)S(1)}, f32[40,256]{1,0:T(8,128)S(1)}, u32[]{:S(2)}, u32[]{:S(2)}) %collective-permute-start) | collective-permute-done | bytes 40992 | tf_op jit(solution)/shard_map/ppermute | solution.py:188
  8.2 1.9 %collective-permute-start.3 = (bf16[2,40,256]{2,1,0:T(8,128)(2,1)S(1)}, bf16[2,40,256]{2,1,0:T(8,128)(2,1)S(1)}, u32[]{:S(2)}, u32[]{:S(2)}) collective-permute-start(bf16[2,40,256]{2,1,0:T(8,128)(2,1)S(1)} %get-tuple-element.27.refs_0_.refs_2_.refs_9_), channel_id=1, source_target_pairs={{0,12},{1,13},{2,14},{3,15},{4,8},{5,9},{6,10},{7,11},{8,4},{9,5},... | collective-permute-start | bytes 122888 | tf_op jit(solution)/shard_map/ppermute | solution.py:188
  10.2 0.7 %collective-permute-done.2.refs_1_.refs_8_ = f32[40,256]{1,0:T(8,128)S(1)} collective-permute-done((f32[40,256]{1,0:T(8,128)S(1)}, f32[40,256]{1,0:T(8,128)S(1)}, u32[]{:S(2)}, u32[]{:S(2)}) %collective-permute-start.2) | collective-permute-done | bytes 40992 | tf_op jit(solution)/shard_map/ppermute | solution.py:188
  10.9 1.6 %collective-permute-start.4 = (bf16[2,40,256]{2,1,0:T(8,128)(2,1)S(1)}, bf16[2,40,256]{2,1,0:T(8,128)(2,1)S(1)}, u32[]{:S(2)}, u32[]{:S(2)}) collective-permute-start(bf16[2,40,256]{2,1,0:T(8,128)(2,1)S(1)} %get-tuple-element.28.refs_1_.refs_3_.refs_10_), channel_id=1, source_target_pairs={{0,12},{1,13},{2,14},{3,15},{4,8},{5,9},{6,10},{7,11},{8,4},{9,5},... | collective-permute-start | bytes 122888 | tf_op jit(solution)/shard_map/ppermute | solution.py:188
  12.5 0.1 collective-permute-start.5
  12.6 1.1 %shard_map.63 = (f32[32,1024]{1,0:T(8,128)S(1)}, bf16[256,1024]{1,0:T(8,128)(2,1)S(1)}) custom-call(bf16[16,512]{1,0:T(8,128)(2,1)S(1)} %get-tuple-element.25.refs_0_, bf16[16,512]{1,0:T(8,128)(2,1)S(1)} %get-tuple-element.26.refs_1_, bf16[2,40,256]{2,1,0:T(8,128)(2,1)S(1)} %get-tuple-element.27.refs_0_.refs_2_.refs_9_, ...), custom_call_target="tpu_custom_call" | custom-call | flops 10000000000 | bytes 10000000000 | tf_op jit(solution)/shard_map/pallas_call | solution.py:210
  13.6 0.1 collective-permute-done.5.refs_2_
  13.8 1.0 %shard_map.64 = (f32[32,1024]{1,0:T(8,128)S(1)}, bf16[256,1024]{1,0:T(8,128)(2,1)S(1)}) custom-call(bf16[16,512]{1,0:T(8,128)(2,1)S(1)} %get-tuple-element.25.refs_0_, bf16[16,512]{1,0:T(8,128)(2,1)S(1)} %get-tuple-element.26.refs_1_, bf16[4,40,256]{2,1,0:T(8,128)(2,1)S(1)} %collective-permute-done.5.refs_2_, f32[32,1024]{1,0:T(8,128)S(1)} %get-tuple-element.29.refs_3_), custom_call_target="tpu_custom_call" | custom-call | flops 10000000000 | bytes 10000000000 | tf_op jit(solution)/shard_map/pallas_call | solution.py:210
  14.8 0.0 collective-permute-done.4.refs_1_.refs_3_
  14.9 0.4 %collective-permute-start.6 = (bf16[4,40,256]{2,1,0:T(8,128)(2,1)S(1)}, bf16[4,40,256]{2,1,0:T(8,128)(2,1)S(1)}, u32[]{:S(2)}, u32[]{:S(2)}) collective-permute-start(bf16[4,40,256]{2,1,0:T(8,128)(2,1)S(1)} %shard_map.65), channel_id=1, source_target_pairs={{0,4},{1,5},{2,6},{3,7},{4,0},{5,1},{6,2},{7,3},{8,12},{9,13},{10,... | collective-permute-start | bytes 245768 | tf_op jit(solution)/shard_map/ppermute | solution.py:188
  15.2 1.1 %shard_map.66 = (f32[32,1024]{1,0:T(8,128)S(1)}, bf16[256,1024]{1,0:T(8,128)(2,1)S(1)}) custom-call(bf16[16,512]{1,0:T(8,128)(2,1)S(1)} %get-tuple-element.25.refs_0_, bf16[16,512]{1,0:T(8,128)(2,1)S(1)} %get-tuple-element.26.refs_1_, bf16[2,40,256]{2,1,0:T(8,128)(2,1)S(1)} %collective-permute-done.3.refs_0_.refs_2_, ...), custom_call_target="tpu_custom_call" | custom-call | flops 10000000000 | bytes 10000000000 | tf_op jit(solution)/shard_map/pallas_call | solution.py:210
  16.3 0.0 collective-permute-done.6.refs_2_
  16.3 1.3 %shard_map.67 = (bf16[32,1024]{1,0:T(8,128)(2,1)S(1)}, bf16[256,1024]{1,0:T(8,128)(2,1)S(1)}) custom-call(bf16[16,512]{1,0:T(8,128)(2,1)S(1)} %get-tuple-element.25.refs_0_, bf16[16,512]{1,0:T(8,128)(2,1)S(1)} %get-tuple-element.26.refs_1_, bf16[4,40,256]{2,1,0:T(8,128)(2,1)S(1)} %collective-permute-done.6.refs_2_, ...), custom_call_target="tpu_custom_call" | custom-call | flops 10000000000 | bytes 10000000000 | tf_op jit(solution)/shard_map/pallas_call | solution.py:210
  17.6 0.2 %shard_map.68 = f32[1,32,256]{2,1,0:T(8,128)S(1)} custom-call(bf16[32,1024]{1,0:T(8,128)(2,1)S(1)} %get-tuple-element.36.q_ref, bf16[256,1024]{1,0:T(8,128)(2,1)S(1)} %get-tuple-element.35.refs_0_), custom_call_target="tpu_custom_call" | custom-call | flops 10000000000 | bytes 10000000000 | tf_op jit(solution)/shard_map/pallas_call | solution.py:210
  17.8 0.2 %collective-permute-start.7 = (f32[1,32,256]{2,1,0:T(8,128)S(1)}, f32[1,32,256]{2,1,0:T(8,128)S(1)}, u32[]{:S(2)}, u32[]{:S(2)}) collective-permute-start(f32[1,32,256]{2,1,0:T(8,128)S(1)} %shard_map.68), channel_id=1, source_target_pairs={{0,4},{1,5},{2,6},{3,7},{4,0},{5,1},{6,2},{7,3},{8,12},{9,13},{10,... | collective-permute-start | bytes 98312 | tf_op jit(solution)/shard_map/ppermute | solution.py:188
  18.1 0.5 %shard_map.69 = (f32[32,256]{1,0:T(8,128)S(1)}, f32[32,256]{1,0:T(8,128)S(1)}, f32[32,256]{1,0:T(8,128)S(1)}) custom-call(bf16[32,1024]{1,0:T(8,128)(2,1)S(1)} %get-tuple-element.36.q_ref, bf16[256,1024]{1,0:T(8,128)(2,1)S(1)} %get-tuple-element.37.refs_0_, bf16[256,1024]{1,0:T(8,128)(2,1)S(1)} %get-tuple-element.38.refs_1_, ...), custom_call_target="tpu_custom_call" | custom-call | flops 10000000000 | bytes 10000000000 | tf_op jit(solution)/shard_map/pallas_call | solution.py:210
  18.6 0.5 %collective-permute-done.7.given_ref = f32[1,32,256]{2,1,0:T(8,128)S(1)} collective-permute-done((f32[1,32,256]{2,1,0:T(8,128)S(1)}, f32[1,32,256]{2,1,0:T(8,128)S(1)}, u32[]{:S(2)}, u32[]{:S(2)}) %collective-permute-start.7) | collective-permute-done | bytes 32800 | tf_op jit(solution)/shard_map/ppermute | solution.py:188
  19.1 1.0 %collective-permute-start.8 = (f32[32,256]{1,0:T(8,128)S(1)}, f32[32,256]{1,0:T(8,128)S(1)}, u32[]{:S(2)}, u32[]{:S(2)}) collective-permute-start(f32[32,256]{1,0:T(8,128)S(1)} %shard_map.70), channel_id=1, source_target_pairs={{0,12},{1,13},{2,14},{3,15},{4,8},{5,9},{6,10},{7,11},{8,4},{9,5},... | collective-permute-start | bytes 98312 | tf_op jit(solution)/shard_map/ppermute | solution.py:188
  20.0 0.3 %collective-permute-start.9 = (f32[32,256]{1,0:T(8,128)S(1)}, f32[32,256]{1,0:T(8,128)S(1)}, u32[]{:S(2)}, u32[]{:S(2)}) collective-permute-start(f32[32,256]{1,0:T(8,128)S(1)} %get-tuple-element.45), channel_id=1, source_target_pairs={{0,4},{1,5},{2,6},{3,7},{4,0},{5,1},{6,2},{7,3},{8,12},{9,13},{10,... | collective-permute-start | bytes 98312 | tf_op jit(solution)/shard_map/ppermute | solution.py:188
  20.4 2.0 %collective-permute-done.8.refs_1_ = f32[32,256]{1,0:T(8,128)S(1)} collective-permute-done((f32[32,256]{1,0:T(8,128)S(1)}, f32[32,256]{1,0:T(8,128)S(1)}, u32[]{:S(2)}, u32[]{:S(2)}) %collective-permute-start.8) | collective-permute-done | bytes 32800 | tf_op jit(solution)/shard_map/ppermute | solution.py:188
  22.4 0.8 %shard_map.71 = (f32[32,256]{1,0:T(8,128)}, f32[32,256]{1,0:T(8,128)}) custom-call(bf16[32,1024]{1,0:T(8,128)(2,1)S(1)} %get-tuple-element.36.q_ref, f32[40,256]{1,0:T(8,128)S(1)} %get-tuple-element.24.refs_0_.refs_5_.near_ref, f32[32,32]{1,0:T(8,128)S(1)} %get-tuple-element.33.refs_4_.compat_ref, f32[32,256]{1,0:T(8,128)S(1)} %get-tuple-element.40.refs_0_, ...), custom_call_target="tpu_custom_call" | custom-call | flops 10000000000 | bytes 10000000000 | tf_op jit(solution)/shard_map/pallas_call | solution.py:210
  (9 shorter events, 0.1 us)
Async XLA Ops:
  1.7 6.5 %collective-permute-start = (f32[40,256]{1,0:T(8,128)S(1)}, f32[40,256]{1,0:T(8,128)S(1)}, u32[]{:S(2)}, u32[]{:S(2)}) collective-permute-start(f32[40,256]{1,0:T(8,128)S(1)} %get-tuple-element.24.refs_0_.refs_5_.near_ref), channel_id=1, source_target_pairs={{0,7},{1,6},{2,5},{3,4},{4,3},{5,2},{6,1},{7,0},{8,15},{9,14},{10,... | collective-permute-start | bytes 122888 | tf_op jit(solution)/shard_map/ppermute | solution.py:188
  6.2 4.6 %collective-permute-start.2 = (f32[40,256]{1,0:T(8,128)S(1)}, f32[40,256]{1,0:T(8,128)S(1)}, u32[]{:S(2)}, u32[]{:S(2)}) collective-permute-start(f32[40,256]{1,0:T(8,128)S(1)} %get-tuple-element.24.refs_0_.refs_5_.near_ref), channel_id=1, source_target_pairs={{0,1},{1,0},{2,3},{3,2},{4,5},{5,4},{6,7},{7,6},{8,9},{9,8},{10,11... | collective-permute-start | bytes 122888 | tf_op jit(solution)/shard_map/ppermute | solution.py:188
  6.3 4.6 %collective-permute-start.1 = (f32[40,256]{1,0:T(8,128)S(1)}, f32[40,256]{1,0:T(8,128)S(1)}, u32[]{:S(2)}, u32[]{:S(2)}) collective-permute-start(f32[40,256]{1,0:T(8,128)S(1)} %get-tuple-element.24.refs_0_.refs_5_.near_ref), channel_id=1, source_target_pairs={{0,6},{1,7},{2,4},{3,5},{4,2},{5,3},{6,0},{7,1},{8,14},{9,15},{10,... | collective-permute-start | bytes 122888 | tf_op jit(solution)/shard_map/ppermute | solution.py:188
  8.2 6.6 %collective-permute-start.3 = (bf16[2,40,256]{2,1,0:T(8,128)(2,1)S(1)}, bf16[2,40,256]{2,1,0:T(8,128)(2,1)S(1)}, u32[]{:S(2)}, u32[]{:S(2)}) collective-permute-start(bf16[2,40,256]{2,1,0:T(8,128)(2,1)S(1)} %get-tuple-element.27.refs_0_.refs_2_.refs_9_), channel_id=1, source_target_pairs={{0,12},{1,13},{2,14},{3,15},{4,8},{5,9},{6,10},{7,11},{8,4},{9,5},... | collective-permute-start | bytes 122888 | tf_op jit(solution)/shard_map/ppermute | solution.py:188
  10.9 4.0 %collective-permute-start.4 = (bf16[2,40,256]{2,1,0:T(8,128)(2,1)S(1)}, bf16[2,40,256]{2,1,0:T(8,128)(2,1)S(1)}, u32[]{:S(2)}, u32[]{:S(2)}) collective-permute-start(bf16[2,40,256]{2,1,0:T(8,128)(2,1)S(1)} %get-tuple-element.28.refs_1_.refs_3_.refs_10_), channel_id=1, source_target_pairs={{0,12},{1,13},{2,14},{3,15},{4,8},{5,9},{6,10},{7,11},{8,4},{9,5},... | collective-permute-start | bytes 122888 | tf_op jit(solution)/shard_map/ppermute | solution.py:188
  12.5 1.3 %collective-permute-start.5 = (bf16[4,40,256]{2,1,0:T(8,128)(2,1)S(1)}, bf16[4,40,256]{2,1,0:T(8,128)(2,1)S(1)}, u32[]{:S(2)}, u32[]{:S(2)}) collective-permute-start(bf16[4,40,256]{2,1,0:T(8,128)(2,1)S(1)} %shard_map.62), channel_id=1, source_target_pairs={{0,4},{1,5},{2,6},{3,7},{4,0},{5,1},{6,2},{7,3},{8,12},{9,13},{10,... | collective-permute-start | bytes 245768 | tf_op jit(solution)/shard_map/ppermute | solution.py:188
  14.9 1.4 %collective-permute-start.6 = (bf16[4,40,256]{2,1,0:T(8,128)(2,1)S(1)}, bf16[4,40,256]{2,1,0:T(8,128)(2,1)S(1)}, u32[]{:S(2)}, u32[]{:S(2)}) collective-permute-start(bf16[4,40,256]{2,1,0:T(8,128)(2,1)S(1)} %shard_map.65), channel_id=1, source_target_pairs={{0,4},{1,5},{2,6},{3,7},{4,0},{5,1},{6,2},{7,3},{8,12},{9,13},{10,... | collective-permute-start | bytes 245768 | tf_op jit(solution)/shard_map/ppermute | solution.py:188
  17.8 1.2 %collective-permute-start.7 = (f32[1,32,256]{2,1,0:T(8,128)S(1)}, f32[1,32,256]{2,1,0:T(8,128)S(1)}, u32[]{:S(2)}, u32[]{:S(2)}) collective-permute-start(f32[1,32,256]{2,1,0:T(8,128)S(1)} %shard_map.68), channel_id=1, source_target_pairs={{0,4},{1,5},{2,6},{3,7},{4,0},{5,1},{6,2},{7,3},{8,12},{9,13},{10,... | collective-permute-start | bytes 98312 | tf_op jit(solution)/shard_map/ppermute | solution.py:188
  19.1 3.3 %collective-permute-start.8 = (f32[32,256]{1,0:T(8,128)S(1)}, f32[32,256]{1,0:T(8,128)S(1)}, u32[]{:S(2)}, u32[]{:S(2)}) collective-permute-start(f32[32,256]{1,0:T(8,128)S(1)} %shard_map.70), channel_id=1, source_target_pairs={{0,12},{1,13},{2,14},{3,15},{4,8},{5,9},{6,10},{7,11},{8,4},{9,5},... | collective-permute-start | bytes 98312 | tf_op jit(solution)/shard_map/ppermute | solution.py:188
  20.0 2.4 %collective-permute-start.9 = (f32[32,256]{1,0:T(8,128)S(1)}, f32[32,256]{1,0:T(8,128)S(1)}, u32[]{:S(2)}, u32[]{:S(2)}) collective-permute-start(f32[32,256]{1,0:T(8,128)S(1)} %get-tuple-element.45), channel_id=1, source_target_pairs={{0,4},{1,5},{2,6},{3,7},{4,0},{5,1},{6,2},{7,3},{8,12},{9,13},{10,... | collective-permute-start | bytes 98312 | tf_op jit(solution)/shard_map/ppermute | solution.py:188

commit v25 on v24

--- a/solution.py
+++ b/solution.py
@@ -64,14 +64,18 @@
     return columns.astype(jnp.bfloat16), rows.astype(jnp.bfloat16)
 
 
-def pack_kernel(labels, *refs):
-    near_refs, packed_ref, rows_ref = refs[:-2], refs[-2], refs[-1]
-    for place, near_ref in enumerate(near_refs):
-        own = near_ref.shape[1]
-        feats = near_ref[pl.ds(labels, 8), :]
-        probs = normalize(-near_ref[pl.ds(0, labels), :])
-        packed_ref[place] = jnp.concatenate([probs, feats], axis=0).astype(jnp.bfloat16)
+def pack_kernel(labels, counts, unused, *refs):
+    *near_refs, packed_ref, rows_ref, unary_ref = refs[unused:]
+    for place, count in enumerate(counts):
+        near = near_refs.pop(0)[...]
+        for _ in range(count - 1):
+            near = near + near_refs.pop(0)[...]
+        own = near.shape[1]
+        unary, feats = near[:labels], near[labels:]
+        packed = jnp.concatenate([normalize(-unary), feats], axis=0)
+        packed_ref[place] = packed.astype(jnp.bfloat16)
         rows_ref[:, pl.ds(place * own, own)] = product_sides(feats)[1]
+        unary_ref[:, pl.ds(place * own, own)] = unary
 
 
 def join_kernel(*refs):
@@ -91,7 +95,7 @@
     return normalize(-unary - pairwise), pairwise
 
 
-def first_part(labels, row_refs, stack_refs, total, tile_ref):
+def first_part(labels, own_place, row_refs, stack_refs, total, tile_ref):
     blocks = [(ref, index) for ref in stack_refs for index in range(ref.shape[0])]
     rows = jnp.concatenate([ref[...] for ref in row_refs], axis=1)
 
@@ -108,34 +112,31 @@
         if place + 1 < len(blocks):
             ahead = exponents(place + 1)
         tile = jnp.exp(exponent).astype(jnp.bfloat16)
-        if place == 0:
+        if place == own_place:
             tile_ref[...] = tile
         total = total + jnp.dot(ref[index][:labels], tile, preferred_element_type=jnp.float32)
     return total
 
 
-def first_opening(labels, *refs):
+def first_opening(labels, own_place, *refs):
     total_ref, tile_ref = refs[-2:]
     start = jnp.zeros(total_ref.shape, jnp.float32)
-    total_ref[...] = first_part(labels, refs[:2], refs[2:-2], start, tile_ref)
-
-
-def first_middle(labels, *refs):
+    total_ref[...] = first_part(labels, own_place, refs[:2], refs[2:-2], start, tile_ref)
+
+
+def first_middle(labels, own_place, *refs):
     sum_ref, total_ref, tile_ref = refs[-3:]
-    total_ref[...] = first_part(labels, refs[:2], refs[2:-3], sum_ref[...], tile_ref)
-
-
-def first_closing(labels, nears, stacks, *refs):
+    total_ref[...] = first_part(labels, own_place, refs[:2], refs[2:-3], sum_ref[...], tile_ref)
+
+
+def first_closing(labels, own_place, stacks, *refs):
     row_refs, refs = refs[:2], refs[2:]
     stack_refs, (sum_ref, compat_ref, *refs) = refs[:stacks], refs[stacks:]
-    near_refs, refs = refs[:nears], refs[nears:]
-    own_refs, (q_ref, tile_ref) = refs[:-2], refs[-2:]
-    total = first_part(labels, row_refs, stack_refs, sum_ref[...], tile_ref)
+    unary_refs, own_refs, (q_ref, tile_ref) = refs[:2], refs[2:-2], refs[-2:]
+    total = first_part(labels, own_place, row_refs, stack_refs, sum_ref[...], tile_ref)
     labels_now = [ref[index][:labels] for ref in own_refs for index in range(ref.shape[0])]
-    unary = [near_ref[pl.ds(0, labels), :] for near_ref in near_refs]
-    probs, _ = finish(
-        total, jnp.concatenate(labels_now, axis=1), jnp.concatenate(unary, axis=1), compat_ref
-    )
+    unary = jnp.concatenate([ref[...] for ref in unary_refs], axis=1)
+    probs, _ = finish(total, jnp.concatenate(labels_now, axis=1), unary, compat_ref)
     q_ref[...] = probs.astype(jnp.bfloat16)
 
 
@@ -162,19 +163,21 @@
         refs[count + index][...] = refs[index][...] + given_ref[index]
 
 
-def second_closing(q_ref, near_ref, compat_ref, *refs):
+def second_closing(own_place, q_ref, near_ref, compat_ref, *refs):
     probs_ref, pairwise_ref = refs[-2:]
     labels, own = probs_ref.shape
     total = refs[0][...]
     for part_ref in refs[1:-2]:
         total = total + part_ref[...]
     unary = near_ref[pl.ds(0, labels), :]
-    probs, pairwise = finish(total, q_ref[:, pl.ds(0, own)], unary, compat_ref)
+    probs, pairwise = finish(
+        total, q_ref[:, pl.ds(own_place * own, own)], unary, compat_ref
+    )
     probs_ref[...] = probs
     pairwise_ref[...] = pairwise
 
 
-def swap(value, blk_steps, grp_steps=0):
+def swap(value, blk_steps, grp_steps=0, rising=None):
     blks, grps = lax.axis_size("blk"), lax.axis_size("grp")
     pairs = [
         (
@@ -185,16 +188,26 @@
         for blk in range(blks)
         for grp in range(grps)
     ]
+    if rising is not None:
+        pairs = [pair for pair in pairs if (pair[0] % grps < pair[1] % grps) == rising]
     return lax.ppermute(value, ("blk", "grp"), pairs)
 
 
 def group_partners(value):
     count = lax.axis_size("grp")
-    order = sorted(range(1, count), reverse=True)
     crossed = paired("blk") and paired("grp") and lax.axis_size("blk") > 1
-    return [value] + [
-        swap(value, 2 * steps // count if crossed else 0, steps) for steps in order
-    ]
+    step = lambda steps, rising=None: swap(
+        value, 2 * steps // count if crossed else 0, steps, rising
+    )
+    if count < 4:
+        near = [(value,)] + [(step(steps),) for steps in range(1, count)]
+        return near[1:], near[:1]
+    falling = step(count - 1, False)
+    rising = step(count - 1, True)
+    half = count // 2
+    near = [(value,)] + [(step(steps),) for steps in range(half, count - 1)]
+    rest = [(falling, rising)] + [(step(steps),) for steps in range(half - 1, 0, -1)]
+    return rest, near, falling
 
 
 def paired(axis):
@@ -238,20 +251,21 @@
         [kept((labels + 8, own), jnp.float32), kept(compat.shape, jnp.float32)],
         features, member[None], unary, compat,
     )
-    near = group_partners(sent)
-    half = max(1, nears // 2)
+    late_half, early_half, *early_also = group_partners(sent)
+    own_place = len(late_half)
     halves = [
         call(
-            functools.partial(pack_kernel, labels),
+            functools.partial(pack_kernel, labels, [len(arrays) for arrays in some], len(also)),
             [
                 kept((len(some), labels + 8, own), jnp.bfloat16),
                 kept((AUX, len(some) * own), jnp.bfloat16),
+                kept((labels, len(some) * own), jnp.float32),
             ],
-            *hold(*some),
-        )
-        for some in (near[:half], near[half:])
+            *hold(*also, *[array for arrays in some for array in arrays]),
+        )
+        for some, also in ((late_half, []), (early_half, early_also))
     ]
-    packed, rows = zip(*halves)
+    packed, rows, near_unary = zip(*halves)
     parts = lax.axis_size("blk")
     tile_kind = kept((own, nears * own), jnp.bfloat16, parts)
     total_kind = kept((labels, nears * own), jnp.float32)
@@ -259,7 +273,7 @@
 
     def first(*stack):
         total, tile = call(
-            functools.partial(first_middle if totals else first_opening, labels),
+            functools.partial(first_middle if totals else first_opening, labels, own_place),
             [total_kind, tile_kind], *hold(*rows, *stack, *totals[-1:]),
         )
         tiles.append(tile)
@@ -276,9 +290,9 @@
         far = [[swap(some, step) for step in steps] for some in packed]
         beside = swap(joined, 1)
         first(*packed)
-        early, late = far
+        late, early = far
         *late, _ = lax.optimization_barrier((*late, first(beside)))
-        stacks = list(zip(early, late))
+        stacks = list(zip(late, early))
         stacks += [(swap(join(some), 1),) for some in stacks]
         steps = [0, 1] + steps + [step - 1 for step in steps]
     else:
@@ -290,9 +304,9 @@
     for stack in middle:
         first(*stack)
     q_near, tile = call(
-        functools.partial(first_closing, labels, nears, len(last)),
+        functools.partial(first_closing, labels, own_place, len(last)),
         [kept((labels, nears * own), jnp.bfloat16), tile_kind],
-        *hold(*rows, *last, totals[-1], held, *near, *packed),
+        *hold(*rows, *last, totals[-1], held, *near_unary, *packed),
     )
     tiles.append(tile)
 
@@ -321,7 +335,7 @@
         )
         arrived = [swap(part, parts - step) for part, step in zip(away, steps[1:])]
     return call(
-        second_closing,
+        functools.partial(second_closing, own_place),
         [jax.ShapeDtypeStruct((labels, own), jnp.float32)] * 2,
         *hold(q_near, sent, held, here, *arrived),
     )

time: 23.4 us -> 27.7 us (1.18)
  starting transfers between devices: 10.4 us -> 16 us
  waiting for transfers between devices: 4.94 us -> 3.61 us
    ppermute x10 -> x11, starting transfers between devices: 10.4 us -> 16 us  [swap(): return lax.ppermute(value, ('blk', 'grp'), pairs)]
    ppermute x10 -> x11, waiting for transfers between devices: 4.94 us -> 3.61 us  [swap(): return lax.ppermute(value, ('blk', 'grp'), pairs)]
  transfers between devices with their start and end apart: 10 -> 11, of which waited for: 5 -> 5; matrix products, arithmetic and copies ran while one was open for 0% -> 0% of each run, Pallas kernels for 16% -> 14%
where the time goes in v25:
time: 27.7 us; the launch traced here: 27.5 us
  starting transfers between devices  16 us (58%)
  Pallas kernels  7.15 us (26%)
  waiting for transfers between devices  3.61 us (13%)
  between operations  0.71 us (3%)
    ppermute x11, starting transfers between devices, swap(): return lax.ppermute(value, ('blk', 'grp'), pairs)  16 us
    pallas_call x13, Pallas kernels, call(): pl.pallas_call(kernel, out_shape=tuple(out_shapes), cost_estimate=pl.Cost...  7.15 us
    ppermute x11, waiting for transfers between devices, swap(): return lax.ppermute(value, ('blk', 'grp'), pairs)  3.61 us
  transfers between devices with their start and end apart: 11, of which 5 were waited for; matrix products, arithmetic and copies ran while one was open for 0% of the time, Pallas kernels for 14%

profile of v25, /device:TPU:0, one launch (start us, length us, event | category | flops | bytes accessed | tf_op | source)
XLA Modules:
  0.0 27.5 jit_solution(7177956713716921744)
XLA Ops:
  0.6 1.1 %shard_map.59 = (f32[40,256]{1,0:T(8,128)S(1)}, f32[32,32]{1,0:T(8,128)S(1)}) custom-call(bf16[6,4096]{1,0:T(8,128)(2,1)} %features_ref.1, s32[1,256]{1,0:T(1,128)} %bitcast.1, f32[32,256]{1,0:T(8,128)} %unary_ref.1, f32[32,32]{1,0:T(8,128)} %compat_ref.1), custom_call_target="tpu_custom_call" | custom-call | flops 10000000000 | bytes 10000000000 | tf_op jit(solution)/shard_map/pallas_call | solution.py:223
  1.7 3.5 %collective-permute-start.3 = (f32[40,256]{1,0:T(8,128)S(1)}, f32[40,256]{1,0:T(8,128)S(1)}, u32[]{:S(2)}, u32[]{:S(2)}) collective-permute-start(f32[40,256]{1,0:T(8,128)S(1)} %get-tuple-element.26.refs_1_.near_ref), channel_id=1, source_target_pairs={{0,6},{1,7},{2,4},{3,5},{4,2},{5,3},{6,0},{7,1},{8,14},{9,15},{10,... | collective-permute-start | bytes 122888 | tf_op jit(solution)/shard_map/ppermute | solution.py:193
  5.2 1.3 %collective-permute-start = (f32[40,256]{1,0:T(8,128)S(1)}, f32[40,256]{1,0:T(8,128)S(1)}, u32[]{:S(2)}, u32[]{:S(2)}) collective-permute-start(f32[40,256]{1,0:T(8,128)S(1)} %get-tuple-element.26.refs_1_.near_ref), channel_id=1, source_target_pairs={{2,5},{3,4},{6,1},{7,0},{10,13},{11,12},{14,9},{15,8},{18,21},{19,... | collective-permute-start | bytes 122888 | tf_op jit(solution)/shard_map/ppermute | solution.py:193
  6.5 1.6 %collective-permute-start.2 = (f32[40,256]{1,0:T(8,128)S(1)}, f32[40,256]{1,0:T(8,128)S(1)}, u32[]{:S(2)}, u32[]{:S(2)}) collective-permute-start(f32[40,256]{1,0:T(8,128)S(1)} %get-tuple-element.26.refs_1_.near_ref), channel_id=1, source_target_pairs={{0,1},{1,0},{2,3},{3,2},{4,5},{5,4},{6,7},{7,6},{8,9},{9,8},{10,11... | collective-permute-start | bytes 122888 | tf_op jit(solution)/shard_map/ppermute | solution.py:193
  8.2 4.9 %collective-permute-start.1 = (f32[40,256]{1,0:T(8,128)S(1)}, f32[40,256]{1,0:T(8,128)S(1)}, u32[]{:S(2)}, u32[]{:S(2)}) collective-permute-start(f32[40,256]{1,0:T(8,128)S(1)} %get-tuple-element.26.refs_1_.near_ref), channel_id=1, source_target_pairs={{0,7},{1,6},{4,3},{5,2},{8,15},{9,14},{12,11},{13,10},{16,23},{17,... | collective-permute-start | bytes 122888 | tf_op jit(solution)/shard_map/ppermute | solution.py:193
  13.1 2.1 %collective-permute-start.6 = (bf16[2,40,256]{2,1,0:T(8,128)(2,1)S(1)}, bf16[2,40,256]{2,1,0:T(8,128)(2,1)S(1)}, u32[]{:S(2)}, u32[]{:S(2)}) collective-permute-start(bf16[2,40,256]{2,1,0:T(8,128)(2,1)S(1)} %get-tuple-element.30.refs_1_.refs_3_.refs_8_), channel_id=1, source_target_pairs={{0,12},{1,13},{2,14},{3,15},{4,8},{5,9},{6,10},{7,11},{8,4},{9,5},... | collective-permute-start | bytes 122888 | tf_op jit(solution)/shard_map/ppermute | solution.py:193
  15.3 1.0 %collective-permute-start.4 = (bf16[2,40,256]{2,1,0:T(8,128)(2,1)S(1)}, bf16[2,40,256]{2,1,0:T(8,128)(2,1)S(1)}, u32[]{:S(2)}, u32[]{:S(2)}) collective-permute-start(bf16[2,40,256]{2,1,0:T(8,128)(2,1)S(1)} %get-tuple-element.29.refs_0_.refs_2_.refs_7_), channel_id=1, source_target_pairs={{0,12},{1,13},{2,14},{3,15},{4,8},{5,9},{6,10},{7,11},{8,4},{9,5},... | collective-permute-start | bytes 122888 | tf_op jit(solution)/shard_map/ppermute | solution.py:193
  16.3 0.1 collective-permute-start.5
  16.5 1.1 %shard_map.63 = (f32[32,1024]{1,0:T(8,128)S(1)}, bf16[256,1024]{1,0:T(8,128)(2,1)S(1)}) custom-call(bf16[16,512]{1,0:T(8,128)(2,1)S(1)} %get-tuple-element.27.refs_0_, bf16[16,512]{1,0:T(8,128)(2,1)S(1)} %get-tuple-element.28.refs_1_, bf16[2,40,256]{2,1,0:T(8,128)(2,1)S(1)} %get-tuple-element.29.refs_0_.refs_2_.refs_7_, ...), custom_call_target="tpu_custom_call" | custom-call | flops 10000000000 | bytes 10000000000 | tf_op jit(solution)/shard_map/pallas_call | solution.py:223
  17.6 0.1 collective-permute-done.5.refs_2_
  17.6 1.1 %shard_map.64 = (f32[32,1024]{1,0:T(8,128)S(1)}, bf16[256,1024]{1,0:T(8,128)(2,1)S(1)}) custom-call(bf16[16,512]{1,0:T(8,128)(2,1)S(1)} %get-tuple-element.27.refs_0_, bf16[16,512]{1,0:T(8,128)(2,1)S(1)} %get-tuple-element.28.refs_1_, bf16[4,40,256]{2,1,0:T(8,128)(2,1)S(1)} %collective-permute-done.5.refs_2_, f32[32,1024]{1,0:T(8,128)S(1)} %get-tuple-element.31.refs_3_), custom_call_target="tpu_custom_call" | custom-call | flops 10000000000 | bytes 10000000000 | tf_op jit(solution)/shard_map/pallas_call | solution.py:223
  18.7 0.5 %collective-permute-done.4.refs_0_.refs_2_ = bf16[2,40,256]{2,1,0:T(8,128)(2,1)S(1)} collective-permute-done((bf16[2,40,256]{2,1,0:T(8,128)(2,1)S(1)}, bf16[2,40,256]{2,1,0:T(8,128)(2,1)S(1)}, u32[]{:S(2)}, u32[]{:S(2)}) %collective-permute-start.4) | collective-permute-done | bytes 40992 | tf_op jit(solution)/shard_map/ppermute | solution.py:193
  19.2 0.2 collective-permute-start.7
  19.4 1.1 %shard_map.66 = (f32[32,1024]{1,0:T(8,128)S(1)}, bf16[256,1024]{1,0:T(8,128)(2,1)S(1)}) custom-call(bf16[16,512]{1,0:T(8,128)(2,1)S(1)} %get-tuple-element.27.refs_0_, bf16[16,512]{1,0:T(8,128)(2,1)S(1)} %get-tuple-element.28.refs_1_, bf16[2,40,256]{2,1,0:T(8,128)(2,1)S(1)} %collective-permute-done.4.refs_0_.refs_2_, ...), custom_call_target="tpu_custom_call" | custom-call | flops 10000000000 | bytes 10000000000 | tf_op jit(solution)/shard_map/pallas_call | solution.py:223
  20.5 0.1 collective-permute-done.7.refs_2_
  20.6 1.3 %shard_map.67 = (bf16[32,1024]{1,0:T(8,128)(2,1)S(1)}, bf16[256,1024]{1,0:T(8,128)(2,1)S(1)}) custom-call(bf16[16,512]{1,0:T(8,128)(2,1)S(1)} %get-tuple-element.27.refs_0_, bf16[16,512]{1,0:T(8,128)(2,1)S(1)} %get-tuple-element.28.refs_1_, bf16[4,40,256]{2,1,0:T(8,128)(2,1)S(1)} %collective-permute-done.7.refs_2_, ...), custom_call_target="tpu_custom_call" | custom-call | flops 10000000000 | bytes 10000000000 | tf_op jit(solution)/shard_map/pallas_call | solution.py:223
  21.8 0.2 shard_map.68
  22.1 0.3 %collective-permute-start.8 = (f32[1,32,256]{2,1,0:T(8,128)S(1)}, f32[1,32,256]{2,1,0:T(8,128)S(1)}, u32[]{:S(2)}, u32[]{:S(2)}) collective-permute-start(f32[1,32,256]{2,1,0:T(8,128)S(1)} %shard_map.68), channel_id=1, source_target_pairs={{0,4},{1,5},{2,6},{3,7},{4,0},{5,1},{6,2},{7,3},{8,12},{9,13},{10,... | collective-permute-start | bytes 98312 | tf_op jit(solution)/shard_map/ppermute | solution.py:193
  22.4 0.5 %shard_map.69 = (f32[32,256]{1,0:T(8,128)S(1)}, f32[32,256]{1,0:T(8,128)S(1)}, f32[32,256]{1,0:T(8,128)S(1)}) custom-call(bf16[32,1024]{1,0:T(8,128)(2,1)S(1)} %get-tuple-element.40.q_ref, bf16[256,1024]{1,0:T(8,128)(2,1)S(1)} %get-tuple-element.41.refs_0_, bf16[256,1024]{1,0:T(8,128)(2,1)S(1)} %get-tuple-element.42.refs_1_, ...), custom_call_target="tpu_custom_call" | custom-call | flops 10000000000 | bytes 10000000000 | tf_op jit(solution)/shard_map/pallas_call | solution.py:223
  22.9 0.4 %collective-permute-done.8.given_ref = f32[1,32,256]{2,1,0:T(8,128)S(1)} collective-permute-done((f32[1,32,256]{2,1,0:T(8,128)S(1)}, f32[1,32,256]{2,1,0:T(8,128)S(1)}, u32[]{:S(2)}, u32[]{:S(2)}) %collective-permute-start.8) | collective-permute-done | bytes 32800 | tf_op jit(solution)/shard_map/ppermute | solution.py:193
  23.3 0.5 %collective-permute-start.9 = (f32[32,256]{1,0:T(8,128)S(1)}, f32[32,256]{1,0:T(8,128)S(1)}, u32[]{:S(2)}, u32[]{:S(2)}) collective-permute-start(f32[32,256]{1,0:T(8,128)S(1)} %shard_map.70), channel_id=1, source_target_pairs={{0,12},{1,13},{2,14},{3,15},{4,8},{5,9},{6,10},{7,11},{8,4},{9,5},... | collective-permute-start | bytes 98312 | tf_op jit(solution)/shard_map/ppermute | solution.py:193
  23.9 0.3 %collective-permute-start.10 = (f32[32,256]{1,0:T(8,128)S(1)}, f32[32,256]{1,0:T(8,128)S(1)}, u32[]{:S(2)}, u32[]{:S(2)}) collective-permute-start(f32[32,256]{1,0:T(8,128)S(1)} %get-tuple-element.49), channel_id=1, source_target_pairs={{0,4},{1,5},{2,6},{3,7},{4,0},{5,1},{6,2},{7,3},{8,12},{9,13},{10,... | collective-permute-start | bytes 98312 | tf_op jit(solution)/shard_map/ppermute | solution.py:193
  24.2 2.5 %collective-permute-done.9.refs_1_ = f32[32,256]{1,0:T(8,128)S(1)} collective-permute-done((f32[32,256]{1,0:T(8,128)S(1)}, f32[32,256]{1,0:T(8,128)S(1)}, u32[]{:S(2)}, u32[]{:S(2)}) %collective-permute-start.9) | collective-permute-done | bytes 32800 | tf_op jit(solution)/shard_map/ppermute | solution.py:193
  26.7 0.8 %shard_map.71 = (f32[32,256]{1,0:T(8,128)}, f32[32,256]{1,0:T(8,128)}) custom-call(bf16[32,1024]{1,0:T(8,128)(2,1)S(1)} %get-tuple-element.40.q_ref, f32[40,256]{1,0:T(8,128)S(1)} %get-tuple-element.26.refs_1_.near_ref, f32[32,32]{1,0:T(8,128)S(1)} %get-tuple-element.35.refs_4_.compat_ref, f32[32,256]{1,0:T(8,128)S(1)} %get-tuple-element.44.refs_0_, ...), custom_call_target="tpu_custom_call" | custom-call | flops 10000000000 | bytes 10000000000 | tf_op jit(solution)/shard_map/pallas_call | solution.py:223
  (11 shorter events, 0.1 us)
Async XLA Ops:
  1.7 11.4 %collective-permute-start.3 = (f32[40,256]{1,0:T(8,128)S(1)}, f32[40,256]{1,0:T(8,128)S(1)}, u32[]{:S(2)}, u32[]{:S(2)}) collective-permute-start(f32[40,256]{1,0:T(8,128)S(1)} %get-tuple-element.26.refs_1_.near_ref), channel_id=1, source_target_pairs={{0,6},{1,7},{2,4},{3,5},{4,2},{5,3},{6,0},{7,1},{8,14},{9,15},{10,... | collective-permute-start | bytes 122888 | tf_op jit(solution)/shard_map/ppermute | solution.py:193
  5.2 7.8 %collective-permute-start = (f32[40,256]{1,0:T(8,128)S(1)}, f32[40,256]{1,0:T(8,128)S(1)}, u32[]{:S(2)}, u32[]{:S(2)}) collective-permute-start(f32[40,256]{1,0:T(8,128)S(1)} %get-tuple-element.26.refs_1_.near_ref), channel_id=1, source_target_pairs={{2,5},{3,4},{6,1},{7,0},{10,13},{11,12},{14,9},{15,8},{18,21},{19,... | collective-permute-start | bytes 122888 | tf_op jit(solution)/shard_map/ppermute | solution.py:193
  6.5 8.7 %collective-permute-start.2 = (f32[40,256]{1,0:T(8,128)S(1)}, f32[40,256]{1,0:T(8,128)S(1)}, u32[]{:S(2)}, u32[]{:S(2)}) collective-permute-start(f32[40,256]{1,0:T(8,128)S(1)} %get-tuple-element.26.refs_1_.near_ref), channel_id=1, source_target_pairs={{0,1},{1,0},{2,3},{3,2},{4,5},{5,4},{6,7},{7,6},{8,9},{9,8},{10,11... | collective-permute-start | bytes 122888 | tf_op jit(solution)/shard_map/ppermute | solution.py:193
  8.2 7.1 %collective-permute-start.1 = (f32[40,256]{1,0:T(8,128)S(1)}, f32[40,256]{1,0:T(8,128)S(1)}, u32[]{:S(2)}, u32[]{:S(2)}) collective-permute-start(f32[40,256]{1,0:T(8,128)S(1)} %get-tuple-element.26.refs_1_.near_ref), channel_id=1, source_target_pairs={{0,7},{1,6},{4,3},{5,2},{8,15},{9,14},{12,11},{13,10},{16,23},{17,... | collective-permute-start | bytes 122888 | tf_op jit(solution)/shard_map/ppermute | solution.py:193
  13.1 6.1 %collective-permute-start.6 = (bf16[2,40,256]{2,1,0:T(8,128)(2,1)S(1)}, bf16[2,40,256]{2,1,0:T(8,128)(2,1)S(1)}, u32[]{:S(2)}, u32[]{:S(2)}) collective-permute-start(bf16[2,40,256]{2,1,0:T(8,128)(2,1)S(1)} %get-tuple-element.30.refs_1_.refs_3_.refs_8_), channel_id=1, source_target_pairs={{0,12},{1,13},{2,14},{3,15},{4,8},{5,9},{6,10},{7,11},{8,4},{9,5},... | collective-permute-start | bytes 122888 | tf_op jit(solution)/shard_map/ppermute | solution.py:193
  15.3 3.9 %collective-permute-start.4 = (bf16[2,40,256]{2,1,0:T(8,128)(2,1)S(1)}, bf16[2,40,256]{2,1,0:T(8,128)(2,1)S(1)}, u32[]{:S(2)}, u32[]{:S(2)}) collective-permute-start(bf16[2,40,256]{2,1,0:T(8,128)(2,1)S(1)} %get-tuple-element.29.refs_0_.refs_2_.refs_7_), channel_id=1, source_target_pairs={{0,12},{1,13},{2,14},{3,15},{4,8},{5,9},{6,10},{7,11},{8,4},{9,5},... | collective-permute-start | bytes 122888 | tf_op jit(solution)/shard_map/ppermute | solution.py:193
  16.3 1.3 %collective-permute-start.5 = (bf16[4,40,256]{2,1,0:T(8,128)(2,1)S(1)}, bf16[4,40,256]{2,1,0:T(8,128)(2,1)S(1)}, u32[]{:S(2)}, u32[]{:S(2)}) collective-permute-start(bf16[4,40,256]{2,1,0:T(8,128)(2,1)S(1)} %shard_map.62), channel_id=1, source_target_pairs={{0,4},{1,5},{2,6},{3,7},{4,0},{5,1},{6,2},{7,3},{8,12},{9,13},{10,... | collective-permute-start | bytes 245768 | tf_op jit(solution)/shard_map/ppermute | solution.py:193
  19.2 1.3 %collective-permute-start.7 = (bf16[4,40,256]{2,1,0:T(8,128)(2,1)S(1)}, bf16[4,40,256]{2,1,0:T(8,128)(2,1)S(1)}, u32[]{:S(2)}, u32[]{:S(2)}) collective-permute-start(bf16[4,40,256]{2,1,0:T(8,128)(2,1)S(1)} %shard_map.65), channel_id=1, source_target_pairs={{0,4},{1,5},{2,6},{3,7},{4,0},{5,1},{6,2},{7,3},{8,12},{9,13},{10,... | collective-permute-start | bytes 245768 | tf_op jit(solution)/shard_map/ppermute | solution.py:193
  22.1 1.2 %collective-permute-start.8 = (f32[1,32,256]{2,1,0:T(8,128)S(1)}, f32[1,32,256]{2,1,0:T(8,128)S(1)}, u32[]{:S(2)}, u32[]{:S(2)}) collective-permute-start(f32[1,32,256]{2,1,0:T(8,128)S(1)} %shard_map.68), channel_id=1, source_target_pairs={{0,4},{1,5},{2,6},{3,7},{4,0},{5,1},{6,2},{7,3},{8,12},{9,13},{10,... | collective-permute-start | bytes 98312 | tf_op jit(solution)/shard_map/ppermute | solution.py:193
  23.3 3.3 %collective-permute-start.9 = (f32[32,256]{1,0:T(8,128)S(1)}, f32[32,256]{1,0:T(8,128)S(1)}, u32[]{:S(2)}, u32[]{:S(2)}) collective-permute-start(f32[32,256]{1,0:T(8,128)S(1)} %shard_map.70), channel_id=1, source_target_pairs={{0,12},{1,13},{2,14},{3,15},{4,8},{5,9},{6,10},{7,11},{8,4},{9,5},... | collective-permute-start | bytes 98312 | tf_op jit(solution)/shard_map/ppermute | solution.py:193
  23.9 2.8 %collective-permute-start.10 = (f32[32,256]{1,0:T(8,128)S(1)}, f32[32,256]{1,0:T(8,128)S(1)}, u32[]{:S(2)}, u32[]{:S(2)}) collective-permute-start(f32[32,256]{1,0:T(8,128)S(1)} %get-tuple-element.49), channel_id=1, source_target_pairs={{0,4},{1,5},{2,6},{3,7},{4,0},{5,1},{6,2},{7,3},{8,12},{9,13},{10,... | collective-permute-start | bytes 98312 | tf_op jit(solution)/shard_map/ppermute | solution.py:193

commit v26 on v24

--- a/solution.py
+++ b/solution.py
@@ -108,16 +108,27 @@
         if place + 1 < len(blocks):
             ahead = exponents(place + 1)
         tile = jnp.exp(exponent).astype(jnp.bfloat16)
-        if place == 0:
+        if place == 0 and tile_ref is not None:
             tile_ref[...] = tile
         total = total + jnp.dot(ref[index][:labels], tile, preferred_element_type=jnp.float32)
     return total
 
 
+def first_early(labels, rows_ref, packed_ref, total_ref, tile_ref):
+    start = jnp.zeros(total_ref.shape, jnp.float32)
+    total_ref[...] = first_part(labels, [rows_ref], [packed_ref], start, tile_ref)
+
+
 def first_opening(labels, *refs):
-    total_ref, tile_ref = refs[-2:]
-    start = jnp.zeros(total_ref.shape, jnp.float32)
-    total_ref[...] = first_part(labels, refs[:2], refs[2:-2], start, tile_ref)
+    near_rows, rest_rows, near_ref, rest_ref, sum_ref, early_tile_ref, total_ref, tile_ref = refs
+    near, rest = near_rows.shape[1], rest_rows.shape[1]
+    beyond = first_part(
+        labels, [rest_rows], [near_ref], jnp.zeros((labels, rest), jnp.float32),
+        tile_ref.at[:, pl.ds(near, rest)],
+    )
+    tile_ref[:, pl.ds(0, near)] = early_tile_ref[...]
+    start = jnp.concatenate([sum_ref[...], beyond], axis=1)
+    total_ref[...] = first_part(labels, [near_rows, rest_rows], [rest_ref], start, None)
 
 
 def first_middle(labels, *refs):
@@ -240,8 +251,9 @@
     )
     near = group_partners(sent)
     half = max(1, nears // 2)
-    halves = [
-        call(
+
+    def pack_half(some):
+        return call(
             functools.partial(pack_kernel, labels),
             [
                 kept((len(some), labels + 8, own), jnp.bfloat16),
@@ -249,9 +261,16 @@
             ],
             *hold(*some),
         )
-        for some in (near[:half], near[half:])
-    ]
-    packed, rows = zip(*halves)
+
+    near_packed, near_rows = pack_half(near[:half])
+    early_sum, early_tile = call(
+        functools.partial(first_early, labels),
+        [kept((labels, half * own), jnp.float32), kept((own, half * own), jnp.bfloat16)],
+        *hold(near_rows, near_packed),
+    )
+    early_sum, *rest = lax.optimization_barrier((early_sum, *near[half:]))
+    rest_packed, rest_rows = pack_half(rest)
+    packed, rows = (near_packed, rest_packed), (near_rows, rest_rows)
     parts = lax.axis_size("blk")
     tile_kind = kept((own, nears * own), jnp.bfloat16, parts)
     total_kind = kept((labels, nears * own), jnp.float32)
@@ -260,7 +279,8 @@
     def first(*stack):
         total, tile = call(
             functools.partial(first_middle if totals else first_opening, labels),
-            [total_kind, tile_kind], *hold(*rows, *stack, *totals[-1:]),
+            [total_kind, tile_kind],
+            *hold(*rows, *stack, *(totals[-1:] or [early_sum, early_tile])),
         )
         tiles.append(tile)
         totals.append(total)

time: 23.4 us -> 23.3 us (level)
  waiting for transfers between devices: 4.94 us -> 4.37 us
  Pallas kernels: 7.13 us -> 7.55 us
    ppermute x10, waiting for transfers between devices: 4.94 us -> 4.37 us  [swap(): return lax.ppermute(value, ('blk', 'grp'), pairs)]
    pallas_call x13 -> x14, Pallas kernels: 7.13 us -> 7.55 us  [call(): pl.pallas_call(kernel, out_shape=tuple(out_shapes), cost_estimate=pl.Cost...]
  transfers between devices with their start and end apart: 10 -> 10, of which waited for: 5 -> 5; matrix products, arithmetic and copies ran while one was open for 0% -> 0% of each run, Pallas kernels for 16% -> 18%
where the time goes in v26:
time: 23.3 us; the launch traced here: 23.1 us
  starting transfers between devices  10.5 us (45%)
  Pallas kernels  7.55 us (32%)
  waiting for transfers between devices  4.37 us (19%)
  between operations  0.7 us (3%)
    ppermute x10, starting transfers between devices, swap(): return lax.ppermute(value, ('blk', 'grp'), pairs)  10.5 us
    pallas_call x14, Pallas kernels, call(): pl.pallas_call(kernel, out_shape=tuple(out_shapes), cost_estimate=pl.Cost...  7.55 us
    ppermute x10, waiting for transfers between devices, swap(): return lax.ppermute(value, ('blk', 'grp'), pairs)  4.37 us
  transfers between devices with their start and end apart: 10, of which 5 were waited for; matrix products, arithmetic and copies ran while one was open for 0% of the time, Pallas kernels for 18%

profile of v26, /device:TPU:0, one launch (start us, length us, event | category | flops | bytes accessed | tf_op | source)
XLA Modules:
  0.0 23.1 jit_solution(9797104927620309518)
XLA Ops:
  0.6 1.1 %shard_map.59 = (f32[40,256]{1,0:T(8,128)S(1)}, f32[32,32]{1,0:T(8,128)S(1)}) custom-call(bf16[6,4096]{1,0:T(8,128)(2,1)} %features_ref.1, s32[1,256]{1,0:T(1,128)} %bitcast.1, f32[32,256]{1,0:T(8,128)} %unary_ref.1, f32[32,32]{1,0:T(8,128)} %compat_ref.1), custom_call_target="tpu_custom_call" | custom-call | flops 10000000000 | bytes 10000000000 | tf_op jit(solution)/shard_map/pallas_call | solution.py:221
  1.7 4.6 %collective-permute-start = (f32[40,256]{1,0:T(8,128)S(1)}, f32[40,256]{1,0:T(8,128)S(1)}, u32[]{:S(2)}, u32[]{:S(2)}) collective-permute-start(f32[40,256]{1,0:T(8,128)S(1)} %get-tuple-element.29.refs_0_.refs_5_.near_ref), channel_id=1, source_target_pairs={{0,7},{1,6},{2,5},{3,4},{4,3},{5,2},{6,1},{7,0},{8,15},{9,14},{10,... | collective-permute-start | bytes 122888 | tf_op jit(solution)/shard_map/ppermute | solution.py:199
  6.3 0.4 %collective-permute-start.1 = (f32[40,256]{1,0:T(8,128)S(1)}, f32[40,256]{1,0:T(8,128)S(1)}, u32[]{:S(2)}, u32[]{:S(2)}) collective-permute-start(f32[40,256]{1,0:T(8,128)S(1)} %get-tuple-element.29.refs_0_.refs_5_.near_ref), channel_id=1, source_target_pairs={{0,6},{1,7},{2,4},{3,5},{4,2},{5,3},{6,0},{7,1},{8,14},{9,15},{10,... | collective-permute-start | bytes 122888 | tf_op jit(solution)/shard_map/ppermute | solution.py:199
  6.6 1.6 %collective-permute-done.refs_1_.refs_6_ = f32[40,256]{1,0:T(8,128)S(1)} collective-permute-done((f32[40,256]{1,0:T(8,128)S(1)}, f32[40,256]{1,0:T(8,128)S(1)}, u32[]{:S(2)}, u32[]{:S(2)}) %collective-permute-start) | collective-permute-done | bytes 40992 | tf_op jit(solution)/shard_map/ppermute | solution.py:199
  8.2 1.9 %collective-permute-start.3 = (bf16[2,40,256]{2,1,0:T(8,128)(2,1)S(1)}, bf16[2,40,256]{2,1,0:T(8,128)(2,1)S(1)}, u32[]{:S(2)}, u32[]{:S(2)}) collective-permute-start(bf16[2,40,256]{2,1,0:T(8,128)(2,1)S(1)} %get-tuple-element.31.packed_ref.refs_0_.refs_2_.refs_9_), channel_id=1, source_target_pairs={{0,12},{1,13},{2,14},{3,15},{4,8},{5,9},{6,10},{7,11},{8,4},{9,5},... | collective-permute-start | bytes 122888 | tf_op jit(solution)/shard_map/ppermute | solution.py:199
  10.2 0.5 %shard_map.61 = (f32[32,512]{1,0:T(8,128)S(1)}, bf16[256,512]{1,0:T(8,128)(2,1)S(1)}) custom-call(bf16[16,512]{1,0:T(8,128)(2,1)S(1)} %get-tuple-element.30.rows_ref.refs_0_, bf16[2,40,256]{2,1,0:T(8,128)(2,1)S(1)} %get-tuple-element.31.packed_ref.refs_0_.refs_2_.refs_9_), custom_call_target="tpu_custom_call" | custom-call | flops 10000000000 | bytes 10000000000 | tf_op jit(solution)/shard_map/pallas_call | solution.py:221
  10.7 0.1 collective-permute-done.2.refs_1_.refs_8_
  10.9 1.6 %collective-permute-start.4 = (bf16[2,40,256]{2,1,0:T(8,128)(2,1)S(1)}, bf16[2,40,256]{2,1,0:T(8,128)(2,1)S(1)}, u32[]{:S(2)}, u32[]{:S(2)}) collective-permute-start(bf16[2,40,256]{2,1,0:T(8,128)(2,1)S(1)} %get-tuple-element.36.refs_1_.refs_3_.refs_10_), channel_id=1, source_target_pairs={{0,12},{1,13},{2,14},{3,15},{4,8},{5,9},{6,10},{7,11},{8,4},{9,5},... | collective-permute-start | bytes 122888 | tf_op jit(solution)/shard_map/ppermute | solution.py:199
  12.5 0.1 collective-permute-start.5
  12.6 1.0 %shard_map.64 = (f32[32,1024]{1,0:T(8,128)S(1)}, bf16[256,1024]{1,0:T(8,128)(2,1)S(1)}) custom-call(bf16[16,512]{1,0:T(8,128)(2,1)S(1)} %get-tuple-element.30.rows_ref.refs_0_, bf16[16,512]{1,0:T(8,128)(2,1)S(1)} %get-tuple-element.35.refs_1_, bf16[2,40,256]{2,1,0:T(8,128)(2,1)S(1)} %get-tuple-element.31.packed_ref.refs_0_.refs_2_.refs_9_, ...), custom_call_target="tpu_custom_call" | custom-call | flops 10000000000 | bytes 10000000000 | tf_op jit(solution)/shard_map/pallas_call | solution.py:221
  13.5 0.2 %collective-permute-done.5.refs_2_ = bf16[4,40,256]{2,1,0:T(8,128)(2,1)S(1)} collective-permute-done((bf16[4,40,256]{2,1,0:T(8,128)(2,1)S(1)}, bf16[4,40,256]{2,1,0:T(8,128)(2,1)S(1)}, u32[]{:S(2)}, u32[]{:S(2)}) %collective-permute-start.5) | collective-permute-done | bytes 81952 | tf_op jit(solution)/shard_map/ppermute | solution.py:199
  13.8 1.0 %shard_map.65 = (f32[32,1024]{1,0:T(8,128)S(1)}, bf16[256,1024]{1,0:T(8,128)(2,1)S(1)}) custom-call(bf16[16,512]{1,0:T(8,128)(2,1)S(1)} %get-tuple-element.30.rows_ref.refs_0_, bf16[16,512]{1,0:T(8,128)(2,1)S(1)} %get-tuple-element.35.refs_1_, bf16[4,40,256]{2,1,0:T(8,128)(2,1)S(1)} %collective-permute-done.5.refs_2_, f32[32,1024]{1,0:T(8,128)S(1)} %get-tuple-element.39.refs_3_), custom_call_target="tpu_custom_call" | custom-call | flops 10000000000 | bytes 10000000000 | tf_op jit(solution)/shard_map/pallas_call | solution.py:221
  14.8 0.0 collective-permute-done.4.refs_1_.refs_3_
  14.9 0.3 %collective-permute-start.6 = (bf16[4,40,256]{2,1,0:T(8,128)(2,1)S(1)}, bf16[4,40,256]{2,1,0:T(8,128)(2,1)S(1)}, u32[]{:S(2)}, u32[]{:S(2)}) collective-permute-start(bf16[4,40,256]{2,1,0:T(8,128)(2,1)S(1)} %shard_map.66), channel_id=1, source_target_pairs={{0,4},{1,5},{2,6},{3,7},{4,0},{5,1},{6,2},{7,3},{8,12},{9,13},{10,... | collective-permute-start | bytes 245768 | tf_op jit(solution)/shard_map/ppermute | solution.py:199
  15.2 1.1 %shard_map.67 = (f32[32,1024]{1,0:T(8,128)S(1)}, bf16[256,1024]{1,0:T(8,128)(2,1)S(1)}) custom-call(bf16[16,512]{1,0:T(8,128)(2,1)S(1)} %get-tuple-element.30.rows_ref.refs_0_, bf16[16,512]{1,0:T(8,128)(2,1)S(1)} %get-tuple-element.35.refs_1_, bf16[2,40,256]{2,1,0:T(8,128)(2,1)S(1)} %collective-permute-done.3.refs_0_.refs_2_, ...), custom_call_target="tpu_custom_call" | custom-call | flops 10000000000 | bytes 10000000000 | tf_op jit(solution)/shard_map/pallas_call | solution.py:221
  16.2 1.3 %shard_map.68 = (bf16[32,1024]{1,0:T(8,128)(2,1)S(1)}, bf16[256,1024]{1,0:T(8,128)(2,1)S(1)}) custom-call(bf16[16,512]{1,0:T(8,128)(2,1)S(1)} %get-tuple-element.30.rows_ref.refs_0_, bf16[16,512]{1,0:T(8,128)(2,1)S(1)} %get-tuple-element.35.refs_1_, bf16[4,40,256]{2,1,0:T(8,128)(2,1)S(1)} %collective-permute-done.6.refs_2_, ...), custom_call_target="tpu_custom_call" | custom-call | flops 10000000000 | bytes 10000000000 | tf_op jit(solution)/shard_map/pallas_call | solution.py:221
  17.5 0.2 %shard_map.69 = f32[1,32,256]{2,1,0:T(8,128)S(1)} custom-call(bf16[32,1024]{1,0:T(8,128)(2,1)S(1)} %get-tuple-element.46.q_ref, bf16[256,1024]{1,0:T(8,128)(2,1)S(1)} %get-tuple-element.45.refs_0_), custom_call_target="tpu_custom_call" | custom-call | flops 10000000000 | bytes 10000000000 | tf_op jit(solution)/shard_map/pallas_call | solution.py:221
  17.7 0.3 %collective-permute-start.7 = (f32[1,32,256]{2,1,0:T(8,128)S(1)}, f32[1,32,256]{2,1,0:T(8,128)S(1)}, u32[]{:S(2)}, u32[]{:S(2)}) collective-permute-start(f32[1,32,256]{2,1,0:T(8,128)S(1)} %shard_map.69), channel_id=1, source_target_pairs={{0,4},{1,5},{2,6},{3,7},{4,0},{5,1},{6,2},{7,3},{8,12},{9,13},{10,... | collective-permute-start | bytes 98312 | tf_op jit(solution)/shard_map/ppermute | solution.py:199
  18.1 0.5 %shard_map.70 = (f32[32,256]{1,0:T(8,128)S(1)}, f32[32,256]{1,0:T(8,128)S(1)}, f32[32,256]{1,0:T(8,128)S(1)}) custom-call(bf16[32,1024]{1,0:T(8,128)(2,1)S(1)} %get-tuple-element.46.q_ref, bf16[256,1024]{1,0:T(8,128)(2,1)S(1)} %get-tuple-element.47.refs_0_, bf16[256,1024]{1,0:T(8,128)(2,1)S(1)} %get-tuple-element.48.refs_1_, ...), custom_call_target="tpu_custom_call" | custom-call | flops 10000000000 | bytes 10000000000 | tf_op jit(solution)/shard_map/pallas_call | solution.py:221
  18.6 0.4 %collective-permute-done.7.given_ref = f32[1,32,256]{2,1,0:T(8,128)S(1)} collective-permute-done((f32[1,32,256]{2,1,0:T(8,128)S(1)}, f32[1,32,256]{2,1,0:T(8,128)S(1)}, u32[]{:S(2)}, u32[]{:S(2)}) %collective-permute-start.7) | collective-permute-done | bytes 32800 | tf_op jit(solution)/shard_map/ppermute | solution.py:199
  19.0 1.1 %collective-permute-start.8 = (f32[32,256]{1,0:T(8,128)S(1)}, f32[32,256]{1,0:T(8,128)S(1)}, u32[]{:S(2)}, u32[]{:S(2)}) collective-permute-start(f32[32,256]{1,0:T(8,128)S(1)} %shard_map.71), channel_id=1, source_target_pairs={{0,12},{1,13},{2,14},{3,15},{4,8},{5,9},{6,10},{7,11},{8,4},{9,5},... | collective-permute-start | bytes 98312 | tf_op jit(solution)/shard_map/ppermute | solution.py:199
  20.0 0.3 %collective-permute-start.9 = (f32[32,256]{1,0:T(8,128)S(1)}, f32[32,256]{1,0:T(8,128)S(1)}, u32[]{:S(2)}, u32[]{:S(2)}) collective-permute-start(f32[32,256]{1,0:T(8,128)S(1)} %get-tuple-element.55), channel_id=1, source_target_pairs={{0,4},{1,5},{2,6},{3,7},{4,0},{5,1},{6,2},{7,3},{8,12},{9,13},{10,... | collective-permute-start | bytes 98312 | tf_op jit(solution)/shard_map/ppermute | solution.py:199
  20.3 2.0 %collective-permute-done.8.refs_1_ = f32[32,256]{1,0:T(8,128)S(1)} collective-permute-done((f32[32,256]{1,0:T(8,128)S(1)}, f32[32,256]{1,0:T(8,128)S(1)}, u32[]{:S(2)}, u32[]{:S(2)}) %collective-permute-start.8) | collective-permute-done | bytes 32800 | tf_op jit(solution)/shard_map/ppermute | solution.py:199
  22.3 0.8 %shard_map.72 = (f32[32,256]{1,0:T(8,128)}, f32[32,256]{1,0:T(8,128)}) custom-call(bf16[32,1024]{1,0:T(8,128)(2,1)S(1)} %get-tuple-element.46.q_ref, f32[40,256]{1,0:T(8,128)S(1)} %get-tuple-element.29.refs_0_.refs_5_.near_ref, f32[32,32]{1,0:T(8,128)S(1)} %get-tuple-element.43.refs_4_.compat_ref, f32[32,256]{1,0:T(8,128)S(1)} %get-tuple-element.50.refs_0_, ...), custom_call_target="tpu_custom_call" | custom-call | flops 10000000000 | bytes 10000000000 | tf_op jit(solution)/shard_map/pallas_call | solution.py:221
  (10 shorter events, 0.1 us)
Async XLA Ops:
  1.7 6.5 %collective-permute-start = (f32[40,256]{1,0:T(8,128)S(1)}, f32[40,256]{1,0:T(8,128)S(1)}, u32[]{:S(2)}, u32[]{:S(2)}) collective-permute-start(f32[40,256]{1,0:T(8,128)S(1)} %get-tuple-element.29.refs_0_.refs_5_.near_ref), channel_id=1, source_target_pairs={{0,7},{1,6},{2,5},{3,4},{4,3},{5,2},{6,1},{7,0},{8,15},{9,14},{10,... | collective-permute-start | bytes 122888 | tf_op jit(solution)/shard_map/ppermute | solution.py:199
  6.2 4.6 %collective-permute-start.2 = (f32[40,256]{1,0:T(8,128)S(1)}, f32[40,256]{1,0:T(8,128)S(1)}, u32[]{:S(2)}, u32[]{:S(2)}) collective-permute-start(f32[40,256]{1,0:T(8,128)S(1)} %get-tuple-element.29.refs_0_.refs_5_.near_ref), channel_id=1, source_target_pairs={{0,1},{1,0},{2,3},{3,2},{4,5},{5,4},{6,7},{7,6},{8,9},{9,8},{10,11... | collective-permute-start | bytes 122888 | tf_op jit(solution)/shard_map/ppermute | solution.py:199
  6.3 4.6 %collective-permute-start.1 = (f32[40,256]{1,0:T(8,128)S(1)}, f32[40,256]{1,0:T(8,128)S(1)}, u32[]{:S(2)}, u32[]{:S(2)}) collective-permute-start(f32[40,256]{1,0:T(8,128)S(1)} %get-tuple-element.29.refs_0_.refs_5_.near_ref), channel_id=1, source_target_pairs={{0,6},{1,7},{2,4},{3,5},{4,2},{5,3},{6,0},{7,1},{8,14},{9,15},{10,... | collective-permute-start | bytes 122888 | tf_op jit(solution)/shard_map/ppermute | solution.py:199
  8.2 6.6 %collective-permute-start.3 = (bf16[2,40,256]{2,1,0:T(8,128)(2,1)S(1)}, bf16[2,40,256]{2,1,0:T(8,128)(2,1)S(1)}, u32[]{:S(2)}, u32[]{:S(2)}) collective-permute-start(bf16[2,40,256]{2,1,0:T(8,128)(2,1)S(1)} %get-tuple-element.31.packed_ref.refs_0_.refs_2_.refs_9_), channel_id=1, source_target_pairs={{0,12},{1,13},{2,14},{3,15},{4,8},{5,9},{6,10},{7,11},{8,4},{9,5},... | collective-permute-start | bytes 122888 | tf_op jit(solution)/shard_map/ppermute | solution.py:199
  10.9 4.0 %collective-permute-start.4 = (bf16[2,40,256]{2,1,0:T(8,128)(2,1)S(1)}, bf16[2,40,256]{2,1,0:T(8,128)(2,1)S(1)}, u32[]{:S(2)}, u32[]{:S(2)}) collective-permute-start(bf16[2,40,256]{2,1,0:T(8,128)(2,1)S(1)} %get-tuple-element.36.refs_1_.refs_3_.refs_10_), channel_id=1, source_target_pairs={{0,12},{1,13},{2,14},{3,15},{4,8},{5,9},{6,10},{7,11},{8,4},{9,5},... | collective-permute-start | bytes 122888 | tf_op jit(solution)/shard_map/ppermute | solution.py:199
  12.5 1.3 %collective-permute-start.5 = (bf16[4,40,256]{2,1,0:T(8,128)(2,1)S(1)}, bf16[4,40,256]{2,1,0:T(8,128)(2,1)S(1)}, u32[]{:S(2)}, u32[]{:S(2)}) collective-permute-start(bf16[4,40,256]{2,1,0:T(8,128)(2,1)S(1)} %shard_map.63), channel_id=1, source_target_pairs={{0,4},{1,5},{2,6},{3,7},{4,0},{5,1},{6,2},{7,3},{8,12},{9,13},{10,... | collective-permute-start | bytes 245768 | tf_op jit(solution)/shard_map/ppermute | solution.py:199
  14.9 1.3 %collective-permute-start.6 = (bf16[4,40,256]{2,1,0:T(8,128)(2,1)S(1)}, bf16[4,40,256]{2,1,0:T(8,128)(2,1)S(1)}, u32[]{:S(2)}, u32[]{:S(2)}) collective-permute-start(bf16[4,40,256]{2,1,0:T(8,128)(2,1)S(1)} %shard_map.66), channel_id=1, source_target_pairs={{0,4},{1,5},{2,6},{3,7},{4,0},{5,1},{6,2},{7,3},{8,12},{9,13},{10,... | collective-permute-start | bytes 245768 | tf_op jit(solution)/shard_map/ppermute | solution.py:199
  17.7 1.2 %collective-permute-start.7 = (f32[1,32,256]{2,1,0:T(8,128)S(1)}, f32[1,32,256]{2,1,0:T(8,128)S(1)}, u32[]{:S(2)}, u32[]{:S(2)}) collective-permute-start(f32[1,32,256]{2,1,0:T(8,128)S(1)} %shard_map.69), channel_id=1, source_target_pairs={{0,4},{1,5},{2,6},{3,7},{4,0},{5,1},{6,2},{7,3},{8,12},{9,13},{10,... | collective-permute-start | bytes 98312 | tf_op jit(solution)/shard_map/ppermute | solution.py:199
  19.0 3.3 %collective-permute-start.8 = (f32[32,256]{1,0:T(8,128)S(1)}, f32[32,256]{1,0:T(8,128)S(1)}, u32[]{:S(2)}, u32[]{:S(2)}) collective-permute-start(f32[32,256]{1,0:T(8,128)S(1)} %shard_map.71), channel_id=1, source_target_pairs={{0,12},{1,13},{2,14},{3,15},{4,8},{5,9},{6,10},{7,11},{8,4},{9,5},... | collective-permute-start | bytes 98312 | tf_op jit(solution)/shard_map/ppermute | solution.py:199
  20.0 2.3 %collective-permute-start.9 = (f32[32,256]{1,0:T(8,128)S(1)}, f32[32,256]{1,0:T(8,128)S(1)}, u32[]{:S(2)}, u32[]{:S(2)}) collective-permute-start(f32[32,256]{1,0:T(8,128)S(1)} %get-tuple-element.55), channel_id=1, source_target_pairs={{0,4},{1,5},{2,6},{3,7},{4,0},{5,1},{6,2},{7,3},{8,12},{9,13},{10,... | collective-permute-start | bytes 98312 | tf_op jit(solution)/shard_map/ppermute | solution.py:199

commit v27 on v26

--- a/solution.py
+++ b/solution.py
@@ -263,12 +263,16 @@
         )
 
     near_packed, near_rows = pack_half(near[:half])
+    copied = call(join_kernel, [kept(near_packed.shape, jnp.bfloat16)], *hold(near_packed))[0]
+    beside_near = swap(copied, 1)
     early_sum, early_tile = call(
         functools.partial(first_early, labels),
         [kept((labels, half * own), jnp.float32), kept((own, half * own), jnp.bfloat16)],
         *hold(near_rows, near_packed),
     )
-    early_sum, *rest = lax.optimization_barrier((early_sum, *near[half:]))
+    early_sum, beside_near, *rest = lax.optimization_barrier(
+        (early_sum, beside_near, *near[half:])
+    )
     rest_packed, rest_rows = pack_half(rest)
     packed, rows = (near_packed, rest_packed), (near_rows, rest_rows)
     parts = lax.axis_size("blk")
@@ -287,22 +291,23 @@
         return total
 
     def join(some):
-        kind = kept((nears, labels + 8, own), jnp.bfloat16)
+        blocks = sum(stack.shape[0] for stack in some)
+        kind = kept((blocks, labels + 8, own), jnp.bfloat16)
         return call(join_kernel, [kind], *hold(*some))[0]
 
-    joined = join(packed)
     if paired("blk"):
         steps = list(range(3, parts, 2))
         far = [[swap(some, step) for step in steps] for some in packed]
-        beside = swap(joined, 1)
+        beside = [beside_near, swap(join([rest_packed]), 1)]
         first(*packed)
         early, late = far
-        *late, _ = lax.optimization_barrier((*late, first(beside)))
+        *late, _ = lax.optimization_barrier((*late, first(*beside)))
         stacks = list(zip(early, late))
         stacks += [(swap(join(some), 1),) for some in stacks]
         steps = [0, 1] + steps + [step - 1 for step in steps]
     else:
         steps = list(range(parts))
+        joined = join(packed)
         stacks = [[swap(joined, step)] for step in steps[1:]]
         first(*packed)
         first(*stacks.pop(0))

time: 23.3 us -> 23.5 us (level)
  waiting for transfers between devices: 4.37 us -> 5.08 us
  starting transfers between devices: 10.5 us -> 10 us
    ppermute x10 -> x11, waiting for transfers between devices: 4.37 us -> 5.08 us  [swap(): return lax.ppermute(value, ('blk', 'grp'), pairs)]
    ppermute x10 -> x11, starting transfers between devices: 10.5 us -> 10 us  [swap(): return lax.ppermute(value, ('blk', 'grp'), pairs)]
    pallas_call x14 -> x15, Pallas kernels: 7.55 us -> 7.54 us  [call(): pl.pallas_call(kernel, out_shape=tuple(out_shapes), cost_estimate=pl.Cost...]
  transfers between devices with their start and end apart: 10 -> 11, of which waited for: 5 -> 7; matrix products, arithmetic and copies ran while one was open for 0% -> 0% of each run, Pallas kernels for 18% -> 18%
where the time goes in v27:
time: 23.5 us; the launch traced here: 23.3 us
  starting transfers between devices  10 us (43%)
  Pallas kernels  7.54 us (32%)
  waiting for transfers between devices  5.08 us (22%)
  between operations  0.7 us (3%)
    ppermute x11, starting transfers between devices, swap(): return lax.ppermute(value, ('blk', 'grp'), pairs)  10 us
    pallas_call x15, Pallas kernels, call(): pl.pallas_call(kernel, out_shape=tuple(out_shapes), cost_estimate=pl.Cost...  7.54 us
    ppermute x11, waiting for transfers between devices, swap(): return lax.ppermute(value, ('blk', 'grp'), pairs)  5.08 us
  transfers between devices with their start and end apart: 11, of which 7 were waited for; matrix products, arithmetic and copies ran while one was open for 0% of the time, Pallas kernels for 18%

profile of v27, /device:TPU:0, one launch (start us, length us, event | category | flops | bytes accessed | tf_op | source)
XLA Modules:
  0.0 23.3 jit_solution(17648668626442190428)
XLA Ops:
  0.6 1.1 %shard_map.59 = (f32[40,256]{1,0:T(8,128)S(1)}, f32[32,32]{1,0:T(8,128)S(1)}) custom-call(bf16[6,4096]{1,0:T(8,128)(2,1)} %features_ref.1, s32[1,256]{1,0:T(1,128)} %bitcast.1, f32[32,256]{1,0:T(8,128)} %unary_ref.1, f32[32,32]{1,0:T(8,128)} %compat_ref.1), custom_call_target="tpu_custom_call" | custom-call | flops 10000000000 | bytes 10000000000 | tf_op jit(solution)/shard_map/pallas_call | solution.py:221
  1.7 4.6 %collective-permute-start = (f32[40,256]{1,0:T(8,128)S(1)}, f32[40,256]{1,0:T(8,128)S(1)}, u32[]{:S(2)}, u32[]{:S(2)}) collective-permute-start(f32[40,256]{1,0:T(8,128)S(1)} %get-tuple-element.30.refs_0_.refs_5_.near_ref), channel_id=1, source_target_pairs={{0,7},{1,6},{2,5},{3,4},{4,3},{5,2},{6,1},{7,0},{8,15},{9,14},{10,... | collective-permute-start | bytes 122888 | tf_op jit(solution)/shard_map/ppermute | solution.py:199
  6.3 0.4 %collective-permute-start.2 = (f32[40,256]{1,0:T(8,128)S(1)}, f32[40,256]{1,0:T(8,128)S(1)}, u32[]{:S(2)}, u32[]{:S(2)}) collective-permute-start(f32[40,256]{1,0:T(8,128)S(1)} %get-tuple-element.30.refs_0_.refs_5_.near_ref), channel_id=1, source_target_pairs={{0,6},{1,7},{2,4},{3,5},{4,2},{5,3},{6,0},{7,1},{8,14},{9,15},{10,... | collective-permute-start | bytes 122888 | tf_op jit(solution)/shard_map/ppermute | solution.py:199
  6.6 1.6 %collective-permute-done.refs_1_.refs_6_ = f32[40,256]{1,0:T(8,128)S(1)} collective-permute-done((f32[40,256]{1,0:T(8,128)S(1)}, f32[40,256]{1,0:T(8,128)S(1)}, u32[]{:S(2)}, u32[]{:S(2)}) %collective-permute-start) | collective-permute-done | bytes 40992 | tf_op jit(solution)/shard_map/ppermute | solution.py:199
  8.3 1.9 %collective-permute-start.4 = (bf16[2,40,256]{2,1,0:T(8,128)(2,1)S(1)}, bf16[2,40,256]{2,1,0:T(8,128)(2,1)S(1)}, u32[]{:S(2)}, u32[]{:S(2)}) collective-permute-start(bf16[2,40,256]{2,1,0:T(8,128)(2,1)S(1)} %get-tuple-element.32.packed_ref.refs_0_.refs_2_.refs_9_), channel_id=1, source_target_pairs={{0,12},{1,13},{2,14},{3,15},{4,8},{5,9},{6,10},{7,11},{8,4},{9,5},... | collective-permute-start | bytes 122888 | tf_op jit(solution)/shard_map/ppermute | solution.py:199
  10.2 0.2 %collective-permute-start.1 = (bf16[2,40,256]{2,1,0:T(8,128)(2,1)S(1)}, bf16[2,40,256]{2,1,0:T(8,128)(2,1)S(1)}, u32[]{:S(2)}, u32[]{:S(2)}) collective-permute-start(bf16[2,40,256]{2,1,0:T(8,128)(2,1)S(1)} %shard_map.62), channel_id=1, source_target_pairs={{0,4},{1,5},{2,6},{3,7},{4,0},{5,1},{6,2},{7,3},{8,12},{9,13},{10,... | collective-permute-start | bytes 122888 | tf_op jit(solution)/shard_map/ppermute | solution.py:199
  10.4 0.5 %shard_map.61 = (f32[32,512]{1,0:T(8,128)S(1)}, bf16[256,512]{1,0:T(8,128)(2,1)S(1)}) custom-call(bf16[16,512]{1,0:T(8,128)(2,1)S(1)} %get-tuple-element.31.rows_ref.refs_0_, bf16[2,40,256]{2,1,0:T(8,128)(2,1)S(1)} %get-tuple-element.32.packed_ref.refs_0_.refs_2_.refs_9_), custom_call_target="tpu_custom_call" | custom-call | flops 10000000000 | bytes 10000000000 | tf_op jit(solution)/shard_map/pallas_call | solution.py:221
  11.0 0.5 %collective-permute-done.1.refs_2_ = bf16[2,40,256]{2,1,0:T(8,128)(2,1)S(1)} collective-permute-done((bf16[2,40,256]{2,1,0:T(8,128)(2,1)S(1)}, bf16[2,40,256]{2,1,0:T(8,128)(2,1)S(1)}, u32[]{:S(2)}, u32[]{:S(2)}) %collective-permute-start.1) | collective-permute-done | bytes 40992 | tf_op jit(solution)/shard_map/ppermute | solution.py:199
  11.5 1.0 %collective-permute-start.5 = (bf16[2,40,256]{2,1,0:T(8,128)(2,1)S(1)}, bf16[2,40,256]{2,1,0:T(8,128)(2,1)S(1)}, u32[]{:S(2)}, u32[]{:S(2)}) collective-permute-start(bf16[2,40,256]{2,1,0:T(8,128)(2,1)S(1)} %get-tuple-element.37.refs_0_.refs_3_.refs_10_), channel_id=1, source_target_pairs={{0,12},{1,13},{2,14},{3,15},{4,8},{5,9},{6,10},{7,11},{8,4},{9,5},... | collective-permute-start | bytes 122888 | tf_op jit(solution)/shard_map/ppermute | solution.py:199
  12.6 1.0 %shard_map.65 = (f32[32,1024]{1,0:T(8,128)S(1)}, bf16[256,1024]{1,0:T(8,128)(2,1)S(1)}) custom-call(bf16[16,512]{1,0:T(8,128)(2,1)S(1)} %get-tuple-element.31.rows_ref.refs_0_, bf16[16,512]{1,0:T(8,128)(2,1)S(1)} %get-tuple-element.36.refs_1_, bf16[2,40,256]{2,1,0:T(8,128)(2,1)S(1)} %get-tuple-element.32.packed_ref.refs_0_.refs_2_.refs_9_, ...), custom_call_target="tpu_custom_call" | custom-call | flops 10000000000 | bytes 10000000000 | tf_op jit(solution)/shard_map/pallas_call | solution.py:221
  13.6 0.2 collective-permute-done.6.refs_3_
  13.7 1.1 %shard_map.66 = (f32[32,1024]{1,0:T(8,128)S(1)}, bf16[256,1024]{1,0:T(8,128)(2,1)S(1)}) custom-call(bf16[16,512]{1,0:T(8,128)(2,1)S(1)} %get-tuple-element.31.rows_ref.refs_0_, bf16[16,512]{1,0:T(8,128)(2,1)S(1)} %get-tuple-element.36.refs_1_, bf16[2,40,256]{2,1,0:T(8,128)(2,1)S(1)} %collective-permute-done.1.refs_2_, ...), custom_call_target="tpu_custom_call" | custom-call | flops 10000000000 | bytes 10000000000 | tf_op jit(solution)/shard_map/pallas_call | solution.py:221
  14.8 0.3 %collective-permute-done.5.refs_1_.refs_3_ = bf16[2,40,256]{2,1,0:T(8,128)(2,1)S(1)} collective-permute-done((bf16[2,40,256]{2,1,0:T(8,128)(2,1)S(1)}, bf16[2,40,256]{2,1,0:T(8,128)(2,1)S(1)}, u32[]{:S(2)}, u32[]{:S(2)}) %collective-permute-start.5) | collective-permute-done | bytes 40992 | tf_op jit(solution)/shard_map/ppermute | solution.py:199
  15.1 0.2 %collective-permute-start.7 = (bf16[4,40,256]{2,1,0:T(8,128)(2,1)S(1)}, bf16[4,40,256]{2,1,0:T(8,128)(2,1)S(1)}, u32[]{:S(2)}, u32[]{:S(2)}) collective-permute-start(bf16[4,40,256]{2,1,0:T(8,128)(2,1)S(1)} %shard_map.67), channel_id=1, source_target_pairs={{0,4},{1,5},{2,6},{3,7},{4,0},{5,1},{6,2},{7,3},{8,12},{9,13},{10,... | collective-permute-start | bytes 245768 | tf_op jit(solution)/shard_map/ppermute | solution.py:199
  15.3 1.0 %shard_map.68 = (f32[32,1024]{1,0:T(8,128)S(1)}, bf16[256,1024]{1,0:T(8,128)(2,1)S(1)}) custom-call(bf16[16,512]{1,0:T(8,128)(2,1)S(1)} %get-tuple-element.31.rows_ref.refs_0_, bf16[16,512]{1,0:T(8,128)(2,1)S(1)} %get-tuple-element.36.refs_1_, bf16[2,40,256]{2,1,0:T(8,128)(2,1)S(1)} %collective-permute-done.4.refs_0_.refs_2_, ...), custom_call_target="tpu_custom_call" | custom-call | flops 10000000000 | bytes 10000000000 | tf_op jit(solution)/shard_map/pallas_call | solution.py:221
  16.4 1.3 %shard_map.69 = (bf16[32,1024]{1,0:T(8,128)(2,1)S(1)}, bf16[256,1024]{1,0:T(8,128)(2,1)S(1)}) custom-call(bf16[16,512]{1,0:T(8,128)(2,1)S(1)} %get-tuple-element.31.rows_ref.refs_0_, bf16[16,512]{1,0:T(8,128)(2,1)S(1)} %get-tuple-element.36.refs_1_, bf16[4,40,256]{2,1,0:T(8,128)(2,1)S(1)} %collective-permute-done.7.refs_2_, ...), custom_call_target="tpu_custom_call" | custom-call | flops 10000000000 | bytes 10000000000 | tf_op jit(solution)/shard_map/pallas_call | solution.py:221
  17.7 0.2 shard_map.70
  17.9 0.3 %collective-permute-start.8 = (f32[1,32,256]{2,1,0:T(8,128)S(1)}, f32[1,32,256]{2,1,0:T(8,128)S(1)}, u32[]{:S(2)}, u32[]{:S(2)}) collective-permute-start(f32[1,32,256]{2,1,0:T(8,128)S(1)} %shard_map.70), channel_id=1, source_target_pairs={{0,4},{1,5},{2,6},{3,7},{4,0},{5,1},{6,2},{7,3},{8,12},{9,13},{10,... | collective-permute-start | bytes 98312 | tf_op jit(solution)/shard_map/ppermute | solution.py:199
  18.2 0.5 %shard_map.71 = (f32[32,256]{1,0:T(8,128)S(1)}, f32[32,256]{1,0:T(8,128)S(1)}, f32[32,256]{1,0:T(8,128)S(1)}) custom-call(bf16[32,1024]{1,0:T(8,128)(2,1)S(1)} %get-tuple-element.48.q_ref, bf16[256,1024]{1,0:T(8,128)(2,1)S(1)} %get-tuple-element.49.refs_0_, bf16[256,1024]{1,0:T(8,128)(2,1)S(1)} %get-tuple-element.50.refs_1_, ...), custom_call_target="tpu_custom_call" | custom-call | flops 10000000000 | bytes 10000000000 | tf_op jit(solution)/shard_map/pallas_call | solution.py:221
  18.8 0.4 %collective-permute-done.8.given_ref = f32[1,32,256]{2,1,0:T(8,128)S(1)} collective-permute-done((f32[1,32,256]{2,1,0:T(8,128)S(1)}, f32[1,32,256]{2,1,0:T(8,128)S(1)}, u32[]{:S(2)}, u32[]{:S(2)}) %collective-permute-start.8) | collective-permute-done | bytes 32800 | tf_op jit(solution)/shard_map/ppermute | solution.py:199
  19.2 0.9 %collective-permute-start.9 = (f32[32,256]{1,0:T(8,128)S(1)}, f32[32,256]{1,0:T(8,128)S(1)}, u32[]{:S(2)}, u32[]{:S(2)}) collective-permute-start(f32[32,256]{1,0:T(8,128)S(1)} %shard_map.72), channel_id=1, source_target_pairs={{0,12},{1,13},{2,14},{3,15},{4,8},{5,9},{6,10},{7,11},{8,4},{9,5},... | collective-permute-start | bytes 98312 | tf_op jit(solution)/shard_map/ppermute | solution.py:199
  20.1 0.3 %collective-permute-start.10 = (f32[32,256]{1,0:T(8,128)S(1)}, f32[32,256]{1,0:T(8,128)S(1)}, u32[]{:S(2)}, u32[]{:S(2)}) collective-permute-start(f32[32,256]{1,0:T(8,128)S(1)} %get-tuple-element.57), channel_id=1, source_target_pairs={{0,4},{1,5},{2,6},{3,7},{4,0},{5,1},{6,2},{7,3},{8,12},{9,13},{10,... | collective-permute-start | bytes 98312 | tf_op jit(solution)/shard_map/ppermute | solution.py:199
  20.4 2.1 %collective-permute-done.9.refs_1_ = f32[32,256]{1,0:T(8,128)S(1)} collective-permute-done((f32[32,256]{1,0:T(8,128)S(1)}, f32[32,256]{1,0:T(8,128)S(1)}, u32[]{:S(2)}, u32[]{:S(2)}) %collective-permute-start.9) | collective-permute-done | bytes 32800 | tf_op jit(solution)/shard_map/ppermute | solution.py:199
  22.5 0.8 %shard_map.73 = (f32[32,256]{1,0:T(8,128)}, f32[32,256]{1,0:T(8,128)}) custom-call(bf16[32,1024]{1,0:T(8,128)(2,1)S(1)} %get-tuple-element.48.q_ref, f32[40,256]{1,0:T(8,128)S(1)} %get-tuple-element.30.refs_0_.refs_5_.near_ref, f32[32,32]{1,0:T(8,128)S(1)} %get-tuple-element.45.refs_4_.compat_ref, f32[32,256]{1,0:T(8,128)S(1)} %get-tuple-element.52.refs_0_, ...), custom_call_target="tpu_custom_call" | custom-call | flops 10000000000 | bytes 10000000000 | tf_op jit(solution)/shard_map/pallas_call | solution.py:221
  (13 shorter events, 0.2 us)
Async XLA Ops:
  1.7 6.5 %collective-permute-start = (f32[40,256]{1,0:T(8,128)S(1)}, f32[40,256]{1,0:T(8,128)S(1)}, u32[]{:S(2)}, u32[]{:S(2)}) collective-permute-start(f32[40,256]{1,0:T(8,128)S(1)} %get-tuple-element.30.refs_0_.refs_5_.near_ref), channel_id=1, source_target_pairs={{0,7},{1,6},{2,5},{3,4},{4,3},{5,2},{6,1},{7,0},{8,15},{9,14},{10,... | collective-permute-start | bytes 122888 | tf_op jit(solution)/shard_map/ppermute | solution.py:199
  6.2 4.7 %collective-permute-start.3 = (f32[40,256]{1,0:T(8,128)S(1)}, f32[40,256]{1,0:T(8,128)S(1)}, u32[]{:S(2)}, u32[]{:S(2)}) collective-permute-start(f32[40,256]{1,0:T(8,128)S(1)} %get-tuple-element.30.refs_0_.refs_5_.near_ref), channel_id=1, source_target_pairs={{0,1},{1,0},{2,3},{3,2},{4,5},{5,4},{6,7},{7,6},{8,9},{9,8},{10,11... | collective-permute-start | bytes 122888 | tf_op jit(solution)/shard_map/ppermute | solution.py:199
  6.3 4.7 %collective-permute-start.2 = (f32[40,256]{1,0:T(8,128)S(1)}, f32[40,256]{1,0:T(8,128)S(1)}, u32[]{:S(2)}, u32[]{:S(2)}) collective-permute-start(f32[40,256]{1,0:T(8,128)S(1)} %get-tuple-element.30.refs_0_.refs_5_.near_ref), channel_id=1, source_target_pairs={{0,6},{1,7},{2,4},{3,5},{4,2},{5,3},{6,0},{7,1},{8,14},{9,15},{10,... | collective-permute-start | bytes 122888 | tf_op jit(solution)/shard_map/ppermute | solution.py:199
  8.3 6.8 %collective-permute-start.4 = (bf16[2,40,256]{2,1,0:T(8,128)(2,1)S(1)}, bf16[2,40,256]{2,1,0:T(8,128)(2,1)S(1)}, u32[]{:S(2)}, u32[]{:S(2)}) collective-permute-start(bf16[2,40,256]{2,1,0:T(8,128)(2,1)S(1)} %get-tuple-element.32.packed_ref.refs_0_.refs_2_.refs_9_), channel_id=1, source_target_pairs={{0,12},{1,13},{2,14},{3,15},{4,8},{5,9},{6,10},{7,11},{8,4},{9,5},... | collective-permute-start | bytes 122888 | tf_op jit(solution)/shard_map/ppermute | solution.py:199
  10.2 1.2 %collective-permute-start.1 = (bf16[2,40,256]{2,1,0:T(8,128)(2,1)S(1)}, bf16[2,40,256]{2,1,0:T(8,128)(2,1)S(1)}, u32[]{:S(2)}, u32[]{:S(2)}) collective-permute-start(bf16[2,40,256]{2,1,0:T(8,128)(2,1)S(1)} %shard_map.62), channel_id=1, source_target_pairs={{0,4},{1,5},{2,6},{3,7},{4,0},{5,1},{6,2},{7,3},{8,12},{9,13},{10,... | collective-permute-start | bytes 122888 | tf_op jit(solution)/shard_map/ppermute | solution.py:199
  11.5 3.6 %collective-permute-start.5 = (bf16[2,40,256]{2,1,0:T(8,128)(2,1)S(1)}, bf16[2,40,256]{2,1,0:T(8,128)(2,1)S(1)}, u32[]{:S(2)}, u32[]{:S(2)}) collective-permute-start(bf16[2,40,256]{2,1,0:T(8,128)(2,1)S(1)} %get-tuple-element.37.refs_0_.refs_3_.refs_10_), channel_id=1, source_target_pairs={{0,12},{1,13},{2,14},{3,15},{4,8},{5,9},{6,10},{7,11},{8,4},{9,5},... | collective-permute-start | bytes 122888 | tf_op jit(solution)/shard_map/ppermute | solution.py:199
  12.5 1.2 %collective-permute-start.6 = (bf16[2,40,256]{2,1,0:T(8,128)(2,1)S(1)}, bf16[2,40,256]{2,1,0:T(8,128)(2,1)S(1)}, u32[]{:S(2)}, u32[]{:S(2)}) collective-permute-start(bf16[2,40,256]{2,1,0:T(8,128)(2,1)S(1)} %shard_map.64), channel_id=1, source_target_pairs={{0,4},{1,5},{2,6},{3,7},{4,0},{5,1},{6,2},{7,3},{8,12},{9,13},{10,... | collective-permute-start | bytes 122888 | tf_op jit(solution)/shard_map/ppermute | solution.py:199
  15.1 1.3 %collective-permute-start.7 = (bf16[4,40,256]{2,1,0:T(8,128)(2,1)S(1)}, bf16[4,40,256]{2,1,0:T(8,128)(2,1)S(1)}, u32[]{:S(2)}, u32[]{:S(2)}) collective-permute-start(bf16[4,40,256]{2,1,0:T(8,128)(2,1)S(1)} %shard_map.67), channel_id=1, source_target_pairs={{0,4},{1,5},{2,6},{3,7},{4,0},{5,1},{6,2},{7,3},{8,12},{9,13},{10,... | collective-permute-start | bytes 245768 | tf_op jit(solution)/shard_map/ppermute | solution.py:199
  17.9 1.2 %collective-permute-start.8 = (f32[1,32,256]{2,1,0:T(8,128)S(1)}, f32[1,32,256]{2,1,0:T(8,128)S(1)}, u32[]{:S(2)}, u32[]{:S(2)}) collective-permute-start(f32[1,32,256]{2,1,0:T(8,128)S(1)} %shard_map.70), channel_id=1, source_target_pairs={{0,4},{1,5},{2,6},{3,7},{4,0},{5,1},{6,2},{7,3},{8,12},{9,13},{10,... | collective-permute-start | bytes 98312 | tf_op jit(solution)/shard_map/ppermute | solution.py:199
  19.2 3.3 %collective-permute-start.9 = (f32[32,256]{1,0:T(8,128)S(1)}, f32[32,256]{1,0:T(8,128)S(1)}, u32[]{:S(2)}, u32[]{:S(2)}) collective-permute-start(f32[32,256]{1,0:T(8,128)S(1)} %shard_map.72), channel_id=1, source_target_pairs={{0,12},{1,13},{2,14},{3,15},{4,8},{5,9},{6,10},{7,11},{8,4},{9,5},... | collective-permute-start | bytes 98312 | tf_op jit(solution)/shard_map/ppermute | solution.py:199
  20.1 2.5 %collective-permute-start.10 = (f32[32,256]{1,0:T(8,128)S(1)}, f32[32,256]{1,0:T(8,128)S(1)}, u32[]{:S(2)}, u32[]{:S(2)}) collective-permute-start(f32[32,256]{1,0:T(8,128)S(1)} %get-tuple-element.57), channel_id=1, source_target_pairs={{0,4},{1,5},{2,6},{3,7},{4,0},{5,1},{6,2},{7,3},{8,12},{9,13},{10,... | collective-permute-start | bytes 98312 | tf_op jit(solution)/shard_map/ppermute | solution.py:199

commit v28 on v26

--- a/solution.py
+++ b/solution.py
@@ -201,7 +201,7 @@
 
 def group_partners(value):
     count = lax.axis_size("grp")
-    order = sorted(range(1, count), reverse=True)
+    order = sorted(range(1, count), key=lambda steps: (steps != count - 1, steps))
     crossed = paired("blk") and paired("grp") and lax.axis_size("blk") > 1
     return [value] + [
         swap(value, 2 * steps // count if crossed else 0, steps) for steps in order

time: 23.3 us -> 23.3 us (level)
  no operation moved by 1% of the time
where the time goes in v28:
time: 23.3 us; the launch traced here: 23.1 us
  starting transfers between devices  10.7 us (46%)
  Pallas kernels  7.56 us (32%)
  waiting for transfers between devices  4.21 us (18%)
  between operations  0.69 us (3%)
    ppermute x10, starting transfers between devices, swap(): return lax.ppermute(value, ('blk', 'grp'), pairs)  10.7 us
    pallas_call x14, Pallas kernels, call(): pl.pallas_call(kernel, out_shape=tuple(out_shapes), cost_estimate=pl.Cost...  7.56 us
    ppermute x10, waiting for transfers between devices, swap(): return lax.ppermute(value, ('blk', 'grp'), pairs)  4.21 us
  transfers between devices with their start and end apart: 10, of which 5 were waited for; matrix products, arithmetic and copies ran while one was open for 0% of the time, Pallas kernels for 18%

profile of v28, /device:TPU:0, one launch (start us, length us, event | category | flops | bytes accessed | tf_op | source)
XLA Modules:
  0.0 23.1 jit_solution(17780803522065244484)
XLA Ops:
  0.6 1.1 %shard_map.59 = (f32[40,256]{1,0:T(8,128)S(1)}, f32[32,32]{1,0:T(8,128)S(1)}) custom-call(bf16[6,4096]{1,0:T(8,128)(2,1)} %features_ref.1, s32[1,256]{1,0:T(1,128)} %bitcast.1, f32[32,256]{1,0:T(8,128)} %unary_ref.1, f32[32,32]{1,0:T(8,128)} %compat_ref.1), custom_call_target="tpu_custom_call" | custom-call | flops 10000000000 | bytes 10000000000 | tf_op jit(solution)/shard_map/pallas_call | solution.py:221
  1.7 4.6 %collective-permute-start = (f32[40,256]{1,0:T(8,128)S(1)}, f32[40,256]{1,0:T(8,128)S(1)}, u32[]{:S(2)}, u32[]{:S(2)}) collective-permute-start(f32[40,256]{1,0:T(8,128)S(1)} %get-tuple-element.29.refs_0_.refs_5_.near_ref), channel_id=1, source_target_pairs={{0,7},{1,6},{2,5},{3,4},{4,3},{5,2},{6,1},{7,0},{8,15},{9,14},{10,... | collective-permute-start | bytes 122888 | tf_op jit(solution)/shard_map/ppermute | solution.py:199
  6.3 0.6 %collective-permute-start.1 = (f32[40,256]{1,0:T(8,128)S(1)}, f32[40,256]{1,0:T(8,128)S(1)}, u32[]{:S(2)}, u32[]{:S(2)}) collective-permute-start(f32[40,256]{1,0:T(8,128)S(1)} %get-tuple-element.29.refs_0_.refs_5_.near_ref), channel_id=1, source_target_pairs={{0,1},{1,0},{2,3},{3,2},{4,5},{5,4},{6,7},{7,6},{8,9},{9,8},{10,11... | collective-permute-start | bytes 122888 | tf_op jit(solution)/shard_map/ppermute | solution.py:199
  6.9 1.3 %collective-permute-done.refs_1_.refs_6_ = f32[40,256]{1,0:T(8,128)S(1)} collective-permute-done((f32[40,256]{1,0:T(8,128)S(1)}, f32[40,256]{1,0:T(8,128)S(1)}, u32[]{:S(2)}, u32[]{:S(2)}) %collective-permute-start) | collective-permute-done | bytes 40992 | tf_op jit(solution)/shard_map/ppermute | solution.py:199
  8.2 1.8 %collective-permute-start.3 = (bf16[2,40,256]{2,1,0:T(8,128)(2,1)S(1)}, bf16[2,40,256]{2,1,0:T(8,128)(2,1)S(1)}, u32[]{:S(2)}, u32[]{:S(2)}) collective-permute-start(bf16[2,40,256]{2,1,0:T(8,128)(2,1)S(1)} %get-tuple-element.31.packed_ref.refs_0_.refs_2_.refs_9_), channel_id=1, source_target_pairs={{0,12},{1,13},{2,14},{3,15},{4,8},{5,9},{6,10},{7,11},{8,4},{9,5},... | collective-permute-start | bytes 122888 | tf_op jit(solution)/shard_map/ppermute | solution.py:199
  10.0 0.5 %shard_map.61 = (f32[32,512]{1,0:T(8,128)S(1)}, bf16[256,512]{1,0:T(8,128)(2,1)S(1)}) custom-call(bf16[16,512]{1,0:T(8,128)(2,1)S(1)} %get-tuple-element.30.rows_ref.refs_0_, bf16[2,40,256]{2,1,0:T(8,128)(2,1)S(1)} %get-tuple-element.31.packed_ref.refs_0_.refs_2_.refs_9_), custom_call_target="tpu_custom_call" | custom-call | flops 10000000000 | bytes 10000000000 | tf_op jit(solution)/shard_map/pallas_call | solution.py:221
  10.5 0.3 %collective-permute-done.2.refs_1_.refs_8_ = f32[40,256]{1,0:T(8,128)S(1)} collective-permute-done((f32[40,256]{1,0:T(8,128)S(1)}, f32[40,256]{1,0:T(8,128)S(1)}, u32[]{:S(2)}, u32[]{:S(2)}) %collective-permute-start.2) | collective-permute-done | bytes 40992 | tf_op jit(solution)/shard_map/ppermute | solution.py:199
  10.9 1.6 %collective-permute-start.4 = (bf16[2,40,256]{2,1,0:T(8,128)(2,1)S(1)}, bf16[2,40,256]{2,1,0:T(8,128)(2,1)S(1)}, u32[]{:S(2)}, u32[]{:S(2)}) collective-permute-start(bf16[2,40,256]{2,1,0:T(8,128)(2,1)S(1)} %get-tuple-element.36.refs_1_.refs_3_.refs_10_), channel_id=1, source_target_pairs={{0,12},{1,13},{2,14},{3,15},{4,8},{5,9},{6,10},{7,11},{8,4},{9,5},... | collective-permute-start | bytes 122888 | tf_op jit(solution)/shard_map/ppermute | solution.py:199
  12.5 0.1 collective-permute-start.5
  12.6 1.0 %shard_map.64 = (f32[32,1024]{1,0:T(8,128)S(1)}, bf16[256,1024]{1,0:T(8,128)(2,1)S(1)}) custom-call(bf16[16,512]{1,0:T(8,128)(2,1)S(1)} %get-tuple-element.30.rows_ref.refs_0_, bf16[16,512]{1,0:T(8,128)(2,1)S(1)} %get-tuple-element.35.refs_1_, bf16[2,40,256]{2,1,0:T(8,128)(2,1)S(1)} %get-tuple-element.31.packed_ref.refs_0_.refs_2_.refs_9_, ...), custom_call_target="tpu_custom_call" | custom-call | flops 10000000000 | bytes 10000000000 | tf_op jit(solution)/shard_map/pallas_call | solution.py:221
  13.6 0.2 collective-permute-done.5.refs_2_
  13.8 1.1 %shard_map.65 = (f32[32,1024]{1,0:T(8,128)S(1)}, bf16[256,1024]{1,0:T(8,128)(2,1)S(1)}) custom-call(bf16[16,512]{1,0:T(8,128)(2,1)S(1)} %get-tuple-element.30.rows_ref.refs_0_, bf16[16,512]{1,0:T(8,128)(2,1)S(1)} %get-tuple-element.35.refs_1_, bf16[4,40,256]{2,1,0:T(8,128)(2,1)S(1)} %collective-permute-done.5.refs_2_, f32[32,1024]{1,0:T(8,128)S(1)} %get-tuple-element.39.refs_3_), custom_call_target="tpu_custom_call" | custom-call | flops 10000000000 | bytes 10000000000 | tf_op jit(solution)/shard_map/pallas_call | solution.py:221
  14.9 0.3 %collective-permute-start.6 = (bf16[4,40,256]{2,1,0:T(8,128)(2,1)S(1)}, bf16[4,40,256]{2,1,0:T(8,128)(2,1)S(1)}, u32[]{:S(2)}, u32[]{:S(2)}) collective-permute-start(bf16[4,40,256]{2,1,0:T(8,128)(2,1)S(1)} %shard_map.66), channel_id=1, source_target_pairs={{0,4},{1,5},{2,6},{3,7},{4,0},{5,1},{6,2},{7,3},{8,12},{9,13},{10,... | collective-permute-start | bytes 245768 | tf_op jit(solution)/shard_map/ppermute | solution.py:199
  15.1 1.1 %shard_map.67 = (f32[32,1024]{1,0:T(8,128)S(1)}, bf16[256,1024]{1,0:T(8,128)(2,1)S(1)}) custom-call(bf16[16,512]{1,0:T(8,128)(2,1)S(1)} %get-tuple-element.30.rows_ref.refs_0_, bf16[16,512]{1,0:T(8,128)(2,1)S(1)} %get-tuple-element.35.refs_1_, bf16[2,40,256]{2,1,0:T(8,128)(2,1)S(1)} %collective-permute-done.3.refs_0_.refs_2_, ...), custom_call_target="tpu_custom_call" | custom-call | flops 10000000000 | bytes 10000000000 | tf_op jit(solution)/shard_map/pallas_call | solution.py:221
  16.2 0.0 collective-permute-done.6.refs_2_
  16.2 1.3 %shard_map.68 = (bf16[32,1024]{1,0:T(8,128)(2,1)S(1)}, bf16[256,1024]{1,0:T(8,128)(2,1)S(1)}) custom-call(bf16[16,512]{1,0:T(8,128)(2,1)S(1)} %get-tuple-element.30.rows_ref.refs_0_, bf16[16,512]{1,0:T(8,128)(2,1)S(1)} %get-tuple-element.35.refs_1_, bf16[4,40,256]{2,1,0:T(8,128)(2,1)S(1)} %collective-permute-done.6.refs_2_, ...), custom_call_target="tpu_custom_call" | custom-call | flops 10000000000 | bytes 10000000000 | tf_op jit(solution)/shard_map/pallas_call | solution.py:221
  17.5 0.2 %shard_map.69 = f32[1,32,256]{2,1,0:T(8,128)S(1)} custom-call(bf16[32,1024]{1,0:T(8,128)(2,1)S(1)} %get-tuple-element.46.q_ref, bf16[256,1024]{1,0:T(8,128)(2,1)S(1)} %get-tuple-element.45.refs_0_), custom_call_target="tpu_custom_call" | custom-call | flops 10000000000 | bytes 10000000000 | tf_op jit(solution)/shard_map/pallas_call | solution.py:221
  17.7 0.4 %collective-permute-start.7 = (f32[1,32,256]{2,1,0:T(8,128)S(1)}, f32[1,32,256]{2,1,0:T(8,128)S(1)}, u32[]{:S(2)}, u32[]{:S(2)}) collective-permute-start(f32[1,32,256]{2,1,0:T(8,128)S(1)} %shard_map.69), channel_id=1, source_target_pairs={{0,4},{1,5},{2,6},{3,7},{4,0},{5,1},{6,2},{7,3},{8,12},{9,13},{10,... | collective-permute-start | bytes 98312 | tf_op jit(solution)/shard_map/ppermute | solution.py:199
  18.1 0.5 %shard_map.70 = (f32[32,256]{1,0:T(8,128)S(1)}, f32[32,256]{1,0:T(8,128)S(1)}, f32[32,256]{1,0:T(8,128)S(1)}) custom-call(bf16[32,1024]{1,0:T(8,128)(2,1)S(1)} %get-tuple-element.46.q_ref, bf16[256,1024]{1,0:T(8,128)(2,1)S(1)} %get-tuple-element.47.refs_0_, bf16[256,1024]{1,0:T(8,128)(2,1)S(1)} %get-tuple-element.48.refs_1_, ...), custom_call_target="tpu_custom_call" | custom-call | flops 10000000000 | bytes 10000000000 | tf_op jit(solution)/shard_map/pallas_call | solution.py:221
  18.6 0.4 %collective-permute-done.7.given_ref = f32[1,32,256]{2,1,0:T(8,128)S(1)} collective-permute-done((f32[1,32,256]{2,1,0:T(8,128)S(1)}, f32[1,32,256]{2,1,0:T(8,128)S(1)}, u32[]{:S(2)}, u32[]{:S(2)}) %collective-permute-start.7) | collective-permute-done | bytes 32800 | tf_op jit(solution)/shard_map/ppermute | solution.py:199
  19.0 1.0 %collective-permute-start.8 = (f32[32,256]{1,0:T(8,128)S(1)}, f32[32,256]{1,0:T(8,128)S(1)}, u32[]{:S(2)}, u32[]{:S(2)}) collective-permute-start(f32[32,256]{1,0:T(8,128)S(1)} %shard_map.71), channel_id=1, source_target_pairs={{0,12},{1,13},{2,14},{3,15},{4,8},{5,9},{6,10},{7,11},{8,4},{9,5},... | collective-permute-start | bytes 98312 | tf_op jit(solution)/shard_map/ppermute | solution.py:199
  20.0 0.3 %collective-permute-start.9 = (f32[32,256]{1,0:T(8,128)S(1)}, f32[32,256]{1,0:T(8,128)S(1)}, u32[]{:S(2)}, u32[]{:S(2)}) collective-permute-start(f32[32,256]{1,0:T(8,128)S(1)} %get-tuple-element.55), channel_id=1, source_target_pairs={{0,4},{1,5},{2,6},{3,7},{4,0},{5,1},{6,2},{7,3},{8,12},{9,13},{10,... | collective-permute-start | bytes 98312 | tf_op jit(solution)/shard_map/ppermute | solution.py:199
  20.3 2.0 %collective-permute-done.8.refs_1_ = f32[32,256]{1,0:T(8,128)S(1)} collective-permute-done((f32[32,256]{1,0:T(8,128)S(1)}, f32[32,256]{1,0:T(8,128)S(1)}, u32[]{:S(2)}, u32[]{:S(2)}) %collective-permute-start.8) | collective-permute-done | bytes 32800 | tf_op jit(solution)/shard_map/ppermute | solution.py:199
  22.3 0.8 %shard_map.72 = (f32[32,256]{1,0:T(8,128)}, f32[32,256]{1,0:T(8,128)}) custom-call(bf16[32,1024]{1,0:T(8,128)(2,1)S(1)} %get-tuple-element.46.q_ref, f32[40,256]{1,0:T(8,128)S(1)} %get-tuple-element.29.refs_0_.refs_5_.near_ref, f32[32,32]{1,0:T(8,128)S(1)} %get-tuple-element.43.refs_4_.compat_ref, f32[32,256]{1,0:T(8,128)S(1)} %get-tuple-element.50.refs_0_, ...), custom_call_target="tpu_custom_call" | custom-call | flops 10000000000 | bytes 10000000000 | tf_op jit(solution)/shard_map/pallas_call | solution.py:221
  (10 shorter events, 0.1 us)
Async XLA Ops:
  1.7 6.5 %collective-permute-start = (f32[40,256]{1,0:T(8,128)S(1)}, f32[40,256]{1,0:T(8,128)S(1)}, u32[]{:S(2)}, u32[]{:S(2)}) collective-permute-start(f32[40,256]{1,0:T(8,128)S(1)} %get-tuple-element.29.refs_0_.refs_5_.near_ref), channel_id=1, source_target_pairs={{0,7},{1,6},{2,5},{3,4},{4,3},{5,2},{6,1},{7,0},{8,15},{9,14},{10,... | collective-permute-start | bytes 122888 | tf_op jit(solution)/shard_map/ppermute | solution.py:199
  6.2 4.6 %collective-permute-start.2 = (f32[40,256]{1,0:T(8,128)S(1)}, f32[40,256]{1,0:T(8,128)S(1)}, u32[]{:S(2)}, u32[]{:S(2)}) collective-permute-start(f32[40,256]{1,0:T(8,128)S(1)} %get-tuple-element.29.refs_0_.refs_5_.near_ref), channel_id=1, source_target_pairs={{0,6},{1,7},{2,4},{3,5},{4,2},{5,3},{6,0},{7,1},{8,14},{9,15},{10,... | collective-permute-start | bytes 122888 | tf_op jit(solution)/shard_map/ppermute | solution.py:199
  6.3 4.6 %collective-permute-start.1 = (f32[40,256]{1,0:T(8,128)S(1)}, f32[40,256]{1,0:T(8,128)S(1)}, u32[]{:S(2)}, u32[]{:S(2)}) collective-permute-start(f32[40,256]{1,0:T(8,128)S(1)} %get-tuple-element.29.refs_0_.refs_5_.near_ref), channel_id=1, source_target_pairs={{0,1},{1,0},{2,3},{3,2},{4,5},{5,4},{6,7},{7,6},{8,9},{9,8},{10,11... | collective-permute-start | bytes 122888 | tf_op jit(solution)/shard_map/ppermute | solution.py:199
  8.2 6.6 %collective-permute-start.3 = (bf16[2,40,256]{2,1,0:T(8,128)(2,1)S(1)}, bf16[2,40,256]{2,1,0:T(8,128)(2,1)S(1)}, u32[]{:S(2)}, u32[]{:S(2)}) collective-permute-start(bf16[2,40,256]{2,1,0:T(8,128)(2,1)S(1)} %get-tuple-element.31.packed_ref.refs_0_.refs_2_.refs_9_), channel_id=1, source_target_pairs={{0,12},{1,13},{2,14},{3,15},{4,8},{5,9},{6,10},{7,11},{8,4},{9,5},... | collective-permute-start | bytes 122888 | tf_op jit(solution)/shard_map/ppermute | solution.py:199
  10.9 3.9 %collective-permute-start.4 = (bf16[2,40,256]{2,1,0:T(8,128)(2,1)S(1)}, bf16[2,40,256]{2,1,0:T(8,128)(2,1)S(1)}, u32[]{:S(2)}, u32[]{:S(2)}) collective-permute-start(bf16[2,40,256]{2,1,0:T(8,128)(2,1)S(1)} %get-tuple-element.36.refs_1_.refs_3_.refs_10_), channel_id=1, source_target_pairs={{0,12},{1,13},{2,14},{3,15},{4,8},{5,9},{6,10},{7,11},{8,4},{9,5},... | collective-permute-start | bytes 122888 | tf_op jit(solution)/shard_map/ppermute | solution.py:199
  12.5 1.3 %collective-permute-start.5 = (bf16[4,40,256]{2,1,0:T(8,128)(2,1)S(1)}, bf16[4,40,256]{2,1,0:T(8,128)(2,1)S(1)}, u32[]{:S(2)}, u32[]{:S(2)}) collective-permute-start(bf16[4,40,256]{2,1,0:T(8,128)(2,1)S(1)} %shard_map.63), channel_id=1, source_target_pairs={{0,4},{1,5},{2,6},{3,7},{4,0},{5,1},{6,2},{7,3},{8,12},{9,13},{10,... | collective-permute-start | bytes 245768 | tf_op jit(solution)/shard_map/ppermute | solution.py:199
  14.9 1.3 %collective-permute-start.6 = (bf16[4,40,256]{2,1,0:T(8,128)(2,1)S(1)}, bf16[4,40,256]{2,1,0:T(8,128)(2,1)S(1)}, u32[]{:S(2)}, u32[]{:S(2)}) collective-permute-start(bf16[4,40,256]{2,1,0:T(8,128)(2,1)S(1)} %shard_map.66), channel_id=1, source_target_pairs={{0,4},{1,5},{2,6},{3,7},{4,0},{5,1},{6,2},{7,3},{8,12},{9,13},{10,... | collective-permute-start | bytes 245768 | tf_op jit(solution)/shard_map/ppermute | solution.py:199
  17.7 1.2 %collective-permute-start.7 = (f32[1,32,256]{2,1,0:T(8,128)S(1)}, f32[1,32,256]{2,1,0:T(8,128)S(1)}, u32[]{:S(2)}, u32[]{:S(2)}) collective-permute-start(f32[1,32,256]{2,1,0:T(8,128)S(1)} %shard_map.69), channel_id=1, source_target_pairs={{0,4},{1,5},{2,6},{3,7},{4,0},{5,1},{6,2},{7,3},{8,12},{9,13},{10,... | collective-permute-start | bytes 98312 | tf_op jit(solution)/shard_map/ppermute | solution.py:199
  19.0 3.3 %collective-permute-start.8 = (f32[32,256]{1,0:T(8,128)S(1)}, f32[32,256]{1,0:T(8,128)S(1)}, u32[]{:S(2)}, u32[]{:S(2)}) collective-permute-start(f32[32,256]{1,0:T(8,128)S(1)} %shard_map.71), channel_id=1, source_target_pairs={{0,12},{1,13},{2,14},{3,15},{4,8},{5,9},{6,10},{7,11},{8,4},{9,5},... | collective-permute-start | bytes 98312 | tf_op jit(solution)/shard_map/ppermute | solution.py:199
  20.0 2.3 %collective-permute-start.9 = (f32[32,256]{1,0:T(8,128)S(1)}, f32[32,256]{1,0:T(8,128)S(1)}, u32[]{:S(2)}, u32[]{:S(2)}) collective-permute-start(f32[32,256]{1,0:T(8,128)S(1)} %get-tuple-element.55), channel_id=1, source_target_pairs={{0,4},{1,5},{2,6},{3,7},{4,0},{5,1},{6,2},{7,3},{8,12},{9,13},{10,... | collective-permute-start | bytes 98312 | tf_op jit(solution)/shard_map/ppermute | solution.py:199

commit v29 on v28

--- a/solution.py
+++ b/solution.py
@@ -43,11 +43,19 @@
     return jnp.sum(jnp.where(group == (member // LANES)[None], found, 0.0), axis=0)
 
 
-def prepare_kernel(features_ref, member_ref, unary_ref, compat_ref, sent_ref, held_ref):
-    labels = unary_ref.shape[0]
-    sent_ref[pl.ds(0, labels), :] = unary_ref[...]
-    sent_ref[pl.ds(labels, 8), :] = pick_features(features_ref, member_ref[...])
+def prepare_kernel(
+    features_ref, member_ref, unary_ref, compat_ref, sent_ref, held_ref, held_unary_ref
+):
+    unary = unary_ref[...]
+    high, low, _ = three_parts(unary)
+    feats = pick_features(features_ref, member_ref[...])
+    sent_ref[...] = jnp.concatenate([high, low, feats], axis=0).astype(jnp.bfloat16)
     held_ref[...] = compat_ref[...]
+    held_unary_ref[...] = unary
+
+
+def unary_of(near, labels):
+    return near[:labels].astype(jnp.float32) + near[labels:2 * labels].astype(jnp.float32)
 
 
 def half_norms(feats):
@@ -68,8 +76,9 @@
     near_refs, packed_ref, rows_ref = refs[:-2], refs[-2], refs[-1]
     for place, near_ref in enumerate(near_refs):
         own = near_ref.shape[1]
-        feats = near_ref[pl.ds(labels, 8), :]
-        probs = normalize(-near_ref[pl.ds(0, labels), :])
+        near = near_ref[...]
+        feats = near[2 * labels:].astype(jnp.float32)
+        probs = normalize(-unary_of(near, labels))
         packed_ref[place] = jnp.concatenate([probs, feats], axis=0).astype(jnp.bfloat16)
         rows_ref[:, pl.ds(place * own, own)] = product_sides(feats)[1]
 
@@ -143,7 +152,7 @@
     own_refs, (q_ref, tile_ref) = refs[:-2], refs[-2:]
     total = first_part(labels, row_refs, stack_refs, sum_ref[...], tile_ref)
     labels_now = [ref[index][:labels] for ref in own_refs for index in range(ref.shape[0])]
-    unary = [near_ref[pl.ds(0, labels), :] for near_ref in near_refs]
+    unary = [unary_of(near_ref[...], labels) for near_ref in near_refs]
     probs, _ = finish(
         total, jnp.concatenate(labels_now, axis=1), jnp.concatenate(unary, axis=1), compat_ref
     )
@@ -179,7 +188,7 @@
     total = refs[0][...]
     for part_ref in refs[1:-2]:
         total = total + part_ref[...]
-    unary = near_ref[pl.ds(0, labels), :]
+    unary = near_ref[...]
     probs, pairwise = finish(total, q_ref[:, pl.ds(0, own)], unary, compat_ref)
     probs_ref[...] = probs
     pairwise_ref[...] = pairwise
@@ -244,9 +253,13 @@
     labels, own = unary.shape
     nears = lax.axis_size("grp")
     count = lax.axis_size("blk") * nears
-    sent, held = call(
+    sent, held, held_unary = call(
         prepare_kernel,
-        [kept((labels + 8, own), jnp.float32), kept(compat.shape, jnp.float32)],
+        [
+            kept((2 * labels + 8, own), jnp.bfloat16),
+            kept(compat.shape, jnp.float32),
+            kept(unary.shape, jnp.float32),
+        ],
         features, member[None], unary, compat,
     )
     near = group_partners(sent)
@@ -343,7 +356,7 @@
     return call(
         second_closing,
         [jax.ShapeDtypeStruct((labels, own), jnp.float32)] * 2,
-        *hold(q_near, sent, held, here, *arrived),
+        *hold(q_near, held_unary, held, here, *arrived),
     )
 
 

time: 23.3 us -> 23.2 us (level)
  no operation moved by 1% of the time
where the time goes in v29:
time: 23.2 us; the launch traced here: 23.1 us
  starting transfers between devices  10.6 us (46%)
  Pallas kernels  7.54 us (32%)
  waiting for transfers between devices  4.25 us (18%)
  between operations  0.69 us (3%)
    ppermute x10, starting transfers between devices, swap(): return lax.ppermute(value, ('blk', 'grp'), pairs)  10.6 us
    pallas_call x14, Pallas kernels, call(): pl.pallas_call(kernel, out_shape=tuple(out_shapes), cost_estimate=pl.Cost...  7.54 us
    ppermute x10, waiting for transfers between devices, swap(): return lax.ppermute(value, ('blk', 'grp'), pairs)  4.25 us
  transfers between devices with their start and end apart: 10, of which 5 were waited for; matrix products, arithmetic and copies ran while one was open for 0% of the time, Pallas kernels for 18%

profile of v29, /device:TPU:0, one launch (start us, length us, event | category | flops | bytes accessed | tf_op | source)
XLA Modules:
  0.0 23.1 jit_solution(16456978166951064000)
XLA Ops:
  0.6 1.1 %shard_map.59 = (bf16[72,256]{1,0:T(8,128)(2,1)S(1)}, f32[32,32]{1,0:T(8,128)S(1)}, f32[32,256]{1,0:T(8,128)S(1)}) custom-call(bf16[6,4096]{1,0:T(8,128)(2,1)} %features_ref.1, s32[1,256]{1,0:T(1,128)} %bitcast.1, f32[32,256]{1,0:T(8,128)} %unary_ref.1, f32[32,32]{1,0:T(8,128)} %compat_ref.1), custom_call_target="tpu_custom_call" | custom-call | flops 10000000000 | bytes 10000000000 | tf_op jit(solution)/shard_map/pallas_call | solution.py:230
  1.7 4.6 %collective-permute-start = (bf16[72,256]{1,0:T(8,128)(2,1)S(1)}, bf16[72,256]{1,0:T(8,128)(2,1)S(1)}, u32[]{:S(2)}, u32[]{:S(2)}) collective-permute-start(bf16[72,256]{1,0:T(8,128)(2,1)S(1)} %get-tuple-element.30.refs_0_.refs_5_), channel_id=1, source_target_pairs={{0,7},{1,6},{2,5},{3,4},{4,3},{5,2},{6,1},{7,0},{8,15},{9,14},{10,... | collective-permute-start | bytes 110600 | tf_op jit(solution)/shard_map/ppermute | solution.py:208
  6.3 0.6 %collective-permute-start.1 = (bf16[72,256]{1,0:T(8,128)(2,1)S(1)}, bf16[72,256]{1,0:T(8,128)(2,1)S(1)}, u32[]{:S(2)}, u32[]{:S(2)}) collective-permute-start(bf16[72,256]{1,0:T(8,128)(2,1)S(1)} %get-tuple-element.30.refs_0_.refs_5_), channel_id=1, source_target_pairs={{0,1},{1,0},{2,3},{3,2},{4,5},{5,4},{6,7},{7,6},{8,9},{9,8},{10,11... | collective-permute-start | bytes 110600 | tf_op jit(solution)/shard_map/ppermute | solution.py:208
  6.9 1.2 %collective-permute-done.refs_1_.refs_6_ = bf16[72,256]{1,0:T(8,128)(2,1)S(1)} collective-permute-done((bf16[72,256]{1,0:T(8,128)(2,1)S(1)}, bf16[72,256]{1,0:T(8,128)(2,1)S(1)}, u32[]{:S(2)}, u32[]{:S(2)}) %collective-permute-start) | collective-permute-done | bytes 36896 | tf_op jit(solution)/shard_map/ppermute | solution.py:208
  8.2 1.7 %collective-permute-start.3 = (bf16[2,40,256]{2,1,0:T(8,128)(2,1)S(1)}, bf16[2,40,256]{2,1,0:T(8,128)(2,1)S(1)}, u32[]{:S(2)}, u32[]{:S(2)}) collective-permute-start(bf16[2,40,256]{2,1,0:T(8,128)(2,1)S(1)} %get-tuple-element.32.packed_ref.refs_0_.refs_2_.refs_9_), channel_id=1, source_target_pairs={{0,12},{1,13},{2,14},{3,15},{4,8},{5,9},{6,10},{7,11},{8,4},{9,5},... | collective-permute-start | bytes 122888 | tf_op jit(solution)/shard_map/ppermute | solution.py:208
  9.9 0.5 %shard_map.61 = (f32[32,512]{1,0:T(8,128)S(1)}, bf16[256,512]{1,0:T(8,128)(2,1)S(1)}) custom-call(bf16[16,512]{1,0:T(8,128)(2,1)S(1)} %get-tuple-element.31.rows_ref.refs_0_, bf16[2,40,256]{2,1,0:T(8,128)(2,1)S(1)} %get-tuple-element.32.packed_ref.refs_0_.refs_2_.refs_9_), custom_call_target="tpu_custom_call" | custom-call | flops 10000000000 | bytes 10000000000 | tf_op jit(solution)/shard_map/pallas_call | solution.py:230
  10.4 0.4 %collective-permute-done.2.refs_1_.refs_8_ = bf16[72,256]{1,0:T(8,128)(2,1)S(1)} collective-permute-done((bf16[72,256]{1,0:T(8,128)(2,1)S(1)}, bf16[72,256]{1,0:T(8,128)(2,1)S(1)}, u32[]{:S(2)}, u32[]{:S(2)}) %collective-permute-start.2) | collective-permute-done | bytes 36896 | tf_op jit(solution)/shard_map/ppermute | solution.py:208
  10.8 1.6 %collective-permute-start.4 = (bf16[2,40,256]{2,1,0:T(8,128)(2,1)S(1)}, bf16[2,40,256]{2,1,0:T(8,128)(2,1)S(1)}, u32[]{:S(2)}, u32[]{:S(2)}) collective-permute-start(bf16[2,40,256]{2,1,0:T(8,128)(2,1)S(1)} %get-tuple-element.37.refs_1_.refs_3_.refs_10_), channel_id=1, source_target_pairs={{0,12},{1,13},{2,14},{3,15},{4,8},{5,9},{6,10},{7,11},{8,4},{9,5},... | collective-permute-start | bytes 122888 | tf_op jit(solution)/shard_map/ppermute | solution.py:208
  12.5 0.1 collective-permute-start.5
  12.5 1.0 %shard_map.64 = (f32[32,1024]{1,0:T(8,128)S(1)}, bf16[256,1024]{1,0:T(8,128)(2,1)S(1)}) custom-call(bf16[16,512]{1,0:T(8,128)(2,1)S(1)} %get-tuple-element.31.rows_ref.refs_0_, bf16[16,512]{1,0:T(8,128)(2,1)S(1)} %get-tuple-element.36.refs_1_, bf16[2,40,256]{2,1,0:T(8,128)(2,1)S(1)} %get-tuple-element.32.packed_ref.refs_0_.refs_2_.refs_9_, ...), custom_call_target="tpu_custom_call" | custom-call | flops 10000000000 | bytes 10000000000 | tf_op jit(solution)/shard_map/pallas_call | solution.py:230
  13.5 0.3 %collective-permute-done.5.refs_2_ = bf16[4,40,256]{2,1,0:T(8,128)(2,1)S(1)} collective-permute-done((bf16[4,40,256]{2,1,0:T(8,128)(2,1)S(1)}, bf16[4,40,256]{2,1,0:T(8,128)(2,1)S(1)}, u32[]{:S(2)}, u32[]{:S(2)}) %collective-permute-start.5) | collective-permute-done | bytes 81952 | tf_op jit(solution)/shard_map/ppermute | solution.py:208
  13.7 1.0 %shard_map.65 = (f32[32,1024]{1,0:T(8,128)S(1)}, bf16[256,1024]{1,0:T(8,128)(2,1)S(1)}) custom-call(bf16[16,512]{1,0:T(8,128)(2,1)S(1)} %get-tuple-element.31.rows_ref.refs_0_, bf16[16,512]{1,0:T(8,128)(2,1)S(1)} %get-tuple-element.36.refs_1_, bf16[4,40,256]{2,1,0:T(8,128)(2,1)S(1)} %collective-permute-done.5.refs_2_, f32[32,1024]{1,0:T(8,128)S(1)} %get-tuple-element.40.refs_3_), custom_call_target="tpu_custom_call" | custom-call | flops 10000000000 | bytes 10000000000 | tf_op jit(solution)/shard_map/pallas_call | solution.py:230
  14.8 0.3 %collective-permute-start.6 = (bf16[4,40,256]{2,1,0:T(8,128)(2,1)S(1)}, bf16[4,40,256]{2,1,0:T(8,128)(2,1)S(1)}, u32[]{:S(2)}, u32[]{:S(2)}) collective-permute-start(bf16[4,40,256]{2,1,0:T(8,128)(2,1)S(1)} %shard_map.66), channel_id=1, source_target_pairs={{0,4},{1,5},{2,6},{3,7},{4,0},{5,1},{6,2},{7,3},{8,12},{9,13},{10,... | collective-permute-start | bytes 245768 | tf_op jit(solution)/shard_map/ppermute | solution.py:208
  15.1 1.1 %shard_map.67 = (f32[32,1024]{1,0:T(8,128)S(1)}, bf16[256,1024]{1,0:T(8,128)(2,1)S(1)}) custom-call(bf16[16,512]{1,0:T(8,128)(2,1)S(1)} %get-tuple-element.31.rows_ref.refs_0_, bf16[16,512]{1,0:T(8,128)(2,1)S(1)} %get-tuple-element.36.refs_1_, bf16[2,40,256]{2,1,0:T(8,128)(2,1)S(1)} %collective-permute-done.3.refs_0_.refs_2_, ...), custom_call_target="tpu_custom_call" | custom-call | flops 10000000000 | bytes 10000000000 | tf_op jit(solution)/shard_map/pallas_call | solution.py:230
  16.1 0.0 collective-permute-done.6.refs_2_
  16.2 1.3 %shard_map.68 = (bf16[32,1024]{1,0:T(8,128)(2,1)S(1)}, bf16[256,1024]{1,0:T(8,128)(2,1)S(1)}) custom-call(bf16[16,512]{1,0:T(8,128)(2,1)S(1)} %get-tuple-element.31.rows_ref.refs_0_, bf16[16,512]{1,0:T(8,128)(2,1)S(1)} %get-tuple-element.36.refs_1_, bf16[4,40,256]{2,1,0:T(8,128)(2,1)S(1)} %collective-permute-done.6.refs_2_, ...), custom_call_target="tpu_custom_call" | custom-call | flops 10000000000 | bytes 10000000000 | tf_op jit(solution)/shard_map/pallas_call | solution.py:230
  17.4 0.2 %shard_map.69 = f32[1,32,256]{2,1,0:T(8,128)S(1)} custom-call(bf16[32,1024]{1,0:T(8,128)(2,1)S(1)} %get-tuple-element.47.q_ref, bf16[256,1024]{1,0:T(8,128)(2,1)S(1)} %get-tuple-element.46.refs_0_), custom_call_target="tpu_custom_call" | custom-call | flops 10000000000 | bytes 10000000000 | tf_op jit(solution)/shard_map/pallas_call | solution.py:230
  17.7 0.3 %collective-permute-start.7 = (f32[1,32,256]{2,1,0:T(8,128)S(1)}, f32[1,32,256]{2,1,0:T(8,128)S(1)}, u32[]{:S(2)}, u32[]{:S(2)}) collective-permute-start(f32[1,32,256]{2,1,0:T(8,128)S(1)} %shard_map.69), channel_id=1, source_target_pairs={{0,4},{1,5},{2,6},{3,7},{4,0},{5,1},{6,2},{7,3},{8,12},{9,13},{10,... | collective-permute-start | bytes 98312 | tf_op jit(solution)/shard_map/ppermute | solution.py:208
  18.0 0.5 %shard_map.70 = (f32[32,256]{1,0:T(8,128)S(1)}, f32[32,256]{1,0:T(8,128)S(1)}, f32[32,256]{1,0:T(8,128)S(1)}) custom-call(bf16[32,1024]{1,0:T(8,128)(2,1)S(1)} %get-tuple-element.47.q_ref, bf16[256,1024]{1,0:T(8,128)(2,1)S(1)} %get-tuple-element.49.refs_0_, bf16[256,1024]{1,0:T(8,128)(2,1)S(1)} %get-tuple-element.50.refs_1_, ...), custom_call_target="tpu_custom_call" | custom-call | flops 10000000000 | bytes 10000000000 | tf_op jit(solution)/shard_map/pallas_call | solution.py:230
  18.5 0.4 %collective-permute-done.7.given_ref = f32[1,32,256]{2,1,0:T(8,128)S(1)} collective-permute-done((f32[1,32,256]{2,1,0:T(8,128)S(1)}, f32[1,32,256]{2,1,0:T(8,128)S(1)}, u32[]{:S(2)}, u32[]{:S(2)}) %collective-permute-start.7) | collective-permute-done | bytes 32800 | tf_op jit(solution)/shard_map/ppermute | solution.py:208
  18.9 1.1 %collective-permute-start.8 = (f32[32,256]{1,0:T(8,128)S(1)}, f32[32,256]{1,0:T(8,128)S(1)}, u32[]{:S(2)}, u32[]{:S(2)}) collective-permute-start(f32[32,256]{1,0:T(8,128)S(1)} %shard_map.71), channel_id=1, source_target_pairs={{0,12},{1,13},{2,14},{3,15},{4,8},{5,9},{6,10},{7,11},{8,4},{9,5},... | collective-permute-start | bytes 98312 | tf_op jit(solution)/shard_map/ppermute | solution.py:208
  20.0 0.3 %collective-permute-start.9 = (f32[32,256]{1,0:T(8,128)S(1)}, f32[32,256]{1,0:T(8,128)S(1)}, u32[]{:S(2)}, u32[]{:S(2)}) collective-permute-start(f32[32,256]{1,0:T(8,128)S(1)} %get-tuple-element.57), channel_id=1, source_target_pairs={{0,4},{1,5},{2,6},{3,7},{4,0},{5,1},{6,2},{7,3},{8,12},{9,13},{10,... | collective-permute-start | bytes 98312 | tf_op jit(solution)/shard_map/ppermute | solution.py:208
  20.3 2.0 %collective-permute-done.8.refs_1_ = f32[32,256]{1,0:T(8,128)S(1)} collective-permute-done((f32[32,256]{1,0:T(8,128)S(1)}, f32[32,256]{1,0:T(8,128)S(1)}, u32[]{:S(2)}, u32[]{:S(2)}) %collective-permute-start.8) | collective-permute-done | bytes 32800 | tf_op jit(solution)/shard_map/ppermute | solution.py:208
  22.3 0.8 %shard_map.72 = (f32[32,256]{1,0:T(8,128)}, f32[32,256]{1,0:T(8,128)}) custom-call(bf16[32,1024]{1,0:T(8,128)(2,1)S(1)} %get-tuple-element.47.q_ref, f32[32,256]{1,0:T(8,128)S(1)} %get-tuple-element.48.near_ref, f32[32,32]{1,0:T(8,128)S(1)} %get-tuple-element.44.refs_4_.compat_ref, f32[32,256]{1,0:T(8,128)S(1)} %get-tuple-element.52.refs_0_, ...), custom_call_target="tpu_custom_call" | custom-call | flops 10000000000 | bytes 10000000000 | tf_op jit(solution)/shard_map/pallas_call | solution.py:230
  (10 shorter events, 0.1 us)
Async XLA Ops:
  1.7 6.4 %collective-permute-start = (bf16[72,256]{1,0:T(8,128)(2,1)S(1)}, bf16[72,256]{1,0:T(8,128)(2,1)S(1)}, u32[]{:S(2)}, u32[]{:S(2)}) collective-permute-start(bf16[72,256]{1,0:T(8,128)(2,1)S(1)} %get-tuple-element.30.refs_0_.refs_5_), channel_id=1, source_target_pairs={{0,7},{1,6},{2,5},{3,4},{4,3},{5,2},{6,1},{7,0},{8,15},{9,14},{10,... | collective-permute-start | bytes 110600 | tf_op jit(solution)/shard_map/ppermute | solution.py:208
  6.2 4.5 %collective-permute-start.2 = (bf16[72,256]{1,0:T(8,128)(2,1)S(1)}, bf16[72,256]{1,0:T(8,128)(2,1)S(1)}, u32[]{:S(2)}, u32[]{:S(2)}) collective-permute-start(bf16[72,256]{1,0:T(8,128)(2,1)S(1)} %get-tuple-element.30.refs_0_.refs_5_), channel_id=1, source_target_pairs={{0,6},{1,7},{2,4},{3,5},{4,2},{5,3},{6,0},{7,1},{8,14},{9,15},{10,... | collective-permute-start | bytes 110600 | tf_op jit(solution)/shard_map/ppermute | solution.py:208
  6.3 4.5 %collective-permute-start.1 = (bf16[72,256]{1,0:T(8,128)(2,1)S(1)}, bf16[72,256]{1,0:T(8,128)(2,1)S(1)}, u32[]{:S(2)}, u32[]{:S(2)}) collective-permute-start(bf16[72,256]{1,0:T(8,128)(2,1)S(1)} %get-tuple-element.30.refs_0_.refs_5_), channel_id=1, source_target_pairs={{0,1},{1,0},{2,3},{3,2},{4,5},{5,4},{6,7},{7,6},{8,9},{9,8},{10,11... | collective-permute-start | bytes 110600 | tf_op jit(solution)/shard_map/ppermute | solution.py:208
  8.2 6.6 %collective-permute-start.3 = (bf16[2,40,256]{2,1,0:T(8,128)(2,1)S(1)}, bf16[2,40,256]{2,1,0:T(8,128)(2,1)S(1)}, u32[]{:S(2)}, u32[]{:S(2)}) collective-permute-start(bf16[2,40,256]{2,1,0:T(8,128)(2,1)S(1)} %get-tuple-element.32.packed_ref.refs_0_.refs_2_.refs_9_), channel_id=1, source_target_pairs={{0,12},{1,13},{2,14},{3,15},{4,8},{5,9},{6,10},{7,11},{8,4},{9,5},... | collective-permute-start | bytes 122888 | tf_op jit(solution)/shard_map/ppermute | solution.py:208
  10.8 4.0 %collective-permute-start.4 = (bf16[2,40,256]{2,1,0:T(8,128)(2,1)S(1)}, bf16[2,40,256]{2,1,0:T(8,128)(2,1)S(1)}, u32[]{:S(2)}, u32[]{:S(2)}) collective-permute-start(bf16[2,40,256]{2,1,0:T(8,128)(2,1)S(1)} %get-tuple-element.37.refs_1_.refs_3_.refs_10_), channel_id=1, source_target_pairs={{0,12},{1,13},{2,14},{3,15},{4,8},{5,9},{6,10},{7,11},{8,4},{9,5},... | collective-permute-start | bytes 122888 | tf_op jit(solution)/shard_map/ppermute | solution.py:208
  12.5 1.3 %collective-permute-start.5 = (bf16[4,40,256]{2,1,0:T(8,128)(2,1)S(1)}, bf16[4,40,256]{2,1,0:T(8,128)(2,1)S(1)}, u32[]{:S(2)}, u32[]{:S(2)}) collective-permute-start(bf16[4,40,256]{2,1,0:T(8,128)(2,1)S(1)} %shard_map.63), channel_id=1, source_target_pairs={{0,4},{1,5},{2,6},{3,7},{4,0},{5,1},{6,2},{7,3},{8,12},{9,13},{10,... | collective-permute-start | bytes 245768 | tf_op jit(solution)/shard_map/ppermute | solution.py:208
  14.8 1.3 %collective-permute-start.6 = (bf16[4,40,256]{2,1,0:T(8,128)(2,1)S(1)}, bf16[4,40,256]{2,1,0:T(8,128)(2,1)S(1)}, u32[]{:S(2)}, u32[]{:S(2)}) collective-permute-start(bf16[4,40,256]{2,1,0:T(8,128)(2,1)S(1)} %shard_map.66), channel_id=1, source_target_pairs={{0,4},{1,5},{2,6},{3,7},{4,0},{5,1},{6,2},{7,3},{8,12},{9,13},{10,... | collective-permute-start | bytes 245768 | tf_op jit(solution)/shard_map/ppermute | solution.py:208
  17.7 1.2 %collective-permute-start.7 = (f32[1,32,256]{2,1,0:T(8,128)S(1)}, f32[1,32,256]{2,1,0:T(8,128)S(1)}, u32[]{:S(2)}, u32[]{:S(2)}) collective-permute-start(f32[1,32,256]{2,1,0:T(8,128)S(1)} %shard_map.69), channel_id=1, source_target_pairs={{0,4},{1,5},{2,6},{3,7},{4,0},{5,1},{6,2},{7,3},{8,12},{9,13},{10,... | collective-permute-start | bytes 98312 | tf_op jit(solution)/shard_map/ppermute | solution.py:208
  18.9 3.3 %collective-permute-start.8 = (f32[32,256]{1,0:T(8,128)S(1)}, f32[32,256]{1,0:T(8,128)S(1)}, u32[]{:S(2)}, u32[]{:S(2)}) collective-permute-start(f32[32,256]{1,0:T(8,128)S(1)} %shard_map.71), channel_id=1, source_target_pairs={{0,12},{1,13},{2,14},{3,15},{4,8},{5,9},{6,10},{7,11},{8,4},{9,5},... | collective-permute-start | bytes 98312 | tf_op jit(solution)/shard_map/ppermute | solution.py:208
  20.0 2.3 %collective-permute-start.9 = (f32[32,256]{1,0:T(8,128)S(1)}, f32[32,256]{1,0:T(8,128)S(1)}, u32[]{:S(2)}, u32[]{:S(2)}) collective-permute-start(f32[32,256]{1,0:T(8,128)S(1)} %get-tuple-element.57), channel_id=1, source_target_pairs={{0,4},{1,5},{2,6},{3,7},{4,0},{5,1},{6,2},{7,3},{8,12},{9,13},{10,... | collective-permute-start | bytes 98312 | tf_op jit(solution)/shard_map/ppermute | solution.py:208

commit v30 on v29

--- a/solution.py
+++ b/solution.py
@@ -131,10 +131,15 @@
 def first_opening(labels, *refs):
     near_rows, rest_rows, near_ref, rest_ref, sum_ref, early_tile_ref, total_ref, tile_ref = refs
     near, rest = near_rows.shape[1], rest_rows.shape[1]
-    beyond = first_part(
-        labels, [rest_rows], [near_ref], jnp.zeros((labels, rest), jnp.float32),
-        tile_ref.at[:, pl.ds(near, rest)],
-    )
+    blocks, _, own = near_ref.shape
+    packed = jnp.concatenate([near_ref[index] for index in range(blocks)], axis=1)
+    columns = product_sides(packed[labels:].astype(jnp.float32))[0]
+    exponent = lax.dot_general(
+        columns, rest_rows[...], (((0,), (0,)), ((), ())), preferred_element_type=jnp.float32
+    )
+    tile = jnp.exp(exponent).astype(jnp.bfloat16)
+    tile_ref[:, pl.ds(near, rest)] = tile[:own]
+    beyond = jnp.dot(packed[:labels], tile, preferred_element_type=jnp.float32)
     tile_ref[:, pl.ds(0, near)] = early_tile_ref[...]
     start = jnp.concatenate([sum_ref[...], beyond], axis=1)
     total_ref[...] = first_part(labels, [near_rows, rest_rows], [rest_ref], start, None)

time: 23.2 us -> 23.2 us (level)
  transfers between devices with their start and end apart: 10 -> 10, of which waited for: 5 -> 6; matrix products, arithmetic and copies ran while one was open for 0% -> 0% of each run, Pallas kernels for 18% -> 18%
where the time goes in v30:
time: 23.2 us; the launch traced here: 23.1 us
  starting transfers between devices  10.6 us (46%)
  Pallas kernels  7.5 us (32%)
  waiting for transfers between devices  4.32 us (19%)
  between operations  0.69 us (3%)
    ppermute x10, starting transfers between devices, swap(): return lax.ppermute(value, ('blk', 'grp'), pairs)  10.6 us
    pallas_call x14, Pallas kernels, call(): pl.pallas_call(kernel, out_shape=tuple(out_shapes), cost_estimate=pl.Cost...  7.5 us
    ppermute x10, waiting for transfers between devices, swap(): return lax.ppermute(value, ('blk', 'grp'), pairs)  4.32 us
  transfers between devices with their start and end apart: 10, of which 6 were waited for; matrix products, arithmetic and copies ran while one was open for 0% of the time, Pallas kernels for 18%

profile of v30, /device:TPU:0, one launch (start us, length us, event | category | flops | bytes accessed | tf_op | source)
XLA Modules:
  0.0 23.1 jit_solution(14086830022240277732)
XLA Ops:
  0.6 1.1 %shard_map.59 = (bf16[72,256]{1,0:T(8,128)(2,1)S(1)}, f32[32,32]{1,0:T(8,128)S(1)}, f32[32,256]{1,0:T(8,128)S(1)}) custom-call(bf16[6,4096]{1,0:T(8,128)(2,1)} %features_ref.1, s32[1,256]{1,0:T(1,128)} %bitcast.1, f32[32,256]{1,0:T(8,128)} %unary_ref.1, f32[32,32]{1,0:T(8,128)} %compat_ref.1), custom_call_target="tpu_custom_call" | custom-call | flops 10000000000 | bytes 10000000000 | tf_op jit(solution)/shard_map/pallas_call | solution.py:235
  1.7 4.6 %collective-permute-start = (bf16[72,256]{1,0:T(8,128)(2,1)S(1)}, bf16[72,256]{1,0:T(8,128)(2,1)S(1)}, u32[]{:S(2)}, u32[]{:S(2)}) collective-permute-start(bf16[72,256]{1,0:T(8,128)(2,1)S(1)} %get-tuple-element.30.refs_0_.refs_5_), channel_id=1, source_target_pairs={{0,7},{1,6},{2,5},{3,4},{4,3},{5,2},{6,1},{7,0},{8,15},{9,14},{10,... | collective-permute-start | bytes 110600 | tf_op jit(solution)/shard_map/ppermute | solution.py:213
  6.3 0.6 %collective-permute-start.1 = (bf16[72,256]{1,0:T(8,128)(2,1)S(1)}, bf16[72,256]{1,0:T(8,128)(2,1)S(1)}, u32[]{:S(2)}, u32[]{:S(2)}) collective-permute-start(bf16[72,256]{1,0:T(8,128)(2,1)S(1)} %get-tuple-element.30.refs_0_.refs_5_), channel_id=1, source_target_pairs={{0,1},{1,0},{2,3},{3,2},{4,5},{5,4},{6,7},{7,6},{8,9},{9,8},{10,11... | collective-permute-start | bytes 110600 | tf_op jit(solution)/shard_map/ppermute | solution.py:213
  6.9 1.2 %collective-permute-done.refs_1_.refs_6_ = bf16[72,256]{1,0:T(8,128)(2,1)S(1)} collective-permute-done((bf16[72,256]{1,0:T(8,128)(2,1)S(1)}, bf16[72,256]{1,0:T(8,128)(2,1)S(1)}, u32[]{:S(2)}, u32[]{:S(2)}) %collective-permute-start) | collective-permute-done | bytes 36896 | tf_op jit(solution)/shard_map/ppermute | solution.py:213
  8.2 1.7 %collective-permute-start.3 = (bf16[2,40,256]{2,1,0:T(8,128)(2,1)S(1)}, bf16[2,40,256]{2,1,0:T(8,128)(2,1)S(1)}, u32[]{:S(2)}, u32[]{:S(2)}) collective-permute-start(bf16[2,40,256]{2,1,0:T(8,128)(2,1)S(1)} %get-tuple-element.32.packed_ref.refs_0_.refs_2_.refs_9_), channel_id=1, source_target_pairs={{0,12},{1,13},{2,14},{3,15},{4,8},{5,9},{6,10},{7,11},{8,4},{9,5},... | collective-permute-start | bytes 122888 | tf_op jit(solution)/shard_map/ppermute | solution.py:213
  9.9 0.5 %shard_map.61 = (f32[32,512]{1,0:T(8,128)S(1)}, bf16[256,512]{1,0:T(8,128)(2,1)S(1)}) custom-call(bf16[16,512]{1,0:T(8,128)(2,1)S(1)} %get-tuple-element.31.rows_ref.refs_0_, bf16[2,40,256]{2,1,0:T(8,128)(2,1)S(1)} %get-tuple-element.32.packed_ref.refs_0_.refs_2_.refs_9_), custom_call_target="tpu_custom_call" | custom-call | flops 10000000000 | bytes 10000000000 | tf_op jit(solution)/shard_map/pallas_call | solution.py:235
  10.4 0.4 %collective-permute-done.2.refs_1_.refs_8_ = bf16[72,256]{1,0:T(8,128)(2,1)S(1)} collective-permute-done((bf16[72,256]{1,0:T(8,128)(2,1)S(1)}, bf16[72,256]{1,0:T(8,128)(2,1)S(1)}, u32[]{:S(2)}, u32[]{:S(2)}) %collective-permute-start.2) | collective-permute-done | bytes 36896 | tf_op jit(solution)/shard_map/ppermute | solution.py:213
  10.8 1.6 %collective-permute-start.4 = (bf16[2,40,256]{2,1,0:T(8,128)(2,1)S(1)}, bf16[2,40,256]{2,1,0:T(8,128)(2,1)S(1)}, u32[]{:S(2)}, u32[]{:S(2)}) collective-permute-start(bf16[2,40,256]{2,1,0:T(8,128)(2,1)S(1)} %get-tuple-element.37.refs_1_.refs_3_.refs_10_), channel_id=1, source_target_pairs={{0,12},{1,13},{2,14},{3,15},{4,8},{5,9},{6,10},{7,11},{8,4},{9,5},... | collective-permute-start | bytes 122888 | tf_op jit(solution)/shard_map/ppermute | solution.py:213
  12.5 0.1 collective-permute-start.5
  12.5 0.9 %shard_map.64 = (f32[32,1024]{1,0:T(8,128)S(1)}, bf16[256,1024]{1,0:T(8,128)(2,1)S(1)}) custom-call(bf16[16,512]{1,0:T(8,128)(2,1)S(1)} %get-tuple-element.31.rows_ref.refs_0_, bf16[16,512]{1,0:T(8,128)(2,1)S(1)} %get-tuple-element.36.refs_1_, bf16[2,40,256]{2,1,0:T(8,128)(2,1)S(1)} %get-tuple-element.32.packed_ref.refs_0_.refs_2_.refs_9_, ...), custom_call_target="tpu_custom_call" | custom-call | flops 10000000000 | bytes 10000000000 | tf_op jit(solution)/shard_map/pallas_call | solution.py:235
  13.4 0.3 %collective-permute-done.5.refs_2_ = bf16[4,40,256]{2,1,0:T(8,128)(2,1)S(1)} collective-permute-done((bf16[4,40,256]{2,1,0:T(8,128)(2,1)S(1)}, bf16[4,40,256]{2,1,0:T(8,128)(2,1)S(1)}, u32[]{:S(2)}, u32[]{:S(2)}) %collective-permute-start.5) | collective-permute-done | bytes 81952 | tf_op jit(solution)/shard_map/ppermute | solution.py:213
  13.7 1.0 %shard_map.65 = (f32[32,1024]{1,0:T(8,128)S(1)}, bf16[256,1024]{1,0:T(8,128)(2,1)S(1)}) custom-call(bf16[16,512]{1,0:T(8,128)(2,1)S(1)} %get-tuple-element.31.rows_ref.refs_0_, bf16[16,512]{1,0:T(8,128)(2,1)S(1)} %get-tuple-element.36.refs_1_, bf16[4,40,256]{2,1,0:T(8,128)(2,1)S(1)} %collective-permute-done.5.refs_2_, f32[32,1024]{1,0:T(8,128)S(1)} %get-tuple-element.40.refs_3_), custom_call_target="tpu_custom_call" | custom-call | flops 10000000000 | bytes 10000000000 | tf_op jit(solution)/shard_map/pallas_call | solution.py:235
  14.8 0.2 %collective-permute-start.6 = (bf16[4,40,256]{2,1,0:T(8,128)(2,1)S(1)}, bf16[4,40,256]{2,1,0:T(8,128)(2,1)S(1)}, u32[]{:S(2)}, u32[]{:S(2)}) collective-permute-start(bf16[4,40,256]{2,1,0:T(8,128)(2,1)S(1)} %shard_map.66), channel_id=1, source_target_pairs={{0,4},{1,5},{2,6},{3,7},{4,0},{5,1},{6,2},{7,3},{8,12},{9,13},{10,... | collective-permute-start | bytes 245768 | tf_op jit(solution)/shard_map/ppermute | solution.py:213
  15.1 1.1 %shard_map.67 = (f32[32,1024]{1,0:T(8,128)S(1)}, bf16[256,1024]{1,0:T(8,128)(2,1)S(1)}) custom-call(bf16[16,512]{1,0:T(8,128)(2,1)S(1)} %get-tuple-element.31.rows_ref.refs_0_, bf16[16,512]{1,0:T(8,128)(2,1)S(1)} %get-tuple-element.36.refs_1_, bf16[2,40,256]{2,1,0:T(8,128)(2,1)S(1)} %collective-permute-done.3.refs_0_.refs_2_, ...), custom_call_target="tpu_custom_call" | custom-call | flops 10000000000 | bytes 10000000000 | tf_op jit(solution)/shard_map/pallas_call | solution.py:235
  16.1 0.1 collective-permute-done.6.refs_2_
  16.2 1.3 %shard_map.68 = (bf16[32,1024]{1,0:T(8,128)(2,1)S(1)}, bf16[256,1024]{1,0:T(8,128)(2,1)S(1)}) custom-call(bf16[16,512]{1,0:T(8,128)(2,1)S(1)} %get-tuple-element.31.rows_ref.refs_0_, bf16[16,512]{1,0:T(8,128)(2,1)S(1)} %get-tuple-element.36.refs_1_, bf16[4,40,256]{2,1,0:T(8,128)(2,1)S(1)} %collective-permute-done.6.refs_2_, ...), custom_call_target="tpu_custom_call" | custom-call | flops 10000000000 | bytes 10000000000 | tf_op jit(solution)/shard_map/pallas_call | solution.py:235
  17.4 0.2 %shard_map.69 = f32[1,32,256]{2,1,0:T(8,128)S(1)} custom-call(bf16[32,1024]{1,0:T(8,128)(2,1)S(1)} %get-tuple-element.47.q_ref, bf16[256,1024]{1,0:T(8,128)(2,1)S(1)} %get-tuple-element.46.refs_0_), custom_call_target="tpu_custom_call" | custom-call | flops 10000000000 | bytes 10000000000 | tf_op jit(solution)/shard_map/pallas_call | solution.py:235
  17.7 0.3 %collective-permute-start.7 = (f32[1,32,256]{2,1,0:T(8,128)S(1)}, f32[1,32,256]{2,1,0:T(8,128)S(1)}, u32[]{:S(2)}, u32[]{:S(2)}) collective-permute-start(f32[1,32,256]{2,1,0:T(8,128)S(1)} %shard_map.69), channel_id=1, source_target_pairs={{0,4},{1,5},{2,6},{3,7},{4,0},{5,1},{6,2},{7,3},{8,12},{9,13},{10,... | collective-permute-start | bytes 98312 | tf_op jit(solution)/shard_map/ppermute | solution.py:213
  18.0 0.5 %shard_map.70 = (f32[32,256]{1,0:T(8,128)S(1)}, f32[32,256]{1,0:T(8,128)S(1)}, f32[32,256]{1,0:T(8,128)S(1)}) custom-call(bf16[32,1024]{1,0:T(8,128)(2,1)S(1)} %get-tuple-element.47.q_ref, bf16[256,1024]{1,0:T(8,128)(2,1)S(1)} %get-tuple-element.49.refs_0_, bf16[256,1024]{1,0:T(8,128)(2,1)S(1)} %get-tuple-element.50.refs_1_, ...), custom_call_target="tpu_custom_call" | custom-call | flops 10000000000 | bytes 10000000000 | tf_op jit(solution)/shard_map/pallas_call | solution.py:235
  18.5 0.4 %collective-permute-done.7.given_ref = f32[1,32,256]{2,1,0:T(8,128)S(1)} collective-permute-done((f32[1,32,256]{2,1,0:T(8,128)S(1)}, f32[1,32,256]{2,1,0:T(8,128)S(1)}, u32[]{:S(2)}, u32[]{:S(2)}) %collective-permute-start.7) | collective-permute-done | bytes 32800 | tf_op jit(solution)/shard_map/ppermute | solution.py:213
  18.9 1.1 %collective-permute-start.8 = (f32[32,256]{1,0:T(8,128)S(1)}, f32[32,256]{1,0:T(8,128)S(1)}, u32[]{:S(2)}, u32[]{:S(2)}) collective-permute-start(f32[32,256]{1,0:T(8,128)S(1)} %shard_map.71), channel_id=1, source_target_pairs={{0,12},{1,13},{2,14},{3,15},{4,8},{5,9},{6,10},{7,11},{8,4},{9,5},... | collective-permute-start | bytes 98312 | tf_op jit(solution)/shard_map/ppermute | solution.py:213
  20.0 0.3 %collective-permute-start.9 = (f32[32,256]{1,0:T(8,128)S(1)}, f32[32,256]{1,0:T(8,128)S(1)}, u32[]{:S(2)}, u32[]{:S(2)}) collective-permute-start(f32[32,256]{1,0:T(8,128)S(1)} %get-tuple-element.57), channel_id=1, source_target_pairs={{0,4},{1,5},{2,6},{3,7},{4,0},{5,1},{6,2},{7,3},{8,12},{9,13},{10,... | collective-permute-start | bytes 98312 | tf_op jit(solution)/shard_map/ppermute | solution.py:213
  20.3 2.0 %collective-permute-done.8.refs_1_ = f32[32,256]{1,0:T(8,128)S(1)} collective-permute-done((f32[32,256]{1,0:T(8,128)S(1)}, f32[32,256]{1,0:T(8,128)S(1)}, u32[]{:S(2)}, u32[]{:S(2)}) %collective-permute-start.8) | collective-permute-done | bytes 32800 | tf_op jit(solution)/shard_map/ppermute | solution.py:213
  22.3 0.8 %shard_map.72 = (f32[32,256]{1,0:T(8,128)}, f32[32,256]{1,0:T(8,128)}) custom-call(bf16[32,1024]{1,0:T(8,128)(2,1)S(1)} %get-tuple-element.47.q_ref, f32[32,256]{1,0:T(8,128)S(1)} %get-tuple-element.48.near_ref, f32[32,32]{1,0:T(8,128)S(1)} %get-tuple-element.44.refs_4_.compat_ref, f32[32,256]{1,0:T(8,128)S(1)} %get-tuple-element.52.refs_0_, ...), custom_call_target="tpu_custom_call" | custom-call | flops 10000000000 | bytes 10000000000 | tf_op jit(solution)/shard_map/pallas_call | solution.py:235
  (10 shorter events, 0.1 us)
Async XLA Ops:
  1.7 6.4 %collective-permute-start = (bf16[72,256]{1,0:T(8,128)(2,1)S(1)}, bf16[72,256]{1,0:T(8,128)(2,1)S(1)}, u32[]{:S(2)}, u32[]{:S(2)}) collective-permute-start(bf16[72,256]{1,0:T(8,128)(2,1)S(1)} %get-tuple-element.30.refs_0_.refs_5_), channel_id=1, source_target_pairs={{0,7},{1,6},{2,5},{3,4},{4,3},{5,2},{6,1},{7,0},{8,15},{9,14},{10,... | collective-permute-start | bytes 110600 | tf_op jit(solution)/shard_map/ppermute | solution.py:213
  6.2 4.5 %collective-permute-start.2 = (bf16[72,256]{1,0:T(8,128)(2,1)S(1)}, bf16[72,256]{1,0:T(8,128)(2,1)S(1)}, u32[]{:S(2)}, u32[]{:S(2)}) collective-permute-start(bf16[72,256]{1,0:T(8,128)(2,1)S(1)} %get-tuple-element.30.refs_0_.refs_5_), channel_id=1, source_target_pairs={{0,6},{1,7},{2,4},{3,5},{4,2},{5,3},{6,0},{7,1},{8,14},{9,15},{10,... | collective-permute-start | bytes 110600 | tf_op jit(solution)/shard_map/ppermute | solution.py:213
  6.3 4.5 %collective-permute-start.1 = (bf16[72,256]{1,0:T(8,128)(2,1)S(1)}, bf16[72,256]{1,0:T(8,128)(2,1)S(1)}, u32[]{:S(2)}, u32[]{:S(2)}) collective-permute-start(bf16[72,256]{1,0:T(8,128)(2,1)S(1)} %get-tuple-element.30.refs_0_.refs_5_), channel_id=1, source_target_pairs={{0,1},{1,0},{2,3},{3,2},{4,5},{5,4},{6,7},{7,6},{8,9},{9,8},{10,11... | collective-permute-start | bytes 110600 | tf_op jit(solution)/shard_map/ppermute | solution.py:213
  8.2 6.6 %collective-permute-start.3 = (bf16[2,40,256]{2,1,0:T(8,128)(2,1)S(1)}, bf16[2,40,256]{2,1,0:T(8,128)(2,1)S(1)}, u32[]{:S(2)}, u32[]{:S(2)}) collective-permute-start(bf16[2,40,256]{2,1,0:T(8,128)(2,1)S(1)} %get-tuple-element.32.packed_ref.refs_0_.refs_2_.refs_9_), channel_id=1, source_target_pairs={{0,12},{1,13},{2,14},{3,15},{4,8},{5,9},{6,10},{7,11},{8,4},{9,5},... | collective-permute-start | bytes 122888 | tf_op jit(solution)/shard_map/ppermute | solution.py:213
  10.8 4.0 %collective-permute-start.4 = (bf16[2,40,256]{2,1,0:T(8,128)(2,1)S(1)}, bf16[2,40,256]{2,1,0:T(8,128)(2,1)S(1)}, u32[]{:S(2)}, u32[]{:S(2)}) collective-permute-start(bf16[2,40,256]{2,1,0:T(8,128)(2,1)S(1)} %get-tuple-element.37.refs_1_.refs_3_.refs_10_), channel_id=1, source_target_pairs={{0,12},{1,13},{2,14},{3,15},{4,8},{5,9},{6,10},{7,11},{8,4},{9,5},... | collective-permute-start | bytes 122888 | tf_op jit(solution)/shard_map/ppermute | solution.py:213
  12.5 1.3 %collective-permute-start.5 = (bf16[4,40,256]{2,1,0:T(8,128)(2,1)S(1)}, bf16[4,40,256]{2,1,0:T(8,128)(2,1)S(1)}, u32[]{:S(2)}, u32[]{:S(2)}) collective-permute-start(bf16[4,40,256]{2,1,0:T(8,128)(2,1)S(1)} %shard_map.63), channel_id=1, source_target_pairs={{0,4},{1,5},{2,6},{3,7},{4,0},{5,1},{6,2},{7,3},{8,12},{9,13},{10,... | collective-permute-start | bytes 245768 | tf_op jit(solution)/shard_map/ppermute | solution.py:213
  14.8 1.3 %collective-permute-start.6 = (bf16[4,40,256]{2,1,0:T(8,128)(2,1)S(1)}, bf16[4,40,256]{2,1,0:T(8,128)(2,1)S(1)}, u32[]{:S(2)}, u32[]{:S(2)}) collective-permute-start(bf16[4,40,256]{2,1,0:T(8,128)(2,1)S(1)} %shard_map.66), channel_id=1, source_target_pairs={{0,4},{1,5},{2,6},{3,7},{4,0},{5,1},{6,2},{7,3},{8,12},{9,13},{10,... | collective-permute-start | bytes 245768 | tf_op jit(solution)/shard_map/ppermute | solution.py:213
  17.7 1.2 %collective-permute-start.7 = (f32[1,32,256]{2,1,0:T(8,128)S(1)}, f32[1,32,256]{2,1,0:T(8,128)S(1)}, u32[]{:S(2)}, u32[]{:S(2)}) collective-permute-start(f32[1,32,256]{2,1,0:T(8,128)S(1)} %shard_map.69), channel_id=1, source_target_pairs={{0,4},{1,5},{2,6},{3,7},{4,0},{5,1},{6,2},{7,3},{8,12},{9,13},{10,... | collective-permute-start | bytes 98312 | tf_op jit(solution)/shard_map/ppermute | solution.py:213
  18.9 3.3 %collective-permute-start.8 = (f32[32,256]{1,0:T(8,128)S(1)}, f32[32,256]{1,0:T(8,128)S(1)}, u32[]{:S(2)}, u32[]{:S(2)}) collective-permute-start(f32[32,256]{1,0:T(8,128)S(1)} %shard_map.71), channel_id=1, source_target_pairs={{0,12},{1,13},{2,14},{3,15},{4,8},{5,9},{6,10},{7,11},{8,4},{9,5},... | collective-permute-start | bytes 98312 | tf_op jit(solution)/shard_map/ppermute | solution.py:213
  20.0 2.3 %collective-permute-start.9 = (f32[32,256]{1,0:T(8,128)S(1)}, f32[32,256]{1,0:T(8,128)S(1)}, u32[]{:S(2)}, u32[]{:S(2)}) collective-permute-start(f32[32,256]{1,0:T(8,128)S(1)} %get-tuple-element.57), channel_id=1, source_target_pairs={{0,4},{1,5},{2,6},{3,7},{4,0},{5,1},{6,2},{7,3},{8,12},{9,13},{10,... | collective-permute-start | bytes 98312 | tf_op jit(solution)/shard_map/ppermute | solution.py:213
